TPU v7x, 32 devices: a whole 2x2x4 slice. The times are simulated.
32 devices in a mesh: expert: 4 (over y, x), rows: 8 (over z, core).
Axes of the slice: x: 2, y: 2, z: 4, core: 2. Of those that a mesh axis runs over, the one named last changes fastest.
Arguments:
- expert_inputs: bfloat16 [65536, 768], P(('expert', 'rows')), may hold values from -54 to 54
- row_expert: int32 [65536, 1], P(('expert', 'rows')), may hold values from 0 to 7; in each aligned block of 2048 rows (0 to 2047, 2048 to 4095, ...) at most 256 rows name the same one
- down_weight: bfloat16 [8, 2048, 768], P('expert', 'rows'), may hold values from -6 to 6
- keep_mask: bfloat16 [8, 2048, 768], P('expert', 'rows'), may hold values from 0 to 1, as said below
Outputs:
- pruned: float32 [8, 2048, 768], P('expert', 'rows')
Inputs may be any that keep to these rules, and one draw needn't show every extreme that they name: `row_expert`: at most 256 of the 2048 rows of one device name the same expert, and in every draw some device names some expert exactly 256 times; every expert is named by some row. `keep_mask`: every entry is 0 or 1.
All inputs are finite; a program needn't handle non-finite values.
Results may differ from a plain program's by a relative error of at most 0.0003.
Values may be sent and summed in bfloat16 or wider, within the bound.
No kernel may reach another device: no remote copies, remote signals or barrier semaphores. Data moves between devices by JAX's collectives and lax.ppermute only.
A program may use at most 64 MiB of HBM per device.

v0:
```python
import jax
import jax.numpy as jnp
from jax import lax
from jax.sharding import PartitionSpec as P

STEPS = 4


relax_factor = 0.5
diagonal_eps = 1e-06


def on_device(expert_inputs, row_expert, down_weight, keep_mask):
    tokens_dev, hidden_dim = expert_inputs.shape
    experts_dev = down_weight.shape[0]
    expert_count = lax.axis_size("expert")
    all_experts = experts_dev * expert_count
    capacity = tokens_dev // 8
    owners = row_expert[:, 0]
    labels = jnp.arange(all_experts, dtype=jnp.int32)
    onehot = (owners[:, None] == labels[None, :]).astype(jnp.int32)
    before = jnp.cumsum(onehot, axis=0) - onehot
    position = jnp.sum(before * onehot, axis=1)
    target = owners * capacity + position
    outgoing = (
        jnp.zeros((all_experts * capacity, hidden_dim), jnp.bfloat16).at[target].set(expert_inputs)
    )
    outgoing = outgoing.reshape(all_experts, capacity, hidden_dim)
    arrived = lax.all_to_all(outgoing, "expert", split_axis=0, concat_axis=1, tiled=True)
    gram_full = lax.psum(
        jnp.einsum("esi,esj->iej", arrived, arrived, preferred_element_type=jnp.float32), "rows"
    )
    inverse = 1.0 / (jnp.diagonal(gram_full, axis1=0, axis2=2) + diagonal_eps)
    target_weight = down_weight.astype(jnp.float32)
    keep_float = keep_mask.astype(jnp.float32)
    pruned = keep_float * target_weight
    for sweep in range(STEPS):
        gradient = jnp.einsum(
            "ecj,jei->eci",
            pruned - target_weight,
            gram_full,
            precision=lax.Precision.HIGHEST,
            preferred_element_type=jnp.float32,
        )
        pruned = keep_float * (pruned - relax_factor * gradient * inverse[:, None, :])
    return pruned


def solution(mesh):
    return jax.shard_map(
        on_device,
        mesh=mesh,
        in_specs=(
            P(("expert", "rows"), None),
            P(("expert", "rows"), None),
            P("expert", "rows", None),
            P("expert", "rows", None),
        ),
        out_specs=P("expert", "rows", None),
        check_vma=False,
    )
```

profile of v0, /device:TPU:0, one launch (start us, length us, event | category | flops | bytes accessed | tf_op | source)
XLA Modules:
  0.0 219.0 jit_solution(8423012439922586230)
XLA Ops:
  6.5 0.0 all-reduce.2.cloned.1.call-start
  6.5 0.7 fusion.12
  7.2 2.3 %reduce-window.6 = s32[8,16,128]{2,1,0:T(8,128)S(1)} reduce-window(s32[8,16,128]{2,1,0:T(8,128)S(1)} %fusion.12, s32[]{:T(128)} %constant.6.clone.1), window={size=1x1x128 pad=0_0x0_0x127_0}, to_apply=%region_0.0 | reduce-window | flops 2080768 | bytes 131076 | tf_op jit(solution)/shard_map/reduce-window
  9.5 0.3 slice_reduce_fusion
  9.8 0.2 reduce-window.9
  10.0 0.1 add_bitcast_fusion
  10.1 0.7 fusion.11
  10.8 0.7 compare_select_fusion
  11.5 11.2 %scatter_custom_fusion = bf16[2048,768]{1,0:T(8,128)(2,1)S(1)} fusion(s32[2048]{0:T(1024)S(1)} %bitcast.49, bf16[2048,768]{1,0:T(8,128)(2,1)} %param.4, bf16[]{:T(256)} %constant.7.clone.1), kind=kCustom, calls=%fused_computation.17 | custom fusion | bytes 3146240 | tf_op jit(solution)/shard_map/scatter | solution.py:26
  22.8 41.6 %all_to_all.18 = bf16[8,256,768]{2,1,0:T(8,128)(2,1)S(1)} all-to-all(bf16[8,256,768]{2,1,0:T(8,128)(2,1)S(1)} %bitcast.42), channel_id=1, replica_groups=mesh['expert'=4,'rows'=8] {'expert'}, dimensions={0} | all-to-all | bytes 6291456 | tf_op jit(solution)/shard_map/all_to_all | solution.py:29
  64.3 0.2 copy.11
  64.6 4.5 %convolution_bitcast_fusion = f32[768,2,768]{0,2,1:T(8,128)} fusion(bf16[2,1024,768]{2,1,0:T(8,128)(2,1)S(1)} %bitcast.44), kind=kOutput, calls=%fused_computation.11 | convolution fusion | flops 2415919104 | bytes 7864320 | tf_op jit(solution)/shard_map/esi,esj->iej/dot_general | solution.py:31
  69.0 0.0 all-reduce.2.cloned.1.call-update
  69.1 106.2 %all-reduce.2.cloned.1.call-done = f32[768,2,768]{0,2,1:T(8,128)} async-done(((f32[768,2,768]{0,2,1:T(8,128)}), f32[768,2,768]{0,2,1:T(8,128)}) %all-reduce.2.cloned.1.call-update) | async-done | bytes 4718608 | tf_op jit(solution)/shard_map/psum | solution.py:30
  175.3 0.0 copy-start
  175.3 0.0 copy-start.1
  175.3 8.3 %copy.14 = f32[2,768,768]{2,0,1:T(2,128)} copy(f32[2,768,768]{1,2,0:T(8,128)} %bitcast.39) | data formatting | bytes 9437184 | tf_op jit(solution)/shard_map/jit(diagonal)/transpose | solution.py:33
  183.7 0.0 slice-start
  183.7 6.9 %gather_fusion = f32[768,2]{0,1:T(2,128)S(1)} fusion(f32[2,768,768]{2,0,1:T(2,128)} %copy.14, s32[768]{0:T(1024)S(1)} %or_reduce_fusion), kind=kCustom, calls=%fused_computation | custom fusion | bytes 18432 | tf_op jit(solution)/shard_map/jit(diagonal)/gather | solution.py:33
  190.6 0.0 copy-done
  190.6 0.0 copy-done.1
  190.6 0.0 slice-start.1
  190.7 6.7 %fusion.1 = f32[2,256,768]{2,1,0:T(8,128)S(1)} fusion(f32[768,2,768]{0,2,1:T(8,128)} %all-reduce.2.cloned.1.call-done, bf16[2,256,768]{2,1,0:T(8,128)(2,1)S(1)} %copy-done, bf16[2,256,768]{2,1,0:T(8,128)(2,1)S(1)} %copy-done.1), kind=kOutput, calls=%fused_computation.13 | convolution fusion | flops 3625451520 | bytes 7864320 | tf_op jit(solution)/shard_map/ecj,jei->eci/dot_general | solution.py:38
  197.3 0.0 slice-done
  197.3 0.0 slice-done.1
  197.4 4.7 %convert_multiply_fusion.3 = f32[2,256,768]{2,1,0:T(8,128)S(1)} fusion(bf16[2,256,768]{2,1,0:T(8,128)(2,1)S(1)} %copy-done.1, f32[768,2,768]{0,2,1:T(8,128)S(1)} %bitcast.41, bf16[2,256,768]{2,1,0:T(8,128)(2,1)S(1)} %copy-done, f32[2,256,768]{2,1,0:T(8,128)S(1)} %fusion.1, f32[2,768]{1,0:T(2,128)S(1)} %multiply_bitcast_fusion), kind=kOutput, calls=%fused_computation.9 | convolution fusion | flops 3630170112 | bytes 9443328 | tf_op jit(solution)/shard_map/ecj,jei->eci/dot_general | solution.py:38
  202.1 4.2 %fusion.3 = f32[2,256,768]{2,1,0:T(8,128)S(1)} fusion(f32[768,2,768]{0,2,1:T(8,128)S(1)} %bitcast.41, f32[2,256,768]{2,1,0:T(8,128)S(1)} %convert_multiply_fusion.3, bf16[2,256,768]{2,1,0:T(8,128)(2,1)S(1)} %copy-done), kind=kOutput, calls=%fused_computation.15 | convolution fusion | flops 3624665088 | bytes 8650752 | tf_op jit(solution)/shard_map/ecj,jei->eci/dot_general | solution.py:38
  206.3 5.8 %convert_multiply_fusion.1 = f32[2,256,768]{2,1,0:T(8,128)} fusion(bf16[2,256,768]{2,1,0:T(8,128)(2,1)S(1)} %copy-done.1, f32[768,2,768]{0,2,1:T(8,128)S(1)} %bitcast.41, bf16[2,256,768]{2,1,0:T(8,128)(2,1)S(1)} %copy-done, f32[2,256,768]{2,1,0:T(8,128)S(1)} %convert_multiply_fusion.3, f32[2,256,768]{2,1,0:T(8,128)S(1)} %fusion.3, ...), kind=kOutput, calls=%fused_computation.7 | convolution fusion | flops 3628990464 | bytes 11016192 | tf_op jit(solution)/shard_map/ecj,jei->eci/dot_general | solution.py:38
  (3 shorter events, 0.0 us)
Async XLA Ops:
  6.5 168.8 %all-reduce.2.cloned.1.call-start = ((), (), s32[]{:S(2)}) async-start(), calls=%async_computation.1 | async-start | bytes 9437184 | tf_op jit(solution)/shard_map/psum | solution.py:30
  175.3 15.3 %copy-start = (bf16[2,256,768]{2,1,0:T(8,128)(2,1)S(1)}, bf16[2,256,768]{2,1,0:T(8,128)(2,1)}, u32[]{:S(2)}) copy-start(bf16[2,256,768]{2,1,0:T(8,128)(2,1)} %param.6) | copy-start | bytes 2359300
  175.3 15.3 %copy-start.1 = (bf16[2,256,768]{2,1,0:T(8,128)(2,1)S(1)}, bf16[2,256,768]{2,1,0:T(8,128)(2,1)}, u32[]{:S(2)}) copy-start(bf16[2,256,768]{2,1,0:T(8,128)(2,1)} %param.7) | copy-start | bytes 2359300
  183.7 13.7 %slice-start = ((s8[4718592]{0:T(1024)(128)(4,1)}), s8[524288]{0:T(1024)(128)(4,1)S(1)}, s32[]{:S(2)}) async-start(s8[4718592]{0:T(1024)(128)(4,1)} %bitcast.40), calls=%async_computation.2 | async-start | bytes 1048576
  190.6 6.7 %slice-start.1 = ((s8[4718592]{0:T(1024)(128)(4,1)}), s8[4194304]{0:T(1024)(128)(4,1)S(1)}, s32[]{:S(2)}) async-start(s8[4718592]{0:T(1024)(128)(4,1)} %bitcast.40), calls=%async_computation.3 | async-start | bytes 8388608
Sparse Core Ops, SparseCore 0:
  69.2 106.0 all-reduce.1
where the time goes:
time: 220 us; the launch traced here: 219 us
  waiting for transfers between devices  106 us (48%)
  blocking collectives  41.6 us (19%)
  local copies, waits for them, and re-layouts  27 us (12%)
  matrix products  25.9 us (12%)
  between operations  13.5 us (6%)
  other arithmetic  4.71 us (2%)
    psum x1, waiting for transfers between devices, on_device(): lax.psum(jnp.einsum('esi,esj->iej', arrived, arrived, preferred_element_t...  106 us
    all_to_all x1, blocking collectives, on_device(): lax.all_to_all(outgoing, 'expert', split_axis=0, concat_axis=1, tiled=True)  41.6 us
    dot_general x4, matrix products, on_device(): jnp.einsum('ecj,jei->eci', pruned - target_weight, gram_full, precision=l...  21.4 us
    scatter x1, local copies, waits for them, and re-layouts, on_device(): jnp.zeros((all_experts * capacity, hidden_dim), jnp.bfloat16).at[target]  11.2 us
    transpose x1, local copies, waits for them, and re-layouts, on_device(): inverse = 1.0 / (jnp.diagonal(gram_full, axis1=0, axis2=2) + diagonal_eps)  8.32 us
    gather x1, local copies, waits for them, and re-layouts, on_device(): inverse = 1.0 / (jnp.diagonal(gram_full, axis1=0, axis2=2) + diagonal_eps)  6.95 us
    dot_general x1, matrix products, on_device(): jnp.einsum('esi,esj->iej', arrived, arrived, preferred_element_type=jnp.f...  4.48 us
  transfers between devices with their start and end apart: 1, of which 1 were waited for; matrix products, arithmetic and copies ran while one was open for 0% of the time, Pallas kernels for 0%

commit v1 on v0

v1 whole, which is shorter than its diff:
```python
import functools

import jax
import jax.numpy as jnp
from jax import lax
from jax.experimental import pallas as pl
from jax.experimental.pallas import tpu as pltpu
from jax.sharding import PartitionSpec as P

STEPS = 4
BLOCK = 128
relax_factor = 0.5
diagonal_eps = 1e-06
VMEM_LIMIT = 50 * 2**20

VMEM = pl.BlockSpec(memory_space=pltpu.VMEM)
SMEM = pl.BlockSpec(memory_space=pltpu.SMEM)
F32, BF16, I32 = jnp.float32, jnp.bfloat16, jnp.int32


def call(kernel, out_shape, in_specs, scratch=(), flops=0, moved=0, out_specs=None, aliases=None, name=None):
    many = isinstance(out_shape, (list, tuple))
    return pl.pallas_call(
        kernel,
        out_shape=out_shape,
        in_specs=in_specs,
        out_specs=out_specs if out_specs is not None else ([VMEM] * len(out_shape) if many else VMEM),
        scratch_shapes=list(scratch),
        input_output_aliases=aliases or {},
        cost_estimate=pl.CostEstimate(flops=flops, bytes_accessed=moved, transcendentals=0),
        compiler_params=pltpu.CompilerParams(vmem_limit_bytes=VMEM_LIMIT),
        name=name,
    )


def slots_of(owners, experts, capacity):
    tokens = owners.shape[1]
    lanes = 128
    blocks = tokens // lanes
    named = owners == lax.broadcasted_iota(I32, (experts, tokens), 0)
    ones = named.astype(F32)
    stacked = jnp.concatenate([ones[:, b * lanes:(b + 1) * lanes] for b in range(blocks)], axis=0)
    upto = lax.broadcasted_iota(I32, (lanes, lanes), 0) <= lax.broadcasted_iota(I32, (lanes, lanes), 1)
    within = jnp.dot(stacked.astype(BF16), upto.astype(F32).astype(BF16), preferred_element_type=F32)
    carry = jnp.zeros((experts, 1), F32)
    parts = []
    for b in range(blocks):
        part = within[b * experts:(b + 1) * experts]
        parts.append(part + carry)
        carry = carry + part[:, lanes - 1:lanes]
    counted = jnp.concatenate(parts, axis=1)
    rank = jnp.sum(jnp.where(named, counted - 1.0, 0.0), axis=0, keepdims=True)
    return owners * capacity + rank.astype(I32)


def place(key, rows_ref, experts, capacity, out_refs):
    tokens, hidden = rows_ref.shape
    places = lax.broadcasted_iota(I32, (capacity, tokens), 0)
    chosen = jnp.concatenate(
        [(places == key - e * capacity).astype(F32).astype(BF16) for e in experts], axis=0
    )
    width = 256
    for c in range(0, hidden, width):
        got = jnp.dot(chosen, rows_ref[:, c:c + width], preferred_element_type=F32).astype(BF16)
        for k, out_ref in enumerate(out_refs):
            out_ref[:, c:c + width] = got[k * capacity:(k + 1) * capacity]


def first_kernel(peers, slots, all_experts, capacity, me_ref, owner_ref, rows_ref, key_ref, *out_refs):
    me = me_ref[0]
    key = slots_of(owner_ref[...], all_experts, capacity)
    key_ref[...] = key
    place(key, rows_ref, [lax.bitwise_xor(me, k) * slots for k in range(1, peers)], capacity, out_refs)


def second_kernel(peers, slots, capacity, me_ref, key_ref, rows_ref, *out_refs):
    me = me_ref[0]
    experts = [me * slots + a for a in range(slots)]
    for a in range(1, slots):
        experts += [lax.bitwise_xor(me, k) * slots + a for k in range(1, peers)]
    place(key_ref[...], rows_ref, experts, capacity, out_refs)


def upper(blocks):
    return [(i, j) for i in range(blocks) for j in range(i, blocks)]


def gram_kernel(pieces, bit, where_ref, *refs):
    chunk_refs, (keep_ref, send_ref, packed) = refs[:pieces], refs[pieces:]
    hidden = chunk_refs[0].shape[1]
    blocks = hidden // BLOCK
    at = {pair: n for n, pair in enumerate(upper(blocks))}
    x = jnp.concatenate([r[...] for r in chunk_refs], axis=0)
    strip = 2 * BLOCK if blocks % 2 == 0 else BLOCK
    for s in range(0, hidden, strip):
        product = lax.dot_general(
            x[:, s:s + strip], x[:, s:], (((0,), (0,)), ((), ())), preferred_element_type=F32
        )
        for i in range(strip // BLOCK):
            for j in range((hidden - s) // BLOCK):
                pair = (s // BLOCK + i, s // BLOCK + j)
                if pair in at:
                    n = at[pair]
                    packed[n * BLOCK:(n + 1) * BLOCK] = product[i * BLOCK:(i + 1) * BLOCK, j * BLOCK:(j + 1) * BLOCK]
    half = keep_ref.shape[0]
    mine = lax.bitwise_and(lax.shift_right_logical(where_ref[0], bit), 1)
    keep_ref[...] = packed[pl.ds(pl.multiple_of(mine * half, 8), half)]
    send_ref[...] = packed[pl.ds(pl.multiple_of((1 - mine) * half, 8), half)]


def halve_kernel(bit, where_ref, keep_ref, got_ref, keep_out, send_out):
    half = keep_out.shape[0]
    mine = lax.bitwise_and(lax.shift_right_logical(where_ref[0], bit), 1)
    ours = pl.ds(pl.multiple_of(mine * half, 8), half)
    theirs = pl.ds(pl.multiple_of((1 - mine) * half, 8), half)
    keep_out[...] = keep_ref[ours] + got_ref[ours]
    send_out[...] = keep_ref[theirs] + got_ref[theirs]


def add_kernel(a_ref, b_ref, out_ref):
    out_ref[...] = a_ref[...] + b_ref[...]


def steps_kernel(bits, flips, where_ref, weight_ref, mask_ref, *refs):
    pieces = len(flips)
    piece_refs = refs[:pieces]
    out_ref, packed, high, low, scale = refs[-5:]
    hidden = weight_ref.shape[-1]
    blocks = hidden // BLOCK
    size = piece_refs[0].shape[0]
    where = where_ref[0]
    for flip, piece_ref in zip(flips, piece_refs):
        owner = lax.bitwise_xor(where, flip)
        start = 0
        length = size * pieces
        for b in range(bits):
            length = length // 2
            start = start + lax.bitwise_and(lax.shift_right_logical(owner, b), 1) * length
        packed[pl.ds(pl.multiple_of(start, 8), size)] = piece_ref[...]
    eye = lax.broadcasted_iota(I32, (BLOCK, BLOCK), 0) == lax.broadcasted_iota(I32, (BLOCK, BLOCK), 1)
    for n, (i, j) in enumerate(upper(blocks)):
        block = packed[n * BLOCK:(n + 1) * BLOCK]
        rows, cols = slice(i * BLOCK, (i + 1) * BLOCK), slice(j * BLOCK, (j + 1) * BLOCK)
        hi = block.astype(BF16)
        high[rows, cols] = hi
        low[rows, cols] = (block - hi.astype(F32)).astype(BF16)
        if i == j:
            diagonal = jnp.sum(jnp.where(eye, block, 0.0), axis=0, keepdims=True)
            scale[:, cols] = relax_factor * (1.0 / (diagonal + diagonal_eps))
        else:
            block = block.T
            hi = block.astype(BF16)
            high[cols, rows] = hi
            low[cols, rows] = (block - hi.astype(F32)).astype(BF16)
    weight = weight_ref[0].astype(F32)
    keep = mask_ref[0].astype(F32)
    factor = scale[...]
    pruned = keep * weight
    for sweep in range(STEPS):
        change = pruned - weight
        top = change.astype(BF16)
        if sweep == 0:
            gradient = jnp.dot(top, high[...], preferred_element_type=F32)
        else:
            rest = (change - top.astype(F32)).astype(BF16)
            both = jnp.dot(jnp.concatenate([top, rest], axis=0), high[...], preferred_element_type=F32)
            gradient = both[:top.shape[0]] + both[top.shape[0]:]
        gradient = gradient + jnp.dot(top, low[...], preferred_element_type=F32)
        pruned = keep * (pruned - gradient * factor)
    out_ref[0] = pruned


def on_device(expert_inputs, row_expert, down_weight, keep_mask):
    tokens, hidden = expert_inputs.shape
    slots, features, _ = down_weight.shape
    peers = lax.axis_size("expert")
    copies = lax.axis_size("rows")
    all_experts = slots * peers
    capacity = tokens // 8
    bits = copies.bit_length() - 1
    me = jnp.reshape(lax.axis_index("expert").astype(I32), (1,))
    where = jnp.reshape(lax.axis_index("rows").astype(I32), (1,))
    owners = row_expert.reshape(1, tokens)

    def over(axis, size, array, flip):
        return lax.ppermute(array, axis, [(i, i ^ flip) for i in range(size)])

    chunk = jax.ShapeDtypeStruct((capacity, hidden), BF16)
    place_flops = 2 * capacity * tokens * hidden
    sent_first = peers - 1
    key, *outgoing = call(
        functools.partial(first_kernel, peers, slots, all_experts, capacity),
        [jax.ShapeDtypeStruct((1, tokens), I32)] + [chunk] * sent_first,
        [SMEM, VMEM, VMEM], flops=place_flops * sent_first, moved=expert_inputs.size * 4, name="place_first",
    )(me, owners, expert_inputs)
    arrived = [[over("expert", peers, outgoing[k - 1], k) for k in range(1, peers)]]
    count = slots + (slots - 1) * (peers - 1)
    rest = call(
        functools.partial(second_kernel, peers, slots, capacity),
        [chunk] * count,
        [SMEM, VMEM, VMEM], flops=place_flops * count, moved=expert_inputs.size * 4, name="place_rest",
    )(me, key, expert_inputs)
    own = rest[:slots]
    for a in range(1, slots):
        outgoing = rest[slots + (a - 1) * (peers - 1):slots + a * (peers - 1)]
        arrived.append([over("expert", peers, outgoing[k - 1], k) for k in range(1, peers)])

    blocks = hidden // BLOCK
    packed_rows = len(upper(blocks)) * BLOCK
    result = None
    for a in range(slots):
        size = packed_rows // 2
        keep, send = call(
            functools.partial(gram_kernel, peers, 0),
            [jax.ShapeDtypeStruct((size, BLOCK), F32)] * 2,
            [SMEM] + [VMEM] * peers,
            scratch=[pltpu.VMEM((packed_rows, BLOCK), F32)],
            flops=2 * capacity * peers * hidden * hidden, moved=packed_rows * BLOCK * 4, name=f"gram_{a}",
        )(where, own[a], *arrived[a])
        for bit in range(1, bits - 1):
            got = over("rows", copies, send, 1 << (bit - 1))
            size = size // 2
            keep, send = call(
                functools.partial(halve_kernel, bit),
                [jax.ShapeDtypeStruct((size, BLOCK), F32)] * 2,
                [SMEM, VMEM, VMEM], moved=size * BLOCK * 4 * 6, name=f"halve_{a}_{bit}",
            )(where, keep, got)
        got = over("rows", copies, send, 1 << (bits - 2))
        whole = call(
            add_kernel, jax.ShapeDtypeStruct((size, BLOCK), F32), [VMEM, VMEM], moved=size * BLOCK * 12,
            name=f"sum_{a}",
        )(keep, got)
        last = over("rows", copies, whole, 1 << (bits - 1))
        whole = call(
            add_kernel, jax.ShapeDtypeStruct((size, BLOCK), F32), [VMEM, VMEM], moved=size * BLOCK * 12,
            name=f"total_{a}",
        )(whole, last)
        held = [(0, whole)]
        for bit in range(bits - 2, -1, -1):
            held += [(flip ^ (1 << bit), over("rows", copies, piece, 1 << bit)) for flip, piece in held]
        pieces = [piece for _, piece in held]
        flips = [flip for flip, _ in held]
        out_spec = pl.BlockSpec((1, features, hidden), functools.partial(lambda a, i: (a, 0, 0), a))
        in_specs = [SMEM, out_spec, out_spec] + [pl.BlockSpec(p.shape, lambda i: (0, 0)) for p in pieces]
        args = [where, down_weight, keep_mask] + pieces
        aliases = {}
        if result is not None:
            in_specs.append(pl.BlockSpec(memory_space=pl.ANY))
            aliases = {len(args): 0}
            args.append(result)
        result = pl.pallas_call(
            functools.partial(steps_kernel, bits - 1, flips),
            out_shape=jax.ShapeDtypeStruct((slots, features, hidden), F32),
            grid=(1,),
            in_specs=in_specs,
            out_specs=out_spec,
            scratch_shapes=[
                pltpu.VMEM((packed_rows, BLOCK), F32),
                pltpu.VMEM((hidden, hidden), BF16),
                pltpu.VMEM((hidden, hidden), BF16),
                pltpu.VMEM((1, hidden), F32),
            ],
            input_output_aliases=aliases,
            cost_estimate=pl.CostEstimate(
                flops=2 * 11 * features * hidden * hidden, bytes_accessed=packed_rows * BLOCK * 4, transcendentals=0
            ),
            compiler_params=pltpu.CompilerParams(vmem_limit_bytes=VMEM_LIMIT),
            name=f"steps_{a}",
        )(*args)
    return result


def solution(mesh):
    return jax.shard_map(
        on_device,
        mesh=mesh,
        in_specs=(
            P(("expert", "rows"), None),
            P(("expert", "rows"), None),
            P("expert", "rows", None),
            P("expert", "rows", None),
        ),
        out_specs=P("expert", "rows", None),
        check_vma=False,
    )
```

time: 220 us -> 117 us (0.53)
  blocking collectives: 41.6 us -> 0 us
  waiting for transfers between devices: 106 us -> 68.6 us
  Pallas kernels: 0 us -> 27.2 us
  matrix products: 25.9 us -> 0 us
  local copies, waits for them, and re-layouts: 27 us -> 3.21 us
  starting transfers between devices: 0.01 us -> 17.2 us
  between operations: 13.5 us -> 0.11 us
  other arithmetic: 4.71 us -> 0 us
    psum x1 -> x0, waiting for transfers between devices: 106 us -> none  [on_device(): lax.psum(jnp.einsum('esi,esj->iej', arrived, arrived, preferred_element_t...]
    ppermute x0 -> x18, waiting for transfers between devices: none -> 68.6 us  [over(): return lax.ppermute(array, axis, [(i, i ^ flip) for i in range(size)])]
    all_to_all x1 -> x0, blocking collectives: 41.6 us -> none  [on_device(): lax.all_to_all(outgoing, 'expert', split_axis=0, concat_axis=1, tiled=True)]
    pallas_call x0 -> x12, Pallas kernels: none -> 27.2 us  [the longest x2 11.6 us: on_device(): pl.pallas_call(functools.partial(steps_kernel, bits - 1, flips), out_shap...]
    dot_general x5 -> x0, matrix products: 25.9 us -> none  [the longest x4 21.4 us: on_device(): jnp.einsum('ecj,jei->eci', pruned - target_weight, gram_full, precision=l...]
    ppermute x0 -> x18, starting transfers between devices: none -> 17.2 us  [over(): return lax.ppermute(array, axis, [(i, i ^ flip) for i in range(size)])]
    scatter x1 -> x0, local copies, waits for them, and re-layouts: 11.2 us -> none  [on_device(): jnp.zeros((all_experts * capacity, hidden_dim), jnp.bfloat16).at[target]]
    transpose x1 -> x0, local copies, waits for them, and re-layouts: 8.32 us -> none  [on_device(): inverse = 1.0 / (jnp.diagonal(gram_full, axis1=0, axis2=2) + diagonal_eps)]
  transfers between devices with their start and end apart: 1 -> 18, of which waited for: 1 -> 11; matrix products, arithmetic and copies ran while one was open for 0% -> 0% of each run, Pallas kernels for 0% -> 14%
where the time goes in v1:
time: 117 us; the launch traced here: 116 us
  waiting for transfers between devices  68.6 us (59%)
  Pallas kernels  27.2 us (23%)
  starting transfers between devices  17.2 us (15%)
  local copies, waits for them, and re-layouts  3.21 us (3%)
    ppermute x18, waiting for transfers between devices, over(): return lax.ppermute(array, axis, [(i, i ^ flip) for i in range(size)])  68.6 us
    ppermute x18, starting transfers between devices, over(): return lax.ppermute(array, axis, [(i, i ^ flip) for i in range(size)])  17.2 us
    pallas_call x2, Pallas kernels, on_device(): pl.pallas_call(functools.partial(steps_kernel, bits - 1, flips), out_shap...  11.6 us
    pallas_call x1, Pallas kernels, on_device(): call(functools.partial(second_kernel, peers, slots, capacity), [chunk] *...  6.16 us
    pallas_call x1, Pallas kernels, on_device(): call(functools.partial(first_kernel, peers, slots, all_experts, capacity)...  4.7 us
    pallas_call x2, Pallas kernels, on_device(): call(functools.partial(gram_kernel, peers, 0), [jax.ShapeDtypeStruct((siz...  4.44 us
    unnamed x14, local copies, waits for them, and re-layouts  3.21 us
  transfers between devices with their start and end apart: 18, of which 11 were waited for; matrix products, arithmetic and copies ran while one was open for 0% of the time, Pallas kernels for 14%

profile of v1, /device:TPU:0, one launch (start us, length us, event | category | flops | bytes accessed | tf_op | source)
XLA Modules:
  0.0 116.4 jit_solution(240553825543166630)
XLA Ops:
  0.0 0.0 copy-start.2
  0.0 0.7 copy-done.2
  0.7 4.7 %place_first.1 = (s32[1,2048]{1,0:T(1,128)S(1)}, bf16[256,768]{1,0:T(8,128)(2,1)S(1)}, bf16[256,768]{1,0:T(8,128)(2,1)S(1)}, bf16[256,768]{1,0:T(8,128)(2,1)S(1)}) custom-call(s32[1]{0:T(128)} %bitcast.1.me_ref, s32[1,2048]{1,0:T(1,128)S(1)} %bitcast.3, bf16[2048,768]{1,0:T(8,128)(2,1)} %rows_ref.3), custom_call_target="tpu_custom_call" | custom-call | flops 2415919104 | bytes 6291456 | tf_op jit(solution)/shard_map/place_first/pallas_call | solution.py:191
  5.4 3.0 %collective-permute-start.9 = (bf16[256,768]{1,0:T(8,128)(2,1)S(1)}, bf16[256,768]{1,0:T(8,128)(2,1)S(1)}, u32[]{:S(2)}, u32[]{:S(2)}) collective-permute-start(bf16[256,768]{1,0:T(8,128)(2,1)S(1)} %get-tuple-element.32), channel_id=1, source_target_pairs={{0,8},{8,0},{16,24},{24,16},{1,9},{9,1},{17,25},{25,17},{2,10},{10... | collective-permute-start | bytes 1179656 | tf_op jit(solution)/shard_map/ppermute | solution.py:186
  8.4 1.5 %collective-permute-start.10 = (bf16[256,768]{1,0:T(8,128)(2,1)S(1)}, bf16[256,768]{1,0:T(8,128)(2,1)S(1)}, u32[]{:S(2)}, u32[]{:S(2)}) collective-permute-start(bf16[256,768]{1,0:T(8,128)(2,1)S(1)} %get-tuple-element.33), channel_id=1, source_target_pairs={{0,16},{8,24},{16,0},{24,8},{1,17},{9,25},{17,1},{25,9},{2,18},{10... | collective-permute-start | bytes 1179656 | tf_op jit(solution)/shard_map/ppermute | solution.py:186
  9.9 0.0 collective-permute-start.11
  9.9 6.2 %place_rest.1 = (bf16[256,768]{1,0:T(8,128)(2,1)S(1)}, bf16[256,768]{1,0:T(8,128)(2,1)S(1)}, bf16[256,768]{1,0:T(8,128)(2,1)S(1)}, bf16[256,768]{1,0:T(8,128)(2,1)S(1)}, bf16[256,768]{1,0:T(8,128)(2,1)S(1)}) custom-call(s32[1]{0:T(128)} %bitcast.1.me_ref, s32[1,2048]{1,0:T(1,128)S(1)} %get-tuple-element.22.key_ref, bf16[2048,768]{1,0:T(8,128)(2,1)} %rows_ref.3), custom_call_target="tpu_custom_call" | custom-call | flops 4026531840 | bytes 6291456 | tf_op jit(solution)/shard_map/place_rest/pallas_call | solution.py:198
  16.1 0.0 copy-start.3
  16.1 0.7 copy-done.3
  16.9 0.0 copy-start.5
  16.9 0.8 copy-done.5
  17.6 1.9 %collective-permute-start = (bf16[256,768]{1,0:T(8,128)(2,1)S(1)}, bf16[256,768]{1,0:T(8,128)(2,1)S(1)}, u32[]{:S(2)}, u32[]{:S(2)}) collective-permute-start(bf16[256,768]{1,0:T(8,128)(2,1)S(1)} %get-tuple-element.24), channel_id=1, source_target_pairs={{0,8},{8,0},{16,24},{24,16},{1,9},{9,1},{17,25},{25,17},{2,10},{10... | collective-permute-start | bytes 1179656 | tf_op jit(solution)/shard_map/ppermute | solution.py:186
  19.6 1.5 %collective-permute-start.1 = (bf16[256,768]{1,0:T(8,128)(2,1)S(1)}, bf16[256,768]{1,0:T(8,128)(2,1)S(1)}, u32[]{:S(2)}, u32[]{:S(2)}) collective-permute-start(bf16[256,768]{1,0:T(8,128)(2,1)S(1)} %get-tuple-element.25), channel_id=1, source_target_pairs={{0,16},{8,24},{16,0},{24,8},{1,17},{9,25},{17,1},{25,9},{2,18},{10... | collective-permute-start | bytes 1179656 | tf_op jit(solution)/shard_map/ppermute | solution.py:186
  21.1 0.0 collective-permute-done.9.refs_1_
  21.1 0.3 collective-permute-start.2
  21.4 6.4 %collective-permute-done.10.refs_2_ = bf16[256,768]{1,0:T(8,128)(2,1)S(1)} collective-permute-done((bf16[256,768]{1,0:T(8,128)(2,1)S(1)}, bf16[256,768]{1,0:T(8,128)(2,1)S(1)}, u32[]{:S(2)}, u32[]{:S(2)}) %collective-permute-start.10) | collective-permute-done | bytes 393248 | tf_op jit(solution)/shard_map/ppermute | solution.py:186
  27.8 0.7 collective-permute-done.11.refs_3_
  28.4 0.0 copy-start.6
  28.4 1.0 copy-done.6
  29.4 0.0 copy-start.4
  29.4 2.2 %gram_0.1 = (f32[1344,128]{1,0:T(8,128)S(1)}, f32[1344,128]{1,0:T(8,128)S(1)}) custom-call(s32[1]{0:T(128)} %bitcast.where_ref, bf16[256,768]{1,0:T(8,128)(2,1)S(1)} %copy-done.6, bf16[256,768]{1,0:T(8,128)(2,1)S(1)} %collective-permute-done.9.refs_1_, bf16[256,768]{1,0:T(8,128)(2,1)S(1)} %collective-permute-done.10.refs_2_, ...), custom_call_target="tpu_custom_call" | custom-call | flops 1207959552 | bytes 1376256 | tf_op jit(solution)/shard_map/gram_0/pallas_call | solution.py:213
  31.7 0.1 collective-permute-start.12
  31.8 3.5 %collective-permute-done.refs_1_ = bf16[256,768]{1,0:T(8,128)(2,1)S(1)} collective-permute-done((bf16[256,768]{1,0:T(8,128)(2,1)S(1)}, bf16[256,768]{1,0:T(8,128)(2,1)S(1)}, u32[]{:S(2)}, u32[]{:S(2)}) %collective-permute-start) | collective-permute-done | bytes 393248 | tf_op jit(solution)/shard_map/ppermute | solution.py:186
  35.2 9.0 %collective-permute-done.1.refs_2_ = bf16[256,768]{1,0:T(8,128)(2,1)S(1)} collective-permute-done((bf16[256,768]{1,0:T(8,128)(2,1)S(1)}, bf16[256,768]{1,0:T(8,128)(2,1)S(1)}, u32[]{:S(2)}, u32[]{:S(2)}) %collective-permute-start.1) | collective-permute-done | bytes 393248 | tf_op jit(solution)/shard_map/ppermute | solution.py:186
  44.3 0.0 collective-permute-done.2.refs_3_
  44.3 0.0 copy-done.4
  44.3 2.2 %gram_1.1 = (f32[1344,128]{1,0:T(8,128)S(1)}, f32[1344,128]{1,0:T(8,128)S(1)}) custom-call(s32[1]{0:T(128)} %bitcast.where_ref, bf16[256,768]{1,0:T(8,128)(2,1)S(1)} %copy-done.4, bf16[256,768]{1,0:T(8,128)(2,1)S(1)} %collective-permute-done.refs_1_, bf16[256,768]{1,0:T(8,128)(2,1)S(1)} %collective-permute-done.1.refs_2_, ...), custom_call_target="tpu_custom_call" | custom-call | flops 1207959552 | bytes 1376256 | tf_op jit(solution)/shard_map/gram_1/pallas_call | solution.py:213
  46.5 0.1 collective-permute-start.3
  46.6 0.0 collective-permute-done.12.got_ref
  46.6 0.1 halve_0_1.1
  46.7 1.7 %collective-permute-start.13 = (f32[672,128]{1,0:T(8,128)S(1)}, f32[672,128]{1,0:T(8,128)S(1)}, u32[]{:S(2)}, u32[]{:S(2)}) collective-permute-start(f32[672,128]{1,0:T(8,128)S(1)} %get-tuple-element.38), channel_id=1, source_target_pairs={{0,2},{1,3},{2,0},{3,1},{4,6},{5,7},{6,4},{7,5},{8,10},{9,11},{10,... | collective-permute-start | bytes 1032200 | tf_op jit(solution)/shard_map/ppermute | solution.py:186
  48.3 0.4 collective-permute-done.3.got_ref
  48.7 0.1 halve_1_1.1
  48.7 1.7 %collective-permute-start.4 = (f32[672,128]{1,0:T(8,128)S(1)}, f32[672,128]{1,0:T(8,128)S(1)}, u32[]{:S(2)}, u32[]{:S(2)}) collective-permute-start(f32[672,128]{1,0:T(8,128)S(1)} %get-tuple-element.30), channel_id=1, source_target_pairs={{0,2},{1,3},{2,0},{3,1},{4,6},{5,7},{6,4},{7,5},{8,10},{9,11},{10,... | collective-permute-start | bytes 1032200 | tf_op jit(solution)/shard_map/ppermute | solution.py:186
  50.4 7.2 %collective-permute-done.13.b_ref = f32[672,128]{1,0:T(8,128)S(1)} collective-permute-done((f32[672,128]{1,0:T(8,128)S(1)}, f32[672,128]{1,0:T(8,128)S(1)}, u32[]{:S(2)}, u32[]{:S(2)}) %collective-permute-start.13) | collective-permute-done | bytes 344096 | tf_op jit(solution)/shard_map/ppermute | solution.py:186
  57.6 0.0 copy-start
  57.6 0.0 copy-start.1
  57.7 2.7 %collective-permute-start.14 = (f32[672,128]{1,0:T(8,128)S(1)}, f32[672,128]{1,0:T(8,128)S(1)}, u32[]{:S(2)}, u32[]{:S(2)}) collective-permute-start(f32[672,128]{1,0:T(8,128)S(1)} %sum_0.1.a_ref), channel_id=1, source_target_pairs={{0,4},{1,5},{2,6},{3,7},{4,0},{5,1},{6,2},{7,3},{8,12},{9,13},{10,... | collective-permute-start | bytes 1032200 | tf_op jit(solution)/shard_map/ppermute | solution.py:186
  60.3 10.4 %collective-permute-done.4.b_ref = f32[672,128]{1,0:T(8,128)S(1)} collective-permute-done((f32[672,128]{1,0:T(8,128)S(1)}, f32[672,128]{1,0:T(8,128)S(1)}, u32[]{:S(2)}, u32[]{:S(2)}) %collective-permute-start.4) | collective-permute-done | bytes 344096 | tf_op jit(solution)/shard_map/ppermute | solution.py:186
  70.7 0.1 collective-permute-start.5
  70.8 13.0 %collective-permute-done.14.b_ref = f32[672,128]{1,0:T(8,128)S(1)} collective-permute-done((f32[672,128]{1,0:T(8,128)S(1)}, f32[672,128]{1,0:T(8,128)S(1)}, u32[]{:S(2)}, u32[]{:S(2)}) %collective-permute-start.14) | collective-permute-done | bytes 344096 | tf_op jit(solution)/shard_map/ppermute | solution.py:186
  83.9 1.4 %collective-permute-start.15 = (f32[672,128]{1,0:T(8,128)S(1)}, f32[672,128]{1,0:T(8,128)S(1)}, u32[]{:S(2)}, u32[]{:S(2)}) collective-permute-start(f32[672,128]{1,0:T(8,128)S(1)} %total_0.1.refs_0_), channel_id=1, source_target_pairs={{0,2},{1,3},{2,0},{3,1},{4,6},{5,7},{6,4},{7,5},{8,10},{9,11},{10,... | collective-permute-start | bytes 1032200 | tf_op jit(solution)/shard_map/ppermute | solution.py:186
  85.3 4.8 %collective-permute-done.5.b_ref = f32[672,128]{1,0:T(8,128)S(1)} collective-permute-done((f32[672,128]{1,0:T(8,128)S(1)}, f32[672,128]{1,0:T(8,128)S(1)}, u32[]{:S(2)}, u32[]{:S(2)}) %collective-permute-start.5) | collective-permute-done | bytes 344096 | tf_op jit(solution)/shard_map/ppermute | solution.py:186
  90.1 0.8 collective-permute-start.6
  90.9 0.0 collective-permute-start.16
  90.9 6.5 %collective-permute-done.15.refs_1_ = f32[672,128]{1,0:T(8,128)S(1)} collective-permute-done((f32[672,128]{1,0:T(8,128)S(1)}, f32[672,128]{1,0:T(8,128)S(1)}, u32[]{:S(2)}, u32[]{:S(2)}) %collective-permute-start.15) | collective-permute-done | bytes 344096 | tf_op jit(solution)/shard_map/ppermute | solution.py:186
  97.4 0.0 collective-permute-start.17
  97.4 0.5 collective-permute-start.7
  97.9 6.8 %collective-permute-done.6.refs_1_ = f32[672,128]{1,0:T(8,128)S(1)} collective-permute-done((f32[672,128]{1,0:T(8,128)S(1)}, f32[672,128]{1,0:T(8,128)S(1)}, u32[]{:S(2)}, u32[]{:S(2)}) %collective-permute-start.6) | collective-permute-done | bytes 344096 | tf_op jit(solution)/shard_map/ppermute | solution.py:186
  104.7 0.0 collective-permute-start.8
  104.7 0.0 collective-permute-done.16.refs_2_
  104.7 0.0 collective-permute-done.17.refs_3_
  104.7 0.0 copy-done
  104.7 0.0 copy-done.1
  104.8 5.9 %steps_0.1.refs_4_ = f32[2,256,768]{2,1,0:T(8,128)} custom-call(s32[1]{0:T(128)} %bitcast.where_ref, bf16[2,256,768]{2,1,0:T(8,128)(2,1)S(1)} %copy-done, bf16[2,256,768]{2,1,0:T(8,128)(2,1)S(1)} %copy-done.1, f32[672,128]{1,0:T(8,128)S(1)} %total_0.1.refs_0_, f32[672,128]{1,0:T(8,128)S(1)} %collective-permute-done.15.refs_1_, ...), custom_call_target="tpu_custom_call" | custom-call | flops 3321888768 | bytes 1376256 | tf_op jit(solution)/shard_map/steps_0/pallas_call | solution.py:251
  110.7 0.0 collective-permute-done.7.refs_2_
  110.7 0.0 collective-permute-done.8.refs_3_
  110.7 5.7 %steps_1.1 = f32[2,256,768]{2,1,0:T(8,128)} custom-call(s32[1]{0:T(128)} %bitcast.where_ref, bf16[2,256,768]{2,1,0:T(8,128)(2,1)S(1)} %copy-done, bf16[2,256,768]{2,1,0:T(8,128)(2,1)S(1)} %copy-done.1, f32[672,128]{1,0:T(8,128)S(1)} %total_1.1.refs_0_, f32[672,128]{1,0:T(8,128)S(1)} %collective-permute-done.6.refs_1_, ...), custom_call_target="tpu_custom_call", output_to_operand_aliasing={{}: (7, {})} | custom-call | flops 3321888768 | bytes 1376256 | tf_op jit(solution)/shard_map/steps_1/pallas_call | solution.py:251
  (4 shorter events, 0.1 us)
Async XLA Ops:
  0.0 0.7 copy-start.2
  5.4 15.7 %collective-permute-start.9 = (bf16[256,768]{1,0:T(8,128)(2,1)S(1)}, bf16[256,768]{1,0:T(8,128)(2,1)S(1)}, u32[]{:S(2)}, u32[]{:S(2)}) collective-permute-start(bf16[256,768]{1,0:T(8,128)(2,1)S(1)} %get-tuple-element.32), channel_id=1, source_target_pairs={{0,8},{8,0},{16,24},{24,16},{1,9},{9,1},{17,25},{25,17},{2,10},{10... | collective-permute-start | bytes 1179656 | tf_op jit(solution)/shard_map/ppermute | solution.py:186
  8.4 19.4 %collective-permute-start.10 = (bf16[256,768]{1,0:T(8,128)(2,1)S(1)}, bf16[256,768]{1,0:T(8,128)(2,1)S(1)}, u32[]{:S(2)}, u32[]{:S(2)}) collective-permute-start(bf16[256,768]{1,0:T(8,128)(2,1)S(1)} %get-tuple-element.33), channel_id=1, source_target_pairs={{0,16},{8,24},{16,0},{24,8},{1,17},{9,25},{17,1},{25,9},{2,18},{10... | collective-permute-start | bytes 1179656 | tf_op jit(solution)/shard_map/ppermute | solution.py:186
  9.9 18.5 %collective-permute-start.11 = (bf16[256,768]{1,0:T(8,128)(2,1)S(1)}, bf16[256,768]{1,0:T(8,128)(2,1)}, u32[]{:S(2)}, u32[]{:S(2)}) collective-permute-start(bf16[256,768]{1,0:T(8,128)(2,1)S(1)} %get-tuple-element.34), channel_id=1, source_target_pairs={{0,24},{8,16},{16,8},{24,0},{1,25},{9,17},{17,9},{25,1},{2,26},{10... | collective-permute-start | bytes 1179656 | tf_op jit(solution)/shard_map/ppermute | solution.py:186
  16.1 0.7 copy-start.3
  16.9 0.8 copy-start.5
  17.6 17.6 %collective-permute-start = (bf16[256,768]{1,0:T(8,128)(2,1)S(1)}, bf16[256,768]{1,0:T(8,128)(2,1)S(1)}, u32[]{:S(2)}, u32[]{:S(2)}) collective-permute-start(bf16[256,768]{1,0:T(8,128)(2,1)S(1)} %get-tuple-element.24), channel_id=1, source_target_pairs={{0,8},{8,0},{16,24},{24,16},{1,9},{9,1},{17,25},{25,17},{2,10},{10... | collective-permute-start | bytes 1179656 | tf_op jit(solution)/shard_map/ppermute | solution.py:186
  19.6 24.7 %collective-permute-start.1 = (bf16[256,768]{1,0:T(8,128)(2,1)S(1)}, bf16[256,768]{1,0:T(8,128)(2,1)S(1)}, u32[]{:S(2)}, u32[]{:S(2)}) collective-permute-start(bf16[256,768]{1,0:T(8,128)(2,1)S(1)} %get-tuple-element.25), channel_id=1, source_target_pairs={{0,16},{8,24},{16,0},{24,8},{1,17},{9,25},{17,1},{25,9},{2,18},{10... | collective-permute-start | bytes 1179656 | tf_op jit(solution)/shard_map/ppermute | solution.py:186
  21.1 23.2 %collective-permute-start.2 = (bf16[256,768]{1,0:T(8,128)(2,1)S(1)}, bf16[256,768]{1,0:T(8,128)(2,1)}, u32[]{:S(2)}, u32[]{:S(2)}) collective-permute-start(bf16[256,768]{1,0:T(8,128)(2,1)S(1)} %get-tuple-element.26), channel_id=1, source_target_pairs={{0,24},{8,16},{16,8},{24,0},{1,25},{9,17},{17,9},{25,1},{2,26},{10... | collective-permute-start | bytes 1179656 | tf_op jit(solution)/shard_map/ppermute | solution.py:186
  28.4 1.0 copy-start.6
  29.4 14.8 %copy-start.4 = (bf16[256,768]{1,0:T(8,128)(2,1)S(1)}, bf16[256,768]{1,0:T(8,128)(2,1)}, u32[]{:S(2)}) copy-start(bf16[256,768]{1,0:T(8,128)(2,1)} %copy-done.3) | copy-start | bytes 1179652
  31.7 14.9 %collective-permute-start.12 = (f32[1344,128]{1,0:T(8,128)S(1)}, f32[1344,128]{1,0:T(8,128)S(1)}, u32[]{:S(2)}, u32[]{:S(2)}) collective-permute-start(f32[1344,128]{1,0:T(8,128)S(1)} %get-tuple-element.36), channel_id=1, source_target_pairs={{0,1},{1,0},{2,3},{3,2},{4,5},{5,4},{6,7},{7,6},{8,9},{9,8},{10,11... | collective-permute-start | bytes 2064392 | tf_op jit(solution)/shard_map/ppermute | solution.py:186
  46.5 2.2 %collective-permute-start.3 = (f32[1344,128]{1,0:T(8,128)S(1)}, f32[1344,128]{1,0:T(8,128)S(1)}, u32[]{:S(2)}, u32[]{:S(2)}) collective-permute-start(f32[1344,128]{1,0:T(8,128)S(1)} %get-tuple-element.28), channel_id=1, source_target_pairs={{0,1},{1,0},{2,3},{3,2},{4,5},{5,4},{6,7},{7,6},{8,9},{9,8},{10,11... | collective-permute-start | bytes 2064392 | tf_op jit(solution)/shard_map/ppermute | solution.py:186
  46.7 10.9 %collective-permute-start.13 = (f32[672,128]{1,0:T(8,128)S(1)}, f32[672,128]{1,0:T(8,128)S(1)}, u32[]{:S(2)}, u32[]{:S(2)}) collective-permute-start(f32[672,128]{1,0:T(8,128)S(1)} %get-tuple-element.38), channel_id=1, source_target_pairs={{0,2},{1,3},{2,0},{3,1},{4,6},{5,7},{6,4},{7,5},{8,10},{9,11},{10,... | collective-permute-start | bytes 1032200 | tf_op jit(solution)/shard_map/ppermute | solution.py:186
  48.7 21.9 %collective-permute-start.4 = (f32[672,128]{1,0:T(8,128)S(1)}, f32[672,128]{1,0:T(8,128)S(1)}, u32[]{:S(2)}, u32[]{:S(2)}) collective-permute-start(f32[672,128]{1,0:T(8,128)S(1)} %get-tuple-element.30), channel_id=1, source_target_pairs={{0,2},{1,3},{2,0},{3,1},{4,6},{5,7},{6,4},{7,5},{8,10},{9,11},{10,... | collective-permute-start | bytes 1032200 | tf_op jit(solution)/shard_map/ppermute | solution.py:186
  57.6 47.1 %copy-start = (bf16[2,256,768]{2,1,0:T(8,128)(2,1)S(1)}, bf16[2,256,768]{2,1,0:T(8,128)(2,1)}, u32[]{:S(2)}) copy-start(bf16[2,256,768]{2,1,0:T(8,128)(2,1)} %weight_ref.3) | copy-start | bytes 2359300
  57.6 47.1 %copy-start.1 = (bf16[2,256,768]{2,1,0:T(8,128)(2,1)S(1)}, bf16[2,256,768]{2,1,0:T(8,128)(2,1)}, u32[]{:S(2)}) copy-start(bf16[2,256,768]{2,1,0:T(8,128)(2,1)} %mask_ref.3) | copy-start | bytes 2359300
  57.7 26.2 %collective-permute-start.14 = (f32[672,128]{1,0:T(8,128)S(1)}, f32[672,128]{1,0:T(8,128)S(1)}, u32[]{:S(2)}, u32[]{:S(2)}) collective-permute-start(f32[672,128]{1,0:T(8,128)S(1)} %sum_0.1.a_ref), channel_id=1, source_target_pairs={{0,4},{1,5},{2,6},{3,7},{4,0},{5,1},{6,2},{7,3},{8,12},{9,13},{10,... | collective-permute-start | bytes 1032200 | tf_op jit(solution)/shard_map/ppermute | solution.py:186
  70.7 19.4 %collective-permute-start.5 = (f32[672,128]{1,0:T(8,128)S(1)}, f32[672,128]{1,0:T(8,128)S(1)}, u32[]{:S(2)}, u32[]{:S(2)}) collective-permute-start(f32[672,128]{1,0:T(8,128)S(1)} %sum_1.1.a_ref), channel_id=1, source_target_pairs={{0,4},{1,5},{2,6},{3,7},{4,0},{5,1},{6,2},{7,3},{8,12},{9,13},{10,... | collective-permute-start | bytes 1032200 | tf_op jit(solution)/shard_map/ppermute | solution.py:186
  83.9 13.6 %collective-permute-start.15 = (f32[672,128]{1,0:T(8,128)S(1)}, f32[672,128]{1,0:T(8,128)S(1)}, u32[]{:S(2)}, u32[]{:S(2)}) collective-permute-start(f32[672,128]{1,0:T(8,128)S(1)} %total_0.1.refs_0_), channel_id=1, source_target_pairs={{0,2},{1,3},{2,0},{3,1},{4,6},{5,7},{6,4},{7,5},{8,10},{9,11},{10,... | collective-permute-start | bytes 1032200 | tf_op jit(solution)/shard_map/ppermute | solution.py:186
  90.1 14.6 %collective-permute-start.6 = (f32[672,128]{1,0:T(8,128)S(1)}, f32[672,128]{1,0:T(8,128)S(1)}, u32[]{:S(2)}, u32[]{:S(2)}) collective-permute-start(f32[672,128]{1,0:T(8,128)S(1)} %total_1.1.refs_0_), channel_id=1, source_target_pairs={{0,2},{1,3},{2,0},{3,1},{4,6},{5,7},{6,4},{7,5},{8,10},{9,11},{10,... | collective-permute-start | bytes 1032200 | tf_op jit(solution)/shard_map/ppermute | solution.py:186
  90.9 13.8 %collective-permute-start.16 = (f32[672,128]{1,0:T(8,128)S(1)}, f32[672,128]{1,0:T(8,128)S(1)}, u32[]{:S(2)}, u32[]{:S(2)}) collective-permute-start(f32[672,128]{1,0:T(8,128)S(1)} %total_0.1.refs_0_), channel_id=1, source_target_pairs={{0,1},{1,0},{2,3},{3,2},{4,5},{5,4},{6,7},{7,6},{8,9},{9,8},{10,11... | collective-permute-start | bytes 1032200 | tf_op jit(solution)/shard_map/ppermute | solution.py:186
  97.4 7.3 %collective-permute-start.17 = (f32[672,128]{1,0:T(8,128)S(1)}, f32[672,128]{1,0:T(8,128)S(1)}, u32[]{:S(2)}, u32[]{:S(2)}) collective-permute-start(f32[672,128]{1,0:T(8,128)S(1)} %collective-permute-done.15.refs_1_), channel_id=1, source_target_pairs={{0,1},{1,0},{2,3},{3,2},{4,5},{5,4},{6,7},{7,6},{8,9},{9,8},{10,11... | collective-permute-start | bytes 1032200 | tf_op jit(solution)/shard_map/ppermute | solution.py:186
  97.4 13.2 %collective-permute-start.7 = (f32[672,128]{1,0:T(8,128)S(1)}, f32[672,128]{1,0:T(8,128)S(1)}, u32[]{:S(2)}, u32[]{:S(2)}) collective-permute-start(f32[672,128]{1,0:T(8,128)S(1)} %total_1.1.refs_0_), channel_id=1, source_target_pairs={{0,1},{1,0},{2,3},{3,2},{4,5},{5,4},{6,7},{7,6},{8,9},{9,8},{10,11... | collective-permute-start | bytes 1032200 | tf_op jit(solution)/shard_map/ppermute | solution.py:186
  104.7 6.0 %collective-permute-start.8 = (f32[672,128]{1,0:T(8,128)S(1)}, f32[672,128]{1,0:T(8,128)S(1)}, u32[]{:S(2)}, u32[]{:S(2)}) collective-permute-start(f32[672,128]{1,0:T(8,128)S(1)} %collective-permute-done.6.refs_1_), channel_id=1, source_target_pairs={{0,1},{1,0},{2,3},{3,2},{4,5},{5,4},{6,7},{7,6},{8,9},{9,8},{10,11... | collective-permute-start | bytes 1032200 | tf_op jit(solution)/shard_map/ppermute | solution.py:186

commit v2 on v1

v2 whole, which is shorter than its diff:
```python
import functools

import jax
import jax.numpy as jnp
from jax import lax
from jax.experimental import pallas as pl
from jax.experimental.pallas import tpu as pltpu
from jax.sharding import PartitionSpec as P

STEPS = 4
BLOCK = 128
CHUNKS = 2
relax_factor = 0.5
diagonal_eps = 1e-06
VMEM_LIMIT = 50 * 2**20

VMEM = pl.BlockSpec(memory_space=pltpu.VMEM)
ANY = pl.BlockSpec(memory_space=pl.ANY)
SMEM = pl.BlockSpec(memory_space=pltpu.SMEM)
F32, BF16, I32 = jnp.float32, jnp.bfloat16, jnp.int32


def call(kernel, out_shape, in_specs, scratch=(), flops=0, moved=0, out_specs=None, aliases=None, name=None, after=()):
    many = isinstance(out_shape, (list, tuple))
    used, idle = len(in_specs), len(after)

    def body(*refs):
        kernel(*refs[:used], *refs[used + idle:])

    inner = pl.pallas_call(
        body,
        out_shape=out_shape,
        in_specs=list(in_specs) + [ANY] * idle,
        out_specs=out_specs if out_specs is not None else ([VMEM] * len(out_shape) if many else VMEM),
        scratch_shapes=list(scratch),
        input_output_aliases=aliases or {},
        cost_estimate=pl.CostEstimate(flops=flops, bytes_accessed=moved, transcendentals=0),
        compiler_params=pltpu.CompilerParams(vmem_limit_bytes=VMEM_LIMIT),
        name=name,
    )
    return lambda *args: inner(*args, *after)


def cuts(size, chunks):
    ends = [size * (c + 1) // (8 * chunks) * 8 for c in range(chunks)]
    return [end - start for start, end in zip([0] + ends, ends)]


def slots_of(owners, experts, capacity):
    tokens = owners.shape[1]
    lanes = 128
    blocks = tokens // lanes
    named = owners == lax.broadcasted_iota(I32, (experts, tokens), 0)
    ones = named.astype(F32)
    stacked = jnp.concatenate([ones[:, b * lanes:(b + 1) * lanes] for b in range(blocks)], axis=0)
    upto = lax.broadcasted_iota(I32, (lanes, lanes), 0) <= lax.broadcasted_iota(I32, (lanes, lanes), 1)
    within = jnp.dot(stacked.astype(BF16), upto.astype(F32).astype(BF16), preferred_element_type=F32)
    carry = jnp.zeros((experts, 1), F32)
    parts = []
    for b in range(blocks):
        part = within[b * experts:(b + 1) * experts]
        parts.append(part + carry)
        carry = carry + part[:, lanes - 1:lanes]
    counted = jnp.concatenate(parts, axis=1)
    rank = jnp.sum(jnp.where(named, counted - 1.0, 0.0), axis=0, keepdims=True)
    return owners * capacity + rank.astype(I32)


def place(key, rows_ref, experts, capacity, out_refs):
    tokens, hidden = rows_ref.shape
    places = lax.broadcasted_iota(I32, (capacity, tokens), 0)
    chosen = jnp.concatenate(
        [(places == key - e * capacity).astype(F32).astype(BF16) for e in experts], axis=0
    )
    width = 256
    for c in range(0, hidden, width):
        got = jnp.dot(chosen, rows_ref[:, c:c + width], preferred_element_type=F32).astype(BF16)
        for k, out_ref in enumerate(out_refs):
            out_ref[:, c:c + width] = got[k * capacity:(k + 1) * capacity]


def first_kernel(peers, slots, all_experts, capacity, me_ref, owner_ref, rows_ref, key_ref, *out_refs):
    me = me_ref[0]
    key = slots_of(owner_ref[...], all_experts, capacity)
    key_ref[...] = key
    place(key, rows_ref, [lax.bitwise_xor(me, k) * slots for k in range(1, peers)], capacity, out_refs)


def second_kernel(peers, slots, capacity, me_ref, key_ref, rows_ref, *out_refs):
    me = me_ref[0]
    experts = [me * slots + a for a in range(slots)]
    for a in range(1, slots):
        experts += [lax.bitwise_xor(me, k) * slots + a for k in range(1, peers)]
    place(key_ref[...], rows_ref, experts, capacity, out_refs)


def layout(hidden, halvings):
    blocks = hidden // BLOCK
    off = [(i, j) for i in range(blocks) for j in range(i + 1, blocks)]
    pairs = [(i, i + 1 if i + 1 < blocks else None) for i in range(0, blocks, 2)]
    tail = (len(off) + len(pairs)) * BLOCK
    unit = 8 << halvings
    return off, pairs, tail, -(-(tail + len(pairs)) // unit) * unit


def eye_of(compare):
    return compare(lax.broadcasted_iota(I32, (BLOCK, BLOCK), 0), lax.broadcasted_iota(I32, (BLOCK, BLOCK), 1))


def bit_of(where, bit):
    return lax.bitwise_and(lax.shift_right_logical(where, bit), 1)


def gram_kernel(halvings, pieces, where_ref, *refs):
    chunk_refs, (keep_ref, send_ref, packed) = refs[:pieces], refs[pieces:]
    hidden = chunk_refs[0].shape[1]
    off, pairs, tail, length = layout(hidden, halvings)
    at = {pair: n for n, pair in enumerate(off)}
    x = jnp.concatenate([r[...] for r in chunk_refs], axis=0)
    strip = 2 * BLOCK
    packed[tail:length] = jnp.zeros((length - tail, BLOCK), F32)
    for n, (first, second) in enumerate(pairs):
        low, high = first * BLOCK, min(first * BLOCK + strip, hidden)
        product = lax.dot_general(
            x[:, low:high], x[:, low:], (((0,), (0,)), ((), ())), preferred_element_type=F32
        )
        for i in range((high - low) // BLOCK):
            for j in range((hidden - low) // BLOCK):
                pair = (first + i, first + j)
                if pair in at:
                    row = at[pair] * BLOCK
                    packed[row:row + BLOCK] = product[i * BLOCK:(i + 1) * BLOCK, j * BLOCK:(j + 1) * BLOCK]
        mixed = product[:BLOCK, :BLOCK]
        if second is not None:
            other = product[BLOCK:, BLOCK:2 * BLOCK]
            mixed = jnp.where(eye_of(lax.le), mixed, other)
            packed[tail + n:tail + n + 1] = jnp.sum(jnp.where(eye_of(lax.eq), other, 0.0), axis=0, keepdims=True)
        row = (len(off) + n) * BLOCK
        packed[row:row + BLOCK] = mixed
    half = keep_ref.shape[0]
    mine = bit_of(where_ref[0], 0)
    keep_ref[...] = packed[pl.ds(pl.multiple_of(mine * half, 8), half)]
    send_ref[...] = packed[pl.ds(pl.multiple_of((1 - mine) * half, 8), half)]


def halve_kernel(bit, where_ref, keep_ref, got_ref, *out_refs):
    chunks = len(out_refs) // 2
    half = keep_ref.shape[0] // 2
    mine = bit_of(where_ref[0], bit)
    for side, refs in ((mine, out_refs[:chunks]), (1 - mine, out_refs[chunks:])):
        start = 0
        for ref in refs:
            size = ref.shape[0]
            part = pl.ds(pl.multiple_of(side * half + start, 8), size)
            ref[...] = keep_ref[part] + got_ref[part]
            start += size


def add_kernel(a_ref, b_ref, out_ref):
    out_ref[...] = a_ref[...] + b_ref[...]


def steps_kernel(slot, halvings, places, where_ref, weight_ref, mask_ref, *refs):
    piece_refs = refs[:len(places)]
    out_ref, token_ref, packed, high, low, scale, result, done = refs[-8:]
    hidden = weight_ref.shape[-1]
    off, pairs, tail, length = layout(hidden, halvings)
    where = where_ref[0]
    for (flip, offset), piece_ref in zip(places, piece_refs):
        owner = lax.bitwise_xor(where, flip)
        start = offset
        for b in range(halvings):
            start = start + bit_of(owner, b) * (length >> (b + 1))
        packed[pl.ds(pl.multiple_of(start, 8), piece_ref.shape[0])] = piece_ref[...]

    def put(i, j, block):
        rows, cols = slice(i * BLOCK, (i + 1) * BLOCK), slice(j * BLOCK, (j + 1) * BLOCK)
        hi = block.astype(BF16)
        high[rows, cols] = hi
        low[rows, cols] = (block - hi.astype(F32)).astype(BF16)

    for n, (i, j) in enumerate(off):
        block = packed[n * BLOCK:(n + 1) * BLOCK]
        put(i, j, block)
        put(j, i, block.T)
    eye = eye_of(lax.eq)
    for n, (first, second) in enumerate(pairs):
        row = (len(off) + n) * BLOCK
        block = packed[row:row + BLOCK]
        turned = block.T
        put(first, first, jnp.where(eye_of(lax.le), block, turned))
        diagonals = [(first, jnp.sum(jnp.where(eye, block, 0.0), axis=0, keepdims=True))]
        if second is not None:
            diagonal = packed[tail + n:tail + n + 1]
            put(second, second, jnp.where(eye, diagonal, jnp.where(eye_of(lax.gt), block, turned)))
            diagonals.append((second, diagonal))
        for i, diagonal in diagonals:
            scale[:, i * BLOCK:(i + 1) * BLOCK] = relax_factor * (1.0 / (diagonal + diagonal_eps))
    weight = weight_ref[slot].astype(F32)
    keep = mask_ref[slot].astype(F32)
    factor = scale[...]
    pruned = keep * weight
    for sweep in range(STEPS):
        change = pruned - weight
        top = change.astype(BF16)
        if sweep == 0:
            gradient = jnp.dot(top, high[...], preferred_element_type=F32)
        else:
            rest = (change - top.astype(F32)).astype(BF16)
            both = jnp.dot(jnp.concatenate([top, rest], axis=0), high[...], preferred_element_type=F32)
            gradient = both[:top.shape[0]] + both[top.shape[0]:]
        gradient = gradient + jnp.dot(top, low[...], preferred_element_type=F32)
        pruned = keep * (pruned - gradient * factor)
    result[...] = pruned
    token_ref[...] = pruned[:8, :BLOCK]
    copy = pltpu.make_async_copy(result, out_ref.at[slot], done)
    copy.start()
    copy.wait()


def on_device(expert_inputs, row_expert, down_weight, keep_mask):
    tokens, hidden = expert_inputs.shape
    slots, features, _ = down_weight.shape
    peers = lax.axis_size("expert")
    copies = lax.axis_size("rows")
    all_experts = slots * peers
    capacity = tokens // 8
    bits = copies.bit_length() - 1
    me = jnp.reshape(lax.axis_index("expert").astype(I32), (1,))
    where = jnp.reshape(lax.axis_index("rows").astype(I32), (1,))
    owners = row_expert.reshape(1, tokens)

    def over(axis, size, array, flip):
        return lax.ppermute(array, axis, [(i, i ^ flip) for i in range(size)])

    chunk = jax.ShapeDtypeStruct((capacity, hidden), BF16)
    place_flops = 2 * capacity * tokens * hidden
    sent_first = peers - 1
    key, *outgoing = call(
        functools.partial(first_kernel, peers, slots, all_experts, capacity),
        [jax.ShapeDtypeStruct((1, tokens), I32)] + [chunk] * sent_first,
        [SMEM, VMEM, VMEM], flops=place_flops * sent_first, moved=expert_inputs.size * 4, name="place_first",
    )(me, owners, expert_inputs)
    arrived = [[over("expert", peers, outgoing[k - 1], k) for k in range(1, peers)]]
    count = slots + (slots - 1) * (peers - 1)
    rest = call(
        functools.partial(second_kernel, peers, slots, capacity),
        [chunk] * count,
        [SMEM, VMEM, VMEM], flops=place_flops * count, moved=expert_inputs.size * 4, name="place_rest",
    )(me, key, expert_inputs)
    own = rest[:slots]
    for a in range(1, slots):
        outgoing = rest[slots + (a - 1) * (peers - 1):slots + a * (peers - 1)]
        arrived.append([over("expert", peers, outgoing[k - 1], k) for k in range(1, peers)])

    halvings = bits - 1
    length = layout(hidden, halvings)[3]

    def rows_of(size):
        return jax.ShapeDtypeStruct((size, BLOCK), F32)

    def over_rows(array, bit):
        return over("rows", copies, array, 1 << bit)

    def add(a, b, name, after=()):
        return call(
            add_kernel, rows_of(a.shape[0]), [VMEM, VMEM], moved=a.size * 12, name=name, after=after,
        )(a, b)

    def steps(slot, pieces, places, result, after=()):
        in_specs = [SMEM] + [VMEM] * (2 + len(pieces))
        args = [where, down_weight, keep_mask] + pieces
        aliases = {}
        if result is not None:
            aliases = {len(args): 0}
            in_specs.append(ANY)
            args.append(result)
        return call(
            functools.partial(steps_kernel, slot, halvings, places),
            [jax.ShapeDtypeStruct((slots, features, hidden), F32), rows_of(8)],
            in_specs,
            out_specs=[ANY, VMEM],
            scratch=[
                pltpu.VMEM((length, BLOCK), F32),
                pltpu.VMEM((hidden, hidden), BF16),
                pltpu.VMEM((hidden, hidden), BF16),
                pltpu.VMEM((1, hidden), F32),
                pltpu.VMEM((features, hidden), F32),
                pltpu.SemaphoreType.DMA,
            ],
            aliases=aliases,
            flops=2 * 11 * features * hidden * hidden, moved=length * BLOCK * 4, name=f"steps_{slot}", after=after,
        )(*args)

    result, waiting, summed, token = None, None, (), ()
    for a in range(slots):
        size = length // 2
        keep, send = call(
            functools.partial(gram_kernel, halvings, peers),
            [rows_of(size)] * 2,
            [SMEM] + [VMEM] * peers,
            scratch=[pltpu.VMEM((length, BLOCK), F32)],
            flops=2 * capacity * peers * hidden * hidden, moved=length * BLOCK * 4, name=f"gram_{a}",
            after=summed,
        )(where, own[a], *arrived[a])
        keep, send = [keep], [send]
        for bit in range(1, halvings):
            got = over_rows(send[0], bit - 1)
            size = size // 2
            chunks = CHUNKS if bit == halvings - 1 and a == slots - 1 else 1
            shapes = [rows_of(n) for n in cuts(size, chunks)]
            halves = call(
                functools.partial(halve_kernel, bit), shapes * 2,
                [SMEM, VMEM, VMEM], moved=size * BLOCK * 4 * 6, name=f"halve_{a}_{bit}",
            )(where, keep[0], got)
            keep, send = halves[:chunks], halves[chunks:]
        summed = [
            add(mine, over_rows(theirs, halvings - 1), f"sum_{a}_{c}") for c, (mine, theirs) in enumerate(zip(keep, send))
        ]
        if waiting is not None:
            result, *token = steps(*waiting, result, after=summed)
        pieces, places, offset = [], [], 0
        for c, mine in enumerate(summed):
            total = add(mine, over_rows(mine, halvings), f"total_{a}_{c}", after=token)
            held = [(0, total)]
            for bit in range(halvings - 1, -1, -1):
                held += [(flip ^ (1 << bit), over_rows(piece, bit)) for flip, piece in held]
            places += [(flip, offset) for flip, _ in held]
            pieces += [piece for _, piece in held]
            offset += mine.shape[0]
        waiting = (a, pieces, places)
    return steps(*waiting, result)[0]


def solution(mesh):
    return jax.shard_map(
        on_device,
        mesh=mesh,
        in_specs=(
            P(("expert", "rows"), None),
            P(("expert", "rows"), None),
            P("expert", "rows", None),
            P("expert", "rows", None),
        ),
        out_specs=P("expert", "rows", None),
        check_vma=False,
    )
```

time: 117 us -> 107 us (0.915)
  waiting for transfers between devices: 68.6 us -> 58.4 us
  starting transfers between devices: 17.2 us -> 21.6 us
  local copies, waits for them, and re-layouts: 3.21 us -> 0.71 us
  Pallas kernels: 27.2 us -> 25.8 us
    ppermute x18 -> x23, waiting for transfers between devices: 68.6 us -> 58.4 us  [over(): return lax.ppermute(array, axis, [(i, i ^ flip) for i in range(size)])]
    ppermute x18 -> x23, starting transfers between devices: 17.2 us -> 21.6 us  [over(): return lax.ppermute(array, axis, [(i, i ^ flip) for i in range(size)])]
    unnamed x14 -> x6, local copies, waits for them, and re-layouts: 3.21 us -> 0.71 us
    pallas_call x12 -> x14, Pallas kernels: 27.2 us -> 25.8 us  [call(): return lambda *args: inner(*args, *after)]
  transfers between devices with their start and end apart: 18 -> 23, of which waited for: 11 -> 12; matrix products, arithmetic and copies ran while one was open for 0% -> 0% of each run, Pallas kernels for 14% -> 13%
where the time goes in v2:
time: 107 us
  waiting for transfers between devices  58.4 us (55%)
  Pallas kernels  25.8 us (24%)
  starting transfers between devices  21.6 us (20%)
    ppermute x23, waiting for transfers between devices, over(): return lax.ppermute(array, axis, [(i, i ^ flip) for i in range(size)])  58.4 us
    pallas_call x14, Pallas kernels, call(): return lambda *args: inner(*args, *after)  25.8 us
    ppermute x23, starting transfers between devices, over(): return lax.ppermute(array, axis, [(i, i ^ flip) for i in range(size)])  21.6 us
  transfers between devices with their start and end apart: 23, of which 12 were waited for; matrix products, arithmetic and copies ran while one was open for 0% of the time, Pallas kernels for 13%

profile of v2, /device:TPU:0, one launch (start us, length us, event | category | flops | bytes accessed | tf_op | source)
XLA Modules:
  0.0 106.8 jit_solution(2501291608106022728)
XLA Ops:
  0.0 0.0 copy-start.2
  0.0 0.7 copy-done.2
  0.7 4.7 %place_first.1 = (s32[1,2048]{1,0:T(1,128)S(1)}, bf16[256,768]{1,0:T(8,128)(2,1)S(1)}, bf16[256,768]{1,0:T(8,128)(2,1)S(1)}, bf16[256,768]{1,0:T(8,128)(2,1)S(1)}) custom-call(s32[1]{0:T(128)} %bitcast.1.refs_0_, s32[1,2048]{1,0:T(1,128)S(1)} %bitcast.3, bf16[2048,768]{1,0:T(8,128)(2,1)} %refs_2_.5), custom_call_target="tpu_custom_call" | custom-call | flops 2415919104 | bytes 6291456 | tf_op jit(solution)/shard_map/place_first/pallas_call | solution.py:41
  5.4 3.0 %collective-permute-start.3 = (bf16[256,768]{1,0:T(8,128)(2,1)S(1)}, bf16[256,768]{1,0:T(8,128)(2,1)S(1)}, u32[]{:S(2)}, u32[]{:S(2)}) collective-permute-start(bf16[256,768]{1,0:T(8,128)(2,1)S(1)} %get-tuple-element.33), channel_id=1, source_target_pairs={{0,8},{8,0},{16,24},{24,16},{1,9},{9,1},{17,25},{25,17},{2,10},{10... | collective-permute-start | bytes 1179656 | tf_op jit(solution)/shard_map/ppermute | solution.py:234
  8.4 1.5 %collective-permute-start.4 = (bf16[256,768]{1,0:T(8,128)(2,1)S(1)}, bf16[256,768]{1,0:T(8,128)(2,1)S(1)}, u32[]{:S(2)}, u32[]{:S(2)}) collective-permute-start(bf16[256,768]{1,0:T(8,128)(2,1)S(1)} %get-tuple-element.34), channel_id=1, source_target_pairs={{0,16},{8,24},{16,0},{24,8},{1,17},{9,25},{17,1},{25,9},{2,18},{10... | collective-permute-start | bytes 1179656 | tf_op jit(solution)/shard_map/ppermute | solution.py:234
  9.9 0.0 collective-permute-start.5
  9.9 6.2 %place_rest.1 = (bf16[256,768]{1,0:T(8,128)(2,1)S(1)}, bf16[256,768]{1,0:T(8,128)(2,1)S(1)}, bf16[256,768]{1,0:T(8,128)(2,1)S(1)}, bf16[256,768]{1,0:T(8,128)(2,1)S(1)}, bf16[256,768]{1,0:T(8,128)(2,1)S(1)}) custom-call(s32[1]{0:T(128)} %bitcast.1.refs_0_, s32[1,2048]{1,0:T(1,128)S(1)} %get-tuple-element.27.refs_1_, bf16[2048,768]{1,0:T(8,128)(2,1)} %refs_2_.5), custom_call_target="tpu_custom_call" | custom-call | flops 4026531840 | bytes 6291456 | tf_op jit(solution)/shard_map/place_rest/pallas_call | solution.py:41
  16.1 2.2 %collective-permute-done.3.refs_2_ = bf16[256,768]{1,0:T(8,128)(2,1)S(1)} collective-permute-done((bf16[256,768]{1,0:T(8,128)(2,1)S(1)}, bf16[256,768]{1,0:T(8,128)(2,1)S(1)}, u32[]{:S(2)}, u32[]{:S(2)}) %collective-permute-start.3) | collective-permute-done | bytes 393248 | tf_op jit(solution)/shard_map/ppermute | solution.py:234
  18.3 9.1 %collective-permute-done.4.refs_3_ = bf16[256,768]{1,0:T(8,128)(2,1)S(1)} collective-permute-done((bf16[256,768]{1,0:T(8,128)(2,1)S(1)}, bf16[256,768]{1,0:T(8,128)(2,1)S(1)}, u32[]{:S(2)}, u32[]{:S(2)}) %collective-permute-start.4) | collective-permute-done | bytes 393248 | tf_op jit(solution)/shard_map/ppermute | solution.py:234
  27.4 0.0 collective-permute-done.5.refs_4_
  27.4 1.2 %gram_0.1 = (f32[1168,128]{1,0:T(8,128)S(1)}, f32[1168,128]{1,0:T(8,128)S(1)}) custom-call(s32[1]{0:T(128)} %bitcast.refs_0_, bf16[256,768]{1,0:T(8,128)(2,1)S(1)} %get-tuple-element.32.refs_1_, bf16[256,768]{1,0:T(8,128)(2,1)S(1)} %collective-permute-done.3.refs_2_, bf16[256,768]{1,0:T(8,128)(2,1)S(1)} %collective-permute-done.4.refs_3_, ...), custom_call_target="tpu_custom_call" | custom-call | flops 1207959552 | bytes 1196032 | tf_op jit(solution)/shard_map/gram_0/pallas_call | solution.py:41
  28.6 0.1 collective-permute-start.6
  28.7 1.3 %collective-permute-start = (bf16[256,768]{1,0:T(8,128)(2,1)S(1)}, bf16[256,768]{1,0:T(8,128)(2,1)S(1)}, u32[]{:S(2)}, u32[]{:S(2)}) collective-permute-start(bf16[256,768]{1,0:T(8,128)(2,1)S(1)} %get-tuple-element.29), channel_id=1, source_target_pairs={{0,8},{8,0},{16,24},{24,16},{1,9},{9,1},{17,25},{25,17},{2,10},{10... | collective-permute-start | bytes 1179656 | tf_op jit(solution)/shard_map/ppermute | solution.py:234
  30.0 0.8 collective-permute-start.1
  30.8 1.4 %collective-permute-start.2 = (bf16[256,768]{1,0:T(8,128)(2,1)S(1)}, bf16[256,768]{1,0:T(8,128)(2,1)S(1)}, u32[]{:S(2)}, u32[]{:S(2)}) collective-permute-start(bf16[256,768]{1,0:T(8,128)(2,1)S(1)} %get-tuple-element.31), channel_id=1, source_target_pairs={{0,24},{8,16},{16,8},{24,0},{1,25},{9,17},{17,9},{25,1},{2,26},{10... | collective-permute-start | bytes 1179656 | tf_op jit(solution)/shard_map/ppermute | solution.py:234
  32.3 0.0 collective-permute-done.6.refs_2_
  32.3 0.1 halve_0_1.1
  32.3 1.6 %collective-permute-start.7 = (f32[584,128]{1,0:T(8,128)S(1)}, f32[584,128]{1,0:T(8,128)S(1)}, u32[]{:S(2)}, u32[]{:S(2)}) collective-permute-start(f32[584,128]{1,0:T(8,128)S(1)} %get-tuple-element.39), channel_id=1, source_target_pairs={{0,2},{1,3},{2,0},{3,1},{4,6},{5,7},{6,4},{7,5},{8,10},{9,11},{10,... | collective-permute-start | bytes 897032 | tf_op jit(solution)/shard_map/ppermute | solution.py:234
  34.0 7.0 %collective-permute-done.7.refs_1_ = f32[584,128]{1,0:T(8,128)S(1)} collective-permute-done((f32[584,128]{1,0:T(8,128)S(1)}, f32[584,128]{1,0:T(8,128)S(1)}, u32[]{:S(2)}, u32[]{:S(2)}) %collective-permute-start.7) | collective-permute-done | bytes 299040 | tf_op jit(solution)/shard_map/ppermute | solution.py:234
  41.0 2.7 %collective-permute-start.11 = (f32[584,128]{1,0:T(8,128)S(1)}, f32[584,128]{1,0:T(8,128)S(1)}, u32[]{:S(2)}, u32[]{:S(2)}) collective-permute-start(f32[584,128]{1,0:T(8,128)S(1)} %sum_0_0.1.refs_5_.refs_0_), channel_id=1, source_target_pairs={{0,4},{1,5},{2,6},{3,7},{4,0},{5,1},{6,2},{7,3},{8,12},{9,13},{10,... | collective-permute-start | bytes 897032 | tf_op jit(solution)/shard_map/ppermute | solution.py:234
  43.7 0.0 collective-permute-done.refs_2_
  43.7 4.3 %collective-permute-done.1.refs_3_ = bf16[256,768]{1,0:T(8,128)(2,1)S(1)} collective-permute-done((bf16[256,768]{1,0:T(8,128)(2,1)S(1)}, bf16[256,768]{1,0:T(8,128)(2,1)S(1)}, u32[]{:S(2)}, u32[]{:S(2)}) %collective-permute-start.1) | collective-permute-done | bytes 393248 | tf_op jit(solution)/shard_map/ppermute | solution.py:234
  48.0 1.6 %collective-permute-done.2.refs_4_ = bf16[256,768]{1,0:T(8,128)(2,1)S(1)} collective-permute-done((bf16[256,768]{1,0:T(8,128)(2,1)S(1)}, bf16[256,768]{1,0:T(8,128)(2,1)S(1)}, u32[]{:S(2)}, u32[]{:S(2)}) %collective-permute-start.2) | collective-permute-done | bytes 393248 | tf_op jit(solution)/shard_map/ppermute | solution.py:234
  49.6 1.2 %gram_1.1 = (f32[1168,128]{1,0:T(8,128)S(1)}, f32[1168,128]{1,0:T(8,128)S(1)}) custom-call(s32[1]{0:T(128)} %bitcast.refs_0_, bf16[256,768]{1,0:T(8,128)(2,1)S(1)} %get-tuple-element.28.refs_1_, bf16[256,768]{1,0:T(8,128)(2,1)S(1)} %collective-permute-done.refs_2_, bf16[256,768]{1,0:T(8,128)(2,1)S(1)} %collective-permute-done.1.refs_3_, ...), custom_call_target="tpu_custom_call" | custom-call | flops 1207959552 | bytes 1196032 | tf_op jit(solution)/shard_map/gram_1/pallas_call | solution.py:41
  50.8 0.0 copy-start
  50.9 0.0 copy-start.1
  50.9 0.1 collective-permute-start.8
  50.9 5.2 %collective-permute-done.11.refs_1_ = f32[584,128]{1,0:T(8,128)S(1)} collective-permute-done((f32[584,128]{1,0:T(8,128)S(1)}, f32[584,128]{1,0:T(8,128)S(1)}, u32[]{:S(2)}, u32[]{:S(2)}) %collective-permute-start.11) | collective-permute-done | bytes 299040 | tf_op jit(solution)/shard_map/ppermute | solution.py:234
  56.2 0.7 collective-permute-start.12
  56.9 0.0 collective-permute-start.13
  56.9 7.3 %collective-permute-done.12.refs_4_ = f32[584,128]{1,0:T(8,128)S(1)} collective-permute-done((f32[584,128]{1,0:T(8,128)S(1)}, f32[584,128]{1,0:T(8,128)S(1)}, u32[]{:S(2)}, u32[]{:S(2)}) %collective-permute-start.12) | collective-permute-done | bytes 299040 | tf_op jit(solution)/shard_map/ppermute | solution.py:234
  64.2 0.0 collective-permute-start.14
  64.2 0.0 collective-permute-done.8.refs_2_
  64.2 0.1 halve_1_1.1
  64.3 1.8 %collective-permute-start.15 = (f32[296,128]{1,0:T(8,128)S(1)}, f32[296,128]{1,0:T(8,128)S(1)}, u32[]{:S(2)}, u32[]{:S(2)}) collective-permute-start(f32[296,128]{1,0:T(8,128)S(1)} %get-tuple-element.45), channel_id=1, source_target_pairs={{0,2},{1,3},{2,0},{3,1},{4,6},{5,7},{6,4},{7,5},{8,10},{9,11},{10,... | collective-permute-start | bytes 454664 | tf_op jit(solution)/shard_map/ppermute | solution.py:234
  66.1 0.3 collective-permute-start.9
  66.3 7.5 %collective-permute-done.9.refs_1_ = f32[288,128]{1,0:T(8,128)S(1)} collective-permute-done((f32[288,128]{1,0:T(8,128)S(1)}, f32[288,128]{1,0:T(8,128)S(1)}, u32[]{:S(2)}, u32[]{:S(2)}) %collective-permute-start.9) | collective-permute-done | bytes 147488 | tf_op jit(solution)/shard_map/ppermute | solution.py:234
  73.9 3.4 %collective-permute-start.10 = (f32[288,128]{1,0:T(8,128)S(1)}, f32[288,128]{1,0:T(8,128)S(1)}, u32[]{:S(2)}, u32[]{:S(2)}) collective-permute-start(f32[288,128]{1,0:T(8,128)S(1)} %sum_1_0.1.refs_7_.refs_0_), channel_id=1, source_target_pairs={{0,4},{1,5},{2,6},{3,7},{4,0},{5,1},{6,2},{7,3},{8,12},{9,13},{10,... | collective-permute-start | bytes 442376 | tf_op jit(solution)/shard_map/ppermute | solution.py:234
  77.3 0.0 collective-permute-done.15.refs_1_
  77.3 0.1 collective-permute-start.19
  77.4 0.0 collective-permute-done.13.refs_5_
  77.4 0.0 collective-permute-done.14.refs_6_
  77.4 0.0 copy-done
  77.4 0.0 copy-done.1
  77.4 5.9 %steps_0.1 = (f32[2,256,768]{2,1,0:T(8,128)}, f32[8,128]{1,0:T(8,128)S(1)}) custom-call(s32[1]{0:T(128)} %bitcast.refs_0_, bf16[2,256,768]{2,1,0:T(8,128)(2,1)S(1)} %copy-done, bf16[2,256,768]{2,1,0:T(8,128)(2,1)S(1)} %copy-done.1, f32[584,128]{1,0:T(8,128)S(1)} %total_0_0.1.refs_3_, f32[584,128]{1,0:T(8,128)S(1)} %collective-permute-done.12.refs_4_, ...), custom_call_target="tpu_custom_call" | custom-call | flops 3321888768 | bytes 1196032 | tf_op jit(solution)/shard_map/steps_0/pallas_call | solution.py:41
  83.4 7.3 %collective-permute-done.19.refs_1_ = f32[296,128]{1,0:T(8,128)S(1)} collective-permute-done((f32[296,128]{1,0:T(8,128)S(1)}, f32[296,128]{1,0:T(8,128)S(1)}, u32[]{:S(2)}, u32[]{:S(2)}) %collective-permute-start.19) | collective-permute-done | bytes 151584 | tf_op jit(solution)/shard_map/ppermute | solution.py:234
  90.7 0.8 collective-permute-start.20
  91.5 0.0 collective-permute-done.10.refs_1_
  91.5 1.4 %collective-permute-start.16 = (f32[288,128]{1,0:T(8,128)S(1)}, f32[288,128]{1,0:T(8,128)S(1)}, u32[]{:S(2)}, u32[]{:S(2)}) collective-permute-start(f32[288,128]{1,0:T(8,128)S(1)} %total_1_0.1.refs_3_), channel_id=1, source_target_pairs={{0,2},{1,3},{2,0},{3,1},{4,6},{5,7},{6,4},{7,5},{8,10},{9,11},{10,... | collective-permute-start | bytes 442376 | tf_op jit(solution)/shard_map/ppermute | solution.py:234
  92.9 0.0 collective-permute-start.21
  92.9 4.5 %collective-permute-done.20.refs_8_ = f32[296,128]{1,0:T(8,128)S(1)} collective-permute-done((f32[296,128]{1,0:T(8,128)S(1)}, f32[296,128]{1,0:T(8,128)S(1)}, u32[]{:S(2)}, u32[]{:S(2)}) %collective-permute-start.20) | collective-permute-done | bytes 151584 | tf_op jit(solution)/shard_map/ppermute | solution.py:234
  97.4 0.0 collective-permute-start.22
  97.4 0.5 collective-permute-start.17
  97.9 1.1 %collective-permute-done.16.refs_4_ = f32[288,128]{1,0:T(8,128)S(1)} collective-permute-done((f32[288,128]{1,0:T(8,128)S(1)}, f32[288,128]{1,0:T(8,128)S(1)}, u32[]{:S(2)}, u32[]{:S(2)}) %collective-permute-start.16) | collective-permute-done | bytes 147488 | tf_op jit(solution)/shard_map/ppermute | solution.py:234
  98.9 0.0 collective-permute-start.18
  98.9 0.0 collective-permute-done.17.refs_5_
  98.9 0.0 collective-permute-done.21.refs_9_
  98.9 1.4 %collective-permute-done.18.refs_6_ = f32[288,128]{1,0:T(8,128)S(1)} collective-permute-done((f32[288,128]{1,0:T(8,128)S(1)}, f32[288,128]{1,0:T(8,128)S(1)}, u32[]{:S(2)}, u32[]{:S(2)}) %collective-permute-start.18) | collective-permute-done | bytes 147488 | tf_op jit(solution)/shard_map/ppermute | solution.py:234
  100.3 0.0 collective-permute-done.22.refs_10_
  100.3 6.3 %steps_1.1 = (f32[2,256,768]{2,1,0:T(8,128)}, f32[8,128]{1,0:T(8,128)}) custom-call(s32[1]{0:T(128)} %bitcast.refs_0_, bf16[2,256,768]{2,1,0:T(8,128)(2,1)S(1)} %copy-done, bf16[2,256,768]{2,1,0:T(8,128)(2,1)S(1)} %copy-done.1, f32[288,128]{1,0:T(8,128)S(1)} %total_1_0.1.refs_3_, ...), custom_call_target="tpu_custom_call", output_to_operand_aliasing={{0}: (11, {})} | custom-call | flops 3321888768 | bytes 1196032 | tf_op jit(solution)/shard_map/steps_1/pallas_call | solution.py:41
  (6 shorter events, 0.2 us)
Async XLA Ops:
  0.0 0.7 copy-start.2
  5.4 13.0 %collective-permute-start.3 = (bf16[256,768]{1,0:T(8,128)(2,1)S(1)}, bf16[256,768]{1,0:T(8,128)(2,1)S(1)}, u32[]{:S(2)}, u32[]{:S(2)}) collective-permute-start(bf16[256,768]{1,0:T(8,128)(2,1)S(1)} %get-tuple-element.33), channel_id=1, source_target_pairs={{0,8},{8,0},{16,24},{24,16},{1,9},{9,1},{17,25},{25,17},{2,10},{10... | collective-permute-start | bytes 1179656 | tf_op jit(solution)/shard_map/ppermute | solution.py:234
  8.4 19.0 %collective-permute-start.4 = (bf16[256,768]{1,0:T(8,128)(2,1)S(1)}, bf16[256,768]{1,0:T(8,128)(2,1)S(1)}, u32[]{:S(2)}, u32[]{:S(2)}) collective-permute-start(bf16[256,768]{1,0:T(8,128)(2,1)S(1)} %get-tuple-element.34), channel_id=1, source_target_pairs={{0,16},{8,24},{16,0},{24,8},{1,17},{9,25},{17,1},{25,9},{2,18},{10... | collective-permute-start | bytes 1179656 | tf_op jit(solution)/shard_map/ppermute | solution.py:234
  9.9 17.5 %collective-permute-start.5 = (bf16[256,768]{1,0:T(8,128)(2,1)S(1)}, bf16[256,768]{1,0:T(8,128)(2,1)S(1)}, u32[]{:S(2)}, u32[]{:S(2)}) collective-permute-start(bf16[256,768]{1,0:T(8,128)(2,1)S(1)} %get-tuple-element.35), channel_id=1, source_target_pairs={{0,24},{8,16},{16,8},{24,0},{1,25},{9,17},{17,9},{25,1},{2,26},{10... | collective-permute-start | bytes 1179656 | tf_op jit(solution)/shard_map/ppermute | solution.py:234
  28.6 3.6 %collective-permute-start.6 = (f32[1168,128]{1,0:T(8,128)S(1)}, f32[1168,128]{1,0:T(8,128)S(1)}, u32[]{:S(2)}, u32[]{:S(2)}) collective-permute-start(f32[1168,128]{1,0:T(8,128)S(1)} %get-tuple-element.37), channel_id=1, source_target_pairs={{0,1},{1,0},{2,3},{3,2},{4,5},{5,4},{6,7},{7,6},{8,9},{9,8},{10,11... | collective-permute-start | bytes 1794056 | tf_op jit(solution)/shard_map/ppermute | solution.py:234
  28.7 15.0 %collective-permute-start = (bf16[256,768]{1,0:T(8,128)(2,1)S(1)}, bf16[256,768]{1,0:T(8,128)(2,1)S(1)}, u32[]{:S(2)}, u32[]{:S(2)}) collective-permute-start(bf16[256,768]{1,0:T(8,128)(2,1)S(1)} %get-tuple-element.29), channel_id=1, source_target_pairs={{0,8},{8,0},{16,24},{24,16},{1,9},{9,1},{17,25},{25,17},{2,10},{10... | collective-permute-start | bytes 1179656 | tf_op jit(solution)/shard_map/ppermute | solution.py:234
  30.0 18.0 %collective-permute-start.1 = (bf16[256,768]{1,0:T(8,128)(2,1)S(1)}, bf16[256,768]{1,0:T(8,128)(2,1)S(1)}, u32[]{:S(2)}, u32[]{:S(2)}) collective-permute-start(bf16[256,768]{1,0:T(8,128)(2,1)S(1)} %get-tuple-element.30), channel_id=1, source_target_pairs={{0,16},{8,24},{16,0},{24,8},{1,17},{9,25},{17,1},{25,9},{2,18},{10... | collective-permute-start | bytes 1179656 | tf_op jit(solution)/shard_map/ppermute | solution.py:234
  30.8 18.8 %collective-permute-start.2 = (bf16[256,768]{1,0:T(8,128)(2,1)S(1)}, bf16[256,768]{1,0:T(8,128)(2,1)S(1)}, u32[]{:S(2)}, u32[]{:S(2)}) collective-permute-start(bf16[256,768]{1,0:T(8,128)(2,1)S(1)} %get-tuple-element.31), channel_id=1, source_target_pairs={{0,24},{8,16},{16,8},{24,0},{1,25},{9,17},{17,9},{25,1},{2,26},{10... | collective-permute-start | bytes 1179656 | tf_op jit(solution)/shard_map/ppermute | solution.py:234
  32.3 8.7 %collective-permute-start.7 = (f32[584,128]{1,0:T(8,128)S(1)}, f32[584,128]{1,0:T(8,128)S(1)}, u32[]{:S(2)}, u32[]{:S(2)}) collective-permute-start(f32[584,128]{1,0:T(8,128)S(1)} %get-tuple-element.39), channel_id=1, source_target_pairs={{0,2},{1,3},{2,0},{3,1},{4,6},{5,7},{6,4},{7,5},{8,10},{9,11},{10,... | collective-permute-start | bytes 897032 | tf_op jit(solution)/shard_map/ppermute | solution.py:234
  41.0 15.1 %collective-permute-start.11 = (f32[584,128]{1,0:T(8,128)S(1)}, f32[584,128]{1,0:T(8,128)S(1)}, u32[]{:S(2)}, u32[]{:S(2)}) collective-permute-start(f32[584,128]{1,0:T(8,128)S(1)} %sum_0_0.1.refs_5_.refs_0_), channel_id=1, source_target_pairs={{0,4},{1,5},{2,6},{3,7},{4,0},{5,1},{6,2},{7,3},{8,12},{9,13},{10,... | collective-permute-start | bytes 897032 | tf_op jit(solution)/shard_map/ppermute | solution.py:234
  50.8 26.6 %copy-start = (bf16[2,256,768]{2,1,0:T(8,128)(2,1)S(1)}, bf16[2,256,768]{2,1,0:T(8,128)(2,1)}, u32[]{:S(2)}) copy-start(bf16[2,256,768]{2,1,0:T(8,128)(2,1)} %refs_1_.3) | copy-start | bytes 2359300
  50.9 26.6 %copy-start.1 = (bf16[2,256,768]{2,1,0:T(8,128)(2,1)S(1)}, bf16[2,256,768]{2,1,0:T(8,128)(2,1)}, u32[]{:S(2)}) copy-start(bf16[2,256,768]{2,1,0:T(8,128)(2,1)} %refs_2_.7) | copy-start | bytes 2359300
  50.9 13.3 %collective-permute-start.8 = (f32[1168,128]{1,0:T(8,128)S(1)}, f32[1168,128]{1,0:T(8,128)S(1)}, u32[]{:S(2)}, u32[]{:S(2)}) collective-permute-start(f32[1168,128]{1,0:T(8,128)S(1)} %get-tuple-element.41), channel_id=1, source_target_pairs={{0,1},{1,0},{2,3},{3,2},{4,5},{5,4},{6,7},{7,6},{8,9},{9,8},{10,11... | collective-permute-start | bytes 1794056 | tf_op jit(solution)/shard_map/ppermute | solution.py:234
  56.2 8.0 %collective-permute-start.12 = (f32[584,128]{1,0:T(8,128)S(1)}, f32[584,128]{1,0:T(8,128)S(1)}, u32[]{:S(2)}, u32[]{:S(2)}) collective-permute-start(f32[584,128]{1,0:T(8,128)S(1)} %total_0_0.1.refs_3_), channel_id=1, source_target_pairs={{0,2},{1,3},{2,0},{3,1},{4,6},{5,7},{6,4},{7,5},{8,10},{9,11},{10,... | collective-permute-start | bytes 897032 | tf_op jit(solution)/shard_map/ppermute | solution.py:234
  56.9 20.5 %collective-permute-start.13 = (f32[584,128]{1,0:T(8,128)S(1)}, f32[584,128]{1,0:T(8,128)S(1)}, u32[]{:S(2)}, u32[]{:S(2)}) collective-permute-start(f32[584,128]{1,0:T(8,128)S(1)} %total_0_0.1.refs_3_), channel_id=1, source_target_pairs={{0,1},{1,0},{2,3},{3,2},{4,5},{5,4},{6,7},{7,6},{8,9},{9,8},{10,11... | collective-permute-start | bytes 897032 | tf_op jit(solution)/shard_map/ppermute | solution.py:234
  64.2 13.3 %collective-permute-start.14 = (f32[584,128]{1,0:T(8,128)S(1)}, f32[584,128]{1,0:T(8,128)S(1)}, u32[]{:S(2)}, u32[]{:S(2)}) collective-permute-start(f32[584,128]{1,0:T(8,128)S(1)} %collective-permute-done.12.refs_4_), channel_id=1, source_target_pairs={{0,1},{1,0},{2,3},{3,2},{4,5},{5,4},{6,7},{7,6},{8,9},{9,8},{10,11... | collective-permute-start | bytes 897032 | tf_op jit(solution)/shard_map/ppermute | solution.py:234
  64.3 13.0 %collective-permute-start.15 = (f32[296,128]{1,0:T(8,128)S(1)}, f32[296,128]{1,0:T(8,128)S(1)}, u32[]{:S(2)}, u32[]{:S(2)}) collective-permute-start(f32[296,128]{1,0:T(8,128)S(1)} %get-tuple-element.45), channel_id=1, source_target_pairs={{0,2},{1,3},{2,0},{3,1},{4,6},{5,7},{6,4},{7,5},{8,10},{9,11},{10,... | collective-permute-start | bytes 454664 | tf_op jit(solution)/shard_map/ppermute | solution.py:234
  66.1 7.8 %collective-permute-start.9 = (f32[288,128]{1,0:T(8,128)S(1)}, f32[288,128]{1,0:T(8,128)S(1)}, u32[]{:S(2)}, u32[]{:S(2)}) collective-permute-start(f32[288,128]{1,0:T(8,128)S(1)} %get-tuple-element.43), channel_id=1, source_target_pairs={{0,2},{1,3},{2,0},{3,1},{4,6},{5,7},{6,4},{7,5},{8,10},{9,11},{10,... | collective-permute-start | bytes 442376 | tf_op jit(solution)/shard_map/ppermute | solution.py:234
  73.9 17.7 %collective-permute-start.10 = (f32[288,128]{1,0:T(8,128)S(1)}, f32[288,128]{1,0:T(8,128)S(1)}, u32[]{:S(2)}, u32[]{:S(2)}) collective-permute-start(f32[288,128]{1,0:T(8,128)S(1)} %sum_1_0.1.refs_7_.refs_0_), channel_id=1, source_target_pairs={{0,4},{1,5},{2,6},{3,7},{4,0},{5,1},{6,2},{7,3},{8,12},{9,13},{10,... | collective-permute-start | bytes 442376 | tf_op jit(solution)/shard_map/ppermute | solution.py:234
  77.3 13.4 %collective-permute-start.19 = (f32[296,128]{1,0:T(8,128)S(1)}, f32[296,128]{1,0:T(8,128)S(1)}, u32[]{:S(2)}, u32[]{:S(2)}) collective-permute-start(f32[296,128]{1,0:T(8,128)S(1)} %sum_1_1.1.refs_8_.refs_0_), channel_id=1, source_target_pairs={{0,4},{1,5},{2,6},{3,7},{4,0},{5,1},{6,2},{7,3},{8,12},{9,13},{10,... | collective-permute-start | bytes 454664 | tf_op jit(solution)/shard_map/ppermute | solution.py:234
  90.7 6.6 %collective-permute-start.20 = (f32[296,128]{1,0:T(8,128)S(1)}, f32[296,128]{1,0:T(8,128)S(1)}, u32[]{:S(2)}, u32[]{:S(2)}) collective-permute-start(f32[296,128]{1,0:T(8,128)S(1)} %total_1_1.1.refs_7_), channel_id=1, source_target_pairs={{0,2},{1,3},{2,0},{3,1},{4,6},{5,7},{6,4},{7,5},{8,10},{9,11},{10,... | collective-permute-start | bytes 454664 | tf_op jit(solution)/shard_map/ppermute | solution.py:234
  91.5 7.4 %collective-permute-start.16 = (f32[288,128]{1,0:T(8,128)S(1)}, f32[288,128]{1,0:T(8,128)S(1)}, u32[]{:S(2)}, u32[]{:S(2)}) collective-permute-start(f32[288,128]{1,0:T(8,128)S(1)} %total_1_0.1.refs_3_), channel_id=1, source_target_pairs={{0,2},{1,3},{2,0},{3,1},{4,6},{5,7},{6,4},{7,5},{8,10},{9,11},{10,... | collective-permute-start | bytes 442376 | tf_op jit(solution)/shard_map/ppermute | solution.py:234
  92.9 6.0 %collective-permute-start.21 = (f32[296,128]{1,0:T(8,128)S(1)}, f32[296,128]{1,0:T(8,128)S(1)}, u32[]{:S(2)}, u32[]{:S(2)}) collective-permute-start(f32[296,128]{1,0:T(8,128)S(1)} %total_1_1.1.refs_7_), channel_id=1, source_target_pairs={{0,1},{1,0},{2,3},{3,2},{4,5},{5,4},{6,7},{7,6},{8,9},{9,8},{10,11... | collective-permute-start | bytes 454664 | tf_op jit(solution)/shard_map/ppermute | solution.py:234
  97.4 3.0 %collective-permute-start.22 = (f32[296,128]{1,0:T(8,128)S(1)}, f32[296,128]{1,0:T(8,128)S(1)}, u32[]{:S(2)}, u32[]{:S(2)}) collective-permute-start(f32[296,128]{1,0:T(8,128)S(1)} %collective-permute-done.20.refs_8_), channel_id=1, source_target_pairs={{0,1},{1,0},{2,3},{3,2},{4,5},{5,4},{6,7},{7,6},{8,9},{9,8},{10,11... | collective-permute-start | bytes 454664 | tf_op jit(solution)/shard_map/ppermute | solution.py:234
  97.4 1.6 %collective-permute-start.17 = (f32[288,128]{1,0:T(8,128)S(1)}, f32[288,128]{1,0:T(8,128)S(1)}, u32[]{:S(2)}, u32[]{:S(2)}) collective-permute-start(f32[288,128]{1,0:T(8,128)S(1)} %total_1_0.1.refs_3_), channel_id=1, source_target_pairs={{0,1},{1,0},{2,3},{3,2},{4,5},{5,4},{6,7},{7,6},{8,9},{9,8},{10,11... | collective-permute-start | bytes 442376 | tf_op jit(solution)/shard_map/ppermute | solution.py:234
  98.9 1.4 %collective-permute-start.18 = (f32[288,128]{1,0:T(8,128)S(1)}, f32[288,128]{1,0:T(8,128)S(1)}, u32[]{:S(2)}, u32[]{:S(2)}) collective-permute-start(f32[288,128]{1,0:T(8,128)S(1)} %collective-permute-done.16.refs_4_), channel_id=1, source_target_pairs={{0,1},{1,0},{2,3},{3,2},{4,5},{5,4},{6,7},{7,6},{8,9},{9,8},{10,11... | collective-permute-start | bytes 442376 | tf_op jit(solution)/shard_map/ppermute | solution.py:234

commit v3 on v2

v3 whole, which is shorter than its diff:
```python
import functools

import jax
import jax.numpy as jnp
from jax import lax
from jax.experimental import pallas as pl
from jax.experimental.pallas import tpu as pltpu
from jax.sharding import PartitionSpec as P

STEPS = 4
BLOCK = 128
TILE = 16
CHUNKS = 1
LEVELS = 32760.0
OCTAVE = 8.0
relax_factor = 0.5
diagonal_eps = 1e-06
tiny = 1e-30
VMEM_LIMIT = 50 * 2**20

VMEM = pl.BlockSpec(memory_space=pltpu.VMEM)
ANY = pl.BlockSpec(memory_space=pl.ANY)
SMEM = pl.BlockSpec(memory_space=pltpu.SMEM)
F32, BF16, I32, I16 = jnp.float32, jnp.bfloat16, jnp.int32, jnp.int16


def call(kernel, out_shape, in_specs, scratch=(), flops=0, moved=0, out_specs=None, aliases=None, name=None, after=()):
    many = isinstance(out_shape, (list, tuple))
    used, idle = len(in_specs), len(after)

    def body(*refs):
        kernel(*refs[:used], *refs[used + idle:])

    inner = pl.pallas_call(
        body,
        out_shape=out_shape,
        in_specs=list(in_specs) + [ANY] * idle,
        out_specs=out_specs if out_specs is not None else ([VMEM] * len(out_shape) if many else VMEM),
        scratch_shapes=list(scratch),
        input_output_aliases=aliases or {},
        cost_estimate=pl.CostEstimate(flops=flops, bytes_accessed=moved, transcendentals=0),
        compiler_params=pltpu.CompilerParams(vmem_limit_bytes=VMEM_LIMIT),
        name=name,
    )
    return lambda *args: inner(*args, *after)


def cuts(size, chunks):
    ends = [size * (c + 1) // (TILE * chunks) * TILE for c in range(chunks)]
    return [end - start for start, end in zip([0] + ends, ends)]


def slots_of(owners, experts, capacity):
    tokens = owners.shape[1]
    lanes = 128
    blocks = tokens // lanes
    named = owners == lax.broadcasted_iota(I32, (experts, tokens), 0)
    ones = named.astype(F32)
    stacked = jnp.concatenate([ones[:, b * lanes:(b + 1) * lanes] for b in range(blocks)], axis=0)
    upto = lax.broadcasted_iota(I32, (lanes, lanes), 0) <= lax.broadcasted_iota(I32, (lanes, lanes), 1)
    within = jnp.dot(stacked.astype(BF16), upto.astype(F32).astype(BF16), preferred_element_type=F32)
    carry = jnp.zeros((experts, 1), F32)
    parts = []
    for b in range(blocks):
        part = within[b * experts:(b + 1) * experts]
        parts.append(part + carry)
        carry = carry + part[:, lanes - 1:lanes]
    counted = jnp.concatenate(parts, axis=1)
    rank = jnp.sum(jnp.where(named, counted - 1.0, 0.0), axis=0, keepdims=True)
    return owners * capacity + rank.astype(I32)


def place(key, rows_ref, experts, capacity, out_refs, squares):
    tokens, hidden = rows_ref.shape
    places = lax.broadcasted_iota(I32, (capacity, tokens), 0)
    chosen = jnp.concatenate(
        [(places == key - e * capacity).astype(F32).astype(BF16) for e in experts], axis=0
    )
    width = 2 * BLOCK
    for c in range(0, hidden, width):
        got = jnp.dot(chosen, rows_ref[:, c:c + width], preferred_element_type=F32)
        for k, (out_ref, (sum_ref, row)) in enumerate(zip(out_refs, squares)):
            part = got[k * capacity:(k + 1) * capacity]
            out_ref[:, c:c + width] = part.astype(BF16)
            sum_ref[row:row + 1, c:c + width] = jnp.sum(part * part, axis=0, keepdims=True)


def first_kernel(peers, slots, all_experts, capacity, me_ref, owner_ref, rows_ref, key_ref, square_ref, *out_refs):
    me = me_ref[0]
    key = slots_of(owner_ref[...], all_experts, capacity)
    key_ref[...] = key
    square_ref[...] = jnp.zeros_like(square_ref)
    others = range(1, peers)
    place(
        key, rows_ref, [lax.bitwise_xor(me, k) * slots for k in others], capacity, out_refs,
        [(square_ref, k * slots) for k in others],
    )


def second_kernel(peers, slots, capacity, me_ref, key_ref, rows_ref, square_ref, near_ref, far_ref, *refs):
    out_refs, total = refs[:-1], refs[-1]
    me = me_ref[0]
    total[...] = square_ref[...]
    where = [(0, a) for a in range(slots)] + [(k, a) for a in range(1, slots) for k in range(1, peers)]
    place(
        key_ref[...], rows_ref, [lax.bitwise_xor(me, k) * slots + a for k, a in where], capacity, out_refs,
        [(total, k * slots + a) for k, a in where],
    )
    half = near_ref.shape[0]
    near_ref[...] = total[:half]
    far_ref[...] = total[half:]


def layout(hidden, halvings):
    blocks = hidden // BLOCK
    off = [(i, j) for i in range(blocks) for j in range(i + 1, blocks)]
    pairs = [(i, i + 1 if i + 1 < blocks else None) for i in range(0, blocks, 2)]
    tail = (len(off) + len(pairs)) * BLOCK
    unit = TILE << halvings
    return off, pairs, tail, -(-tail // unit) * unit


def eye_of(compare):
    return compare(lax.broadcasted_iota(I32, (BLOCK, BLOCK), 0), lax.broadcasted_iota(I32, (BLOCK, BLOCK), 1))


def bit_of(where, bit):
    return lax.bitwise_and(lax.shift_right_logical(where, bit), 1)


def root_of(diagonal):
    return lax.rsqrt(jnp.maximum(diagonal, tiny))


def scale_kernel(slot, halvings, diagonal_ref, out_ref):
    hidden = diagonal_ref.shape[1]
    off, pairs, tail, length = layout(hidden, halvings)
    if length > tail:
        out_ref[tail:length] = jnp.zeros((length - tail, BLOCK), F32)
    root = root_of(diagonal_ref[slot:slot + 1])
    across = [jnp.broadcast_to(root[:, b * BLOCK:(b + 1) * BLOCK], (BLOCK, BLOCK)) for b in range(hidden // BLOCK)]
    down = [a.T for a in across]
    for n, (i, j) in enumerate(off):
        out_ref[n * BLOCK:(n + 1) * BLOCK] = down[i] * across[j]
    for n, (first, second) in enumerate(pairs):
        block = down[first] * across[first]
        if second is not None:
            block = jnp.where(eye_of(lax.lt), block, down[second] * across[second])
        row = (len(off) + n) * BLOCK
        out_ref[row:row + BLOCK] = block


def add_gram(halvings, chunk_refs, before, packed):
    hidden = chunk_refs[0].shape[1]
    off, pairs, tail, length = layout(hidden, halvings)
    at = {pair: n for n, pair in enumerate(off)}
    x = jnp.concatenate([r[...] for r in chunk_refs], axis=0) if len(chunk_refs) > 1 else chunk_refs[0][...]
    strip = 2 * BLOCK

    def put(n, value):
        rows = slice(n * BLOCK, (n + 1) * BLOCK)
        packed[rows] = value if before is None else before[rows] + value

    if length > tail:
        packed[tail:length] = jnp.zeros((length - tail, BLOCK), F32)
    for n, (first, second) in enumerate(pairs):
        low, high = first * BLOCK, min(first * BLOCK + strip, hidden)
        product = lax.dot_general(
            x[:, low:high], x[:, low:], (((0,), (0,)), ((), ())), preferred_element_type=F32
        )
        for i in range((high - low) // BLOCK):
            for j in range((hidden - low) // BLOCK):
                pair = (first + i, first + j)
                if pair in at:
                    put(at[pair], product[i * BLOCK:(i + 1) * BLOCK, j * BLOCK:(j + 1) * BLOCK])
        mixed = product[:BLOCK, :BLOCK]
        if second is not None:
            mixed = jnp.where(eye_of(lax.lt), mixed, product[BLOCK:, BLOCK:2 * BLOCK])
        put(len(off) + n, jnp.where(eye_of(lax.eq), 0.0, mixed))


def early_gram_kernel(halvings, *refs):
    add_gram(halvings, refs[:-1], None, refs[-1])


def late_gram_kernel(halvings, pieces, where_ref, before_ref, *refs):
    chunk_refs, (keep_ref, send_ref, packed) = refs[:pieces], refs[pieces:]
    add_gram(halvings, chunk_refs, before_ref, packed)
    half = keep_ref.shape[0]
    mine = bit_of(where_ref[0], 0)
    keep_ref[...] = packed[pl.ds(pl.multiple_of(mine * half, TILE), half)]
    send_ref[...] = packed[pl.ds(pl.multiple_of((1 - mine) * half, TILE), half)]


def encode(values, ref):
    rows = values.shape[0]
    largest = jnp.max(jnp.abs(values), axis=0, keepdims=True)
    exponent = jnp.ceil(OCTAVE * jnp.log2(jnp.maximum(largest, tiny)))
    factor = jnp.exp2(exponent * (-1.0 / OCTAVE)) * LEVELS
    ref[:rows] = jnp.floor(values * factor + 0.5).astype(I32).astype(I16)
    ref[rows:rows + TILE] = jnp.broadcast_to(exponent, (TILE, BLOCK)).astype(I32).astype(I16)


def decode(coded):
    rows = coded.shape[0] - TILE
    exponent = coded[rows:].astype(I32).astype(F32)[:1]
    return coded[:rows].astype(I32).astype(F32) * (jnp.exp2(exponent * (1.0 / OCTAVE)) * (1.0 / LEVELS))


def scaled_halve_kernel(bit, where_ref, keep_ref, got_ref, scale_ref, *out_refs):
    chunks = len(out_refs) // 2
    half = keep_ref.shape[0] // 2
    where = where_ref[0]
    outer = bit_of(where, 0) * keep_ref.shape[0]
    mine = bit_of(where, bit)
    for side, refs, coded in ((1 - mine, out_refs[chunks:], True), (mine, out_refs[:chunks], False)):
        start = 0
        for ref in refs:
            size = ref.shape[0] - TILE if coded else ref.shape[0]
            part = pl.ds(pl.multiple_of(side * half + start, TILE), size)
            factor = scale_ref[pl.ds(pl.multiple_of(outer + side * half + start, TILE), size)]
            value = (keep_ref[part] + got_ref[part]) * factor
            if coded:
                encode(value, ref)
            else:
                ref[...] = value
            start += size


def halve_kernel(bit, where_ref, keep_ref, got_ref, *refs):
    out_refs, total = refs[:-1], refs[-1]
    chunks = len(out_refs) // 2
    total[...] = keep_ref[...] + decode(got_ref[...])
    half = keep_ref.shape[0] // 2
    mine = bit_of(where_ref[0], bit)
    for side, refs, coded in ((1 - mine, out_refs[chunks:], True), (mine, out_refs[:chunks], False)):
        start = 0
        for ref in refs:
            size = ref.shape[0] - TILE if coded else ref.shape[0]
            value = total[pl.ds(pl.multiple_of(side * half + start, TILE), size)]
            if coded:
                encode(value, ref)
            else:
                ref[...] = value
            start += size


def sum_kernel(keep_ref, got_ref, coded_ref, value_ref):
    value = keep_ref[...] + decode(got_ref[...])
    encode(value, coded_ref)
    value_ref[...] = value


def total_kernel(keep_ref, got_ref, coded_ref):
    encode(keep_ref[...] + decode(got_ref[...]), coded_ref)


def unpack_kernel(slot, halvings, places, where_ref, diagonal_ref, *refs):
    piece_refs, (high_ref, low_ref, packed) = refs[:len(places)], refs[len(places):]
    hidden = diagonal_ref.shape[1]
    off, pairs, tail, length = layout(hidden, halvings)
    where = where_ref[0]
    for (flip, offset), piece_ref in zip(places, piece_refs):
        owner = lax.bitwise_xor(where, flip)
        start = offset
        for b in range(halvings):
            start = start + bit_of(owner, b) * (length >> (b + 1))
        value = decode(piece_ref[...])
        packed[pl.ds(pl.multiple_of(start, TILE), value.shape[0])] = value

    def put(i, j, block):
        rows, cols = slice(i * BLOCK, (i + 1) * BLOCK), slice(j * BLOCK, (j + 1) * BLOCK)
        hi = block.astype(BF16)
        high_ref[rows, cols] = hi
        low_ref[rows, cols] = (block - hi.astype(F32)).astype(BF16)

    for n, (i, j) in enumerate(off):
        block = packed[n * BLOCK:(n + 1) * BLOCK]
        put(i, j, block)
        put(j, i, block.T)
    diagonal = diagonal_ref[slot:slot + 1]
    root = root_of(diagonal)
    ones = diagonal * root * root
    for n, (first, second) in enumerate(pairs):
        row = (len(off) + n) * BLOCK
        block = packed[row:row + BLOCK]
        turned = block.T
        for i, above in ((first, lax.lt), (second, lax.gt)):
            if i is not None:
                whole = jnp.where(eye_of(above), block, turned)
                put(i, i, jnp.where(eye_of(lax.eq), ones[:, i * BLOCK:(i + 1) * BLOCK], whole))


def sweeps_kernel(slot, diagonal_ref, weight_ref, mask_ref, high_ref, low_ref, *refs):
    out_ref, token_ref, result, done = refs[-4:]
    diagonal = diagonal_ref[slot:slot + 1]
    back = 1.0 / root_of(diagonal)
    factor = relax_factor * (1.0 / (diagonal + diagonal_eps)) * back
    weight = weight_ref[slot].astype(F32)
    keep = mask_ref[slot].astype(F32)
    pruned = keep * weight
    for sweep in range(STEPS):
        change = (pruned - weight) * back
        top = change.astype(BF16)
        rest = (change - top.astype(F32)).astype(BF16)
        both = jnp.dot(jnp.concatenate([top, rest], axis=0), high_ref[...], preferred_element_type=F32)
        gradient = both[:top.shape[0]] + both[top.shape[0]:]
        gradient = gradient + jnp.dot(top, low_ref[...], preferred_element_type=F32)
        pruned = keep * (pruned - gradient * factor)
    result[...] = pruned
    token_ref[...] = pruned[:8, :BLOCK]
    copy = pltpu.make_async_copy(result, out_ref.at[slot], done)
    copy.start()
    copy.wait()


def on_device(expert_inputs, row_expert, down_weight, keep_mask):
    tokens, hidden = expert_inputs.shape
    slots, features, _ = down_weight.shape
    peers = lax.axis_size("expert")
    copies = lax.axis_size("rows")
    all_experts = slots * peers
    capacity = tokens // 8
    halvings = copies.bit_length() - 2
    length = layout(hidden, halvings)[3]
    me = jnp.reshape(lax.axis_index("expert").astype(I32), (1,))
    where = jnp.reshape(lax.axis_index("rows").astype(I32), (1,))
    owners = row_expert.reshape(1, tokens)

    def shape(rows, columns=BLOCK, dtype=F32):
        return jax.ShapeDtypeStruct((rows, columns), dtype)

    def over_experts(array, flip):
        return lax.ppermute(array, "expert", [(i, i ^ flip) for i in range(peers)])

    def over_rows(array, bit):
        return lax.ppermute(array, "rows", [(i, i ^ (1 << bit)) for i in range(copies)])

    chunk = shape(capacity, hidden, BF16)
    place_flops = 2 * capacity * tokens * hidden
    key, squares, *outgoing = call(
        functools.partial(first_kernel, peers, slots, all_experts, capacity),
        [shape(1, tokens, I32), shape(all_experts, hidden)] + [chunk] * (peers - 1),
        [SMEM, VMEM, VMEM], flops=place_flops * (peers - 1), moved=expert_inputs.size * 4, name="place_first",
    )(me, owners, expert_inputs)
    arrived = [[over_experts(outgoing[k - 1], k) for k in range(1, peers)]]
    count = slots + (slots - 1) * (peers - 1)
    near, far, *rest = call(
        functools.partial(second_kernel, peers, slots, capacity),
        [shape(all_experts // 2, hidden)] * 2 + [chunk] * count,
        [SMEM, VMEM, VMEM, VMEM], scratch=[pltpu.VMEM((all_experts, hidden), F32)],
        flops=place_flops * count, moved=expert_inputs.size * 4, name="place_rest",
    )(me, key, expert_inputs, squares)
    own = rest[:slots]
    for a in range(1, slots):
        outgoing = rest[slots + (a - 1) * (peers - 1):slots + a * (peers - 1)]
        arrived.append([over_experts(outgoing[k - 1], k) for k in range(1, peers)])

    flip = peers // 2
    diagonal = near + over_experts(far, flip)
    while flip > 1:
        flip = flip // 2
        half = flip * slots
        diagonal = diagonal[:half] + over_experts(diagonal[half:], flip)
    for bit in range(halvings + 1):
        diagonal = diagonal + over_rows(diagonal, bit)

    def begin(a, after):
        chunks = [own[a]] + arrived[a][:-1]
        return call(
            functools.partial(early_gram_kernel, halvings), shape(length), [VMEM] * len(chunks),
            flops=2 * capacity * len(chunks) * hidden * hidden, moved=length * BLOCK * 4, name=f"begin_{a}", after=after,
        )(*chunks)

    def reduce(a, before, after):
        scale = call(
            functools.partial(scale_kernel, a, halvings), shape(length), [VMEM], moved=length * BLOCK * 4, name=f"scale_{a}",
        )(diagonal)
        size = length // 2
        keep, send = call(
            functools.partial(late_gram_kernel, halvings, 1), [shape(size)] * 2, [SMEM] + [VMEM] * 2,
            scratch=[pltpu.VMEM((length, BLOCK), F32)],
            flops=2 * capacity * hidden * hidden, moved=length * BLOCK * 4, name=f"gram_{a}", after=[*after, scale],
        )(where, before, arrived[a][-1])
        keep, send = [keep], [send]
        for bit in range(1, halvings):
            got = over_rows(send[0], bit - 1)
            size = size // 2
            sizes = cuts(size, CHUNKS if bit == halvings - 1 else 1)
            first = bit == 1
            parts = call(
                functools.partial(scaled_halve_kernel if first else halve_kernel, bit),
                [shape(n) for n in sizes] + [shape(n + TILE, dtype=I16) for n in sizes],
                [SMEM] + [VMEM] * (3 if first else 2),
                scratch=() if first else [pltpu.VMEM((2 * size, BLOCK), F32)],
                moved=size * BLOCK * 4 * 6, name=f"halve_{a}_{bit}",
            )(where, keep[0], got, *([scale] if first else []))
            keep, send = parts[:len(sizes)], parts[len(sizes):]
        sums = []
        for c, (mine, theirs) in enumerate(zip(keep, send)):
            rows = mine.shape[0]
            sums.append(call(
                sum_kernel, [shape(rows + TILE, dtype=I16), shape(rows)], [VMEM, VMEM], moved=rows * BLOCK * 12,
                name=f"sum_{a}_{c}",
            )(mine, over_rows(theirs, halvings - 1)))
        return sums

    def totals(a, sums, after):
        totals = []
        for c, (coded, value) in enumerate(sums):
            rows = value.shape[0]
            totals.append(call(
                total_kernel, shape(rows + TILE, dtype=I16), [VMEM, VMEM], moved=rows * BLOCK * 12,
                name=f"total_{a}_{c}", after=after,
            )(value, over_rows(coded, halvings)))
        return totals

    def gather(a, totals):
        pieces, places, offset = [], [], 0
        for total in totals:
            held = [(0, total)]
            for bit in range(halvings - 1, -1, -1):
                held += [(flip ^ (1 << bit), over_rows(piece, bit)) for flip, piece in held]
            places += [(flip, offset) for flip, _ in held]
            pieces += [piece for _, piece in held]
            offset += total.shape[0] - TILE
        return call(
            functools.partial(unpack_kernel, a, halvings, places),
            [shape(hidden, hidden, BF16)] * 2, [SMEM] + [VMEM] * (1 + len(pieces)),
            scratch=[pltpu.VMEM((length, BLOCK), F32)], moved=length * BLOCK * 4, name=f"unpack_{a}",
        )(where, diagonal, *pieces)

    def sweeps(a, high, low, result, after):
        args = [diagonal, down_weight, keep_mask, high, low] + ([] if result is None else [result])
        return call(
            functools.partial(sweeps_kernel, a),
            [jax.ShapeDtypeStruct((slots, features, hidden), F32), shape(8)],
            [VMEM] * 5 + [ANY] * (len(args) - 5),
            out_specs=[ANY, VMEM],
            scratch=[pltpu.VMEM((features, hidden), F32), pltpu.SemaphoreType.DMA],
            aliases={} if result is None else {5: 0},
            flops=2 * 3 * STEPS * features * hidden * hidden, moved=hidden * hidden * 4, name=f"sweeps_{a}", after=after,
        )(*args)

    result, whole, total, sums = None, None, (), ()
    for a in range(slots):
        before = begin(a, [s[0] for s in sums])
        sums = reduce(a, before, total)
        token = ()
        if a > 0:
            result, *token = sweeps(a - 1, *whole, result, (sums[-1][0],))
        total = totals(a, sums, token)
        whole = gather(a, total)
    return sweeps(slots - 1, *whole, result, ())[0]


def solution(mesh):
    return jax.shard_map(
        on_device,
        mesh=mesh,
        in_specs=(
            P(("expert", "rows"), None),
            P(("expert", "rows"), None),
            P("expert", "rows", None),
            P("expert", "rows", None),
        ),
        out_specs=P("expert", "rows", None),
        check_vma=False,
    )
```

time: 107 us -> 101 us (0.944)
  waiting for transfers between devices: 58.4 us -> 42.7 us
  starting transfers between devices: 21.6 us -> 26.8 us
  Pallas kernels: 25.8 us -> 28.8 us
  local copies, waits for them, and re-layouts: 0.71 us -> 2.21 us
    ppermute x23, waiting for transfers between devices: 58.4 us -> 42.7 us  [the longest x15 24.7 us: over_rows(): lax.ppermute(array, 'rows', [(i, i ^ 1 << bit) for i in range(copies)])]
    ppermute x23, starting transfers between devices: 21.6 us -> 26.8 us  [the longest x15 15.5 us: over_rows(): lax.ppermute(array, 'rows', [(i, i ^ 1 << bit) for i in range(copies)])]
    pallas_call x14 -> x18, Pallas kernels: 25.8 us -> 28.8 us  [call(): return lambda *args: inner(*args, *after)]
    unnamed x6 -> x14, local copies, waits for them, and re-layouts: 0.71 us -> 2.2 us
  transfers between devices with their start and end apart: 23 -> 23, of which waited for: 12 -> 13; matrix products, arithmetic and copies ran while one was open for 0% -> 0% of each run, Pallas kernels for 13% -> 15%
where the time goes in v3:
time: 101 us
  waiting for transfers between devices  42.7 us (42%)
  Pallas kernels  28.8 us (29%)
  starting transfers between devices  26.8 us (27%)
  local copies, waits for them, and re-layouts  2.21 us (2%)
    pallas_call x18, Pallas kernels, call(): return lambda *args: inner(*args, *after)  28.8 us
    ppermute x15, waiting for transfers between devices, over_rows(): lax.ppermute(array, 'rows', [(i, i ^ 1 << bit) for i in range(copies)])  24.7 us
    ppermute x8, waiting for transfers between devices, over_experts(): return lax.ppermute(array, 'expert', [(i, i ^ flip) for i in range(peers)])  18.1 us
    ppermute x15, starting transfers between devices, over_rows(): lax.ppermute(array, 'rows', [(i, i ^ 1 << bit) for i in range(copies)])  15.5 us
    ppermute x8, starting transfers between devices, over_experts(): return lax.ppermute(array, 'expert', [(i, i ^ flip) for i in range(peers)])  11.3 us
    unnamed x14, local copies, waits for them, and re-layouts  2.2 us
  transfers between devices with their start and end apart: 23, of which 13 were waited for; matrix products, arithmetic and copies ran while one was open for 0% of the time, Pallas kernels for 15%

profile of v3, /device:TPU:0, one launch (start us, length us, event | category | flops | bytes accessed | tf_op | source)
XLA Modules:
  0.0 100.9 jit_solution(4246749336001453610)
XLA Ops:
  0.0 0.7 copy-done.2
  0.7 4.7 %place_first.1 = (s32[1,2048]{1,0:T(1,128)S(1)}, f32[8,768]{1,0:T(8,128)S(1)}, bf16[256,768]{1,0:T(8,128)(2,1)S(1)}, bf16[256,768]{1,0:T(8,128)(2,1)S(1)}, bf16[256,768]{1,0:T(8,128)(2,1)S(1)}) custom-call(s32[1]{0:T(128)} %bitcast.refs_0_, s32[1,2048]{1,0:T(1,128)S(1)} %bitcast.3, bf16[2048,768]{1,0:T(8,128)(2,1)} %refs_2_.5), custom_call_target="tpu_custom_call" | custom-call | flops 2415919104 | bytes 6291456 | tf_op jit(solution)/shard_map/place_first/pallas_call | solution.py:45
  5.4 3.0 %collective-permute-start.7 = (bf16[256,768]{1,0:T(8,128)(2,1)S(1)}, bf16[256,768]{1,0:T(8,128)(2,1)S(1)}, u32[]{:S(2)}, u32[]{:S(2)}) collective-permute-start(bf16[256,768]{1,0:T(8,128)(2,1)S(1)} %get-tuple-element.44), channel_id=1, source_target_pairs={{0,8},{8,0},{16,24},{24,16},{1,9},{9,1},{17,25},{25,17},{2,10},{10... | collective-permute-start | bytes 1179656 | tf_op jit(solution)/shard_map/ppermute | solution.py:334
  8.4 1.5 %collective-permute-start.8 = (bf16[256,768]{1,0:T(8,128)(2,1)S(1)}, bf16[256,768]{1,0:T(8,128)(2,1)S(1)}, u32[]{:S(2)}, u32[]{:S(2)}) collective-permute-start(bf16[256,768]{1,0:T(8,128)(2,1)S(1)} %get-tuple-element.45), channel_id=1, source_target_pairs={{0,16},{8,24},{16,0},{24,8},{1,17},{9,25},{17,1},{25,9},{2,18},{10... | collective-permute-start | bytes 1179656 | tf_op jit(solution)/shard_map/ppermute | solution.py:334
  9.9 0.0 collective-permute-start.9
  10.0 6.3 %place_rest.1 = (f32[4,768]{1,0:T(4,128)S(1)}, f32[4,768]{1,0:T(4,128)S(1)}, bf16[256,768]{1,0:T(8,128)(2,1)S(1)}, bf16[256,768]{1,0:T(8,128)(2,1)S(1)}, bf16[25...) custom-call(s32[1]{0:T(128)} %bitcast.refs_0_, ...), custom_call_target="tpu_custom_call" | custom-call | flops 4026531840 | bytes 6291456 | tf_op jit(solution)/shard_map/place_rest/pallas_call | solution.py:45
  16.2 0.0 copy-start.3
  16.2 0.7 copy-done.3
  17.0 0.7 copy-done.5
  17.7 2.0 %collective-permute-start = (f32[4,768]{1,0:T(4,128)S(1)}, f32[4,768]{1,0:T(4,128)S(1)}, u32[]{:S(2)}, u32[]{:S(2)}) collective-permute-start(f32[4,768]{1,0:T(4,128)S(1)} %get-tuple-element.39), channel_id=1, source_target_pairs={{0,16},{8,24},{16,0},{24,8},{1,17},{9,25},{17,1},{25,9},{2,18},{10... | collective-permute-start | bytes 36872 | tf_op jit(solution)/shard_map/ppermute | solution.py:334
  19.7 8.0 %collective-permute-done = f32[4,768]{1,0:T(4,128)S(1)} collective-permute-done((f32[4,768]{1,0:T(4,128)S(1)}, f32[4,768]{1,0:T(4,128)S(1)}, u32[]{:S(2)}, u32[]{:S(2)}) %collective-permute-start) | collective-permute-done | bytes 12320 | tf_op jit(solution)/shard_map/ppermute | solution.py:334
  27.7 1.2 %collective-permute-start.1 = (f32[2,768]{1,0:T(2,128)S(1)}, f32[2,768]{1,0:T(2,128)S(1)}, u32[]{:S(2)}, u32[]{:S(2)}) collective-permute-start(f32[2,768]{1,0:T(2,128)S(1)} %slice.9), channel_id=1, source_target_pairs={{0,8},{8,0},{16,24},{24,16},{1,9},{9,1},{17,25},{25,17},{2,10},{10... | collective-permute-start | bytes 18440 | tf_op jit(solution)/shard_map/ppermute | solution.py:334
  28.9 2.5 %collective-permute-done.1 = f32[2,768]{1,0:T(2,128)S(1)} collective-permute-done((f32[2,768]{1,0:T(2,128)S(1)}, f32[2,768]{1,0:T(2,128)S(1)}, u32[]{:S(2)}, u32[]{:S(2)}) %collective-permute-start.1) | collective-permute-done | bytes 6176 | tf_op jit(solution)/shard_map/ppermute | solution.py:334
  31.4 0.0 collective-permute-start.2
  31.4 1.2 %collective-permute-done.2 = f32[2,768]{1,0:T(2,128)S(1)} collective-permute-done((f32[2,768]{1,0:T(2,128)S(1)}, f32[2,768]{1,0:T(2,128)S(1)}, u32[]{:S(2)}, u32[]{:S(2)}) %collective-permute-start.2) | collective-permute-done | bytes 6176 | tf_op jit(solution)/shard_map/ppermute | solution.py:337
  32.6 1.6 %collective-permute-start.3 = (f32[2,768]{1,0:T(2,128)S(1)}, f32[2,768]{1,0:T(2,128)S(1)}, u32[]{:S(2)}, u32[]{:S(2)}) collective-permute-start(f32[2,768]{1,0:T(2,128)S(1)} %add.17), channel_id=1, source_target_pairs={{0,2},{1,3},{2,0},{3,1},{4,6},{5,7},{6,4},{7,5},{8,10},{9,11},{10,... | collective-permute-start | bytes 18440 | tf_op jit(solution)/shard_map/ppermute | solution.py:337
  34.1 2.1 %collective-permute-done.3 = f32[2,768]{1,0:T(2,128)S(1)} collective-permute-done((f32[2,768]{1,0:T(2,128)S(1)}, f32[2,768]{1,0:T(2,128)S(1)}, u32[]{:S(2)}, u32[]{:S(2)}) %collective-permute-start.3) | collective-permute-done | bytes 6176 | tf_op jit(solution)/shard_map/ppermute | solution.py:337
  36.2 2.6 %collective-permute-start.4 = (f32[2,768]{1,0:T(2,128)S(1)}, f32[2,768]{1,0:T(2,128)S(1)}, u32[]{:S(2)}, u32[]{:S(2)}) collective-permute-start(f32[2,768]{1,0:T(2,128)S(1)} %add.18), channel_id=1, source_target_pairs={{0,4},{1,5},{2,6},{3,7},{4,0},{5,1},{6,2},{7,3},{8,12},{9,13},{10,... | collective-permute-start | bytes 18440 | tf_op jit(solution)/shard_map/ppermute | solution.py:337
  38.8 1.9 %collective-permute-done.4 = f32[2,768]{1,0:T(2,128)S(1)} collective-permute-done((f32[2,768]{1,0:T(2,128)S(1)}, f32[2,768]{1,0:T(2,128)S(1)}, u32[]{:S(2)}, u32[]{:S(2)}) %collective-permute-start.4) | collective-permute-done | bytes 6176 | tf_op jit(solution)/shard_map/ppermute | solution.py:337
  40.7 0.2 scale_0.1.refs_3_
  40.9 0.0 collective-permute-done.7.refs_1_
  40.9 0.0 collective-permute-done.8.refs_2_
  41.0 0.8 begin_0.1.refs_1_
  41.8 0.0 collective-permute-done.9.refs_2_
  41.8 0.6 gram_0.1
  42.4 0.1 collective-permute-start.10
  42.5 1.2 %collective-permute-start.5 = (bf16[256,768]{1,0:T(8,128)(2,1)S(1)}, bf16[256,768]{1,0:T(8,128)(2,1)S(1)}, u32[]{:S(2)}, u32[]{:S(2)}) collective-permute-start(bf16[256,768]{1,0:T(8,128)(2,1)S(1)} %get-tuple-element.41), channel_id=1, source_target_pairs={{0,8},{8,0},{16,24},{24,16},{1,9},{9,1},{17,25},{25,17},{2,10},{10... | collective-permute-start | bytes 1179656 | tf_op jit(solution)/shard_map/ppermute | solution.py:334
  43.7 0.9 collective-permute-start.6
  44.6 1.4 %collective-permute-start.12 = (bf16[256,768]{1,0:T(8,128)(2,1)S(1)}, bf16[256,768]{1,0:T(8,128)(2,1)S(1)}, u32[]{:S(2)}, u32[]{:S(2)}) collective-permute-start(bf16[256,768]{1,0:T(8,128)(2,1)S(1)} %get-tuple-element.52), channel_id=1, source_target_pairs={{0,24},{8,16},{16,8},{24,0},{1,25},{9,17},{17,9},{25,1},{2,26},{10... | collective-permute-start | bytes 1179656 | tf_op jit(solution)/shard_map/ppermute | solution.py:334
  46.0 0.2 halve_0_1.1
  46.2 0.0 copy-start.4
  46.2 1.6 %collective-permute-start.11 = (s16[592,128]{1,0:T(8,128)(2,1)S(1)}, s16[592,128]{1,0:T(8,128)(2,1)S(1)}, u32[]{:S(2)}, u32[]{:S(2)}) collective-permute-start(s16[592,128]{1,0:T(8,128)(2,1)S(1)} %get-tuple-element.50), channel_id=1, source_target_pairs={{0,2},{1,3},{2,0},{3,1},{4,6},{5,7},{6,4},{7,5},{8,10},{9,11},{10,... | collective-permute-start | bytes 454664 | tf_op jit(solution)/shard_map/ppermute | solution.py:337
  47.9 3.9 %collective-permute-done.11.refs_1_ = s16[592,128]{1,0:T(8,128)(2,1)S(1)} collective-permute-done((s16[592,128]{1,0:T(8,128)(2,1)S(1)}, s16[592,128]{1,0:T(8,128)(2,1)S(1)}, u32[]{:S(2)}, u32[]{:S(2)}) %collective-permute-start.11) | collective-permute-done | bytes 151584 | tf_op jit(solution)/shard_map/ppermute | solution.py:337
  51.8 0.1 sum_0_0.1
  51.9 2.7 %collective-permute-start.13 = (s16[592,128]{1,0:T(8,128)(2,1)S(1)}, s16[592,128]{1,0:T(8,128)(2,1)S(1)}, u32[]{:S(2)}, u32[]{:S(2)}) collective-permute-start(s16[592,128]{1,0:T(8,128)(2,1)S(1)} %get-tuple-element.51.refs_3_), channel_id=1, source_target_pairs={{0,4},{1,5},{2,6},{3,7},{4,0},{5,1},{6,2},{7,3},{8,12},{9,13},{10,... | collective-permute-start | bytes 454664 | tf_op jit(solution)/shard_map/ppermute | solution.py:337
  54.6 0.2 scale_1.1.refs_4_.refs_3_
  54.8 7.0 %collective-permute-done.6.refs_2_ = bf16[256,768]{1,0:T(8,128)(2,1)S(1)} collective-permute-done((bf16[256,768]{1,0:T(8,128)(2,1)S(1)}, bf16[256,768]{1,0:T(8,128)(2,1)S(1)}, u32[]{:S(2)}, u32[]{:S(2)}) %collective-permute-start.6) | collective-permute-done | bytes 393248 | tf_op jit(solution)/shard_map/ppermute | solution.py:334
  61.7 0.8 begin_1.1.refs_1_
  62.6 0.0 collective-permute-done.13.refs_1_
  62.6 0.1 total_0_0.1.refs_3_.refs_2_
  62.7 0.6 collective-permute-done.12.refs_2_
  63.4 0.6 gram_1.1
  64.0 0.1 collective-permute-start.14
  64.0 1.6 %collective-permute-start.17 = (s16[592,128]{1,0:T(8,128)(2,1)S(1)}, s16[592,128]{1,0:T(8,128)(2,1)S(1)}, u32[]{:S(2)}, u32[]{:S(2)}) collective-permute-start(s16[592,128]{1,0:T(8,128)(2,1)S(1)} %total_0_0.1.refs_3_.refs_2_), channel_id=1, source_target_pairs={{0,2},{1,3},{2,0},{3,1},{4,6},{5,7},{6,4},{7,5},{8,10},{9,11},{10,... | collective-permute-start | bytes 454664 | tf_op jit(solution)/shard_map/ppermute | solution.py:337
  65.7 0.2 collective-permute-start.18
  65.9 4.5 %collective-permute-done.17.refs_3_ = s16[592,128]{1,0:T(8,128)(2,1)S(1)} collective-permute-done((s16[592,128]{1,0:T(8,128)(2,1)S(1)}, s16[592,128]{1,0:T(8,128)(2,1)S(1)}, u32[]{:S(2)}, u32[]{:S(2)}) %collective-permute-start.17) | collective-permute-done | bytes 151584 | tf_op jit(solution)/shard_map/ppermute | solution.py:337
  70.4 0.0 collective-permute-start.19
  70.4 0.0 collective-permute-done.14.refs_2_
  70.4 0.0 copy-start.1
  70.4 0.2 halve_1_1.1
  70.6 1.6 %collective-permute-start.15 = (s16[592,128]{1,0:T(8,128)(2,1)S(1)}, s16[592,128]{1,0:T(8,128)(2,1)S(1)}, u32[]{:S(2)}, u32[]{:S(2)}) collective-permute-start(s16[592,128]{1,0:T(8,128)(2,1)S(1)} %get-tuple-element.57), channel_id=1, source_target_pairs={{0,2},{1,3},{2,0},{3,1},{4,6},{5,7},{6,4},{7,5},{8,10},{9,11},{10,... | collective-permute-start | bytes 454664 | tf_op jit(solution)/shard_map/ppermute | solution.py:337
  72.3 0.0 collective-permute-done.18.refs_4_
  72.3 0.7 unpack_0.1
  73.0 4.0 %collective-permute-done.15.refs_1_ = s16[592,128]{1,0:T(8,128)(2,1)S(1)} collective-permute-done((s16[592,128]{1,0:T(8,128)(2,1)S(1)}, s16[592,128]{1,0:T(8,128)(2,1)S(1)}, u32[]{:S(2)}, u32[]{:S(2)}) %collective-permute-start.15) | collective-permute-done | bytes 151584 | tf_op jit(solution)/shard_map/ppermute | solution.py:337
  77.0 0.1 sum_1_0.1
  77.2 2.7 %collective-permute-start.16 = (s16[592,128]{1,0:T(8,128)(2,1)S(1)}, s16[592,128]{1,0:T(8,128)(2,1)S(1)}, u32[]{:S(2)}, u32[]{:S(2)}) collective-permute-start(s16[592,128]{1,0:T(8,128)(2,1)S(1)} %get-tuple-element.59.refs_5_), channel_id=1, source_target_pairs={{0,4},{1,5},{2,6},{3,7},{4,0},{5,1},{6,2},{7,3},{8,12},{9,13},{10,... | collective-permute-start | bytes 454664 | tf_op jit(solution)/shard_map/ppermute | solution.py:337
  79.8 5.9 %sweeps_0.1 = (f32[2,256,768]{2,1,0:T(8,128)}, f32[8,128]{1,0:T(8,128)S(1)}) custom-call(f32[2,768]{1,0:T(2,128)S(1)} %add.19.refs_0_.refs_1_, bf16[2,256,768]{2,1,0:T(8,128)(2,1)S(1)} %copy-done, bf16[2,256,768]{2,1,0:T(8,128)(2,1)S(1)} %copy-done.1, bf16[768,768]{1,0:T(8,128)(2,1)S(1)} %get-tuple-element.60.refs_3_, ...), custom_call_target="tpu_custom_call" | custom-call | flops 3623878656 | bytes 2359296 | tf_op jit(solution)/shard_map/sweeps_0/pallas_call | solution.py:45
  85.8 1.2 %collective-permute-done.16.refs_1_ = s16[592,128]{1,0:T(8,128)(2,1)S(1)} collective-permute-done((s16[592,128]{1,0:T(8,128)(2,1)S(1)}, s16[592,128]{1,0:T(8,128)(2,1)S(1)}, u32[]{:S(2)}, u32[]{:S(2)}) %collective-permute-start.16) | collective-permute-done | bytes 151584 | tf_op jit(solution)/shard_map/ppermute | solution.py:337
  86.9 0.1 total_1_0.1.refs_2_
  87.1 0.7 collective-permute-start.20
  87.8 4.5 %collective-permute-done.20.refs_3_ = s16[592,128]{1,0:T(8,128)(2,1)S(1)} collective-permute-done((s16[592,128]{1,0:T(8,128)(2,1)S(1)}, s16[592,128]{1,0:T(8,128)(2,1)S(1)}, u32[]{:S(2)}, u32[]{:S(2)}) %collective-permute-start.20) | collective-permute-done | bytes 151584 | tf_op jit(solution)/shard_map/ppermute | solution.py:337
  92.3 1.4 %collective-permute-done.22.refs_5_ = s16[592,128]{1,0:T(8,128)(2,1)S(1)} collective-permute-done((s16[592,128]{1,0:T(8,128)(2,1)S(1)}, s16[592,128]{1,0:T(8,128)(2,1)S(1)}, u32[]{:S(2)}, u32[]{:S(2)}) %collective-permute-start.22) | collective-permute-done | bytes 151584 | tf_op jit(solution)/shard_map/ppermute | solution.py:337
  93.7 0.7 unpack_1.1
  94.4 6.3 %sweeps_1.1 = (f32[2,256,768]{2,1,0:T(8,128)}, f32[8,128]{1,0:T(8,128)}) custom-call(f32[2,768]{1,0:T(2,128)S(1)} %add.19.refs_0_.refs_1_, bf16[2,256,768]{2,1,0:T(8,128)(2,1)S(1)} %copy-done, bf16[2,256,768]{2,1,0:T(8,128)(2,1)S(1)} %copy-done.1, bf16[768,768]{1,0:T(8,128)(2,1)S(1)} %get-tuple-element.63.refs_3_, ...), custom_call_target="tpu_custom_call", output_to_operand_aliasing={{0}: (5, {})} | custom-call | flops 3623878656 | bytes 2359296 | tf_op jit(solution)/shard_map/sweeps_1/pallas_call | solution.py:45
  (20 shorter events, 0.1 us)
Async XLA Ops:
  0.0 0.7 copy-start.2
  5.4 35.5 %collective-permute-start.7 = (bf16[256,768]{1,0:T(8,128)(2,1)S(1)}, bf16[256,768]{1,0:T(8,128)(2,1)S(1)}, u32[]{:S(2)}, u32[]{:S(2)}) collective-permute-start(bf16[256,768]{1,0:T(8,128)(2,1)S(1)} %get-tuple-element.44), channel_id=1, source_target_pairs={{0,8},{8,0},{16,24},{24,16},{1,9},{9,1},{17,25},{25,17},{2,10},{10... | collective-permute-start | bytes 1179656 | tf_op jit(solution)/shard_map/ppermute | solution.py:334
  8.4 32.5 %collective-permute-start.8 = (bf16[256,768]{1,0:T(8,128)(2,1)S(1)}, bf16[256,768]{1,0:T(8,128)(2,1)S(1)}, u32[]{:S(2)}, u32[]{:S(2)}) collective-permute-start(bf16[256,768]{1,0:T(8,128)(2,1)S(1)} %get-tuple-element.45), channel_id=1, source_target_pairs={{0,16},{8,24},{16,0},{24,8},{1,17},{9,25},{17,1},{25,9},{2,18},{10... | collective-permute-start | bytes 1179656 | tf_op jit(solution)/shard_map/ppermute | solution.py:334
  9.9 31.8 %collective-permute-start.9 = (bf16[256,768]{1,0:T(8,128)(2,1)S(1)}, bf16[256,768]{1,0:T(8,128)(2,1)S(1)}, u32[]{:S(2)}, u32[]{:S(2)}) collective-permute-start(bf16[256,768]{1,0:T(8,128)(2,1)S(1)} %get-tuple-element.46), channel_id=1, source_target_pairs={{0,24},{8,16},{16,8},{24,0},{1,25},{9,17},{17,9},{25,1},{2,26},{10... | collective-permute-start | bytes 1179656 | tf_op jit(solution)/shard_map/ppermute | solution.py:334
  16.2 0.7 copy-start.3
  17.0 0.7 copy-start.5
  17.7 10.0 %collective-permute-start = (f32[4,768]{1,0:T(4,128)S(1)}, f32[4,768]{1,0:T(4,128)S(1)}, u32[]{:S(2)}, u32[]{:S(2)}) collective-permute-start(f32[4,768]{1,0:T(4,128)S(1)} %get-tuple-element.39), channel_id=1, source_target_pairs={{0,16},{8,24},{16,0},{24,8},{1,17},{9,25},{17,1},{25,9},{2,18},{10... | collective-permute-start | bytes 36872 | tf_op jit(solution)/shard_map/ppermute | solution.py:334
  27.7 3.7 %collective-permute-start.1 = (f32[2,768]{1,0:T(2,128)S(1)}, f32[2,768]{1,0:T(2,128)S(1)}, u32[]{:S(2)}, u32[]{:S(2)}) collective-permute-start(f32[2,768]{1,0:T(2,128)S(1)} %slice.9), channel_id=1, source_target_pairs={{0,8},{8,0},{16,24},{24,16},{1,9},{9,1},{17,25},{25,17},{2,10},{10... | collective-permute-start | bytes 18440 | tf_op jit(solution)/shard_map/ppermute | solution.py:334
  31.4 1.2 %collective-permute-start.2 = (f32[2,768]{1,0:T(2,128)S(1)}, f32[2,768]{1,0:T(2,128)S(1)}, u32[]{:S(2)}, u32[]{:S(2)}) collective-permute-start(f32[2,768]{1,0:T(2,128)S(1)} %slice_add_fusion), channel_id=1, source_target_pairs={{0,1},{1,0},{2,3},{3,2},{4,5},{5,4},{6,7},{7,6},{8,9},{9,8},{10,11... | collective-permute-start | bytes 18440 | tf_op jit(solution)/shard_map/ppermute | solution.py:337
  32.6 3.6 %collective-permute-start.3 = (f32[2,768]{1,0:T(2,128)S(1)}, f32[2,768]{1,0:T(2,128)S(1)}, u32[]{:S(2)}, u32[]{:S(2)}) collective-permute-start(f32[2,768]{1,0:T(2,128)S(1)} %add.17), channel_id=1, source_target_pairs={{0,2},{1,3},{2,0},{3,1},{4,6},{5,7},{6,4},{7,5},{8,10},{9,11},{10,... | collective-permute-start | bytes 18440 | tf_op jit(solution)/shard_map/ppermute | solution.py:337
  36.2 4.5 %collective-permute-start.4 = (f32[2,768]{1,0:T(2,128)S(1)}, f32[2,768]{1,0:T(2,128)S(1)}, u32[]{:S(2)}, u32[]{:S(2)}) collective-permute-start(f32[2,768]{1,0:T(2,128)S(1)} %add.18), channel_id=1, source_target_pairs={{0,4},{1,5},{2,6},{3,7},{4,0},{5,1},{6,2},{7,3},{8,12},{9,13},{10,... | collective-permute-start | bytes 18440 | tf_op jit(solution)/shard_map/ppermute | solution.py:337
  38.8 2.2 %copy-start.6 = (bf16[256,768]{1,0:T(8,128)(2,1)S(1)}, bf16[256,768]{1,0:T(8,128)(2,1)}, u32[]{:S(2)}) copy-start(bf16[256,768]{1,0:T(8,128)(2,1)} %copy-done.5) | copy-start | bytes 1179652
  42.4 3.6 %collective-permute-start.10 = (f32[1152,128]{1,0:T(8,128)S(1)}, f32[1152,128]{1,0:T(8,128)S(1)}, u32[]{:S(2)}, u32[]{:S(2)}) collective-permute-start(f32[1152,128]{1,0:T(8,128)S(1)} %get-tuple-element.48), channel_id=1, source_target_pairs={{0,1},{1,0},{2,3},{3,2},{4,5},{5,4},{6,7},{7,6},{8,9},{9,8},{10,11... | collective-permute-start | bytes 1769480 | tf_op jit(solution)/shard_map/ppermute | solution.py:337
  42.5 12.3 %collective-permute-start.5 = (bf16[256,768]{1,0:T(8,128)(2,1)S(1)}, bf16[256,768]{1,0:T(8,128)(2,1)S(1)}, u32[]{:S(2)}, u32[]{:S(2)}) collective-permute-start(bf16[256,768]{1,0:T(8,128)(2,1)S(1)} %get-tuple-element.41), channel_id=1, source_target_pairs={{0,8},{8,0},{16,24},{24,16},{1,9},{9,1},{17,25},{25,17},{2,10},{10... | collective-permute-start | bytes 1179656 | tf_op jit(solution)/shard_map/ppermute | solution.py:334
  43.7 18.1 %collective-permute-start.6 = (bf16[256,768]{1,0:T(8,128)(2,1)S(1)}, bf16[256,768]{1,0:T(8,128)(2,1)S(1)}, u32[]{:S(2)}, u32[]{:S(2)}) collective-permute-start(bf16[256,768]{1,0:T(8,128)(2,1)S(1)} %get-tuple-element.42), channel_id=1, source_target_pairs={{0,16},{8,24},{16,0},{24,8},{1,17},{9,25},{17,1},{25,9},{2,18},{10... | collective-permute-start | bytes 1179656 | tf_op jit(solution)/shard_map/ppermute | solution.py:334
  44.6 18.8 %collective-permute-start.12 = (bf16[256,768]{1,0:T(8,128)(2,1)S(1)}, bf16[256,768]{1,0:T(8,128)(2,1)S(1)}, u32[]{:S(2)}, u32[]{:S(2)}) collective-permute-start(bf16[256,768]{1,0:T(8,128)(2,1)S(1)} %get-tuple-element.52), channel_id=1, source_target_pairs={{0,24},{8,16},{16,8},{24,0},{1,25},{9,17},{17,9},{25,1},{2,26},{10... | collective-permute-start | bytes 1179656 | tf_op jit(solution)/shard_map/ppermute | solution.py:334
  46.2 15.5 %copy-start.4 = (bf16[256,768]{1,0:T(8,128)(2,1)S(1)}, bf16[256,768]{1,0:T(8,128)(2,1)}, u32[]{:S(2)}) copy-start(bf16[256,768]{1,0:T(8,128)(2,1)} %copy-done.3) | copy-start | bytes 1179652
  46.2 5.5 %collective-permute-start.11 = (s16[592,128]{1,0:T(8,128)(2,1)S(1)}, s16[592,128]{1,0:T(8,128)(2,1)S(1)}, u32[]{:S(2)}, u32[]{:S(2)}) collective-permute-start(s16[592,128]{1,0:T(8,128)(2,1)S(1)} %get-tuple-element.50), channel_id=1, source_target_pairs={{0,2},{1,3},{2,0},{3,1},{4,6},{5,7},{6,4},{7,5},{8,10},{9,11},{10,... | collective-permute-start | bytes 454664 | tf_op jit(solution)/shard_map/ppermute | solution.py:337
  51.9 10.7 %collective-permute-start.13 = (s16[592,128]{1,0:T(8,128)(2,1)S(1)}, s16[592,128]{1,0:T(8,128)(2,1)S(1)}, u32[]{:S(2)}, u32[]{:S(2)}) collective-permute-start(s16[592,128]{1,0:T(8,128)(2,1)S(1)} %get-tuple-element.51.refs_3_), channel_id=1, source_target_pairs={{0,4},{1,5},{2,6},{3,7},{4,0},{5,1},{6,2},{7,3},{8,12},{9,13},{10,... | collective-permute-start | bytes 454664 | tf_op jit(solution)/shard_map/ppermute | solution.py:337
  64.0 6.4 %collective-permute-start.14 = (f32[1152,128]{1,0:T(8,128)S(1)}, f32[1152,128]{1,0:T(8,128)S(1)}, u32[]{:S(2)}, u32[]{:S(2)}) collective-permute-start(f32[1152,128]{1,0:T(8,128)S(1)} %get-tuple-element.55), channel_id=1, source_target_pairs={{0,1},{1,0},{2,3},{3,2},{4,5},{5,4},{6,7},{7,6},{8,9},{9,8},{10,11... | collective-permute-start | bytes 1769480 | tf_op jit(solution)/shard_map/ppermute | solution.py:337
  64.0 6.4 %collective-permute-start.17 = (s16[592,128]{1,0:T(8,128)(2,1)S(1)}, s16[592,128]{1,0:T(8,128)(2,1)S(1)}, u32[]{:S(2)}, u32[]{:S(2)}) collective-permute-start(s16[592,128]{1,0:T(8,128)(2,1)S(1)} %total_0_0.1.refs_3_.refs_2_), channel_id=1, source_target_pairs={{0,2},{1,3},{2,0},{3,1},{4,6},{5,7},{6,4},{7,5},{8,10},{9,11},{10,... | collective-permute-start | bytes 454664 | tf_op jit(solution)/shard_map/ppermute | solution.py:337
  65.7 6.6 %collective-permute-start.18 = (s16[592,128]{1,0:T(8,128)(2,1)S(1)}, s16[592,128]{1,0:T(8,128)(2,1)S(1)}, u32[]{:S(2)}, u32[]{:S(2)}) collective-permute-start(s16[592,128]{1,0:T(8,128)(2,1)S(1)} %total_0_0.1.refs_3_.refs_2_), channel_id=1, source_target_pairs={{0,1},{1,0},{2,3},{3,2},{4,5},{5,4},{6,7},{7,6},{8,9},{9,8},{10,11... | collective-permute-start | bytes 454664 | tf_op jit(solution)/shard_map/ppermute | solution.py:337
  70.4 1.9 %collective-permute-start.19 = (s16[592,128]{1,0:T(8,128)(2,1)S(1)}, s16[592,128]{1,0:T(8,128)(2,1)S(1)}, u32[]{:S(2)}, u32[]{:S(2)}) collective-permute-start(s16[592,128]{1,0:T(8,128)(2,1)S(1)} %collective-permute-done.17.refs_3_), channel_id=1, source_target_pairs={{0,1},{1,0},{2,3},{3,2},{4,5},{5,4},{6,7},{7,6},{8,9},{9,8},{10,11... | collective-permute-start | bytes 454664 | tf_op jit(solution)/shard_map/ppermute | solution.py:337
  70.4 9.4 %copy-start = (bf16[2,256,768]{2,1,0:T(8,128)(2,1)S(1)}, bf16[2,256,768]{2,1,0:T(8,128)(2,1)}, u32[]{:S(2)}) copy-start(bf16[2,256,768]{2,1,0:T(8,128)(2,1)} %refs_1_.3) | copy-start | bytes 2359300
  70.4 9.4 %copy-start.1 = (bf16[2,256,768]{2,1,0:T(8,128)(2,1)S(1)}, bf16[2,256,768]{2,1,0:T(8,128)(2,1)}, u32[]{:S(2)}) copy-start(bf16[2,256,768]{2,1,0:T(8,128)(2,1)} %refs_2_.7) | copy-start | bytes 2359300
  70.6 6.4 %collective-permute-start.15 = (s16[592,128]{1,0:T(8,128)(2,1)S(1)}, s16[592,128]{1,0:T(8,128)(2,1)S(1)}, u32[]{:S(2)}, u32[]{:S(2)}) collective-permute-start(s16[592,128]{1,0:T(8,128)(2,1)S(1)} %get-tuple-element.57), channel_id=1, source_target_pairs={{0,2},{1,3},{2,0},{3,1},{4,6},{5,7},{6,4},{7,5},{8,10},{9,11},{10,... | collective-permute-start | bytes 454664 | tf_op jit(solution)/shard_map/ppermute | solution.py:337
  77.2 9.8 %collective-permute-start.16 = (s16[592,128]{1,0:T(8,128)(2,1)S(1)}, s16[592,128]{1,0:T(8,128)(2,1)S(1)}, u32[]{:S(2)}, u32[]{:S(2)}) collective-permute-start(s16[592,128]{1,0:T(8,128)(2,1)S(1)} %get-tuple-element.59.refs_5_), channel_id=1, source_target_pairs={{0,4},{1,5},{2,6},{3,7},{4,0},{5,1},{6,2},{7,3},{8,12},{9,13},{10,... | collective-permute-start | bytes 454664 | tf_op jit(solution)/shard_map/ppermute | solution.py:337
  87.1 5.3 %collective-permute-start.20 = (s16[592,128]{1,0:T(8,128)(2,1)S(1)}, s16[592,128]{1,0:T(8,128)(2,1)S(1)}, u32[]{:S(2)}, u32[]{:S(2)}) collective-permute-start(s16[592,128]{1,0:T(8,128)(2,1)S(1)} %total_1_0.1.refs_2_), channel_id=1, source_target_pairs={{0,2},{1,3},{2,0},{3,1},{4,6},{5,7},{6,4},{7,5},{8,10},{9,11},{10,... | collective-permute-start | bytes 454664 | tf_op jit(solution)/shard_map/ppermute | solution.py:337
  87.8 4.5 %collective-permute-start.21 = (s16[592,128]{1,0:T(8,128)(2,1)S(1)}, s16[592,128]{1,0:T(8,128)(2,1)S(1)}, u32[]{:S(2)}, u32[]{:S(2)}) collective-permute-start(s16[592,128]{1,0:T(8,128)(2,1)S(1)} %total_1_0.1.refs_2_), channel_id=1, source_target_pairs={{0,1},{1,0},{2,3},{3,2},{4,5},{5,4},{6,7},{7,6},{8,9},{9,8},{10,11... | collective-permute-start | bytes 454664 | tf_op jit(solution)/shard_map/ppermute | solution.py:337
  92.3 1.4 %collective-permute-start.22 = (s16[592,128]{1,0:T(8,128)(2,1)S(1)}, s16[592,128]{1,0:T(8,128)(2,1)S(1)}, u32[]{:S(2)}, u32[]{:S(2)}) collective-permute-start(s16[592,128]{1,0:T(8,128)(2,1)S(1)} %collective-permute-done.20.refs_3_), channel_id=1, source_target_pairs={{0,1},{1,0},{2,3},{3,2},{4,5},{5,4},{6,7},{7,6},{8,9},{9,8},{10,11... | collective-permute-start | bytes 454664 | tf_op jit(solution)/shard_map/ppermute | solution.py:337

commit v4 on v3

v4 whole, which is shorter than its diff:
```python
import functools

import jax
import jax.numpy as jnp
from jax import lax
from jax.experimental import pallas as pl
from jax.experimental.pallas import tpu as pltpu
from jax.sharding import PartitionSpec as P

STEPS = 4
BLOCK = 128
TILE = 16
PARTS = 2
LEVELS = 32760.0
OCTAVE = 8.0
relax_factor = 0.5
diagonal_eps = 1e-06
tiny = 1e-30
VMEM_LIMIT = 50 * 2**20

VMEM = pl.BlockSpec(memory_space=pltpu.VMEM)
ANY = pl.BlockSpec(memory_space=pl.ANY)
SMEM = pl.BlockSpec(memory_space=pltpu.SMEM)
F32, BF16, I32, I16 = jnp.float32, jnp.bfloat16, jnp.int32, jnp.int16


def call(kernel, out_shape, in_specs, scratch=(), flops=0, moved=0, out_specs=None, aliases=None, name=None, after=()):
    many = isinstance(out_shape, (list, tuple))
    used, idle = len(in_specs), len(after)

    def body(*refs):
        kernel(*refs[:used], *refs[used + idle:])

    inner = pl.pallas_call(
        body,
        out_shape=out_shape,
        in_specs=list(in_specs) + [ANY] * idle,
        out_specs=out_specs if out_specs is not None else ([VMEM] * len(out_shape) if many else VMEM),
        scratch_shapes=list(scratch),
        input_output_aliases=aliases or {},
        cost_estimate=pl.CostEstimate(flops=flops, bytes_accessed=moved, transcendentals=0),
        compiler_params=pltpu.CompilerParams(vmem_limit_bytes=VMEM_LIMIT),
        name=name,
    )
    return lambda *args: inner(*args, *after)


def cuts(size, chunks):
    ends = [size * (c + 1) // (TILE * chunks) * TILE for c in range(chunks)]
    return [end - start for start, end in zip([0] + ends, ends)]


def slots_of(owners, experts, capacity):
    tokens = owners.shape[1]
    lanes = 128
    blocks = tokens // lanes
    named = owners == lax.broadcasted_iota(I32, (experts, tokens), 0)
    ones = named.astype(F32)
    stacked = jnp.concatenate([ones[:, b * lanes:(b + 1) * lanes] for b in range(blocks)], axis=0)
    upto = lax.broadcasted_iota(I32, (lanes, lanes), 0) <= lax.broadcasted_iota(I32, (lanes, lanes), 1)
    within = jnp.dot(stacked.astype(BF16), upto.astype(F32).astype(BF16), preferred_element_type=F32)
    carry = jnp.zeros((experts, 1), F32)
    parts = []
    for b in range(blocks):
        part = within[b * experts:(b + 1) * experts]
        parts.append(part + carry)
        carry = carry + part[:, lanes - 1:lanes]
    counted = jnp.concatenate(parts, axis=1)
    rank = jnp.sum(jnp.where(named, counted - 1.0, 0.0), axis=0, keepdims=True)
    return owners * capacity + rank.astype(I32)


def place(key, rows_ref, experts, capacity, out_refs):
    tokens, hidden = rows_ref.shape
    places = lax.broadcasted_iota(I32, (capacity, tokens), 0)
    chosen = jnp.concatenate(
        [(places == key - e * capacity).astype(F32).astype(BF16) for e in experts], axis=0
    )
    width = 2 * BLOCK
    for c in range(0, hidden, width):
        got = jnp.dot(chosen, rows_ref[:, c:c + width], preferred_element_type=F32).astype(BF16)
        for k, out_ref in enumerate(out_refs):
            out_ref[:, c:c + width] = got[k * capacity:(k + 1) * capacity]


def first_kernel(peers, slots, all_experts, capacity, me_ref, owner_ref, rows_ref, key_ref, *out_refs):
    me = me_ref[0]
    key = slots_of(owner_ref[...], all_experts, capacity)
    key_ref[...] = key
    place(key, rows_ref, [lax.bitwise_xor(me, k) * slots for k in range(1, peers)], capacity, out_refs)


def second_kernel(peers, slots, capacity, me_ref, key_ref, rows_ref, *out_refs):
    me = me_ref[0]
    where = [(0, a) for a in range(slots)] + [(k, a) for a in range(1, slots) for k in range(1, peers)]
    place(key_ref[...], rows_ref, [lax.bitwise_xor(me, k) * slots + a for k, a in where], capacity, out_refs)


def layout(hidden, halvings):
    blocks = hidden // BLOCK
    off = [(i, j) for i in range(blocks) for j in range(i + 1, blocks)]
    pairs = [(i, i + 1 if i + 1 < blocks else None) for i in range(0, blocks, 2)]
    tail = (len(off) + len(pairs)) * BLOCK
    unit = TILE << halvings
    return off, pairs, tail, -(-tail // unit) * unit


def eye_of(compare):
    return compare(lax.broadcasted_iota(I32, (BLOCK, BLOCK), 0), lax.broadcasted_iota(I32, (BLOCK, BLOCK), 1))


def bit_of(where, bit):
    return lax.bitwise_and(lax.shift_right_logical(where, bit), 1)


def diagonal_rows(hidden):
    return -(-(hidden // BLOCK) // 8) * 8


def exponent_of(diagonal):
    return jnp.ceil(0.5 * jnp.log2(jnp.maximum(diagonal, tiny)))


def spread(hidden, halvings, factor, out_ref):
    off, pairs, tail, length = layout(hidden, halvings)
    if length > tail:
        out_ref[tail:length] = jnp.zeros((length - tail, BLOCK), F32)
    across = [jnp.broadcast_to(factor[b:b + 1], (BLOCK, BLOCK)) for b in range(hidden // BLOCK)]
    down = [a.T for a in across]
    for n, (i, j) in enumerate(off):
        out_ref[n * BLOCK:(n + 1) * BLOCK] = down[i] * across[j]
    for n, (first, second) in enumerate(pairs):
        block = down[first] * across[first]
        if second is not None:
            block = jnp.where(eye_of(lax.lt), block, down[second] * across[second])
        row = (len(off) + n) * BLOCK
        out_ref[row:row + BLOCK] = block


def add_gram(halvings, chunk_refs, before, packed):
    hidden = chunk_refs[0].shape[1]
    off, pairs, tail, length = layout(hidden, halvings)
    at = {pair: n for n, pair in enumerate(off)}
    x = jnp.concatenate([r[...] for r in chunk_refs], axis=0) if len(chunk_refs) > 1 else chunk_refs[0][...]
    strip = 2 * BLOCK

    def put(n, value):
        rows = slice(n * BLOCK, (n + 1) * BLOCK)
        packed[rows] = value if before is None else before[rows] + value

    def put_diagonal(i, block):
        value = jnp.sum(jnp.where(eye_of(lax.eq), block, 0.0), axis=0, keepdims=True)
        row = slice(length + i, length + i + 1)
        packed[row] = value if before is None else before[row] + value

    packed[tail:] = jnp.zeros((packed.shape[0] - tail, BLOCK), F32)
    for n, (first, second) in enumerate(pairs):
        low, high = first * BLOCK, min(first * BLOCK + strip, hidden)
        product = lax.dot_general(
            x[:, low:high], x[:, low:], (((0,), (0,)), ((), ())), preferred_element_type=F32
        )
        for i in range((high - low) // BLOCK):
            for j in range((hidden - low) // BLOCK):
                pair = (first + i, first + j)
                if pair in at:
                    put(at[pair], product[i * BLOCK:(i + 1) * BLOCK, j * BLOCK:(j + 1) * BLOCK])
        mixed = product[:BLOCK, :BLOCK]
        put_diagonal(first, mixed)
        if second is not None:
            other = product[BLOCK:, BLOCK:2 * BLOCK]
            put_diagonal(second, other)
            mixed = jnp.where(eye_of(lax.lt), mixed, other)
        put(len(off) + n, jnp.where(eye_of(lax.eq), 0.0, mixed))


def early_gram_kernel(halvings, *refs):
    add_gram(halvings, refs[:-1], None, refs[-1])


def late_gram_kernel(halvings, pieces, where_ref, before_ref, *refs):
    chunk_refs, (keep_ref, diagonal_ref, *send_refs, packed) = refs[:pieces], refs[pieces:]
    add_gram(halvings, chunk_refs, before_ref, packed)
    half, rows = keep_ref.shape[0], diagonal_ref.shape[0]
    mine = bit_of(where_ref[0], 0)
    keep_ref[...] = packed[pl.ds(pl.multiple_of(mine * half, TILE), half)]
    diagonal = packed[2 * half:]
    diagonal_ref[...] = diagonal
    start = 0
    for n, send_ref in enumerate(send_refs):
        size = send_ref.shape[0] - (rows if n == 0 else 0)
        send_ref[:size] = packed[pl.ds(pl.multiple_of((1 - mine) * half + start, TILE), size)]
        if n == 0:
            send_ref[size:] = diagonal
        start += size


def encode(values, ref, exponent=None, digits=()):
    rows = values.shape[0]
    largest = jnp.max(jnp.abs(values), axis=0, keepdims=True)
    steps = jnp.ceil(OCTAVE * jnp.log2(jnp.maximum(largest, tiny)))
    factor = jnp.exp2(steps * (-1.0 / OCTAVE)) * LEVELS
    ref[:rows] = jnp.floor(values * factor + 0.5).astype(I32).astype(I16)
    notes = [jnp.broadcast_to(steps, (8, BLOCK))]
    if exponent is None:
        notes += notes
    else:
        notes += [exponent, *digits]
    notes = jnp.concatenate(notes, axis=0)
    if notes.shape[0] < ref.shape[0] - rows:
        notes = jnp.concatenate([notes, jnp.zeros((ref.shape[0] - rows - notes.shape[0], BLOCK), F32)], axis=0)
    ref[rows:] = notes.astype(I32).astype(I16)


def decode(ref, rows):
    notes = ref[rows:].astype(I32).astype(F32)
    return ref[:rows].astype(I32).astype(F32) * (jnp.exp2(notes[:1] * (1.0 / OCTAVE)) * (1.0 / LEVELS)), notes[8:]


def digits_of(diagonal, exponent):
    value = diagonal * jnp.exp2(-2.0 * exponent) * LEVELS
    first = jnp.floor(value + 0.5)
    return first, jnp.floor((value - first) * LEVELS + 0.5)


def from_digits(first, second, exponent):
    return (first + second * (1.0 / LEVELS)) * (1.0 / LEVELS) * jnp.exp2(2.0 * exponent)


def stage_kernel(hidden, halvings, bit, first, cut, parts, where_ref, keep_ref, diagonal_ref, *refs):
    got_refs, refs = refs[:parts], refs[parts:]
    sent_ref, diagonal_out, *kept, factors, total = refs
    rows, many = keep_ref.shape[0], diagonal_ref.shape[0]
    length = layout(hidden, halvings)[3]
    where = where_ref[0]
    place = sum(bit_of(where, b) * (length >> (b + 1)) for b in range(bit))
    here = pl.ds(pl.multiple_of(place, TILE), rows)
    diagonal = diagonal_ref[...]
    if first:
        start = 0
        for n, ref in enumerate(got_refs):
            size = ref.shape[0] - (many if n == 0 else 0)
            total[start:start + size] = keep_ref[start:start + size] + ref[:size]
            if n == 0:
                diagonal = diagonal + ref[size:]
            start += size
    else:
        value, notes = decode(got_refs[0], rows)
        theirs = notes[:many]
        spread(hidden, halvings, jnp.exp2(theirs), factors)
        total[...] = keep_ref[...] + value * factors[here]
        exponent = exponent_of(diagonal)
        ours = from_digits(*digits_of(diagonal, exponent), exponent)
        diagonal = ours + from_digits(notes[many:2 * many], notes[2 * many:3 * many], theirs)
    diagonal_out[...] = diagonal
    exponent = exponent_of(diagonal)
    spread(hidden, halvings, jnp.exp2(-exponent), factors)
    if cut:
        half = rows // 2
        mine = bit_of(where, bit)
        kept[0][...] = total[pl.ds(pl.multiple_of(mine * half, TILE), half)]
        away = (1 - mine) * half
        value = total[pl.ds(pl.multiple_of(away, TILE), half)] * factors[pl.ds(pl.multiple_of(place + away, TILE), half)]
        encode(value, sent_ref, exponent, digits_of(diagonal, exponent))
    elif kept:
        kept[0][...] = total[...]
        encode(total[...] * factors[here], sent_ref, exponent, digits_of(diagonal, exponent))
    else:
        encode(total[...] * factors[here], sent_ref)


def unpack_kernel(hidden, halvings, flips, where_ref, diagonal_ref, *refs):
    piece_refs, (high_ref, low_ref, packed) = refs[:len(flips)], refs[len(flips):]
    off, pairs, tail, length = layout(hidden, halvings)
    where = where_ref[0]
    rows = length >> halvings
    for flip, piece_ref in zip(flips, piece_refs):
        owner = lax.bitwise_xor(where, flip)
        start = sum(bit_of(owner, b) * (length >> (b + 1)) for b in range(halvings))
        packed[pl.ds(pl.multiple_of(start, TILE), rows)] = decode(piece_ref, rows)[0]

    def put(i, j, block):
        rows, cols = slice(i * BLOCK, (i + 1) * BLOCK), slice(j * BLOCK, (j + 1) * BLOCK)
        hi = block.astype(BF16)
        high_ref[rows, cols] = hi
        low_ref[rows, cols] = (block - hi.astype(F32)).astype(BF16)

    for n, (i, j) in enumerate(off):
        block = packed[n * BLOCK:(n + 1) * BLOCK]
        put(i, j, block)
        put(j, i, block.T)
    diagonal = diagonal_ref[...]
    ones = diagonal * jnp.exp2(-2.0 * exponent_of(diagonal))
    for n, (first, second) in enumerate(pairs):
        row = (len(off) + n) * BLOCK
        block = packed[row:row + BLOCK]
        turned = block.T
        for i, above in ((first, lax.lt), (second, lax.gt)):
            if i is not None:
                whole = jnp.where(eye_of(above), block, turned)
                put(i, i, jnp.where(eye_of(lax.eq), ones[i:i + 1], whole))


def sweeps_kernel(slot, diagonal_ref, weight_ref, mask_ref, high_ref, low_ref, *refs):
    out_ref, token_ref, result, done = refs[-4:]
    diagonal = jnp.concatenate([diagonal_ref[b:b + 1] for b in range(weight_ref.shape[-1] // BLOCK)], axis=1)
    back = jnp.exp2(exponent_of(diagonal))
    factor = relax_factor * (1.0 / (diagonal + diagonal_eps)) * back
    weight = weight_ref[slot].astype(F32)
    keep = mask_ref[slot].astype(F32)
    pruned = keep * weight
    for sweep in range(STEPS):
        change = (pruned - weight) * back
        top = change.astype(BF16)
        if sweep == 0:
            gradient = jnp.dot(top, high_ref[...], preferred_element_type=F32)
        else:
            rest = (change - top.astype(F32)).astype(BF16)
            both = jnp.dot(jnp.concatenate([top, rest], axis=0), high_ref[...], preferred_element_type=F32)
            gradient = both[:top.shape[0]] + both[top.shape[0]:]
        gradient = gradient + jnp.dot(top, low_ref[...], preferred_element_type=F32)
        pruned = keep * (pruned - gradient * factor)
    result[...] = pruned
    token_ref[...] = pruned[:8, :BLOCK]
    copy = pltpu.make_async_copy(result, out_ref.at[slot], done)
    copy.start()
    copy.wait()


def on_device(expert_inputs, row_expert, down_weight, keep_mask):
    tokens, hidden = expert_inputs.shape
    slots, features, _ = down_weight.shape
    peers = lax.axis_size("expert")
    copies = lax.axis_size("rows")
    all_experts = slots * peers
    capacity = tokens // 8
    halvings = copies.bit_length() - 2
    length = layout(hidden, halvings)[3]
    me = jnp.reshape(lax.axis_index("expert").astype(I32), (1,))
    where = jnp.reshape(lax.axis_index("rows").astype(I32), (1,))
    owners = row_expert.reshape(1, tokens)

    def shape(rows, columns=BLOCK, dtype=F32):
        return jax.ShapeDtypeStruct((rows, columns), dtype)

    def over_experts(array, flip):
        return lax.ppermute(array, "expert", [(i, i ^ flip) for i in range(peers)])

    def over_rows(array, bit):
        return lax.ppermute(array, "rows", [(i, i ^ (1 << bit)) for i in range(copies)])

    chunk = shape(capacity, hidden, BF16)
    place_flops = 2 * capacity * tokens * hidden
    key, *outgoing = call(
        functools.partial(first_kernel, peers, slots, all_experts, capacity),
        [shape(1, tokens, I32)] + [chunk] * (peers - 1), [SMEM, VMEM, VMEM],
        flops=place_flops * (peers - 1), moved=expert_inputs.size * 4, name="place_first",
    )(me, owners, expert_inputs)
    arrived = [[over_experts(outgoing[k - 1], k) for k in range(1, peers)]]
    count = slots + (slots - 1) * (peers - 1)
    rest = call(
        functools.partial(second_kernel, peers, slots, capacity), [chunk] * count, [SMEM, VMEM, VMEM],
        flops=place_flops * count, moved=expert_inputs.size * 4, name="place_rest",
    )(me, key, expert_inputs)
    own = rest[:slots]
    for a in range(1, slots):
        outgoing = rest[slots + (a - 1) * (peers - 1):slots + a * (peers - 1)]
        arrived.append([over_experts(outgoing[k - 1], k) for k in range(1, peers)])

    many = diagonal_rows(hidden)
    notes = -(-(8 + 3 * many) // TILE) * TILE

    def begin(a, after):
        chunks = [own[a]] + arrived[a][:-1]
        return call(
            functools.partial(early_gram_kernel, halvings), shape(length + many), [VMEM] * len(chunks),
            flops=2 * capacity * len(chunks) * hidden * hidden, moved=length * BLOCK * 4, name=f"begin_{a}", after=after,
        )(*chunks)

    def stage(name, bit, keep, diagonal, got, cut, kept, after=()):
        rows = keep.shape[0]
        left = rows // 2 if cut else rows
        return call(
            functools.partial(stage_kernel, hidden, halvings, bit, got[0].dtype == F32, cut, len(got)),
            [shape(left + (notes if kept else TILE), dtype=I16), shape(many)] + ([shape(left)] if kept else []),
            [SMEM] + [VMEM] * (2 + len(got)),
            scratch=[pltpu.VMEM((length, BLOCK), F32), pltpu.VMEM((rows, BLOCK), F32)],
            moved=rows * BLOCK * 12, name=name, after=after,
        )(where, keep, diagonal, *got)

    def reduce(a, before, after):
        size = length // 2
        sizes = cuts(size, PARTS)
        keep, diagonal, *sent = call(
            functools.partial(late_gram_kernel, halvings, 1),
            [shape(size), shape(many)] + [shape(n + (many if i == 0 else 0)) for i, n in enumerate(sizes)],
            [SMEM] + [VMEM] * 2, scratch=[pltpu.VMEM((length + many, BLOCK), F32)],
            flops=2 * capacity * hidden * hidden, moved=length * BLOCK * 4, name=f"gram_{a}", after=after,
        )(where, before, arrived[a][-1])
        for bit in range(1, halvings + 1):
            cut = bit < halvings
            got = [over_rows(part, bit - 1) for part in sent]
            coded, diagonal, keep = stage(f"stage_{a}_{bit}", bit, keep, diagonal, got, cut, True)
            sent = [coded]
            if bit == 1:
                halved = coded
        return halved, (coded, diagonal, keep)

    def end(a, sums, after):
        coded, diagonal, keep = sums
        return stage(f"total_{a}", halvings, keep, diagonal, [over_rows(coded, halvings)], False, False, after)

    def gather(a, total, after):
        coded, diagonal = total
        held = [(0, coded)]
        for bit in range(halvings - 1, -1, -1):
            held += [(flip ^ (1 << bit), over_rows(piece, bit)) for flip, piece in held]
        high, low = call(
            functools.partial(unpack_kernel, hidden, halvings, [flip for flip, _ in held]),
            [shape(hidden, hidden, BF16)] * 2, [SMEM] + [VMEM] * (1 + len(held)),
            scratch=[pltpu.VMEM((length, BLOCK), F32)], moved=length * BLOCK * 4, name=f"unpack_{a}", after=after,
        )(where, diagonal, *[piece for _, piece in held])
        return diagonal, high, low

    def sweeps(a, diagonal, high, low, result):
        args = [diagonal, down_weight, keep_mask, high, low] + ([] if result is None else [result])
        return call(
            functools.partial(sweeps_kernel, a),
            [jax.ShapeDtypeStruct((slots, features, hidden), F32), shape(8)],
            [VMEM] * 5 + [ANY] * (len(args) - 5),
            out_specs=[ANY, VMEM],
            scratch=[pltpu.VMEM((features, hidden), F32), pltpu.SemaphoreType.DMA],
            aliases={} if result is None else {5: 0},
            flops=2 * 3 * STEPS * features * hidden * hidden, moved=hidden * hidden * 4, name=f"sweeps_{a}",
        )(*args)

    result, total, halved = None, (), ()
    for a in range(slots):
        before = begin(a, halved)
        halved, sums = reduce(a, before, total[:1])
        halved, token = [halved], ()
        if a > 0:
            result, *token = sweeps(a - 1, *gather(a - 1, total, [sums[0]]), result)
        total = end(a, sums, token)
    return sweeps(slots - 1, *gather(slots - 1, total, ()), result)[0]


def solution(mesh):
    return jax.shard_map(
        on_device,
        mesh=mesh,
        in_specs=(
            P(("expert", "rows"), None),
            P(("expert", "rows"), None),
            P("expert", "rows", None),
            P("expert", "rows", None),
        ),
        out_specs=P("expert", "rows", None),
        check_vma=False,
    )
```

time: 101 us -> 84.6 us (0.84)
  waiting for transfers between devices: 42.7 us -> 33.6 us
  starting transfers between devices: 26.8 us -> 20.3 us
  local copies, waits for them, and re-layouts: 2.21 us -> 0.71 us
    ppermute x15 -> x14, waiting for transfers between devices: 24.7 us -> 15.7 us  [over_rows(): lax.ppermute(array, 'rows', [(i, i ^ 1 << bit) for i in range(copies)])]
    ppermute x8 -> x6, starting transfers between devices: 11.3 us -> 8.03 us  [over_experts(): return lax.ppermute(array, 'expert', [(i, i ^ flip) for i in range(peers)])]
    ppermute x15 -> x14, starting transfers between devices: 15.5 us -> 12.2 us  [over_rows(): lax.ppermute(array, 'rows', [(i, i ^ 1 << bit) for i in range(copies)])]
    unnamed x14 -> x6, local copies, waits for them, and re-layouts: 2.2 us -> 0.71 us
    pallas_call x18 -> x16, Pallas kernels: 28.8 us -> 29.4 us  [call(): return lambda *args: inner(*args, *after)]
    ppermute x8 -> x6, waiting for transfers between devices: 18.1 us -> 17.9 us  [over_experts(): return lax.ppermute(array, 'expert', [(i, i ^ flip) for i in range(peers)])]
  transfers between devices with their start and end apart: 23 -> 20, of which waited for: 13 -> 10; matrix products, arithmetic and copies ran while one was open for 0% -> 0% of each run, Pallas kernels for 15% -> 20%
where the time goes in v4:
time: 84.6 us; the launch traced here: 84.3 us
  waiting for transfers between devices  33.6 us (40%)
  Pallas kernels  29.4 us (35%)
  starting transfers between devices  20.3 us (24%)
    pallas_call x16, Pallas kernels, call(): return lambda *args: inner(*args, *after)  29.4 us
    ppermute x6, waiting for transfers between devices, over_experts(): return lax.ppermute(array, 'expert', [(i, i ^ flip) for i in range(peers)])  17.9 us
    ppermute x14, waiting for transfers between devices, over_rows(): lax.ppermute(array, 'rows', [(i, i ^ 1 << bit) for i in range(copies)])  15.7 us
    ppermute x14, starting transfers between devices, over_rows(): lax.ppermute(array, 'rows', [(i, i ^ 1 << bit) for i in range(copies)])  12.2 us
    ppermute x6, starting transfers between devices, over_experts(): return lax.ppermute(array, 'expert', [(i, i ^ flip) for i in range(peers)])  8.03 us
  transfers between devices with their start and end apart: 20, of which 10 were waited for; matrix products, arithmetic and copies ran while one was open for 0% of the time, Pallas kernels for 20%

profile of v4, /device:TPU:0, one launch (start us, length us, event | category | flops | bytes accessed | tf_op | source)
XLA Modules:
  0.0 84.3 jit_solution(2585217728849325988)
XLA Ops:
  0.0 0.0 copy-start.2
  0.0 0.7 copy-done.2
  0.7 4.7 %place_first.1 = (s32[1,2048]{1,0:T(1,128)S(1)}, bf16[256,768]{1,0:T(8,128)(2,1)S(1)}, bf16[256,768]{1,0:T(8,128)(2,1)S(1)}, bf16[256,768]{1,0:T(8,128)(2,1)S(1)}) custom-call(s32[1]{0:T(128)} %bitcast.1.refs_0_, s32[1,2048]{1,0:T(1,128)S(1)} %bitcast.3, bf16[2048,768]{1,0:T(8,128)(2,1)} %refs_2_.5), custom_call_target="tpu_custom_call" | custom-call | flops 2415919104 | bytes 6291456 | tf_op jit(solution)/shard_map/place_first/pallas_call | solution.py:45
  5.4 3.0 %collective-permute-start.2 = (bf16[256,768]{1,0:T(8,128)(2,1)S(1)}, bf16[256,768]{1,0:T(8,128)(2,1)S(1)}, u32[]{:S(2)}, u32[]{:S(2)}) collective-permute-start(bf16[256,768]{1,0:T(8,128)(2,1)S(1)} %get-tuple-element.50), channel_id=1, source_target_pairs={{0,8},{8,0},{16,24},{24,16},{1,9},{9,1},{17,25},{25,17},{2,10},{10... | collective-permute-start | bytes 1179656 | tf_op jit(solution)/shard_map/ppermute | solution.py:346
  8.4 1.5 %collective-permute-start.3 = (bf16[256,768]{1,0:T(8,128)(2,1)S(1)}, bf16[256,768]{1,0:T(8,128)(2,1)S(1)}, u32[]{:S(2)}, u32[]{:S(2)}) collective-permute-start(bf16[256,768]{1,0:T(8,128)(2,1)S(1)} %get-tuple-element.51), channel_id=1, source_target_pairs={{0,16},{8,24},{16,0},{24,8},{1,17},{9,25},{17,1},{25,9},{2,18},{10... | collective-permute-start | bytes 1179656 | tf_op jit(solution)/shard_map/ppermute | solution.py:346
  9.9 0.0 collective-permute-start.4
  9.9 6.2 %place_rest.1 = (bf16[256,768]{1,0:T(8,128)(2,1)S(1)}, bf16[256,768]{1,0:T(8,128)(2,1)S(1)}, bf16[256,768]{1,0:T(8,128)(2,1)S(1)}, bf16[256,768]{1,0:T(8,128)(2,1)S(1)}, bf16[256,768]{1,0:T(8,128)(2,1)S(1)}) custom-call(s32[1]{0:T(128)} %bitcast.1.refs_0_, s32[1,2048]{1,0:T(1,128)S(1)} %get-tuple-element.45.refs_1_, bf16[2048,768]{1,0:T(8,128)(2,1)} %refs_2_.5), custom_call_target="tpu_custom_call" | custom-call | flops 4026531840 | bytes 6291456 | tf_op jit(solution)/shard_map/place_rest/pallas_call | solution.py:45
  16.1 2.2 %collective-permute-done.2.refs_1_ = bf16[256,768]{1,0:T(8,128)(2,1)S(1)} collective-permute-done((bf16[256,768]{1,0:T(8,128)(2,1)S(1)}, bf16[256,768]{1,0:T(8,128)(2,1)S(1)}, u32[]{:S(2)}, u32[]{:S(2)}) %collective-permute-start.2) | collective-permute-done | bytes 393248 | tf_op jit(solution)/shard_map/ppermute | solution.py:346
  18.3 9.1 %collective-permute-done.3.refs_2_ = bf16[256,768]{1,0:T(8,128)(2,1)S(1)} collective-permute-done((bf16[256,768]{1,0:T(8,128)(2,1)S(1)}, bf16[256,768]{1,0:T(8,128)(2,1)S(1)}, u32[]{:S(2)}, u32[]{:S(2)}) %collective-permute-start.3) | collective-permute-done | bytes 393248 | tf_op jit(solution)/shard_map/ppermute | solution.py:346
  27.4 0.8 begin_0.1.refs_1_
  28.2 0.0 collective-permute-done.4.refs_2_
  28.2 0.6 gram_0.1
  28.9 0.1 collective-permute-start.5
  28.9 0.5 collective-permute-start.6
  29.4 0.4 collective-permute-start
  29.8 1.6 %collective-permute-start.1 = (bf16[256,768]{1,0:T(8,128)(2,1)S(1)}, bf16[256,768]{1,0:T(8,128)(2,1)S(1)}, u32[]{:S(2)}, u32[]{:S(2)}) collective-permute-start(bf16[256,768]{1,0:T(8,128)(2,1)S(1)} %get-tuple-element.48), channel_id=1, source_target_pairs={{0,16},{8,24},{16,0},{24,8},{1,17},{9,25},{17,1},{25,9},{2,18},{10... | collective-permute-start | bytes 1179656 | tf_op jit(solution)/shard_map/ppermute | solution.py:346
  31.5 1.4 %collective-permute-start.7 = (bf16[256,768]{1,0:T(8,128)(2,1)S(1)}, bf16[256,768]{1,0:T(8,128)(2,1)S(1)}, u32[]{:S(2)}, u32[]{:S(2)}) collective-permute-start(bf16[256,768]{1,0:T(8,128)(2,1)S(1)} %get-tuple-element.58), channel_id=1, source_target_pairs={{0,24},{8,16},{16,8},{24,0},{1,25},{9,17},{17,9},{25,1},{2,26},{10... | collective-permute-start | bytes 1179656 | tf_op jit(solution)/shard_map/ppermute | solution.py:346
  32.9 0.0 collective-permute-done.6.refs_4_
  32.9 0.0 collective-permute-done.5.refs_3_
  32.9 0.4 stage_0_1.1
  33.3 1.6 %collective-permute-start.8 = (s16[608,128]{1,0:T(8,128)(2,1)S(1)}, s16[608,128]{1,0:T(8,128)(2,1)S(1)}, u32[]{:S(2)}, u32[]{:S(2)}) collective-permute-start(s16[608,128]{1,0:T(8,128)(2,1)S(1)} %get-tuple-element.57.refs_3_), channel_id=1, source_target_pairs={{0,2},{1,3},{2,0},{3,1},{4,6},{5,7},{6,4},{7,5},{8,10},{9,11},{10,... | collective-permute-start | bytes 466952 | tf_op jit(solution)/shard_map/ppermute | solution.py:349
  35.0 3.7 %collective-permute-done.8.refs_3_ = s16[608,128]{1,0:T(8,128)(2,1)S(1)} collective-permute-done((s16[608,128]{1,0:T(8,128)(2,1)S(1)}, s16[608,128]{1,0:T(8,128)(2,1)S(1)}, u32[]{:S(2)}, u32[]{:S(2)}) %collective-permute-start.8) | collective-permute-done | bytes 155680 | tf_op jit(solution)/shard_map/ppermute | solution.py:349
  38.6 0.6 stage_0_2.1
  39.2 2.7 %collective-permute-start.9 = (s16[608,128]{1,0:T(8,128)(2,1)S(1)}, s16[608,128]{1,0:T(8,128)(2,1)S(1)}, u32[]{:S(2)}, u32[]{:S(2)}) collective-permute-start(s16[608,128]{1,0:T(8,128)(2,1)S(1)} %get-tuple-element.63), channel_id=1, source_target_pairs={{0,4},{1,5},{2,6},{3,7},{4,0},{5,1},{6,2},{7,3},{8,12},{9,13},{10,... | collective-permute-start | bytes 466952 | tf_op jit(solution)/shard_map/ppermute | solution.py:349
  41.9 0.0 collective-permute-done.refs_1_
  41.9 6.4 %collective-permute-done.1.refs_2_ = bf16[256,768]{1,0:T(8,128)(2,1)S(1)} collective-permute-done((bf16[256,768]{1,0:T(8,128)(2,1)S(1)}, bf16[256,768]{1,0:T(8,128)(2,1)S(1)}, u32[]{:S(2)}, u32[]{:S(2)}) %collective-permute-start.1) | collective-permute-done | bytes 393248 | tf_op jit(solution)/shard_map/ppermute | solution.py:346
  48.3 0.8 begin_1.1.refs_1_
  49.1 0.0 collective-permute-done.9.refs_3_
  49.1 0.6 total_0.1
  49.7 0.2 collective-permute-done.7.refs_2_
  49.9 0.6 gram_1.1
  50.5 0.1 collective-permute-start.10
  50.6 0.5 collective-permute-start.11
  51.1 1.6 %collective-permute-start.14 = (s16[592,128]{1,0:T(8,128)(2,1)S(1)}, s16[592,128]{1,0:T(8,128)(2,1)S(1)}, u32[]{:S(2)}, u32[]{:S(2)}) collective-permute-start(s16[592,128]{1,0:T(8,128)(2,1)S(1)} %get-tuple-element.64.refs_3_.refs_2_), channel_id=1, source_target_pairs={{0,2},{1,3},{2,0},{3,1},{4,6},{5,7},{6,4},{7,5},{8,10},{9,11},{10,... | collective-permute-start | bytes 454664 | tf_op jit(solution)/shard_map/ppermute | solution.py:349
  52.7 0.0 collective-permute-done.11.refs_4_
  52.7 0.0 collective-permute-done.10.refs_3_
  52.7 0.0 copy-start
  52.7 0.0 copy-start.1
  52.7 0.4 stage_1_1.1
  53.1 1.5 %collective-permute-start.12 = (s16[608,128]{1,0:T(8,128)(2,1)S(1)}, s16[608,128]{1,0:T(8,128)(2,1)S(1)}, u32[]{:S(2)}, u32[]{:S(2)}) collective-permute-start(s16[608,128]{1,0:T(8,128)(2,1)S(1)} %get-tuple-element.71), channel_id=1, source_target_pairs={{0,2},{1,3},{2,0},{3,1},{4,6},{5,7},{6,4},{7,5},{8,10},{9,11},{10,... | collective-permute-start | bytes 466952 | tf_op jit(solution)/shard_map/ppermute | solution.py:349
  54.7 0.0 collective-permute-start.15
  54.7 3.2 %collective-permute-done.14.refs_3_ = s16[592,128]{1,0:T(8,128)(2,1)S(1)} collective-permute-done((s16[592,128]{1,0:T(8,128)(2,1)S(1)}, s16[592,128]{1,0:T(8,128)(2,1)S(1)}, u32[]{:S(2)}, u32[]{:S(2)}) %collective-permute-start.14) | collective-permute-done | bytes 151584 | tf_op jit(solution)/shard_map/ppermute | solution.py:349
  57.9 0.0 collective-permute-start.16
  57.9 2.5 %collective-permute-done.12.refs_3_ = s16[608,128]{1,0:T(8,128)(2,1)S(1)} collective-permute-done((s16[608,128]{1,0:T(8,128)(2,1)S(1)}, s16[608,128]{1,0:T(8,128)(2,1)S(1)}, u32[]{:S(2)}, u32[]{:S(2)}) %collective-permute-start.12) | collective-permute-done | bytes 155680 | tf_op jit(solution)/shard_map/ppermute | solution.py:349
  60.4 0.6 stage_1_2.1
  61.0 2.7 %collective-permute-start.13 = (s16[608,128]{1,0:T(8,128)(2,1)S(1)}, s16[608,128]{1,0:T(8,128)(2,1)S(1)}, u32[]{:S(2)}, u32[]{:S(2)}) collective-permute-start(s16[608,128]{1,0:T(8,128)(2,1)S(1)} %get-tuple-element.74.refs_6_), channel_id=1, source_target_pairs={{0,4},{1,5},{2,6},{3,7},{4,0},{5,1},{6,2},{7,3},{8,12},{9,13},{10,... | collective-permute-start | bytes 466952 | tf_op jit(solution)/shard_map/ppermute | solution.py:349
  63.6 0.0 collective-permute-done.15.refs_4_
  63.6 0.0 collective-permute-done.16.refs_5_
  63.6 0.9 %unpack_0.1 = (bf16[768,768]{1,0:T(8,128)(2,1)S(1)}, bf16[768,768]{1,0:T(8,128)(2,1)S(1)}) custom-call(s32[1]{0:T(128)} %bitcast.refs_0_, f32[8,128]{1,0:T(8,128)S(1)} %get-tuple-element.75.refs_1_.refs_0_, s16[592,128]{1,0:T(8,128)(2,1)S(1)} %get-tuple-element.64.refs_3_.refs_2_, s16[592,128]{1,0:T(8,128)(2,1)S(1)} %collective-permute-done.14.refs_3_, ...), custom_call_target="tpu_custom_call" | custom-call | bytes 1179648 | tf_op jit(solution)/shard_map/unpack_0/pallas_call | solution.py:45
  64.5 0.0 copy-done
  64.5 0.0 copy-done.1
  64.6 5.2 %sweeps_0.1 = (f32[2,256,768]{2,1,0:T(8,128)}, f32[8,128]{1,0:T(8,128)S(1)}) custom-call(f32[8,128]{1,0:T(8,128)S(1)} %get-tuple-element.75.refs_1_.refs_0_, bf16[2,256,768]{2,1,0:T(8,128)(2,1)S(1)} %copy-done, bf16[2,256,768]{2,1,0:T(8,128)(2,1)S(1)} %copy-done.1, bf16[768,768]{1,0:T(8,128)(2,1)S(1)} %get-tuple-element.76.refs_3_, ...), custom_call_target="tpu_custom_call" | custom-call | flops 3623878656 | bytes 2359296 | tf_op jit(solution)/shard_map/sweeps_0/pallas_call | solution.py:45
  69.8 0.7 collective-permute-done.13.refs_3_
  70.4 0.6 total_1.1
  71.0 1.0 %collective-permute-start.17 = (s16[592,128]{1,0:T(8,128)(2,1)S(1)}, s16[592,128]{1,0:T(8,128)(2,1)S(1)}, u32[]{:S(2)}, u32[]{:S(2)}) collective-permute-start(s16[592,128]{1,0:T(8,128)(2,1)S(1)} %get-tuple-element.80.refs_2_), channel_id=1, source_target_pairs={{0,2},{1,3},{2,0},{3,1},{4,6},{5,7},{6,4},{7,5},{8,10},{9,11},{10,... | collective-permute-start | bytes 454664 | tf_op jit(solution)/shard_map/ppermute | solution.py:349
  72.0 0.0 collective-permute-start.18
  72.0 4.3 %collective-permute-done.17.refs_3_ = s16[592,128]{1,0:T(8,128)(2,1)S(1)} collective-permute-done((s16[592,128]{1,0:T(8,128)(2,1)S(1)}, s16[592,128]{1,0:T(8,128)(2,1)S(1)}, u32[]{:S(2)}, u32[]{:S(2)}) %collective-permute-start.17) | collective-permute-done | bytes 151584 | tf_op jit(solution)/shard_map/ppermute | solution.py:349
  76.3 0.0 collective-permute-start.19
  76.3 0.0 collective-permute-done.18.refs_4_
  76.3 1.4 %collective-permute-done.19.refs_5_ = s16[592,128]{1,0:T(8,128)(2,1)S(1)} collective-permute-done((s16[592,128]{1,0:T(8,128)(2,1)S(1)}, s16[592,128]{1,0:T(8,128)(2,1)S(1)}, u32[]{:S(2)}, u32[]{:S(2)}) %collective-permute-start.19) | collective-permute-done | bytes 151584 | tf_op jit(solution)/shard_map/ppermute | solution.py:349
  77.6 0.7 unpack_1.1
  78.4 5.7 %sweeps_1.1 = (f32[2,256,768]{2,1,0:T(8,128)}, f32[8,128]{1,0:T(8,128)}) custom-call(f32[8,128]{1,0:T(8,128)S(1)} %get-tuple-element.79.refs_1_.refs_0_, bf16[2,256,768]{2,1,0:T(8,128)(2,1)S(1)} %copy-done, bf16[2,256,768]{2,1,0:T(8,128)(2,1)S(1)} %copy-done.1, bf16[768,768]{1,0:T(8,128)(2,1)S(1)} %get-tuple-element.81.refs_3_, ...), custom_call_target="tpu_custom_call", output_to_operand_aliasing={{0}: (5, {})} | custom-call | flops 3623878656 | bytes 2359296 | tf_op jit(solution)/shard_map/sweeps_1/pallas_call | solution.py:45
Async XLA Ops:
  0.0 0.7 copy-start.2
  5.4 13.0 %collective-permute-start.2 = (bf16[256,768]{1,0:T(8,128)(2,1)S(1)}, bf16[256,768]{1,0:T(8,128)(2,1)S(1)}, u32[]{:S(2)}, u32[]{:S(2)}) collective-permute-start(bf16[256,768]{1,0:T(8,128)(2,1)S(1)} %get-tuple-element.50), channel_id=1, source_target_pairs={{0,8},{8,0},{16,24},{24,16},{1,9},{9,1},{17,25},{25,17},{2,10},{10... | collective-permute-start | bytes 1179656 | tf_op jit(solution)/shard_map/ppermute | solution.py:346
  8.4 19.0 %collective-permute-start.3 = (bf16[256,768]{1,0:T(8,128)(2,1)S(1)}, bf16[256,768]{1,0:T(8,128)(2,1)S(1)}, u32[]{:S(2)}, u32[]{:S(2)}) collective-permute-start(bf16[256,768]{1,0:T(8,128)(2,1)S(1)} %get-tuple-element.51), channel_id=1, source_target_pairs={{0,16},{8,24},{16,0},{24,8},{1,17},{9,25},{17,1},{25,9},{2,18},{10... | collective-permute-start | bytes 1179656 | tf_op jit(solution)/shard_map/ppermute | solution.py:346
  9.9 18.3 %collective-permute-start.4 = (bf16[256,768]{1,0:T(8,128)(2,1)S(1)}, bf16[256,768]{1,0:T(8,128)(2,1)S(1)}, u32[]{:S(2)}, u32[]{:S(2)}) collective-permute-start(bf16[256,768]{1,0:T(8,128)(2,1)S(1)} %get-tuple-element.52), channel_id=1, source_target_pairs={{0,24},{8,16},{16,8},{24,0},{1,25},{9,17},{17,9},{25,1},{2,26},{10... | collective-permute-start | bytes 1179656 | tf_op jit(solution)/shard_map/ppermute | solution.py:346
  28.9 4.1 %collective-permute-start.5 = (f32[584,128]{1,0:T(8,128)S(1)}, f32[584,128]{1,0:T(8,128)S(1)}, u32[]{:S(2)}, u32[]{:S(2)}) collective-permute-start(f32[584,128]{1,0:T(8,128)S(1)} %get-tuple-element.55), channel_id=1, source_target_pairs={{0,1},{1,0},{2,3},{3,2},{4,5},{5,4},{6,7},{7,6},{8,9},{9,8},{10,11... | collective-permute-start | bytes 897032 | tf_op jit(solution)/shard_map/ppermute | solution.py:349
  28.9 4.0 %collective-permute-start.6 = (f32[576,128]{1,0:T(8,128)S(1)}, f32[576,128]{1,0:T(8,128)S(1)}, u32[]{:S(2)}, u32[]{:S(2)}) collective-permute-start(f32[576,128]{1,0:T(8,128)S(1)} %get-tuple-element.56), channel_id=1, source_target_pairs={{0,1},{1,0},{2,3},{3,2},{4,5},{5,4},{6,7},{7,6},{8,9},{9,8},{10,11... | collective-permute-start | bytes 884744 | tf_op jit(solution)/shard_map/ppermute | solution.py:349
  29.4 12.5 %collective-permute-start = (bf16[256,768]{1,0:T(8,128)(2,1)S(1)}, bf16[256,768]{1,0:T(8,128)(2,1)S(1)}, u32[]{:S(2)}, u32[]{:S(2)}) collective-permute-start(bf16[256,768]{1,0:T(8,128)(2,1)S(1)} %get-tuple-element.47), channel_id=1, source_target_pairs={{0,8},{8,0},{16,24},{24,16},{1,9},{9,1},{17,25},{25,17},{2,10},{10... | collective-permute-start | bytes 1179656 | tf_op jit(solution)/shard_map/ppermute | solution.py:346
  29.8 18.4 %collective-permute-start.1 = (bf16[256,768]{1,0:T(8,128)(2,1)S(1)}, bf16[256,768]{1,0:T(8,128)(2,1)S(1)}, u32[]{:S(2)}, u32[]{:S(2)}) collective-permute-start(bf16[256,768]{1,0:T(8,128)(2,1)S(1)} %get-tuple-element.48), channel_id=1, source_target_pairs={{0,16},{8,24},{16,0},{24,8},{1,17},{9,25},{17,1},{25,9},{2,18},{10... | collective-permute-start | bytes 1179656 | tf_op jit(solution)/shard_map/ppermute | solution.py:346
  31.5 18.4 %collective-permute-start.7 = (bf16[256,768]{1,0:T(8,128)(2,1)S(1)}, bf16[256,768]{1,0:T(8,128)(2,1)S(1)}, u32[]{:S(2)}, u32[]{:S(2)}) collective-permute-start(bf16[256,768]{1,0:T(8,128)(2,1)S(1)} %get-tuple-element.58), channel_id=1, source_target_pairs={{0,24},{8,16},{16,8},{24,0},{1,25},{9,17},{17,9},{25,1},{2,26},{10... | collective-permute-start | bytes 1179656 | tf_op jit(solution)/shard_map/ppermute | solution.py:346
  33.3 5.3 %collective-permute-start.8 = (s16[608,128]{1,0:T(8,128)(2,1)S(1)}, s16[608,128]{1,0:T(8,128)(2,1)S(1)}, u32[]{:S(2)}, u32[]{:S(2)}) collective-permute-start(s16[608,128]{1,0:T(8,128)(2,1)S(1)} %get-tuple-element.57.refs_3_), channel_id=1, source_target_pairs={{0,2},{1,3},{2,0},{3,1},{4,6},{5,7},{6,4},{7,5},{8,10},{9,11},{10,... | collective-permute-start | bytes 466952 | tf_op jit(solution)/shard_map/ppermute | solution.py:349
  39.2 9.9 %collective-permute-start.9 = (s16[608,128]{1,0:T(8,128)(2,1)S(1)}, s16[608,128]{1,0:T(8,128)(2,1)S(1)}, u32[]{:S(2)}, u32[]{:S(2)}) collective-permute-start(s16[608,128]{1,0:T(8,128)(2,1)S(1)} %get-tuple-element.63), channel_id=1, source_target_pairs={{0,4},{1,5},{2,6},{3,7},{4,0},{5,1},{6,2},{7,3},{8,12},{9,13},{10,... | collective-permute-start | bytes 466952 | tf_op jit(solution)/shard_map/ppermute | solution.py:349
  50.5 2.2 %collective-permute-start.10 = (f32[584,128]{1,0:T(8,128)S(1)}, f32[584,128]{1,0:T(8,128)S(1)}, u32[]{:S(2)}, u32[]{:S(2)}) collective-permute-start(f32[584,128]{1,0:T(8,128)S(1)} %get-tuple-element.67), channel_id=1, source_target_pairs={{0,1},{1,0},{2,3},{3,2},{4,5},{5,4},{6,7},{7,6},{8,9},{9,8},{10,11... | collective-permute-start | bytes 897032 | tf_op jit(solution)/shard_map/ppermute | solution.py:349
  50.6 2.1 %collective-permute-start.11 = (f32[576,128]{1,0:T(8,128)S(1)}, f32[576,128]{1,0:T(8,128)S(1)}, u32[]{:S(2)}, u32[]{:S(2)}) collective-permute-start(f32[576,128]{1,0:T(8,128)S(1)} %get-tuple-element.68), channel_id=1, source_target_pairs={{0,1},{1,0},{2,3},{3,2},{4,5},{5,4},{6,7},{7,6},{8,9},{9,8},{10,11... | collective-permute-start | bytes 884744 | tf_op jit(solution)/shard_map/ppermute | solution.py:349
  51.1 6.8 %collective-permute-start.14 = (s16[592,128]{1,0:T(8,128)(2,1)S(1)}, s16[592,128]{1,0:T(8,128)(2,1)S(1)}, u32[]{:S(2)}, u32[]{:S(2)}) collective-permute-start(s16[592,128]{1,0:T(8,128)(2,1)S(1)} %get-tuple-element.64.refs_3_.refs_2_), channel_id=1, source_target_pairs={{0,2},{1,3},{2,0},{3,1},{4,6},{5,7},{6,4},{7,5},{8,10},{9,11},{10,... | collective-permute-start | bytes 454664 | tf_op jit(solution)/shard_map/ppermute | solution.py:349
  52.7 11.8 %copy-start = (bf16[2,256,768]{2,1,0:T(8,128)(2,1)S(1)}, bf16[2,256,768]{2,1,0:T(8,128)(2,1)}, u32[]{:S(2)}) copy-start(bf16[2,256,768]{2,1,0:T(8,128)(2,1)} %refs_1_.3) | copy-start | bytes 2359300
  52.7 11.9 %copy-start.1 = (bf16[2,256,768]{2,1,0:T(8,128)(2,1)S(1)}, bf16[2,256,768]{2,1,0:T(8,128)(2,1)}, u32[]{:S(2)}) copy-start(bf16[2,256,768]{2,1,0:T(8,128)(2,1)} %refs_2_.7) | copy-start | bytes 2359300
  53.1 7.2 %collective-permute-start.12 = (s16[608,128]{1,0:T(8,128)(2,1)S(1)}, s16[608,128]{1,0:T(8,128)(2,1)S(1)}, u32[]{:S(2)}, u32[]{:S(2)}) collective-permute-start(s16[608,128]{1,0:T(8,128)(2,1)S(1)} %get-tuple-element.71), channel_id=1, source_target_pairs={{0,2},{1,3},{2,0},{3,1},{4,6},{5,7},{6,4},{7,5},{8,10},{9,11},{10,... | collective-permute-start | bytes 466952 | tf_op jit(solution)/shard_map/ppermute | solution.py:349
  54.7 9.0 %collective-permute-start.15 = (s16[592,128]{1,0:T(8,128)(2,1)S(1)}, s16[592,128]{1,0:T(8,128)(2,1)S(1)}, u32[]{:S(2)}, u32[]{:S(2)}) collective-permute-start(s16[592,128]{1,0:T(8,128)(2,1)S(1)} %get-tuple-element.64.refs_3_.refs_2_), channel_id=1, source_target_pairs={{0,1},{1,0},{2,3},{3,2},{4,5},{5,4},{6,7},{7,6},{8,9},{9,8},{10,11... | collective-permute-start | bytes 454664 | tf_op jit(solution)/shard_map/ppermute | solution.py:349
  57.9 5.7 %collective-permute-start.16 = (s16[592,128]{1,0:T(8,128)(2,1)S(1)}, s16[592,128]{1,0:T(8,128)(2,1)S(1)}, u32[]{:S(2)}, u32[]{:S(2)}) collective-permute-start(s16[592,128]{1,0:T(8,128)(2,1)S(1)} %collective-permute-done.14.refs_3_), channel_id=1, source_target_pairs={{0,1},{1,0},{2,3},{3,2},{4,5},{5,4},{6,7},{7,6},{8,9},{9,8},{10,11... | collective-permute-start | bytes 454664 | tf_op jit(solution)/shard_map/ppermute | solution.py:349
  61.0 9.5 %collective-permute-start.13 = (s16[608,128]{1,0:T(8,128)(2,1)S(1)}, s16[608,128]{1,0:T(8,128)(2,1)S(1)}, u32[]{:S(2)}, u32[]{:S(2)}) collective-permute-start(s16[608,128]{1,0:T(8,128)(2,1)S(1)} %get-tuple-element.74.refs_6_), channel_id=1, source_target_pairs={{0,4},{1,5},{2,6},{3,7},{4,0},{5,1},{6,2},{7,3},{8,12},{9,13},{10,... | collective-permute-start | bytes 466952 | tf_op jit(solution)/shard_map/ppermute | solution.py:349
  71.0 5.3 %collective-permute-start.17 = (s16[592,128]{1,0:T(8,128)(2,1)S(1)}, s16[592,128]{1,0:T(8,128)(2,1)S(1)}, u32[]{:S(2)}, u32[]{:S(2)}) collective-permute-start(s16[592,128]{1,0:T(8,128)(2,1)S(1)} %get-tuple-element.80.refs_2_), channel_id=1, source_target_pairs={{0,2},{1,3},{2,0},{3,1},{4,6},{5,7},{6,4},{7,5},{8,10},{9,11},{10,... | collective-permute-start | bytes 454664 | tf_op jit(solution)/shard_map/ppermute | solution.py:349
  72.0 4.3 %collective-permute-start.18 = (s16[592,128]{1,0:T(8,128)(2,1)S(1)}, s16[592,128]{1,0:T(8,128)(2,1)S(1)}, u32[]{:S(2)}, u32[]{:S(2)}) collective-permute-start(s16[592,128]{1,0:T(8,128)(2,1)S(1)} %get-tuple-element.80.refs_2_), channel_id=1, source_target_pairs={{0,1},{1,0},{2,3},{3,2},{4,5},{5,4},{6,7},{7,6},{8,9},{9,8},{10,11... | collective-permute-start | bytes 454664 | tf_op jit(solution)/shard_map/ppermute | solution.py:349
  76.3 1.4 %collective-permute-start.19 = (s16[592,128]{1,0:T(8,128)(2,1)S(1)}, s16[592,128]{1,0:T(8,128)(2,1)S(1)}, u32[]{:S(2)}, u32[]{:S(2)}) collective-permute-start(s16[592,128]{1,0:T(8,128)(2,1)S(1)} %collective-permute-done.17.refs_3_), channel_id=1, source_target_pairs={{0,1},{1,0},{2,3},{3,2},{4,5},{5,4},{6,7},{7,6},{8,9},{9,8},{10,11... | collective-permute-start | bytes 454664 | tf_op jit(solution)/shard_map/ppermute | solution.py:349

commit v5 on v4

--- a/solution.py
+++ b/solution.py
@@ -373,7 +373,7 @@
         chunks = [own[a]] + arrived[a][:-1]
         return call(
             functools.partial(early_gram_kernel, halvings), shape(length + many), [VMEM] * len(chunks),
-            flops=2 * capacity * len(chunks) * hidden * hidden, moved=length * BLOCK * 4, name=f"begin_{a}", after=after,
+            name=f"begin_{a}", after=after,
         )(*chunks)
 
     def stage(name, bit, keep, diagonal, got, cut, kept, after=()):
@@ -387,23 +387,21 @@
             moved=rows * BLOCK * 12, name=name, after=after,
         )(where, keep, diagonal, *got)
 
-    def reduce(a, before, after):
+    def reduce(a, before, after, behind):
         size = length // 2
         sizes = cuts(size, PARTS)
         keep, diagonal, *sent = call(
             functools.partial(late_gram_kernel, halvings, 1),
             [shape(size), shape(many)] + [shape(n + (many if i == 0 else 0)) for i, n in enumerate(sizes)],
             [SMEM] + [VMEM] * 2, scratch=[pltpu.VMEM((length + many, BLOCK), F32)],
-            flops=2 * capacity * hidden * hidden, moved=length * BLOCK * 4, name=f"gram_{a}", after=after,
+            name=f"gram_{a}", after=after,
         )(where, before, arrived[a][-1])
         for bit in range(1, halvings + 1):
             cut = bit < halvings
             got = [over_rows(part, bit - 1) for part in sent]
-            coded, diagonal, keep = stage(f"stage_{a}_{bit}", bit, keep, diagonal, got, cut, True)
+            coded, diagonal, keep = stage(f"stage_{a}_{bit}", bit, keep, diagonal, got, cut, True, behind if bit == 1 else ())
             sent = [coded]
-            if bit == 1:
-                halved = coded
-        return halved, (coded, diagonal, keep)
+        return coded, diagonal, keep
 
     def end(a, sums, after):
         coded, diagonal, keep = sums
@@ -433,11 +431,10 @@
             flops=2 * 3 * STEPS * features * hidden * hidden, moved=hidden * hidden * 4, name=f"sweeps_{a}",
         )(*args)
 
-    result, total, halved = None, (), ()
+    result, total, started = None, (), [begin(a, ()) for a in range(slots)]
     for a in range(slots):
-        before = begin(a, halved)
-        halved, sums = reduce(a, before, total[:1])
-        halved, token = [halved], ()
+        sums = reduce(a, started[a], total[:1], started[a + 1:a + 2])
+        token = ()
         if a > 0:
             result, *token = sweeps(a - 1, *gather(a - 1, total, [sums[0]]), result)
         total = end(a, sums, token)

time: 84.6 us -> 96.3 us (1.14)
  waiting for transfers between devices: 33.6 us -> 47.5 us
  starting transfers between devices: 20.3 us -> 16.7 us
  Pallas kernels: 29.4 us -> 30.8 us
    ppermute x14, waiting for transfers between devices: 15.7 us -> 26.3 us  [over_rows(): lax.ppermute(array, 'rows', [(i, i ^ 1 << bit) for i in range(copies)])]
    ppermute x14, starting transfers between devices: 12.2 us -> 7.72 us  [over_rows(): lax.ppermute(array, 'rows', [(i, i ^ 1 << bit) for i in range(copies)])]
    ppermute x6, waiting for transfers between devices: 17.9 us -> 21.2 us  [over_experts(): return lax.ppermute(array, 'expert', [(i, i ^ flip) for i in range(peers)])]
    pallas_call x16, Pallas kernels: 29.4 us -> 30.8 us  [call(): return lambda *args: inner(*args, *after)]
    ppermute x6, starting transfers between devices: 8.03 us -> 9 us  [over_experts(): return lax.ppermute(array, 'expert', [(i, i ^ flip) for i in range(peers)])]
  transfers between devices with their start and end apart: 20 -> 20, of which waited for: 10 -> 11; matrix products, arithmetic and copies ran while one was open for 0% -> 0% of each run, Pallas kernels for 20% -> 18%
where the time goes in v5:
time: 96.3 us; the launch traced here: 96 us
  waiting for transfers between devices  47.5 us (49%)
  Pallas kernels  30.8 us (32%)
  starting transfers between devices  16.7 us (17%)
    pallas_call x16, Pallas kernels, call(): return lambda *args: inner(*args, *after)  30.8 us
    ppermute x14, waiting for transfers between devices, over_rows(): lax.ppermute(array, 'rows', [(i, i ^ 1 << bit) for i in range(copies)])  26.3 us
    ppermute x6, waiting for transfers between devices, over_experts(): return lax.ppermute(array, 'expert', [(i, i ^ flip) for i in range(peers)])  21.2 us
    ppermute x6, starting transfers between devices, over_experts(): return lax.ppermute(array, 'expert', [(i, i ^ flip) for i in range(peers)])  9 us
    ppermute x14, starting transfers between devices, over_rows(): lax.ppermute(array, 'rows', [(i, i ^ 1 << bit) for i in range(copies)])  7.72 us
  transfers between devices with their start and end apart: 20, of which 11 were waited for; matrix products, arithmetic and copies ran while one was open for 0% of the time, Pallas kernels for 18%

profile of v5, /device:TPU:0, one launch (start us, length us, event | category | flops | bytes accessed | tf_op | source)
XLA Modules:
  0.0 96.0 jit_solution(5661711839866528874)
XLA Ops:
  0.0 0.0 copy-start.2
  0.0 0.7 copy-done.2
  0.7 5.6 %place_first.1 = (s32[1,2048]{1,0:T(1,128)S(1)}, bf16[256,768]{1,0:T(8,128)(2,1)}, bf16[256,768]{1,0:T(8,128)(2,1)}, bf16[256,768]{1,0:T(8,128)(2,1)}) custom-call(s32[1]{0:T(128)} %bitcast.1.refs_0_, s32[1,2048]{1,0:T(1,128)S(1)} %bitcast.3, bf16[2048,768]{1,0:T(8,128)(2,1)} %refs_2_.5), custom_call_target="tpu_custom_call" | custom-call | flops 2415919104 | bytes 6291456 | tf_op jit(solution)/shard_map/place_first/pallas_call | solution.py:45
  6.3 2.9 %collective-permute-start.3 = (bf16[256,768]{1,0:T(8,128)(2,1)}, bf16[256,768]{1,0:T(8,128)(2,1)S(1)}, u32[]{:S(2)}, u32[]{:S(2)}) collective-permute-start(bf16[256,768]{1,0:T(8,128)(2,1)} %get-tuple-element.51), channel_id=1, source_target_pairs={{0,8},{8,0},{16,24},{24,16},{1,9},{9,1},{17,25},{25,17},{2,10},{10... | collective-permute-start | bytes 1179656 | tf_op jit(solution)/shard_map/ppermute | solution.py:346
  9.2 1.5 %collective-permute-start.4 = (bf16[256,768]{1,0:T(8,128)(2,1)}, bf16[256,768]{1,0:T(8,128)(2,1)S(1)}, u32[]{:S(2)}, u32[]{:S(2)}) collective-permute-start(bf16[256,768]{1,0:T(8,128)(2,1)} %get-tuple-element.52), channel_id=1, source_target_pairs={{0,16},{8,24},{16,0},{24,8},{1,17},{9,25},{17,1},{25,9},{2,18},{10... | collective-permute-start | bytes 1179656 | tf_op jit(solution)/shard_map/ppermute | solution.py:346
  10.7 0.0 collective-permute-start.5
  10.7 6.8 %place_rest.1 = (bf16[256,768]{1,0:T(8,128)(2,1)S(1)}, bf16[256,768]{1,0:T(8,128)(2,1)S(1)}, bf16[256,768]{1,0:T(8,128)(2,1)}, bf16[256,768]{1,0:T(8,128)(2,1)S(1)}, bf16[256,768]{1,0:T(8,128)(2,1)S(1)}) custom-call(s32[1]{0:T(128)} %bitcast.1.refs_0_, s32[1,2048]{1,0:T(1,128)S(1)} %get-tuple-element.45.refs_1_, bf16[2048,768]{1,0:T(8,128)(2,1)} %refs_2_.5), custom_call_target="tpu_custom_call" | custom-call | flops 4026531840 | bytes 6291456 | tf_op jit(solution)/shard_map/place_rest/pallas_call | solution.py:45
  17.5 2.0 %collective-permute-start = (bf16[256,768]{1,0:T(8,128)(2,1)}, bf16[256,768]{1,0:T(8,128)(2,1)S(1)}, u32[]{:S(2)}, u32[]{:S(2)}) collective-permute-start(bf16[256,768]{1,0:T(8,128)(2,1)} %get-tuple-element.47), channel_id=1, source_target_pairs={{0,8},{8,0},{16,24},{24,16},{1,9},{9,1},{17,25},{25,17},{2,10},{10... | collective-permute-start | bytes 1179656 | tf_op jit(solution)/shard_map/ppermute | solution.py:346
  19.5 1.5 %collective-permute-start.1 = (bf16[256,768]{1,0:T(8,128)(2,1)S(1)}, bf16[256,768]{1,0:T(8,128)(2,1)S(1)}, u32[]{:S(2)}, u32[]{:S(2)}) collective-permute-start(bf16[256,768]{1,0:T(8,128)(2,1)S(1)} %get-tuple-element.48), channel_id=1, source_target_pairs={{0,16},{8,24},{16,0},{24,8},{1,17},{9,25},{17,1},{25,9},{2,18},{10... | collective-permute-start | bytes 1179656 | tf_op jit(solution)/shard_map/ppermute | solution.py:346
  21.0 0.0 collective-permute-done.3.refs_1_
  21.0 7.9 %collective-permute-done.4.refs_2_ = bf16[256,768]{1,0:T(8,128)(2,1)S(1)} collective-permute-done((bf16[256,768]{1,0:T(8,128)(2,1)}, bf16[256,768]{1,0:T(8,128)(2,1)S(1)}, u32[]{:S(2)}, u32[]{:S(2)}) %collective-permute-start.4) | collective-permute-done | bytes 393248 | tf_op jit(solution)/shard_map/ppermute | solution.py:346
  28.9 0.8 begin_0.1.refs_1_
  29.7 0.0 collective-permute-done.5.refs_2_
  29.7 0.6 gram_0.1
  30.4 0.1 collective-permute-start.6
  30.4 0.5 collective-permute-start.7
  30.9 1.1 %collective-permute-start.2 = (bf16[256,768]{1,0:T(8,128)(2,1)S(1)}, bf16[256,768]{1,0:T(8,128)(2,1)S(1)}, u32[]{:S(2)}, u32[]{:S(2)}) collective-permute-start(bf16[256,768]{1,0:T(8,128)(2,1)S(1)} %get-tuple-element.49), channel_id=1, source_target_pairs={{0,24},{8,16},{16,8},{24,0},{1,25},{9,17},{17,9},{25,1},{2,26},{10... | collective-permute-start | bytes 1179656 | tf_op jit(solution)/shard_map/ppermute | solution.py:346
  32.0 4.0 %collective-permute-done.refs_1_ = bf16[256,768]{1,0:T(8,128)(2,1)S(1)} collective-permute-done((bf16[256,768]{1,0:T(8,128)(2,1)}, bf16[256,768]{1,0:T(8,128)(2,1)S(1)}, u32[]{:S(2)}, u32[]{:S(2)}) %collective-permute-start) | collective-permute-done | bytes 393248 | tf_op jit(solution)/shard_map/ppermute | solution.py:346
  35.9 9.3 %collective-permute-done.1.refs_2_ = bf16[256,768]{1,0:T(8,128)(2,1)S(1)} collective-permute-done((bf16[256,768]{1,0:T(8,128)(2,1)S(1)}, bf16[256,768]{1,0:T(8,128)(2,1)S(1)}, u32[]{:S(2)}, u32[]{:S(2)}) %collective-permute-start.1) | collective-permute-done | bytes 393248 | tf_op jit(solution)/shard_map/ppermute | solution.py:346
  45.3 0.8 begin_1.1.refs_5_.refs_1_
  46.1 0.0 collective-permute-done.7.refs_4_
  46.1 0.0 collective-permute-done.6.refs_3_
  46.1 0.4 stage_0_1.1
  46.5 1.6 %collective-permute-start.8 = (s16[608,128]{1,0:T(8,128)(2,1)S(1)}, s16[608,128]{1,0:T(8,128)(2,1)S(1)}, u32[]{:S(2)}, u32[]{:S(2)}) collective-permute-start(s16[608,128]{1,0:T(8,128)(2,1)S(1)} %get-tuple-element.60), channel_id=1, source_target_pairs={{0,2},{1,3},{2,0},{3,1},{4,6},{5,7},{6,4},{7,5},{8,10},{9,11},{10,... | collective-permute-start | bytes 466952 | tf_op jit(solution)/shard_map/ppermute | solution.py:349
  48.2 4.2 %collective-permute-done.8.refs_3_ = s16[608,128]{1,0:T(8,128)(2,1)S(1)} collective-permute-done((s16[608,128]{1,0:T(8,128)(2,1)S(1)}, s16[608,128]{1,0:T(8,128)(2,1)S(1)}, u32[]{:S(2)}, u32[]{:S(2)}) %collective-permute-start.8) | collective-permute-done | bytes 155680 | tf_op jit(solution)/shard_map/ppermute | solution.py:349
  52.4 0.6 stage_0_2.1
  53.0 2.1 %collective-permute-start.9 = (s16[608,128]{1,0:T(8,128)(2,1)S(1)}, s16[608,128]{1,0:T(8,128)(2,1)S(1)}, u32[]{:S(2)}, u32[]{:S(2)}) collective-permute-start(s16[608,128]{1,0:T(8,128)(2,1)S(1)} %get-tuple-element.63), channel_id=1, source_target_pairs={{0,4},{1,5},{2,6},{3,7},{4,0},{5,1},{6,2},{7,3},{8,12},{9,13},{10,... | collective-permute-start | bytes 466952 | tf_op jit(solution)/shard_map/ppermute | solution.py:349
  55.1 5.8 %collective-permute-done.9.refs_3_ = s16[608,128]{1,0:T(8,128)(2,1)S(1)} collective-permute-done((s16[608,128]{1,0:T(8,128)(2,1)S(1)}, s16[608,128]{1,0:T(8,128)(2,1)S(1)}, u32[]{:S(2)}, u32[]{:S(2)}) %collective-permute-start.9) | collective-permute-done | bytes 155680 | tf_op jit(solution)/shard_map/ppermute | solution.py:349
  60.8 0.6 total_0.1
  61.4 0.0 collective-permute-done.2.refs_2_
  61.4 0.6 gram_1.1
  62.0 0.1 collective-permute-start.10
  62.1 0.5 collective-permute-start.11
  62.6 0.1 collective-permute-start.14
  62.7 1.4 %collective-permute-done.11.refs_4_ = f32[576,128]{1,0:T(8,128)S(1)} collective-permute-done((f32[576,128]{1,0:T(8,128)S(1)}, f32[576,128]{1,0:T(8,128)S(1)}, u32[]{:S(2)}, u32[]{:S(2)}) %collective-permute-start.11) | collective-permute-done | bytes 294944 | tf_op jit(solution)/shard_map/ppermute | solution.py:349
  64.1 0.0 collective-permute-done.10.refs_3_
  64.1 0.0 copy-start
  64.1 0.0 copy-start.1
  64.1 0.4 stage_1_1.1
  64.5 0.6 collective-permute-start.12
  65.1 0.0 collective-permute-start.15
  65.1 4.3 %collective-permute-done.14.refs_3_ = s16[592,128]{1,0:T(8,128)(2,1)S(1)} collective-permute-done((s16[592,128]{1,0:T(8,128)(2,1)S(1)}, s16[592,128]{1,0:T(8,128)(2,1)S(1)}, u32[]{:S(2)}, u32[]{:S(2)}) %collective-permute-start.14) | collective-permute-done | bytes 151584 | tf_op jit(solution)/shard_map/ppermute | solution.py:349
  69.4 0.0 collective-permute-start.16
  69.4 2.5 %collective-permute-done.12.refs_3_ = s16[608,128]{1,0:T(8,128)(2,1)S(1)} collective-permute-done((s16[608,128]{1,0:T(8,128)(2,1)S(1)}, s16[608,128]{1,0:T(8,128)(2,1)S(1)}, u32[]{:S(2)}, u32[]{:S(2)}) %collective-permute-start.12) | collective-permute-done | bytes 155680 | tf_op jit(solution)/shard_map/ppermute | solution.py:349
  71.9 0.6 stage_1_2.1
  72.5 1.8 %collective-permute-start.13 = (s16[608,128]{1,0:T(8,128)(2,1)S(1)}, s16[608,128]{1,0:T(8,128)(2,1)S(1)}, u32[]{:S(2)}, u32[]{:S(2)}) collective-permute-start(s16[608,128]{1,0:T(8,128)(2,1)S(1)} %get-tuple-element.74.refs_6_), channel_id=1, source_target_pairs={{0,4},{1,5},{2,6},{3,7},{4,0},{5,1},{6,2},{7,3},{8,12},{9,13},{10,... | collective-permute-start | bytes 466952 | tf_op jit(solution)/shard_map/ppermute | solution.py:349
  74.3 0.0 collective-permute-done.15.refs_4_
  74.3 0.0 collective-permute-done.16.refs_5_
  74.3 0.9 unpack_0.1
  75.2 0.0 copy-done
  75.2 0.0 copy-done.1
  75.2 5.2 %sweeps_0.1 = (f32[2,256,768]{2,1,0:T(8,128)}, f32[8,128]{1,0:T(8,128)S(1)}) custom-call(f32[8,128]{1,0:T(8,128)S(1)} %get-tuple-element.75.refs_1_.refs_0_, bf16[2,256,768]{2,1,0:T(8,128)(2,1)S(1)} %copy-done, bf16[2,256,768]{2,1,0:T(8,128)(2,1)S(1)} %copy-done.1, bf16[768,768]{1,0:T(8,128)(2,1)S(1)} %get-tuple-element.76.refs_3_, ...), custom_call_target="tpu_custom_call" | custom-call | flops 3623878656 | bytes 2359296 | tf_op jit(solution)/shard_map/sweeps_0/pallas_call | solution.py:45
  80.4 1.6 %collective-permute-done.13.refs_3_ = s16[608,128]{1,0:T(8,128)(2,1)S(1)} collective-permute-done((s16[608,128]{1,0:T(8,128)(2,1)S(1)}, s16[608,128]{1,0:T(8,128)(2,1)S(1)}, u32[]{:S(2)}, u32[]{:S(2)}) %collective-permute-start.13) | collective-permute-done | bytes 155680 | tf_op jit(solution)/shard_map/ppermute | solution.py:349
  81.9 0.6 total_1.1
  82.5 0.3 collective-permute-start.17
  82.8 0.0 collective-permute-start.18
  82.8 5.3 %collective-permute-done.17.refs_3_ = s16[592,128]{1,0:T(8,128)(2,1)S(1)} collective-permute-done((s16[592,128]{1,0:T(8,128)(2,1)S(1)}, s16[592,128]{1,0:T(8,128)(2,1)S(1)}, u32[]{:S(2)}, u32[]{:S(2)}) %collective-permute-start.17) | collective-permute-done | bytes 151584 | tf_op jit(solution)/shard_map/ppermute | solution.py:349
  88.1 0.0 collective-permute-start.19
  88.1 0.0 collective-permute-done.18.refs_4_
  88.1 1.4 %collective-permute-done.19.refs_5_ = s16[592,128]{1,0:T(8,128)(2,1)S(1)} collective-permute-done((s16[592,128]{1,0:T(8,128)(2,1)S(1)}, s16[592,128]{1,0:T(8,128)(2,1)S(1)}, u32[]{:S(2)}, u32[]{:S(2)}) %collective-permute-start.19) | collective-permute-done | bytes 151584 | tf_op jit(solution)/shard_map/ppermute | solution.py:349
  89.4 0.7 unpack_1.1
  90.2 5.7 %sweeps_1.1 = (f32[2,256,768]{2,1,0:T(8,128)}, f32[8,128]{1,0:T(8,128)}) custom-call(f32[8,128]{1,0:T(8,128)S(1)} %get-tuple-element.79.refs_1_.refs_0_, bf16[2,256,768]{2,1,0:T(8,128)(2,1)S(1)} %copy-done, bf16[2,256,768]{2,1,0:T(8,128)(2,1)S(1)} %copy-done.1, bf16[768,768]{1,0:T(8,128)(2,1)S(1)} %get-tuple-element.81.refs_3_, ...), custom_call_target="tpu_custom_call", output_to_operand_aliasing={{0}: (5, {})} | custom-call | flops 3623878656 | bytes 2359296 | tf_op jit(solution)/shard_map/sweeps_1/pallas_call | solution.py:45
Async XLA Ops:
  0.0 0.7 copy-start.2
  6.3 14.8 %collective-permute-start.3 = (bf16[256,768]{1,0:T(8,128)(2,1)}, bf16[256,768]{1,0:T(8,128)(2,1)S(1)}, u32[]{:S(2)}, u32[]{:S(2)}) collective-permute-start(bf16[256,768]{1,0:T(8,128)(2,1)} %get-tuple-element.51), channel_id=1, source_target_pairs={{0,8},{8,0},{16,24},{24,16},{1,9},{9,1},{17,25},{25,17},{2,10},{10... | collective-permute-start | bytes 1179656 | tf_op jit(solution)/shard_map/ppermute | solution.py:346
  9.2 19.7 %collective-permute-start.4 = (bf16[256,768]{1,0:T(8,128)(2,1)}, bf16[256,768]{1,0:T(8,128)(2,1)S(1)}, u32[]{:S(2)}, u32[]{:S(2)}) collective-permute-start(bf16[256,768]{1,0:T(8,128)(2,1)} %get-tuple-element.52), channel_id=1, source_target_pairs={{0,16},{8,24},{16,0},{24,8},{1,17},{9,25},{17,1},{25,9},{2,18},{10... | collective-permute-start | bytes 1179656 | tf_op jit(solution)/shard_map/ppermute | solution.py:346
  10.7 19.0 %collective-permute-start.5 = (bf16[256,768]{1,0:T(8,128)(2,1)}, bf16[256,768]{1,0:T(8,128)(2,1)S(1)}, u32[]{:S(2)}, u32[]{:S(2)}) collective-permute-start(bf16[256,768]{1,0:T(8,128)(2,1)} %get-tuple-element.53), channel_id=1, source_target_pairs={{0,24},{8,16},{16,8},{24,0},{1,25},{9,17},{17,9},{25,1},{2,26},{10... | collective-permute-start | bytes 1179656 | tf_op jit(solution)/shard_map/ppermute | solution.py:346
  17.5 18.4 %collective-permute-start = (bf16[256,768]{1,0:T(8,128)(2,1)}, bf16[256,768]{1,0:T(8,128)(2,1)S(1)}, u32[]{:S(2)}, u32[]{:S(2)}) collective-permute-start(bf16[256,768]{1,0:T(8,128)(2,1)} %get-tuple-element.47), channel_id=1, source_target_pairs={{0,8},{8,0},{16,24},{24,16},{1,9},{9,1},{17,25},{25,17},{2,10},{10... | collective-permute-start | bytes 1179656 | tf_op jit(solution)/shard_map/ppermute | solution.py:346
  19.5 25.8 %collective-permute-start.1 = (bf16[256,768]{1,0:T(8,128)(2,1)S(1)}, bf16[256,768]{1,0:T(8,128)(2,1)S(1)}, u32[]{:S(2)}, u32[]{:S(2)}) collective-permute-start(bf16[256,768]{1,0:T(8,128)(2,1)S(1)} %get-tuple-element.48), channel_id=1, source_target_pairs={{0,16},{8,24},{16,0},{24,8},{1,17},{9,25},{17,1},{25,9},{2,18},{10... | collective-permute-start | bytes 1179656 | tf_op jit(solution)/shard_map/ppermute | solution.py:346
  30.4 15.7 %collective-permute-start.6 = (f32[584,128]{1,0:T(8,128)S(1)}, f32[584,128]{1,0:T(8,128)S(1)}, u32[]{:S(2)}, u32[]{:S(2)}) collective-permute-start(f32[584,128]{1,0:T(8,128)S(1)} %get-tuple-element.56), channel_id=1, source_target_pairs={{0,1},{1,0},{2,3},{3,2},{4,5},{5,4},{6,7},{7,6},{8,9},{9,8},{10,11... | collective-permute-start | bytes 897032 | tf_op jit(solution)/shard_map/ppermute | solution.py:349
  30.4 15.6 %collective-permute-start.7 = (f32[576,128]{1,0:T(8,128)S(1)}, f32[576,128]{1,0:T(8,128)S(1)}, u32[]{:S(2)}, u32[]{:S(2)}) collective-permute-start(f32[576,128]{1,0:T(8,128)S(1)} %get-tuple-element.57), channel_id=1, source_target_pairs={{0,1},{1,0},{2,3},{3,2},{4,5},{5,4},{6,7},{7,6},{8,9},{9,8},{10,11... | collective-permute-start | bytes 884744 | tf_op jit(solution)/shard_map/ppermute | solution.py:349
  30.9 30.5 %collective-permute-start.2 = (bf16[256,768]{1,0:T(8,128)(2,1)S(1)}, bf16[256,768]{1,0:T(8,128)(2,1)S(1)}, u32[]{:S(2)}, u32[]{:S(2)}) collective-permute-start(bf16[256,768]{1,0:T(8,128)(2,1)S(1)} %get-tuple-element.49), channel_id=1, source_target_pairs={{0,24},{8,16},{16,8},{24,0},{1,25},{9,17},{17,9},{25,1},{2,26},{10... | collective-permute-start | bytes 1179656 | tf_op jit(solution)/shard_map/ppermute | solution.py:346
  46.5 5.9 %collective-permute-start.8 = (s16[608,128]{1,0:T(8,128)(2,1)S(1)}, s16[608,128]{1,0:T(8,128)(2,1)S(1)}, u32[]{:S(2)}, u32[]{:S(2)}) collective-permute-start(s16[608,128]{1,0:T(8,128)(2,1)S(1)} %get-tuple-element.60), channel_id=1, source_target_pairs={{0,2},{1,3},{2,0},{3,1},{4,6},{5,7},{6,4},{7,5},{8,10},{9,11},{10,... | collective-permute-start | bytes 466952 | tf_op jit(solution)/shard_map/ppermute | solution.py:349
  53.0 7.9 %collective-permute-start.9 = (s16[608,128]{1,0:T(8,128)(2,1)S(1)}, s16[608,128]{1,0:T(8,128)(2,1)S(1)}, u32[]{:S(2)}, u32[]{:S(2)}) collective-permute-start(s16[608,128]{1,0:T(8,128)(2,1)S(1)} %get-tuple-element.63), channel_id=1, source_target_pairs={{0,4},{1,5},{2,6},{3,7},{4,0},{5,1},{6,2},{7,3},{8,12},{9,13},{10,... | collective-permute-start | bytes 466952 | tf_op jit(solution)/shard_map/ppermute | solution.py:349
  62.0 2.1 %collective-permute-start.10 = (f32[584,128]{1,0:T(8,128)S(1)}, f32[584,128]{1,0:T(8,128)S(1)}, u32[]{:S(2)}, u32[]{:S(2)}) collective-permute-start(f32[584,128]{1,0:T(8,128)S(1)} %get-tuple-element.67), channel_id=1, source_target_pairs={{0,1},{1,0},{2,3},{3,2},{4,5},{5,4},{6,7},{7,6},{8,9},{9,8},{10,11... | collective-permute-start | bytes 897032 | tf_op jit(solution)/shard_map/ppermute | solution.py:349
  62.1 2.0 %collective-permute-start.11 = (f32[576,128]{1,0:T(8,128)S(1)}, f32[576,128]{1,0:T(8,128)S(1)}, u32[]{:S(2)}, u32[]{:S(2)}) collective-permute-start(f32[576,128]{1,0:T(8,128)S(1)} %get-tuple-element.68), channel_id=1, source_target_pairs={{0,1},{1,0},{2,3},{3,2},{4,5},{5,4},{6,7},{7,6},{8,9},{9,8},{10,11... | collective-permute-start | bytes 884744 | tf_op jit(solution)/shard_map/ppermute | solution.py:349
  62.6 6.8 %collective-permute-start.14 = (s16[592,128]{1,0:T(8,128)(2,1)S(1)}, s16[592,128]{1,0:T(8,128)(2,1)S(1)}, u32[]{:S(2)}, u32[]{:S(2)}) collective-permute-start(s16[592,128]{1,0:T(8,128)(2,1)S(1)} %get-tuple-element.64.refs_3_.refs_2_), channel_id=1, source_target_pairs={{0,2},{1,3},{2,0},{3,1},{4,6},{5,7},{6,4},{7,5},{8,10},{9,11},{10,... | collective-permute-start | bytes 454664 | tf_op jit(solution)/shard_map/ppermute | solution.py:349
  64.1 11.1 %copy-start = (bf16[2,256,768]{2,1,0:T(8,128)(2,1)S(1)}, bf16[2,256,768]{2,1,0:T(8,128)(2,1)}, u32[]{:S(2)}) copy-start(bf16[2,256,768]{2,1,0:T(8,128)(2,1)} %refs_1_.3) | copy-start | bytes 2359300
  64.1 11.1 %copy-start.1 = (bf16[2,256,768]{2,1,0:T(8,128)(2,1)S(1)}, bf16[2,256,768]{2,1,0:T(8,128)(2,1)}, u32[]{:S(2)}) copy-start(bf16[2,256,768]{2,1,0:T(8,128)(2,1)} %refs_2_.7) | copy-start | bytes 2359300
  64.5 7.4 %collective-permute-start.12 = (s16[608,128]{1,0:T(8,128)(2,1)S(1)}, s16[608,128]{1,0:T(8,128)(2,1)S(1)}, u32[]{:S(2)}, u32[]{:S(2)}) collective-permute-start(s16[608,128]{1,0:T(8,128)(2,1)S(1)} %get-tuple-element.71), channel_id=1, source_target_pairs={{0,2},{1,3},{2,0},{3,1},{4,6},{5,7},{6,4},{7,5},{8,10},{9,11},{10,... | collective-permute-start | bytes 466952 | tf_op jit(solution)/shard_map/ppermute | solution.py:349
  65.1 9.2 %collective-permute-start.15 = (s16[592,128]{1,0:T(8,128)(2,1)S(1)}, s16[592,128]{1,0:T(8,128)(2,1)S(1)}, u32[]{:S(2)}, u32[]{:S(2)}) collective-permute-start(s16[592,128]{1,0:T(8,128)(2,1)S(1)} %get-tuple-element.64.refs_3_.refs_2_), channel_id=1, source_target_pairs={{0,1},{1,0},{2,3},{3,2},{4,5},{5,4},{6,7},{7,6},{8,9},{9,8},{10,11... | collective-permute-start | bytes 454664 | tf_op jit(solution)/shard_map/ppermute | solution.py:349
  69.4 4.9 %collective-permute-start.16 = (s16[592,128]{1,0:T(8,128)(2,1)S(1)}, s16[592,128]{1,0:T(8,128)(2,1)S(1)}, u32[]{:S(2)}, u32[]{:S(2)}) collective-permute-start(s16[592,128]{1,0:T(8,128)(2,1)S(1)} %collective-permute-done.14.refs_3_), channel_id=1, source_target_pairs={{0,1},{1,0},{2,3},{3,2},{4,5},{5,4},{6,7},{7,6},{8,9},{9,8},{10,11... | collective-permute-start | bytes 454664 | tf_op jit(solution)/shard_map/ppermute | solution.py:349
  72.5 9.5 %collective-permute-start.13 = (s16[608,128]{1,0:T(8,128)(2,1)S(1)}, s16[608,128]{1,0:T(8,128)(2,1)S(1)}, u32[]{:S(2)}, u32[]{:S(2)}) collective-permute-start(s16[608,128]{1,0:T(8,128)(2,1)S(1)} %get-tuple-element.74.refs_6_), channel_id=1, source_target_pairs={{0,4},{1,5},{2,6},{3,7},{4,0},{5,1},{6,2},{7,3},{8,12},{9,13},{10,... | collective-permute-start | bytes 466952 | tf_op jit(solution)/shard_map/ppermute | solution.py:349
  82.5 5.5 %collective-permute-start.17 = (s16[592,128]{1,0:T(8,128)(2,1)S(1)}, s16[592,128]{1,0:T(8,128)(2,1)S(1)}, u32[]{:S(2)}, u32[]{:S(2)}) collective-permute-start(s16[592,128]{1,0:T(8,128)(2,1)S(1)} %get-tuple-element.80.refs_2_), channel_id=1, source_target_pairs={{0,2},{1,3},{2,0},{3,1},{4,6},{5,7},{6,4},{7,5},{8,10},{9,11},{10,... | collective-permute-start | bytes 454664 | tf_op jit(solution)/shard_map/ppermute | solution.py:349
  82.8 5.3 %collective-permute-start.18 = (s16[592,128]{1,0:T(8,128)(2,1)S(1)}, s16[592,128]{1,0:T(8,128)(2,1)S(1)}, u32[]{:S(2)}, u32[]{:S(2)}) collective-permute-start(s16[592,128]{1,0:T(8,128)(2,1)S(1)} %get-tuple-element.80.refs_2_), channel_id=1, source_target_pairs={{0,1},{1,0},{2,3},{3,2},{4,5},{5,4},{6,7},{7,6},{8,9},{9,8},{10,11... | collective-permute-start | bytes 454664 | tf_op jit(solution)/shard_map/ppermute | solution.py:349
  88.1 1.4 %collective-permute-start.19 = (s16[592,128]{1,0:T(8,128)(2,1)S(1)}, s16[592,128]{1,0:T(8,128)(2,1)S(1)}, u32[]{:S(2)}, u32[]{:S(2)}) collective-permute-start(s16[592,128]{1,0:T(8,128)(2,1)S(1)} %collective-permute-done.17.refs_3_), channel_id=1, source_target_pairs={{0,1},{1,0},{2,3},{3,2},{4,5},{5,4},{6,7},{7,6},{8,9},{9,8},{10,11... | collective-permute-start | bytes 454664 | tf_op jit(solution)/shard_map/ppermute | solution.py:349

commit v6 on v4

--- a/solution.py
+++ b/solution.py
@@ -10,7 +10,8 @@
 STEPS = 4
 BLOCK = 128
 TILE = 16
-PARTS = 2
+PARTS = 4
+WIDTH = 2 * BLOCK
 LEVELS = 32760.0
 OCTAVE = 8.0
 relax_factor = 0.5
@@ -70,24 +71,34 @@
     return owners * capacity + rank.astype(I32)
 
 
-def place(key, rows_ref, experts, capacity, out_refs):
+def place(key, rows_ref, experts, capacity, out_refs, ready=lambda c: None):
     tokens, hidden = rows_ref.shape
     places = lax.broadcasted_iota(I32, (capacity, tokens), 0)
     chosen = jnp.concatenate(
         [(places == key - e * capacity).astype(F32).astype(BF16) for e in experts], axis=0
     )
-    width = 2 * BLOCK
-    for c in range(0, hidden, width):
-        got = jnp.dot(chosen, rows_ref[:, c:c + width], preferred_element_type=F32).astype(BF16)
+    for c in range(0, hidden, WIDTH):
+        ready(c // WIDTH)
+        got = jnp.dot(chosen, rows_ref[:, c:c + WIDTH], preferred_element_type=F32).astype(BF16)
         for k, out_ref in enumerate(out_refs):
-            out_ref[:, c:c + width] = got[k * capacity:(k + 1) * capacity]
-
-
-def first_kernel(peers, slots, all_experts, capacity, me_ref, owner_ref, rows_ref, key_ref, *out_refs):
+            out_ref[:, c:c + WIDTH] = got[k * capacity:(k + 1) * capacity]
+
+
+def first_kernel(peers, slots, all_experts, capacity, me_ref, owner_any, rows_any, key_ref, *refs):
+    out_refs, (owner_ref, rows_ref, owner_done, rows_done) = refs[:-4], refs[-4:]
+    owner_copy = pltpu.make_async_copy(owner_any, owner_ref, owner_done)
+    owner_copy.start()
+    copies = []
+    for c in range(rows_ref.shape[1] // WIDTH):
+        columns = pl.ds(c * WIDTH, WIDTH)
+        copies.append(pltpu.make_async_copy(rows_any.at[:, columns], rows_ref.at[:, columns], rows_done.at[c]))
+        copies[-1].start()
     me = me_ref[0]
+    owner_copy.wait()
     key = slots_of(owner_ref[...], all_experts, capacity)
     key_ref[...] = key
-    place(key, rows_ref, [lax.bitwise_xor(me, k) * slots for k in range(1, peers)], capacity, out_refs)
+    experts = [lax.bitwise_xor(me, k) * slots for k in range(1, peers)]
+    place(key, rows_ref, experts, capacity, out_refs, lambda c: copies[c].wait())
 
 
 def second_kernel(peers, slots, capacity, me_ref, key_ref, rows_ref, *out_refs):
@@ -352,7 +363,11 @@
     place_flops = 2 * capacity * tokens * hidden
     key, *outgoing = call(
         functools.partial(first_kernel, peers, slots, all_experts, capacity),
-        [shape(1, tokens, I32)] + [chunk] * (peers - 1), [SMEM, VMEM, VMEM],
+        [shape(1, tokens, I32)] + [chunk] * (peers - 1), [SMEM, ANY, ANY],
+        scratch=[
+            pltpu.VMEM((1, tokens), I32), pltpu.VMEM((tokens, hidden), BF16),
+            pltpu.SemaphoreType.DMA, pltpu.SemaphoreType.DMA((hidden // WIDTH,)),
+        ],
         flops=place_flops * (peers - 1), moved=expert_inputs.size * 4, name="place_first",
     )(me, owners, expert_inputs)
     arrived = [[over_experts(outgoing[k - 1], k) for k in range(1, peers)]]
@@ -370,7 +385,7 @@
     notes = -(-(8 + 3 * many) // TILE) * TILE
 
     def begin(a, after):
-        chunks = [own[a]] + arrived[a][:-1]
+        chunks = [own[a]] + arrived[a][:1]
         return call(
             functools.partial(early_gram_kernel, halvings), shape(length + many), [VMEM] * len(chunks),
             flops=2 * capacity * len(chunks) * hidden * hidden, moved=length * BLOCK * 4, name=f"begin_{a}", after=after,
@@ -387,19 +402,19 @@
             moved=rows * BLOCK * 12, name=name, after=after,
         )(where, keep, diagonal, *got)
 
-    def reduce(a, before, after):
+    def reduce(a, before, after, behind):
         size = length // 2
-        sizes = cuts(size, PARTS)
+        sizes = cuts(size, PARTS if a == slots - 1 else 2)
         keep, diagonal, *sent = call(
-            functools.partial(late_gram_kernel, halvings, 1),
+            functools.partial(late_gram_kernel, halvings, peers - 2),
             [shape(size), shape(many)] + [shape(n + (many if i == 0 else 0)) for i, n in enumerate(sizes)],
-            [SMEM] + [VMEM] * 2, scratch=[pltpu.VMEM((length + many, BLOCK), F32)],
-            flops=2 * capacity * hidden * hidden, moved=length * BLOCK * 4, name=f"gram_{a}", after=after,
-        )(where, before, arrived[a][-1])
+            [SMEM] + [VMEM] * (peers - 1), scratch=[pltpu.VMEM((length + many, BLOCK), F32)],
+            name=f"gram_{a}", after=after,
+        )(where, before, *arrived[a][1:])
         for bit in range(1, halvings + 1):
             cut = bit < halvings
             got = [over_rows(part, bit - 1) for part in sent]
-            coded, diagonal, keep = stage(f"stage_{a}_{bit}", bit, keep, diagonal, got, cut, True)
+            coded, diagonal, keep = stage(f"stage_{a}_{bit}", bit, keep, diagonal, got, cut, True, behind if bit == 1 else ())
             sent = [coded]
             if bit == 1:
                 halved = coded
@@ -409,11 +424,13 @@
         coded, diagonal, keep = sums
         return stage(f"total_{a}", halvings, keep, diagonal, [over_rows(coded, halvings)], False, False, after)
 
-    def gather(a, total, after):
-        coded, diagonal = total
+    def pieces_of(coded):
         held = [(0, coded)]
         for bit in range(halvings - 1, -1, -1):
             held += [(flip ^ (1 << bit), over_rows(piece, bit)) for flip, piece in held]
+        return held
+
+    def gather(a, held, diagonal, after):
         high, low = call(
             functools.partial(unpack_kernel, hidden, halvings, [flip for flip, _ in held]),
             [shape(hidden, hidden, BF16)] * 2, [SMEM] + [VMEM] * (1 + len(held)),
@@ -433,15 +450,16 @@
             flops=2 * 3 * STEPS * features * hidden * hidden, moved=hidden * hidden * 4, name=f"sweeps_{a}",
         )(*args)
 
-    result, total, halved = None, (), ()
+    result, held, halved = None, [], ()
     for a in range(slots):
         before = begin(a, halved)
-        halved, sums = reduce(a, before, total[:1])
+        halved, sums = reduce(a, before, [piece for _, piece in held[:1]], [piece for _, piece in held[1:2]])
         halved, token = [halved], ()
         if a > 0:
-            result, *token = sweeps(a - 1, *gather(a - 1, total, [sums[0]]), result)
-        total = end(a, sums, token)
-    return sweeps(slots - 1, *gather(slots - 1, total, ()), result)[0]
+            result, *token = sweeps(a - 1, *gather(a - 1, held, diagonal, [sums[0]]), result)
+        coded, diagonal = end(a, sums, token)
+        held = pieces_of(coded)
+    return sweeps(slots - 1, *gather(slots - 1, held, diagonal, ()), result)[0]
 
 
 def solution(mesh):

time: 84.6 us -> 84.4 us (level)
  Pallas kernels: 29.4 us -> 30.3 us
    ppermute x6, waiting for transfers between devices: 17.9 us -> 11.4 us  [over_experts(): return lax.ppermute(array, 'expert', [(i, i ^ flip) for i in range(peers)])]
    ppermute x14 -> x16, waiting for transfers between devices: 15.7 us -> 21.9 us  [over_rows(): lax.ppermute(array, 'rows', [(i, i ^ 1 << bit) for i in range(copies)])]
    pallas_call x16, Pallas kernels: 29.4 us -> 30.3 us  [call(): return lambda *args: inner(*args, *after)]
    ppermute x14 -> x16, starting transfers between devices: 12.2 us -> 11.4 us  [over_rows(): lax.ppermute(array, 'rows', [(i, i ^ 1 << bit) for i in range(copies)])]
  transfers between devices with their start and end apart: 20 -> 22, of which waited for: 10 -> 13; matrix products, arithmetic and copies ran while one was open for 0% -> 0% of each run, Pallas kernels for 20% -> 19%
where the time goes in v6:
time: 84.4 us; the launch traced here: 84.1 us
  waiting for transfers between devices  33.3 us (39%)
  Pallas kernels  30.3 us (36%)
  starting transfers between devices  19.5 us (23%)
    pallas_call x16, Pallas kernels, call(): return lambda *args: inner(*args, *after)  30.3 us
    ppermute x16, waiting for transfers between devices, over_rows(): lax.ppermute(array, 'rows', [(i, i ^ 1 << bit) for i in range(copies)])  21.9 us
    ppermute x16, starting transfers between devices, over_rows(): lax.ppermute(array, 'rows', [(i, i ^ 1 << bit) for i in range(copies)])  11.4 us
    ppermute x6, waiting for transfers between devices, over_experts(): return lax.ppermute(array, 'expert', [(i, i ^ flip) for i in range(peers)])  11.4 us
    ppermute x6, starting transfers between devices, over_experts(): return lax.ppermute(array, 'expert', [(i, i ^ flip) for i in range(peers)])  8.03 us
  transfers between devices with their start and end apart: 22, of which 13 were waited for; matrix products, arithmetic and copies ran while one was open for 0% of the time, Pallas kernels for 19%

profile of v6, /device:TPU:0, one launch (start us, length us, event | category | flops | bytes accessed | tf_op | source)
XLA Modules:
  0.0 84.1 jit_solution(4908360881153664563)
XLA Ops:
  0.0 0.0 copy-start.2
  0.0 0.7 copy-done.2
  0.7 5.8 %place_first.1 = (s32[1,2048]{1,0:T(1,128)S(1)}, bf16[256,768]{1,0:T(8,128)(2,1)S(1)}, bf16[256,768]{1,0:T(8,128)(2,1)S(1)}, bf16[256,768]{1,0:T(8,128)(2,1)S(1)}) custom-call(s32[1]{0:T(128)} %bitcast.1.refs_0_, s32[1,2048]{1,0:T(1,128)S(1)} %bitcast.3, bf16[2048,768]{1,0:T(8,128)(2,1)} %refs_2_.5), custom_call_target="tpu_custom_call" | custom-call | flops 2415919104 | bytes 6291456 | tf_op jit(solution)/shard_map/place_first/pallas_call | solution.py:46
  6.5 3.0 %collective-permute-start.1 = (bf16[256,768]{1,0:T(8,128)(2,1)S(1)}, bf16[256,768]{1,0:T(8,128)(2,1)S(1)}, u32[]{:S(2)}, u32[]{:S(2)}) collective-permute-start(bf16[256,768]{1,0:T(8,128)(2,1)S(1)} %get-tuple-element.51), channel_id=1, source_target_pairs={{0,8},{8,0},{16,24},{24,16},{1,9},{9,1},{17,25},{25,17},{2,10},{10... | collective-permute-start | bytes 1179656 | tf_op jit(solution)/shard_map/ppermute | solution.py:357
  9.5 1.5 %collective-permute-start.2 = (bf16[256,768]{1,0:T(8,128)(2,1)S(1)}, bf16[256,768]{1,0:T(8,128)(2,1)S(1)}, u32[]{:S(2)}, u32[]{:S(2)}) collective-permute-start(bf16[256,768]{1,0:T(8,128)(2,1)S(1)} %get-tuple-element.52), channel_id=1, source_target_pairs={{0,16},{8,24},{16,0},{24,8},{1,17},{9,25},{17,1},{25,9},{2,18},{10... | collective-permute-start | bytes 1179656 | tf_op jit(solution)/shard_map/ppermute | solution.py:357
  11.0 0.0 collective-permute-start.3
  11.0 6.2 %place_rest.1 = (bf16[256,768]{1,0:T(8,128)(2,1)S(1)}, bf16[256,768]{1,0:T(8,128)(2,1)S(1)}, bf16[256,768]{1,0:T(8,128)(2,1)S(1)}, bf16[256,768]{1,0:T(8,128)(2,1)S(1)}, bf16[256,768]{1,0:T(8,128)(2,1)S(1)}) custom-call(s32[1]{0:T(128)} %bitcast.1.refs_0_, s32[1,2048]{1,0:T(1,128)S(1)} %get-tuple-element.47.refs_1_, bf16[2048,768]{1,0:T(8,128)(2,1)} %refs_2_.5), custom_call_target="tpu_custom_call" | custom-call | flops 4026531840 | bytes 6291456 | tf_op jit(solution)/shard_map/place_rest/pallas_call | solution.py:46
  17.2 2.2 %collective-permute-done.1.refs_1_ = bf16[256,768]{1,0:T(8,128)(2,1)S(1)} collective-permute-done((bf16[256,768]{1,0:T(8,128)(2,1)S(1)}, bf16[256,768]{1,0:T(8,128)(2,1)S(1)}, u32[]{:S(2)}, u32[]{:S(2)}) %collective-permute-start.1) | collective-permute-done | bytes 393248 | tf_op jit(solution)/shard_map/ppermute | solution.py:357
  19.5 0.6 begin_0.1.refs_1_
  20.1 8.4 %collective-permute-done.2.refs_2_ = bf16[256,768]{1,0:T(8,128)(2,1)S(1)} collective-permute-done((bf16[256,768]{1,0:T(8,128)(2,1)S(1)}, bf16[256,768]{1,0:T(8,128)(2,1)S(1)}, u32[]{:S(2)}, u32[]{:S(2)}) %collective-permute-start.2) | collective-permute-done | bytes 393248 | tf_op jit(solution)/shard_map/ppermute | solution.py:357
  28.5 0.0 collective-permute-done.3.refs_3_
  28.5 0.8 gram_0.1
  29.3 0.1 collective-permute-start.4
  29.4 0.5 collective-permute-start.5
  29.9 1.2 %collective-permute-start = (bf16[256,768]{1,0:T(8,128)(2,1)S(1)}, bf16[256,768]{1,0:T(8,128)(2,1)S(1)}, u32[]{:S(2)}, u32[]{:S(2)}) collective-permute-start(bf16[256,768]{1,0:T(8,128)(2,1)S(1)} %get-tuple-element.49), channel_id=1, source_target_pairs={{0,8},{8,0},{16,24},{24,16},{1,9},{9,1},{17,25},{25,17},{2,10},{10... | collective-permute-start | bytes 1179656 | tf_op jit(solution)/shard_map/ppermute | solution.py:357
  31.1 0.8 collective-permute-start.6
  31.9 1.4 %collective-permute-start.7 = (bf16[256,768]{1,0:T(8,128)(2,1)S(1)}, bf16[256,768]{1,0:T(8,128)(2,1)S(1)}, u32[]{:S(2)}, u32[]{:S(2)}) collective-permute-start(bf16[256,768]{1,0:T(8,128)(2,1)S(1)} %get-tuple-element.60), channel_id=1, source_target_pairs={{0,24},{8,16},{16,8},{24,0},{1,25},{9,17},{17,9},{25,1},{2,26},{10... | collective-permute-start | bytes 1179656 | tf_op jit(solution)/shard_map/ppermute | solution.py:357
  33.4 0.0 collective-permute-done.5.refs_4_
  33.4 0.0 collective-permute-done.4.refs_3_
  33.4 0.4 stage_0_1.1
  33.8 1.6 %collective-permute-start.8 = (s16[608,128]{1,0:T(8,128)(2,1)S(1)}, s16[608,128]{1,0:T(8,128)(2,1)S(1)}, u32[]{:S(2)}, u32[]{:S(2)}) collective-permute-start(s16[608,128]{1,0:T(8,128)(2,1)S(1)} %get-tuple-element.58.refs_2_), channel_id=1, source_target_pairs={{0,2},{1,3},{2,0},{3,1},{4,6},{5,7},{6,4},{7,5},{8,10},{9,11},{10,... | collective-permute-start | bytes 466952 | tf_op jit(solution)/shard_map/ppermute | solution.py:360
  35.4 3.7 %collective-permute-done.8.refs_3_ = s16[608,128]{1,0:T(8,128)(2,1)S(1)} collective-permute-done((s16[608,128]{1,0:T(8,128)(2,1)S(1)}, s16[608,128]{1,0:T(8,128)(2,1)S(1)}, u32[]{:S(2)}, u32[]{:S(2)}) %collective-permute-start.8) | collective-permute-done | bytes 155680 | tf_op jit(solution)/shard_map/ppermute | solution.py:360
  39.1 0.6 stage_0_2.1
  39.7 2.7 %collective-permute-start.9 = (s16[608,128]{1,0:T(8,128)(2,1)S(1)}, s16[608,128]{1,0:T(8,128)(2,1)S(1)}, u32[]{:S(2)}, u32[]{:S(2)}) collective-permute-start(s16[608,128]{1,0:T(8,128)(2,1)S(1)} %get-tuple-element.65), channel_id=1, source_target_pairs={{0,4},{1,5},{2,6},{3,7},{4,0},{5,1},{6,2},{7,3},{8,12},{9,13},{10,... | collective-permute-start | bytes 466952 | tf_op jit(solution)/shard_map/ppermute | solution.py:360
  42.3 0.0 collective-permute-done.refs_1_
  42.3 0.6 begin_1.1.refs_1_
  43.0 5.3 %collective-permute-done.9.refs_3_ = s16[608,128]{1,0:T(8,128)(2,1)S(1)} collective-permute-done((s16[608,128]{1,0:T(8,128)(2,1)S(1)}, s16[608,128]{1,0:T(8,128)(2,1)S(1)}, u32[]{:S(2)}, u32[]{:S(2)}) %collective-permute-start.9) | collective-permute-done | bytes 155680 | tf_op jit(solution)/shard_map/ppermute | solution.py:360
  48.3 0.6 total_0.1
  48.9 0.7 collective-permute-start.14
  49.6 0.0 collective-permute-done.6.refs_2_
  49.6 0.7 collective-permute-done.7.refs_3_
  50.4 0.8 gram_1.1
  51.2 0.1 collective-permute-start.10
  51.2 0.5 collective-permute-start.11
  51.7 0.1 collective-permute-start.12
  51.8 0.4 collective-permute-start.13
  52.3 0.6 collective-permute-done.11.refs_4_
  52.8 0.3 collective-permute-done.12.refs_5_
  53.1 0.2 collective-permute-done.13.refs_6_
  53.3 0.8 collective-permute-done.14.refs_7_.refs_3_
  54.1 0.0 collective-permute-done.10.refs_3_
  54.1 0.6 stage_1_1.1
  54.7 0.9 %collective-permute-start.15 = (s16[608,128]{1,0:T(8,128)(2,1)S(1)}, s16[608,128]{1,0:T(8,128)(2,1)S(1)}, u32[]{:S(2)}, u32[]{:S(2)}) collective-permute-start(s16[608,128]{1,0:T(8,128)(2,1)S(1)} %get-tuple-element.75), channel_id=1, source_target_pairs={{0,2},{1,3},{2,0},{3,1},{4,6},{5,7},{6,4},{7,5},{8,10},{9,11},{10,... | collective-permute-start | bytes 466952 | tf_op jit(solution)/shard_map/ppermute | solution.py:360
  55.6 0.0 collective-permute-start.17
  55.6 0.5 collective-permute-start.18
  56.1 4.2 %collective-permute-done.15.refs_3_ = s16[608,128]{1,0:T(8,128)(2,1)S(1)} collective-permute-done((s16[608,128]{1,0:T(8,128)(2,1)S(1)}, s16[608,128]{1,0:T(8,128)(2,1)S(1)}, u32[]{:S(2)}, u32[]{:S(2)}) %collective-permute-start.15) | collective-permute-done | bytes 155680 | tf_op jit(solution)/shard_map/ppermute | solution.py:360
  60.2 0.6 stage_1_2.1
  60.9 2.7 %collective-permute-start.16 = (s16[608,128]{1,0:T(8,128)(2,1)S(1)}, s16[608,128]{1,0:T(8,128)(2,1)S(1)}, u32[]{:S(2)}, u32[]{:S(2)}) collective-permute-start(s16[608,128]{1,0:T(8,128)(2,1)S(1)} %get-tuple-element.78.refs_6_), channel_id=1, source_target_pairs={{0,4},{1,5},{2,6},{3,7},{4,0},{5,1},{6,2},{7,3},{8,12},{9,13},{10,... | collective-permute-start | bytes 466952 | tf_op jit(solution)/shard_map/ppermute | solution.py:360
  63.6 0.0 collective-permute-done.17.refs_4_
  63.6 0.0 collective-permute-done.18.refs_5_
  63.6 0.7 unpack_0.1
  64.3 0.0 copy-done
  64.3 0.0 copy-done.1
  64.3 5.1 %sweeps_0.1 = (f32[2,256,768]{2,1,0:T(8,128)}, f32[8,128]{1,0:T(8,128)S(1)}) custom-call(f32[8,128]{1,0:T(8,128)S(1)} %get-tuple-element.79.refs_1_.refs_0_, bf16[2,256,768]{2,1,0:T(8,128)(2,1)S(1)} %copy-done, bf16[2,256,768]{2,1,0:T(8,128)(2,1)S(1)} %copy-done.1, bf16[768,768]{1,0:T(8,128)(2,1)S(1)} %get-tuple-element.80.refs_3_, ...), custom_call_target="tpu_custom_call" | custom-call | flops 3623878656 | bytes 2359296 | tf_op jit(solution)/shard_map/sweeps_0/pallas_call | solution.py:46
  69.5 0.9 %collective-permute-done.16.refs_3_ = s16[608,128]{1,0:T(8,128)(2,1)S(1)} collective-permute-done((s16[608,128]{1,0:T(8,128)(2,1)S(1)}, s16[608,128]{1,0:T(8,128)(2,1)S(1)}, u32[]{:S(2)}, u32[]{:S(2)}) %collective-permute-start.16) | collective-permute-done | bytes 155680 | tf_op jit(solution)/shard_map/ppermute | solution.py:360
  70.4 0.6 total_1.1
  70.9 0.7 collective-permute-start.19
  71.6 0.0 collective-permute-start.20
  71.6 4.6 %collective-permute-done.19.refs_3_ = s16[592,128]{1,0:T(8,128)(2,1)S(1)} collective-permute-done((s16[592,128]{1,0:T(8,128)(2,1)S(1)}, s16[592,128]{1,0:T(8,128)(2,1)S(1)}, u32[]{:S(2)}, u32[]{:S(2)}) %collective-permute-start.19) | collective-permute-done | bytes 151584 | tf_op jit(solution)/shard_map/ppermute | solution.py:360
  76.2 0.0 collective-permute-start.21
  76.2 0.0 collective-permute-done.20.refs_4_
  76.2 1.4 %collective-permute-done.21.refs_5_ = s16[592,128]{1,0:T(8,128)(2,1)S(1)} collective-permute-done((s16[592,128]{1,0:T(8,128)(2,1)S(1)}, s16[592,128]{1,0:T(8,128)(2,1)S(1)}, u32[]{:S(2)}, u32[]{:S(2)}) %collective-permute-start.21) | collective-permute-done | bytes 151584 | tf_op jit(solution)/shard_map/ppermute | solution.py:360
  77.6 0.7 unpack_1.1
  78.3 5.7 %sweeps_1.1 = (f32[2,256,768]{2,1,0:T(8,128)}, f32[8,128]{1,0:T(8,128)}) custom-call(f32[8,128]{1,0:T(8,128)S(1)} %get-tuple-element.83.refs_1_.refs_0_, bf16[2,256,768]{2,1,0:T(8,128)(2,1)S(1)} %copy-done, bf16[2,256,768]{2,1,0:T(8,128)(2,1)S(1)} %copy-done.1, bf16[768,768]{1,0:T(8,128)(2,1)S(1)} %get-tuple-element.85.refs_3_, ...), custom_call_target="tpu_custom_call", output_to_operand_aliasing={{0}: (5, {})} | custom-call | flops 3623878656 | bytes 2359296 | tf_op jit(solution)/shard_map/sweeps_1/pallas_call | solution.py:46
  (2 shorter events, 0.0 us)
Async XLA Ops:
  0.0 0.7 copy-start.2
  6.5 13.0 %collective-permute-start.1 = (bf16[256,768]{1,0:T(8,128)(2,1)S(1)}, bf16[256,768]{1,0:T(8,128)(2,1)S(1)}, u32[]{:S(2)}, u32[]{:S(2)}) collective-permute-start(bf16[256,768]{1,0:T(8,128)(2,1)S(1)} %get-tuple-element.51), channel_id=1, source_target_pairs={{0,8},{8,0},{16,24},{24,16},{1,9},{9,1},{17,25},{25,17},{2,10},{10... | collective-permute-start | bytes 1179656 | tf_op jit(solution)/shard_map/ppermute | solution.py:357
  9.5 19.0 %collective-permute-start.2 = (bf16[256,768]{1,0:T(8,128)(2,1)S(1)}, bf16[256,768]{1,0:T(8,128)(2,1)S(1)}, u32[]{:S(2)}, u32[]{:S(2)}) collective-permute-start(bf16[256,768]{1,0:T(8,128)(2,1)S(1)} %get-tuple-element.52), channel_id=1, source_target_pairs={{0,16},{8,24},{16,0},{24,8},{1,17},{9,25},{17,1},{25,9},{2,18},{10... | collective-permute-start | bytes 1179656 | tf_op jit(solution)/shard_map/ppermute | solution.py:357
  11.0 17.5 %collective-permute-start.3 = (bf16[256,768]{1,0:T(8,128)(2,1)S(1)}, bf16[256,768]{1,0:T(8,128)(2,1)S(1)}, u32[]{:S(2)}, u32[]{:S(2)}) collective-permute-start(bf16[256,768]{1,0:T(8,128)(2,1)S(1)} %get-tuple-element.53), channel_id=1, source_target_pairs={{0,24},{8,16},{16,8},{24,0},{1,25},{9,17},{17,9},{25,1},{2,26},{10... | collective-permute-start | bytes 1179656 | tf_op jit(solution)/shard_map/ppermute | solution.py:357
  29.3 4.1 %collective-permute-start.4 = (f32[584,128]{1,0:T(8,128)S(1)}, f32[584,128]{1,0:T(8,128)S(1)}, u32[]{:S(2)}, u32[]{:S(2)}) collective-permute-start(f32[584,128]{1,0:T(8,128)S(1)} %get-tuple-element.56), channel_id=1, source_target_pairs={{0,1},{1,0},{2,3},{3,2},{4,5},{5,4},{6,7},{7,6},{8,9},{9,8},{10,11... | collective-permute-start | bytes 897032 | tf_op jit(solution)/shard_map/ppermute | solution.py:360
  29.4 4.0 %collective-permute-start.5 = (f32[576,128]{1,0:T(8,128)S(1)}, f32[576,128]{1,0:T(8,128)S(1)}, u32[]{:S(2)}, u32[]{:S(2)}) collective-permute-start(f32[576,128]{1,0:T(8,128)S(1)} %get-tuple-element.57), channel_id=1, source_target_pairs={{0,1},{1,0},{2,3},{3,2},{4,5},{5,4},{6,7},{7,6},{8,9},{9,8},{10,11... | collective-permute-start | bytes 884744 | tf_op jit(solution)/shard_map/ppermute | solution.py:360
  29.9 12.5 %collective-permute-start = (bf16[256,768]{1,0:T(8,128)(2,1)S(1)}, bf16[256,768]{1,0:T(8,128)(2,1)S(1)}, u32[]{:S(2)}, u32[]{:S(2)}) collective-permute-start(bf16[256,768]{1,0:T(8,128)(2,1)S(1)} %get-tuple-element.49), channel_id=1, source_target_pairs={{0,8},{8,0},{16,24},{24,16},{1,9},{9,1},{17,25},{25,17},{2,10},{10... | collective-permute-start | bytes 1179656 | tf_op jit(solution)/shard_map/ppermute | solution.py:357
  31.1 18.5 %collective-permute-start.6 = (bf16[256,768]{1,0:T(8,128)(2,1)S(1)}, bf16[256,768]{1,0:T(8,128)(2,1)S(1)}, u32[]{:S(2)}, u32[]{:S(2)}) collective-permute-start(bf16[256,768]{1,0:T(8,128)(2,1)S(1)} %get-tuple-element.59), channel_id=1, source_target_pairs={{0,16},{8,24},{16,0},{24,8},{1,17},{9,25},{17,1},{25,9},{2,18},{10... | collective-permute-start | bytes 1179656 | tf_op jit(solution)/shard_map/ppermute | solution.py:357
  31.9 18.4 %collective-permute-start.7 = (bf16[256,768]{1,0:T(8,128)(2,1)S(1)}, bf16[256,768]{1,0:T(8,128)(2,1)S(1)}, u32[]{:S(2)}, u32[]{:S(2)}) collective-permute-start(bf16[256,768]{1,0:T(8,128)(2,1)S(1)} %get-tuple-element.60), channel_id=1, source_target_pairs={{0,24},{8,16},{16,8},{24,0},{1,25},{9,17},{17,9},{25,1},{2,26},{10... | collective-permute-start | bytes 1179656 | tf_op jit(solution)/shard_map/ppermute | solution.py:357
  33.8 5.3 %collective-permute-start.8 = (s16[608,128]{1,0:T(8,128)(2,1)S(1)}, s16[608,128]{1,0:T(8,128)(2,1)S(1)}, u32[]{:S(2)}, u32[]{:S(2)}) collective-permute-start(s16[608,128]{1,0:T(8,128)(2,1)S(1)} %get-tuple-element.58.refs_2_), channel_id=1, source_target_pairs={{0,2},{1,3},{2,0},{3,1},{4,6},{5,7},{6,4},{7,5},{8,10},{9,11},{10,... | collective-permute-start | bytes 466952 | tf_op jit(solution)/shard_map/ppermute | solution.py:360
  39.7 8.6 %collective-permute-start.9 = (s16[608,128]{1,0:T(8,128)(2,1)S(1)}, s16[608,128]{1,0:T(8,128)(2,1)S(1)}, u32[]{:S(2)}, u32[]{:S(2)}) collective-permute-start(s16[608,128]{1,0:T(8,128)(2,1)S(1)} %get-tuple-element.65), channel_id=1, source_target_pairs={{0,4},{1,5},{2,6},{3,7},{4,0},{5,1},{6,2},{7,3},{8,12},{9,13},{10,... | collective-permute-start | bytes 466952 | tf_op jit(solution)/shard_map/ppermute | solution.py:360
  48.9 5.3 %collective-permute-start.14 = (s16[592,128]{1,0:T(8,128)(2,1)S(1)}, s16[592,128]{1,0:T(8,128)(2,1)S(1)}, u32[]{:S(2)}, u32[]{:S(2)}) collective-permute-start(s16[592,128]{1,0:T(8,128)(2,1)S(1)} %get-tuple-element.66.refs_4_.refs_2_), channel_id=1, source_target_pairs={{0,2},{1,3},{2,0},{3,1},{4,6},{5,7},{6,4},{7,5},{8,10},{9,11},{10,... | collective-permute-start | bytes 454664 | tf_op jit(solution)/shard_map/ppermute | solution.py:360
  51.2 3.0 %collective-permute-start.10 = (f32[296,128]{1,0:T(8,128)S(1)}, f32[296,128]{1,0:T(8,128)S(1)}, u32[]{:S(2)}, u32[]{:S(2)}) collective-permute-start(f32[296,128]{1,0:T(8,128)S(1)} %get-tuple-element.69), channel_id=1, source_target_pairs={{0,1},{1,0},{2,3},{3,2},{4,5},{5,4},{6,7},{7,6},{8,9},{9,8},{10,11... | collective-permute-start | bytes 454664 | tf_op jit(solution)/shard_map/ppermute | solution.py:360
  51.2 1.6 %collective-permute-start.11 = (f32[288,128]{1,0:T(8,128)S(1)}, f32[288,128]{1,0:T(8,128)S(1)}, u32[]{:S(2)}, u32[]{:S(2)}) collective-permute-start(f32[288,128]{1,0:T(8,128)S(1)} %get-tuple-element.70), channel_id=1, source_target_pairs={{0,1},{1,0},{2,3},{3,2},{4,5},{5,4},{6,7},{7,6},{8,9},{9,8},{10,11... | collective-permute-start | bytes 442376 | tf_op jit(solution)/shard_map/ppermute | solution.py:360
  51.7 1.4 %collective-permute-start.12 = (f32[288,128]{1,0:T(8,128)S(1)}, f32[288,128]{1,0:T(8,128)S(1)}, u32[]{:S(2)}, u32[]{:S(2)}) collective-permute-start(f32[288,128]{1,0:T(8,128)S(1)} %get-tuple-element.71), channel_id=1, source_target_pairs={{0,1},{1,0},{2,3},{3,2},{4,5},{5,4},{6,7},{7,6},{8,9},{9,8},{10,11... | collective-permute-start | bytes 442376 | tf_op jit(solution)/shard_map/ppermute | solution.py:360
  51.8 1.5 %collective-permute-start.13 = (f32[288,128]{1,0:T(8,128)S(1)}, f32[288,128]{1,0:T(8,128)S(1)}, u32[]{:S(2)}, u32[]{:S(2)}) collective-permute-start(f32[288,128]{1,0:T(8,128)S(1)} %get-tuple-element.72), channel_id=1, source_target_pairs={{0,1},{1,0},{2,3},{3,2},{4,5},{5,4},{6,7},{7,6},{8,9},{9,8},{10,11... | collective-permute-start | bytes 442376 | tf_op jit(solution)/shard_map/ppermute | solution.py:360
  54.1 10.2 %copy-start = (bf16[2,256,768]{2,1,0:T(8,128)(2,1)S(1)}, bf16[2,256,768]{2,1,0:T(8,128)(2,1)}, u32[]{:S(2)}) copy-start(bf16[2,256,768]{2,1,0:T(8,128)(2,1)} %refs_1_.3) | copy-start | bytes 2359300
  54.1 10.2 %copy-start.1 = (bf16[2,256,768]{2,1,0:T(8,128)(2,1)S(1)}, bf16[2,256,768]{2,1,0:T(8,128)(2,1)}, u32[]{:S(2)}) copy-start(bf16[2,256,768]{2,1,0:T(8,128)(2,1)} %refs_2_.7) | copy-start | bytes 2359300
  54.7 5.5 %collective-permute-start.15 = (s16[608,128]{1,0:T(8,128)(2,1)S(1)}, s16[608,128]{1,0:T(8,128)(2,1)S(1)}, u32[]{:S(2)}, u32[]{:S(2)}) collective-permute-start(s16[608,128]{1,0:T(8,128)(2,1)S(1)} %get-tuple-element.75), channel_id=1, source_target_pairs={{0,2},{1,3},{2,0},{3,1},{4,6},{5,7},{6,4},{7,5},{8,10},{9,11},{10,... | collective-permute-start | bytes 466952 | tf_op jit(solution)/shard_map/ppermute | solution.py:360
  55.6 8.0 %collective-permute-start.17 = (s16[592,128]{1,0:T(8,128)(2,1)S(1)}, s16[592,128]{1,0:T(8,128)(2,1)S(1)}, u32[]{:S(2)}, u32[]{:S(2)}) collective-permute-start(s16[592,128]{1,0:T(8,128)(2,1)S(1)} %get-tuple-element.66.refs_4_.refs_2_), channel_id=1, source_target_pairs={{0,1},{1,0},{2,3},{3,2},{4,5},{5,4},{6,7},{7,6},{8,9},{9,8},{10,11... | collective-permute-start | bytes 454664 | tf_op jit(solution)/shard_map/ppermute | solution.py:360
  55.6 8.0 %collective-permute-start.18 = (s16[592,128]{1,0:T(8,128)(2,1)S(1)}, s16[592,128]{1,0:T(8,128)(2,1)S(1)}, u32[]{:S(2)}, u32[]{:S(2)}) collective-permute-start(s16[592,128]{1,0:T(8,128)(2,1)S(1)} %collective-permute-done.14.refs_7_.refs_3_), channel_id=1, source_target_pairs={{0,1},{1,0},{2,3},{3,2},{4,5},{5,4},{6,7},{7,6},{8,9},{9,8},{10,11... | collective-permute-start | bytes 454664 | tf_op jit(solution)/shard_map/ppermute | solution.py:360
  60.9 9.5 %collective-permute-start.16 = (s16[608,128]{1,0:T(8,128)(2,1)S(1)}, s16[608,128]{1,0:T(8,128)(2,1)S(1)}, u32[]{:S(2)}, u32[]{:S(2)}) collective-permute-start(s16[608,128]{1,0:T(8,128)(2,1)S(1)} %get-tuple-element.78.refs_6_), channel_id=1, source_target_pairs={{0,4},{1,5},{2,6},{3,7},{4,0},{5,1},{6,2},{7,3},{8,12},{9,13},{10,... | collective-permute-start | bytes 466952 | tf_op jit(solution)/shard_map/ppermute | solution.py:360
  70.9 5.3 %collective-permute-start.19 = (s16[592,128]{1,0:T(8,128)(2,1)S(1)}, s16[592,128]{1,0:T(8,128)(2,1)S(1)}, u32[]{:S(2)}, u32[]{:S(2)}) collective-permute-start(s16[592,128]{1,0:T(8,128)(2,1)S(1)} %get-tuple-element.84.refs_2_), channel_id=1, source_target_pairs={{0,2},{1,3},{2,0},{3,1},{4,6},{5,7},{6,4},{7,5},{8,10},{9,11},{10,... | collective-permute-start | bytes 454664 | tf_op jit(solution)/shard_map/ppermute | solution.py:360
  71.6 4.6 %collective-permute-start.20 = (s16[592,128]{1,0:T(8,128)(2,1)S(1)}, s16[592,128]{1,0:T(8,128)(2,1)S(1)}, u32[]{:S(2)}, u32[]{:S(2)}) collective-permute-start(s16[592,128]{1,0:T(8,128)(2,1)S(1)} %get-tuple-element.84.refs_2_), channel_id=1, source_target_pairs={{0,1},{1,0},{2,3},{3,2},{4,5},{5,4},{6,7},{7,6},{8,9},{9,8},{10,11... | collective-permute-start | bytes 454664 | tf_op jit(solution)/shard_map/ppermute | solution.py:360
  76.2 1.4 %collective-permute-start.21 = (s16[592,128]{1,0:T(8,128)(2,1)S(1)}, s16[592,128]{1,0:T(8,128)(2,1)S(1)}, u32[]{:S(2)}, u32[]{:S(2)}) collective-permute-start(s16[592,128]{1,0:T(8,128)(2,1)S(1)} %collective-permute-done.19.refs_3_), channel_id=1, source_target_pairs={{0,1},{1,0},{2,3},{3,2},{4,5},{5,4},{6,7},{7,6},{8,9},{9,8},{10,11... | collective-permute-start | bytes 454664 | tf_op jit(solution)/shard_map/ppermute | solution.py:360

commit v7 on v6

--- a/solution.py
+++ b/solution.py
@@ -21,6 +21,7 @@
 
 VMEM = pl.BlockSpec(memory_space=pltpu.VMEM)
 ANY = pl.BlockSpec(memory_space=pl.ANY)
+HBM = pl.BlockSpec(memory_space=pltpu.HBM)
 SMEM = pl.BlockSpec(memory_space=pltpu.SMEM)
 F32, BF16, I32, I16 = jnp.float32, jnp.bfloat16, jnp.int32, jnp.int16
 
@@ -71,39 +72,39 @@
     return owners * capacity + rank.astype(I32)
 
 
-def place(key, rows_ref, experts, capacity, out_refs, ready=lambda c: None):
+def place(key, rows_ref, experts, capacity, out_refs):
     tokens, hidden = rows_ref.shape
     places = lax.broadcasted_iota(I32, (capacity, tokens), 0)
     chosen = jnp.concatenate(
         [(places == key - e * capacity).astype(F32).astype(BF16) for e in experts], axis=0
     )
     for c in range(0, hidden, WIDTH):
-        ready(c // WIDTH)
         got = jnp.dot(chosen, rows_ref[:, c:c + WIDTH], preferred_element_type=F32).astype(BF16)
         for k, out_ref in enumerate(out_refs):
             out_ref[:, c:c + WIDTH] = got[k * capacity:(k + 1) * capacity]
+
+
+def others(peers):
+    return range(peers - 1, 0, -1)
 
 
 def first_kernel(peers, slots, all_experts, capacity, me_ref, owner_any, rows_any, key_ref, *refs):
     out_refs, (owner_ref, rows_ref, owner_done, rows_done) = refs[:-4], refs[-4:]
     owner_copy = pltpu.make_async_copy(owner_any, owner_ref, owner_done)
     owner_copy.start()
-    copies = []
-    for c in range(rows_ref.shape[1] // WIDTH):
-        columns = pl.ds(c * WIDTH, WIDTH)
-        copies.append(pltpu.make_async_copy(rows_any.at[:, columns], rows_ref.at[:, columns], rows_done.at[c]))
-        copies[-1].start()
+    rows_copy = pltpu.make_async_copy(rows_any, rows_ref, rows_done)
+    rows_copy.start()
     me = me_ref[0]
     owner_copy.wait()
     key = slots_of(owner_ref[...], all_experts, capacity)
     key_ref[...] = key
-    experts = [lax.bitwise_xor(me, k) * slots for k in range(1, peers)]
-    place(key, rows_ref, experts, capacity, out_refs, lambda c: copies[c].wait())
+    rows_copy.wait()
+    place(key, rows_ref, [lax.bitwise_xor(me, k) * slots for k in others(peers)], capacity, out_refs)
 
 
 def second_kernel(peers, slots, capacity, me_ref, key_ref, rows_ref, *out_refs):
     me = me_ref[0]
-    where = [(0, a) for a in range(slots)] + [(k, a) for a in range(1, slots) for k in range(1, peers)]
+    where = [(0, a) for a in range(slots)] + [(k, a) for a in range(1, slots) for k in others(peers)]
     place(key_ref[...], rows_ref, [lax.bitwise_xor(me, k) * slots + a for k, a in where], capacity, out_refs)
 
 
@@ -312,29 +313,45 @@
 
 
 def sweeps_kernel(slot, diagonal_ref, weight_ref, mask_ref, high_ref, low_ref, *refs):
-    out_ref, token_ref, result, done = refs[-4:]
-    diagonal = jnp.concatenate([diagonal_ref[b:b + 1] for b in range(weight_ref.shape[-1] // BLOCK)], axis=1)
+    out_ref, token_ref, result, changes, done = refs[-5:]
+    features, hidden = result.shape
+    columns = [slice(c, c + WIDTH) for c in range(0, hidden, WIDTH)]
+    diagonal = jnp.concatenate([diagonal_ref[b:b + 1] for b in range(hidden // BLOCK)], axis=1)
     back = jnp.exp2(exponent_of(diagonal))
     factor = relax_factor * (1.0 / (diagonal + diagonal_eps)) * back
-    weight = weight_ref[slot].astype(F32)
-    keep = mask_ref[slot].astype(F32)
-    pruned = keep * weight
+    copies = []
+
+    def note(sweep, part, change):
+        change = change * back[:, part]
+        top = change.astype(BF16)
+        changes[sweep % 2, :features, part] = top
+        if sweep > 0:
+            changes[sweep % 2, features:, part] = (change - top.astype(F32)).astype(BF16)
+
+    for part in columns:
+        weight = weight_ref[slot, :, part].astype(F32)
+        pruned = mask_ref[slot, :, part].astype(F32) * weight
+        result[:, part] = pruned
+        note(0, part, pruned - weight)
     for sweep in range(STEPS):
-        change = (pruned - weight) * back
-        top = change.astype(BF16)
-        if sweep == 0:
-            gradient = jnp.dot(top, high_ref[...], preferred_element_type=F32)
-        else:
-            rest = (change - top.astype(F32)).astype(BF16)
-            both = jnp.dot(jnp.concatenate([top, rest], axis=0), high_ref[...], preferred_element_type=F32)
-            gradient = both[:top.shape[0]] + both[top.shape[0]:]
-        gradient = gradient + jnp.dot(top, low_ref[...], preferred_element_type=F32)
-        pruned = keep * (pruned - gradient * factor)
-    result[...] = pruned
-    token_ref[...] = pruned[:8, :BLOCK]
-    copy = pltpu.make_async_copy(result, out_ref.at[slot], done)
-    copy.start()
-    copy.wait()
+        now = changes.at[sweep % 2]
+        for n, part in enumerate(columns):
+            if sweep == 0:
+                gradient = jnp.dot(now[:features], high_ref[:, part], preferred_element_type=F32)
+            else:
+                both = jnp.dot(now[...], high_ref[:, part], preferred_element_type=F32)
+                gradient = both[:features] + both[features:]
+            gradient = gradient + jnp.dot(now[:features], low_ref[:, part], preferred_element_type=F32)
+            pruned = mask_ref[slot, :, part].astype(F32) * (result[:, part] - gradient * factor[:, part])
+            result[:, part] = pruned
+            if sweep < STEPS - 1:
+                note(sweep + 1, part, pruned - weight_ref[slot, :, part].astype(F32))
+            else:
+                copies.append(pltpu.make_async_copy(result.at[:, part], out_ref.at[slot, :, part], done.at[n]))
+                copies[-1].start()
+    token_ref[...] = result[:8, :BLOCK]
+    for copy in copies:
+        copy.wait()
 
 
 def on_device(expert_inputs, row_expert, down_weight, keep_mask):
@@ -363,14 +380,14 @@
     place_flops = 2 * capacity * tokens * hidden
     key, *outgoing = call(
         functools.partial(first_kernel, peers, slots, all_experts, capacity),
-        [shape(1, tokens, I32)] + [chunk] * (peers - 1), [SMEM, ANY, ANY],
+        [shape(1, tokens, I32)] + [chunk] * (peers - 1), [SMEM, HBM, HBM],
         scratch=[
             pltpu.VMEM((1, tokens), I32), pltpu.VMEM((tokens, hidden), BF16),
-            pltpu.SemaphoreType.DMA, pltpu.SemaphoreType.DMA((hidden // WIDTH,)),
+            pltpu.SemaphoreType.DMA, pltpu.SemaphoreType.DMA,
         ],
         flops=place_flops * (peers - 1), moved=expert_inputs.size * 4, name="place_first",
     )(me, owners, expert_inputs)
-    arrived = [[over_experts(outgoing[k - 1], k) for k in range(1, peers)]]
+    arrived = [[over_experts(rows, k) for rows, k in zip(outgoing, others(peers))]]
     count = slots + (slots - 1) * (peers - 1)
     rest = call(
         functools.partial(second_kernel, peers, slots, capacity), [chunk] * count, [SMEM, VMEM, VMEM],
@@ -379,7 +396,7 @@
     own = rest[:slots]
     for a in range(1, slots):
         outgoing = rest[slots + (a - 1) * (peers - 1):slots + a * (peers - 1)]
-        arrived.append([over_experts(outgoing[k - 1], k) for k in range(1, peers)])
+        arrived.append([over_experts(rows, k) for rows, k in zip(outgoing, others(peers))])
 
     many = diagonal_rows(hidden)
     notes = -(-(8 + 3 * many) // TILE) * TILE
@@ -445,7 +462,10 @@
             [jax.ShapeDtypeStruct((slots, features, hidden), F32), shape(8)],
             [VMEM] * 5 + [ANY] * (len(args) - 5),
             out_specs=[ANY, VMEM],
-            scratch=[pltpu.VMEM((features, hidden), F32), pltpu.SemaphoreType.DMA],
+            scratch=[
+                pltpu.VMEM((features, hidden), F32), pltpu.VMEM((2, 2 * features, hidden), BF16),
+                pltpu.SemaphoreType.DMA((hidden // WIDTH,)),
+            ],
             aliases={} if result is None else {5: 0},
             flops=2 * 3 * STEPS * features * hidden * hidden, moved=hidden * hidden * 4, name=f"sweeps_{a}",
         )(*args)

time: 84.4 us -> 82.5 us (0.977)
  Pallas kernels: 30.3 us -> 28.7 us
    pallas_call x16, Pallas kernels: 30.3 us -> 28.7 us  [call(): return lambda *args: inner(*args, *after)]
  transfers between devices with their start and end apart: 22 -> 22, of which waited for: 13 -> 15; matrix products, arithmetic and copies ran while one was open for 0% -> 0% of each run, Pallas kernels for 19% -> 20%
where the time goes in v7:
time: 82.5 us; the launch traced here: 82.3 us
  waiting for transfers between devices  33.2 us (40%)
  Pallas kernels  28.7 us (35%)
  starting transfers between devices  19.5 us (24%)
    pallas_call x16, Pallas kernels, call(): return lambda *args: inner(*args, *after)  28.7 us
    ppermute x16, waiting for transfers between devices, over_rows(): lax.ppermute(array, 'rows', [(i, i ^ 1 << bit) for i in range(copies)])  21.6 us
    ppermute x6, waiting for transfers between devices, over_experts(): return lax.ppermute(array, 'expert', [(i, i ^ flip) for i in range(peers)])  11.5 us
    ppermute x16, starting transfers between devices, over_rows(): lax.ppermute(array, 'rows', [(i, i ^ 1 << bit) for i in range(copies)])  11.4 us
    ppermute x6, starting transfers between devices, over_experts(): return lax.ppermute(array, 'expert', [(i, i ^ flip) for i in range(peers)])  8.09 us
  transfers between devices with their start and end apart: 22, of which 15 were waited for; matrix products, arithmetic and copies ran while one was open for 0% of the time, Pallas kernels for 20%

profile of v7, /device:TPU:0, one launch (start us, length us, event | category | flops | bytes accessed | tf_op | source)
XLA Modules:
  0.0 82.3 jit_solution(4645889150794423420)
XLA Ops:
  0.0 0.0 copy-start.2
  0.0 0.7 copy-done.2
  0.7 4.5 %place_first.1 = (s32[1,2048]{1,0:T(1,128)S(1)}, bf16[256,768]{1,0:T(8,128)(2,1)S(1)}, bf16[256,768]{1,0:T(8,128)(2,1)S(1)}, bf16[256,768]{1,0:T(8,128)(2,1)S(1)}) custom-call(s32[1]{0:T(128)} %bitcast.1.refs_0_, s32[1,2048]{1,0:T(1,128)S(1)} %bitcast.3, bf16[2048,768]{1,0:T(8,128)(2,1)} %refs_2_.5), custom_call_target="tpu_custom_call" | custom-call | flops 2415919104 | bytes 6291456 | tf_op jit(solution)/shard_map/place_first/pallas_call | solution.py:47
  5.2 4.0 %collective-permute-start.1 = (bf16[256,768]{1,0:T(8,128)(2,1)S(1)}, bf16[256,768]{1,0:T(8,128)(2,1)S(1)}, u32[]{:S(2)}, u32[]{:S(2)}) collective-permute-start(bf16[256,768]{1,0:T(8,128)(2,1)S(1)} %get-tuple-element.51), channel_id=1, source_target_pairs={{0,24},{8,16},{16,8},{24,0},{1,25},{9,17},{17,9},{25,1},{2,26},{10... | collective-permute-start | bytes 1179656 | tf_op jit(solution)/shard_map/ppermute | solution.py:374
  9.2 0.5 collective-permute-start.2
  9.7 0.1 collective-permute-start.3
  9.8 6.2 %place_rest.1 = (bf16[256,768]{1,0:T(8,128)(2,1)S(1)}, bf16[256,768]{1,0:T(8,128)(2,1)S(1)}, bf16[256,768]{1,0:T(8,128)(2,1)S(1)}, bf16[256,768]{1,0:T(8,128)(2,1)S(1)}, bf16[256,768]{1,0:T(8,128)(2,1)S(1)}) custom-call(s32[1]{0:T(128)} %bitcast.1.refs_0_, s32[1,2048]{1,0:T(1,128)S(1)} %get-tuple-element.47.refs_1_, bf16[2048,768]{1,0:T(8,128)(2,1)} %refs_2_.5), custom_call_target="tpu_custom_call" | custom-call | flops 4026531840 | bytes 6291456 | tf_op jit(solution)/shard_map/place_rest/pallas_call | solution.py:47
  16.0 3.2 %collective-permute-done.1.refs_1_ = bf16[256,768]{1,0:T(8,128)(2,1)S(1)} collective-permute-done((bf16[256,768]{1,0:T(8,128)(2,1)S(1)}, bf16[256,768]{1,0:T(8,128)(2,1)S(1)}, u32[]{:S(2)}, u32[]{:S(2)}) %collective-permute-start.1) | collective-permute-done | bytes 393248 | tf_op jit(solution)/shard_map/ppermute | solution.py:374
  19.2 0.6 begin_0.1.refs_1_
  19.8 6.9 %collective-permute-done.2.refs_2_ = bf16[256,768]{1,0:T(8,128)(2,1)S(1)} collective-permute-done((bf16[256,768]{1,0:T(8,128)(2,1)S(1)}, bf16[256,768]{1,0:T(8,128)(2,1)S(1)}, u32[]{:S(2)}, u32[]{:S(2)}) %collective-permute-start.2) | collective-permute-done | bytes 393248 | tf_op jit(solution)/shard_map/ppermute | solution.py:374
  26.7 0.3 collective-permute-done.3.refs_3_
  27.0 0.8 gram_0.1
  27.8 0.1 collective-permute-start.4
  27.9 0.5 collective-permute-start.5
  28.4 1.5 %collective-permute-start = (bf16[256,768]{1,0:T(8,128)(2,1)S(1)}, bf16[256,768]{1,0:T(8,128)(2,1)S(1)}, u32[]{:S(2)}, u32[]{:S(2)}) collective-permute-start(bf16[256,768]{1,0:T(8,128)(2,1)S(1)} %get-tuple-element.49), channel_id=1, source_target_pairs={{0,24},{8,16},{16,8},{24,0},{1,25},{9,17},{17,9},{25,1},{2,26},{10... | collective-permute-start | bytes 1179656 | tf_op jit(solution)/shard_map/ppermute | solution.py:374
  29.9 1.4 %collective-permute-start.6 = (bf16[256,768]{1,0:T(8,128)(2,1)S(1)}, bf16[256,768]{1,0:T(8,128)(2,1)S(1)}, u32[]{:S(2)}, u32[]{:S(2)}) collective-permute-start(bf16[256,768]{1,0:T(8,128)(2,1)S(1)} %get-tuple-element.59), channel_id=1, source_target_pairs={{0,16},{8,24},{16,0},{24,8},{1,17},{9,25},{17,1},{25,9},{2,18},{10... | collective-permute-start | bytes 1179656 | tf_op jit(solution)/shard_map/ppermute | solution.py:374
  31.4 0.5 collective-permute-start.7
  31.9 0.0 collective-permute-done.5.refs_4_
  31.9 0.0 collective-permute-done.4.refs_3_
  31.9 0.4 stage_0_1.1
  32.3 1.6 %collective-permute-start.8 = (s16[608,128]{1,0:T(8,128)(2,1)S(1)}, s16[608,128]{1,0:T(8,128)(2,1)S(1)}, u32[]{:S(2)}, u32[]{:S(2)}) collective-permute-start(s16[608,128]{1,0:T(8,128)(2,1)S(1)} %get-tuple-element.58.refs_2_), channel_id=1, source_target_pairs={{0,2},{1,3},{2,0},{3,1},{4,6},{5,7},{6,4},{7,5},{8,10},{9,11},{10,... | collective-permute-start | bytes 466952 | tf_op jit(solution)/shard_map/ppermute | solution.py:377
  33.9 3.6 %collective-permute-done.8.refs_3_ = s16[608,128]{1,0:T(8,128)(2,1)S(1)} collective-permute-done((s16[608,128]{1,0:T(8,128)(2,1)S(1)}, s16[608,128]{1,0:T(8,128)(2,1)S(1)}, u32[]{:S(2)}, u32[]{:S(2)}) %collective-permute-start.8) | collective-permute-done | bytes 155680 | tf_op jit(solution)/shard_map/ppermute | solution.py:377
  37.6 0.6 stage_0_2.1
  38.2 2.7 %collective-permute-start.9 = (s16[608,128]{1,0:T(8,128)(2,1)S(1)}, s16[608,128]{1,0:T(8,128)(2,1)S(1)}, u32[]{:S(2)}, u32[]{:S(2)}) collective-permute-start(s16[608,128]{1,0:T(8,128)(2,1)S(1)} %get-tuple-element.65), channel_id=1, source_target_pairs={{0,4},{1,5},{2,6},{3,7},{4,0},{5,1},{6,2},{7,3},{8,12},{9,13},{10,... | collective-permute-start | bytes 466952 | tf_op jit(solution)/shard_map/ppermute | solution.py:377
  40.9 0.5 collective-permute-done.refs_1_
  41.3 0.6 begin_1.1.refs_1_
  41.9 4.9 %collective-permute-done.9.refs_3_ = s16[608,128]{1,0:T(8,128)(2,1)S(1)} collective-permute-done((s16[608,128]{1,0:T(8,128)(2,1)S(1)}, s16[608,128]{1,0:T(8,128)(2,1)S(1)}, u32[]{:S(2)}, u32[]{:S(2)}) %collective-permute-start.9) | collective-permute-done | bytes 155680 | tf_op jit(solution)/shard_map/ppermute | solution.py:377
  46.8 0.6 total_0.1
  47.4 0.7 collective-permute-start.14
  48.1 0.7 collective-permute-done.6.refs_2_
  48.8 0.0 collective-permute-done.7.refs_3_
  48.8 0.8 gram_1.1
  49.6 0.1 collective-permute-start.10
  49.7 0.5 collective-permute-start.11
  50.2 0.1 collective-permute-start.12
  50.3 0.4 collective-permute-start.13
  50.7 0.6 collective-permute-done.11.refs_4_
  51.3 0.3 collective-permute-done.12.refs_5_
  51.6 0.2 collective-permute-done.13.refs_6_
  51.8 0.9 %collective-permute-done.14.refs_7_.refs_3_ = s16[592,128]{1,0:T(8,128)(2,1)S(1)} collective-permute-done((s16[592,128]{1,0:T(8,128)(2,1)S(1)}, s16[592,128]{1,0:T(8,128)(2,1)S(1)}, u32[]{:S(2)}, u32[]{:S(2)}) %collective-permute-start.14) | collective-permute-done | bytes 151584 | tf_op jit(solution)/shard_map/ppermute | solution.py:377
  52.6 0.0 collective-permute-done.10.refs_3_
  52.7 0.4 stage_1_1.1
  53.1 0.8 collective-permute-start.15
  53.9 0.0 collective-permute-start.17
  53.9 0.5 collective-permute-start.18
  54.4 4.2 %collective-permute-done.15.refs_3_ = s16[608,128]{1,0:T(8,128)(2,1)S(1)} collective-permute-done((s16[608,128]{1,0:T(8,128)(2,1)S(1)}, s16[608,128]{1,0:T(8,128)(2,1)S(1)}, u32[]{:S(2)}, u32[]{:S(2)}) %collective-permute-start.15) | collective-permute-done | bytes 155680 | tf_op jit(solution)/shard_map/ppermute | solution.py:377
  58.5 0.6 stage_1_2.1
  59.2 2.8 %collective-permute-start.16 = (s16[608,128]{1,0:T(8,128)(2,1)S(1)}, s16[608,128]{1,0:T(8,128)(2,1)S(1)}, u32[]{:S(2)}, u32[]{:S(2)}) collective-permute-start(s16[608,128]{1,0:T(8,128)(2,1)S(1)} %get-tuple-element.78.refs_6_), channel_id=1, source_target_pairs={{0,4},{1,5},{2,6},{3,7},{4,0},{5,1},{6,2},{7,3},{8,12},{9,13},{10,... | collective-permute-start | bytes 466952 | tf_op jit(solution)/shard_map/ppermute | solution.py:377
  61.9 0.0 collective-permute-done.17.refs_4_
  61.9 0.0 collective-permute-done.18.refs_5_
  61.9 0.9 %unpack_0.1 = (bf16[768,768]{1,0:T(8,128)(2,1)S(1)}, bf16[768,768]{1,0:T(8,128)(2,1)S(1)}) custom-call(s32[1]{0:T(128)} %bitcast.refs_0_, f32[8,128]{1,0:T(8,128)S(1)} %get-tuple-element.79.refs_1_.refs_0_, s16[592,128]{1,0:T(8,128)(2,1)S(1)} %get-tuple-element.66.refs_4_.refs_2_, s16[592,128]{1,0:T(8,128)(2,1)S(1)} %collective-permute-done.14.refs_7_.refs_3_, ...), custom_call_target="tpu_custom_call" | custom-call | bytes 1179648 | tf_op jit(solution)/shard_map/unpack_0/pallas_call | solution.py:47
  62.8 0.0 copy-done
  62.8 0.0 copy-done.1
  62.8 4.9 %sweeps_0.1 = (f32[2,256,768]{2,1,0:T(8,128)}, f32[8,128]{1,0:T(8,128)S(1)}) custom-call(f32[8,128]{1,0:T(8,128)S(1)} %get-tuple-element.79.refs_1_.refs_0_, bf16[2,256,768]{2,1,0:T(8,128)(2,1)S(1)} %copy-done, bf16[2,256,768]{2,1,0:T(8,128)(2,1)S(1)} %copy-done.1, bf16[768,768]{1,0:T(8,128)(2,1)S(1)} %get-tuple-element.80.refs_3_, ...), custom_call_target="tpu_custom_call" | custom-call | flops 3623878656 | bytes 2359296 | tf_op jit(solution)/shard_map/sweeps_0/pallas_call | solution.py:47
  67.8 0.9 %collective-permute-done.16.refs_3_ = s16[608,128]{1,0:T(8,128)(2,1)S(1)} collective-permute-done((s16[608,128]{1,0:T(8,128)(2,1)S(1)}, s16[608,128]{1,0:T(8,128)(2,1)S(1)}, u32[]{:S(2)}, u32[]{:S(2)}) %collective-permute-start.16) | collective-permute-done | bytes 155680 | tf_op jit(solution)/shard_map/ppermute | solution.py:377
  68.7 0.6 total_1.1
  69.3 0.6 collective-permute-start.19
  69.9 0.0 collective-permute-start.20
  69.9 4.6 %collective-permute-done.19.refs_3_ = s16[592,128]{1,0:T(8,128)(2,1)S(1)} collective-permute-done((s16[592,128]{1,0:T(8,128)(2,1)S(1)}, s16[592,128]{1,0:T(8,128)(2,1)S(1)}, u32[]{:S(2)}, u32[]{:S(2)}) %collective-permute-start.19) | collective-permute-done | bytes 151584 | tf_op jit(solution)/shard_map/ppermute | solution.py:377
  74.6 0.0 collective-permute-start.21
  74.6 0.0 collective-permute-done.20.refs_4_
  74.6 1.4 %collective-permute-done.21.refs_5_ = s16[592,128]{1,0:T(8,128)(2,1)S(1)} collective-permute-done((s16[592,128]{1,0:T(8,128)(2,1)S(1)}, s16[592,128]{1,0:T(8,128)(2,1)S(1)}, u32[]{:S(2)}, u32[]{:S(2)}) %collective-permute-start.21) | collective-permute-done | bytes 151584 | tf_op jit(solution)/shard_map/ppermute | solution.py:377
  75.9 0.7 unpack_1.1
  76.7 5.5 %sweeps_1.1 = (f32[2,256,768]{2,1,0:T(8,128)}, f32[8,128]{1,0:T(8,128)}) custom-call(f32[8,128]{1,0:T(8,128)S(1)} %get-tuple-element.83.refs_1_.refs_0_, bf16[2,256,768]{2,1,0:T(8,128)(2,1)S(1)} %copy-done, bf16[2,256,768]{2,1,0:T(8,128)(2,1)S(1)} %copy-done.1, bf16[768,768]{1,0:T(8,128)(2,1)S(1)} %get-tuple-element.85.refs_3_, ...), custom_call_target="tpu_custom_call", output_to_operand_aliasing={{0}: (5, {})} | custom-call | flops 3623878656 | bytes 2359296 | tf_op jit(solution)/shard_map/sweeps_1/pallas_call | solution.py:47
  (2 shorter events, 0.0 us)
Async XLA Ops:
  0.0 0.7 copy-start.2
  5.2 13.9 %collective-permute-start.1 = (bf16[256,768]{1,0:T(8,128)(2,1)S(1)}, bf16[256,768]{1,0:T(8,128)(2,1)S(1)}, u32[]{:S(2)}, u32[]{:S(2)}) collective-permute-start(bf16[256,768]{1,0:T(8,128)(2,1)S(1)} %get-tuple-element.51), channel_id=1, source_target_pairs={{0,24},{8,16},{16,8},{24,0},{1,25},{9,17},{17,9},{25,1},{2,26},{10... | collective-permute-start | bytes 1179656 | tf_op jit(solution)/shard_map/ppermute | solution.py:374
  9.2 17.5 %collective-permute-start.2 = (bf16[256,768]{1,0:T(8,128)(2,1)S(1)}, bf16[256,768]{1,0:T(8,128)(2,1)S(1)}, u32[]{:S(2)}, u32[]{:S(2)}) collective-permute-start(bf16[256,768]{1,0:T(8,128)(2,1)S(1)} %get-tuple-element.52), channel_id=1, source_target_pairs={{0,16},{8,24},{16,0},{24,8},{1,17},{9,25},{17,1},{25,9},{2,18},{10... | collective-permute-start | bytes 1179656 | tf_op jit(solution)/shard_map/ppermute | solution.py:374
  9.7 17.3 %collective-permute-start.3 = (bf16[256,768]{1,0:T(8,128)(2,1)S(1)}, bf16[256,768]{1,0:T(8,128)(2,1)S(1)}, u32[]{:S(2)}, u32[]{:S(2)}) collective-permute-start(bf16[256,768]{1,0:T(8,128)(2,1)S(1)} %get-tuple-element.53), channel_id=1, source_target_pairs={{0,8},{8,0},{16,24},{24,16},{1,9},{9,1},{17,25},{25,17},{2,10},{10... | collective-permute-start | bytes 1179656 | tf_op jit(solution)/shard_map/ppermute | solution.py:374
  27.8 4.1 %collective-permute-start.4 = (f32[584,128]{1,0:T(8,128)S(1)}, f32[584,128]{1,0:T(8,128)S(1)}, u32[]{:S(2)}, u32[]{:S(2)}) collective-permute-start(f32[584,128]{1,0:T(8,128)S(1)} %get-tuple-element.56), channel_id=1, source_target_pairs={{0,1},{1,0},{2,3},{3,2},{4,5},{5,4},{6,7},{7,6},{8,9},{9,8},{10,11... | collective-permute-start | bytes 897032 | tf_op jit(solution)/shard_map/ppermute | solution.py:377
  27.9 4.0 %collective-permute-start.5 = (f32[576,128]{1,0:T(8,128)S(1)}, f32[576,128]{1,0:T(8,128)S(1)}, u32[]{:S(2)}, u32[]{:S(2)}) collective-permute-start(f32[576,128]{1,0:T(8,128)S(1)} %get-tuple-element.57), channel_id=1, source_target_pairs={{0,1},{1,0},{2,3},{3,2},{4,5},{5,4},{6,7},{7,6},{8,9},{9,8},{10,11... | collective-permute-start | bytes 884744 | tf_op jit(solution)/shard_map/ppermute | solution.py:377
  28.4 12.9 %collective-permute-start = (bf16[256,768]{1,0:T(8,128)(2,1)S(1)}, bf16[256,768]{1,0:T(8,128)(2,1)S(1)}, u32[]{:S(2)}, u32[]{:S(2)}) collective-permute-start(bf16[256,768]{1,0:T(8,128)(2,1)S(1)} %get-tuple-element.49), channel_id=1, source_target_pairs={{0,24},{8,16},{16,8},{24,0},{1,25},{9,17},{17,9},{25,1},{2,26},{10... | collective-permute-start | bytes 1179656 | tf_op jit(solution)/shard_map/ppermute | solution.py:374
  29.9 18.9 %collective-permute-start.6 = (bf16[256,768]{1,0:T(8,128)(2,1)S(1)}, bf16[256,768]{1,0:T(8,128)(2,1)S(1)}, u32[]{:S(2)}, u32[]{:S(2)}) collective-permute-start(bf16[256,768]{1,0:T(8,128)(2,1)S(1)} %get-tuple-element.59), channel_id=1, source_target_pairs={{0,16},{8,24},{16,0},{24,8},{1,17},{9,25},{17,1},{25,9},{2,18},{10... | collective-permute-start | bytes 1179656 | tf_op jit(solution)/shard_map/ppermute | solution.py:374
  31.4 17.5 %collective-permute-start.7 = (bf16[256,768]{1,0:T(8,128)(2,1)S(1)}, bf16[256,768]{1,0:T(8,128)(2,1)S(1)}, u32[]{:S(2)}, u32[]{:S(2)}) collective-permute-start(bf16[256,768]{1,0:T(8,128)(2,1)S(1)} %get-tuple-element.60), channel_id=1, source_target_pairs={{0,8},{8,0},{16,24},{24,16},{1,9},{9,1},{17,25},{25,17},{2,10},{10... | collective-permute-start | bytes 1179656 | tf_op jit(solution)/shard_map/ppermute | solution.py:374
  32.3 5.3 %collective-permute-start.8 = (s16[608,128]{1,0:T(8,128)(2,1)S(1)}, s16[608,128]{1,0:T(8,128)(2,1)S(1)}, u32[]{:S(2)}, u32[]{:S(2)}) collective-permute-start(s16[608,128]{1,0:T(8,128)(2,1)S(1)} %get-tuple-element.58.refs_2_), channel_id=1, source_target_pairs={{0,2},{1,3},{2,0},{3,1},{4,6},{5,7},{6,4},{7,5},{8,10},{9,11},{10,... | collective-permute-start | bytes 466952 | tf_op jit(solution)/shard_map/ppermute | solution.py:377
  38.2 8.6 %collective-permute-start.9 = (s16[608,128]{1,0:T(8,128)(2,1)S(1)}, s16[608,128]{1,0:T(8,128)(2,1)S(1)}, u32[]{:S(2)}, u32[]{:S(2)}) collective-permute-start(s16[608,128]{1,0:T(8,128)(2,1)S(1)} %get-tuple-element.65), channel_id=1, source_target_pairs={{0,4},{1,5},{2,6},{3,7},{4,0},{5,1},{6,2},{7,3},{8,12},{9,13},{10,... | collective-permute-start | bytes 466952 | tf_op jit(solution)/shard_map/ppermute | solution.py:377
  47.4 5.3 %collective-permute-start.14 = (s16[592,128]{1,0:T(8,128)(2,1)S(1)}, s16[592,128]{1,0:T(8,128)(2,1)S(1)}, u32[]{:S(2)}, u32[]{:S(2)}) collective-permute-start(s16[592,128]{1,0:T(8,128)(2,1)S(1)} %get-tuple-element.66.refs_4_.refs_2_), channel_id=1, source_target_pairs={{0,2},{1,3},{2,0},{3,1},{4,6},{5,7},{6,4},{7,5},{8,10},{9,11},{10,... | collective-permute-start | bytes 454664 | tf_op jit(solution)/shard_map/ppermute | solution.py:377
  49.6 3.0 %collective-permute-start.10 = (f32[296,128]{1,0:T(8,128)S(1)}, f32[296,128]{1,0:T(8,128)S(1)}, u32[]{:S(2)}, u32[]{:S(2)}) collective-permute-start(f32[296,128]{1,0:T(8,128)S(1)} %get-tuple-element.69), channel_id=1, source_target_pairs={{0,1},{1,0},{2,3},{3,2},{4,5},{5,4},{6,7},{7,6},{8,9},{9,8},{10,11... | collective-permute-start | bytes 454664 | tf_op jit(solution)/shard_map/ppermute | solution.py:377
  49.7 1.6 %collective-permute-start.11 = (f32[288,128]{1,0:T(8,128)S(1)}, f32[288,128]{1,0:T(8,128)S(1)}, u32[]{:S(2)}, u32[]{:S(2)}) collective-permute-start(f32[288,128]{1,0:T(8,128)S(1)} %get-tuple-element.70), channel_id=1, source_target_pairs={{0,1},{1,0},{2,3},{3,2},{4,5},{5,4},{6,7},{7,6},{8,9},{9,8},{10,11... | collective-permute-start | bytes 442376 | tf_op jit(solution)/shard_map/ppermute | solution.py:377
  50.2 1.4 %collective-permute-start.12 = (f32[288,128]{1,0:T(8,128)S(1)}, f32[288,128]{1,0:T(8,128)S(1)}, u32[]{:S(2)}, u32[]{:S(2)}) collective-permute-start(f32[288,128]{1,0:T(8,128)S(1)} %get-tuple-element.71), channel_id=1, source_target_pairs={{0,1},{1,0},{2,3},{3,2},{4,5},{5,4},{6,7},{7,6},{8,9},{9,8},{10,11... | collective-permute-start | bytes 442376 | tf_op jit(solution)/shard_map/ppermute | solution.py:377
  50.3 1.5 %collective-permute-start.13 = (f32[288,128]{1,0:T(8,128)S(1)}, f32[288,128]{1,0:T(8,128)S(1)}, u32[]{:S(2)}, u32[]{:S(2)}) collective-permute-start(f32[288,128]{1,0:T(8,128)S(1)} %get-tuple-element.72), channel_id=1, source_target_pairs={{0,1},{1,0},{2,3},{3,2},{4,5},{5,4},{6,7},{7,6},{8,9},{9,8},{10,11... | collective-permute-start | bytes 442376 | tf_op jit(solution)/shard_map/ppermute | solution.py:377
  52.7 10.2 %copy-start = (bf16[2,256,768]{2,1,0:T(8,128)(2,1)S(1)}, bf16[2,256,768]{2,1,0:T(8,128)(2,1)}, u32[]{:S(2)}) copy-start(bf16[2,256,768]{2,1,0:T(8,128)(2,1)} %refs_1_.3) | copy-start | bytes 2359300
  52.7 10.2 %copy-start.1 = (bf16[2,256,768]{2,1,0:T(8,128)(2,1)S(1)}, bf16[2,256,768]{2,1,0:T(8,128)(2,1)}, u32[]{:S(2)}) copy-start(bf16[2,256,768]{2,1,0:T(8,128)(2,1)} %refs_2_.7) | copy-start | bytes 2359300
  53.1 5.5 %collective-permute-start.15 = (s16[608,128]{1,0:T(8,128)(2,1)S(1)}, s16[608,128]{1,0:T(8,128)(2,1)S(1)}, u32[]{:S(2)}, u32[]{:S(2)}) collective-permute-start(s16[608,128]{1,0:T(8,128)(2,1)S(1)} %get-tuple-element.75), channel_id=1, source_target_pairs={{0,2},{1,3},{2,0},{3,1},{4,6},{5,7},{6,4},{7,5},{8,10},{9,11},{10,... | collective-permute-start | bytes 466952 | tf_op jit(solution)/shard_map/ppermute | solution.py:377
  53.9 8.1 %collective-permute-start.17 = (s16[592,128]{1,0:T(8,128)(2,1)S(1)}, s16[592,128]{1,0:T(8,128)(2,1)S(1)}, u32[]{:S(2)}, u32[]{:S(2)}) collective-permute-start(s16[592,128]{1,0:T(8,128)(2,1)S(1)} %get-tuple-element.66.refs_4_.refs_2_), channel_id=1, source_target_pairs={{0,1},{1,0},{2,3},{3,2},{4,5},{5,4},{6,7},{7,6},{8,9},{9,8},{10,11... | collective-permute-start | bytes 454664 | tf_op jit(solution)/shard_map/ppermute | solution.py:377
  53.9 8.0 %collective-permute-start.18 = (s16[592,128]{1,0:T(8,128)(2,1)S(1)}, s16[592,128]{1,0:T(8,128)(2,1)S(1)}, u32[]{:S(2)}, u32[]{:S(2)}) collective-permute-start(s16[592,128]{1,0:T(8,128)(2,1)S(1)} %collective-permute-done.14.refs_7_.refs_3_), channel_id=1, source_target_pairs={{0,1},{1,0},{2,3},{3,2},{4,5},{5,4},{6,7},{7,6},{8,9},{9,8},{10,11... | collective-permute-start | bytes 454664 | tf_op jit(solution)/shard_map/ppermute | solution.py:377
  59.2 9.6 %collective-permute-start.16 = (s16[608,128]{1,0:T(8,128)(2,1)S(1)}, s16[608,128]{1,0:T(8,128)(2,1)S(1)}, u32[]{:S(2)}, u32[]{:S(2)}) collective-permute-start(s16[608,128]{1,0:T(8,128)(2,1)S(1)} %get-tuple-element.78.refs_6_), channel_id=1, source_target_pairs={{0,4},{1,5},{2,6},{3,7},{4,0},{5,1},{6,2},{7,3},{8,12},{9,13},{10,... | collective-permute-start | bytes 466952 | tf_op jit(solution)/shard_map/ppermute | solution.py:377
  69.3 5.3 %collective-permute-start.19 = (s16[592,128]{1,0:T(8,128)(2,1)S(1)}, s16[592,128]{1,0:T(8,128)(2,1)S(1)}, u32[]{:S(2)}, u32[]{:S(2)}) collective-permute-start(s16[592,128]{1,0:T(8,128)(2,1)S(1)} %get-tuple-element.84.refs_2_), channel_id=1, source_target_pairs={{0,2},{1,3},{2,0},{3,1},{4,6},{5,7},{6,4},{7,5},{8,10},{9,11},{10,... | collective-permute-start | bytes 454664 | tf_op jit(solution)/shard_map/ppermute | solution.py:377
  69.9 4.7 %collective-permute-start.20 = (s16[592,128]{1,0:T(8,128)(2,1)S(1)}, s16[592,128]{1,0:T(8,128)(2,1)S(1)}, u32[]{:S(2)}, u32[]{:S(2)}) collective-permute-start(s16[592,128]{1,0:T(8,128)(2,1)S(1)} %get-tuple-element.84.refs_2_), channel_id=1, source_target_pairs={{0,1},{1,0},{2,3},{3,2},{4,5},{5,4},{6,7},{7,6},{8,9},{9,8},{10,11... | collective-permute-start | bytes 454664 | tf_op jit(solution)/shard_map/ppermute | solution.py:377
  74.6 1.4 %collective-permute-start.21 = (s16[592,128]{1,0:T(8,128)(2,1)S(1)}, s16[592,128]{1,0:T(8,128)(2,1)S(1)}, u32[]{:S(2)}, u32[]{:S(2)}) collective-permute-start(s16[592,128]{1,0:T(8,128)(2,1)S(1)} %collective-permute-done.19.refs_3_), channel_id=1, source_target_pairs={{0,1},{1,0},{2,3},{3,2},{4,5},{5,4},{6,7},{7,6},{8,9},{9,8},{10,11... | collective-permute-start | bytes 454664 | tf_op jit(solution)/shard_map/ppermute | solution.py:377

commit v8 on v7

--- a/solution.py
+++ b/solution.py
@@ -17,7 +17,7 @@
 relax_factor = 0.5
 diagonal_eps = 1e-06
 tiny = 1e-30
-VMEM_LIMIT = 50 * 2**20
+VMEM_LIMIT = 32 * 2**20
 
 VMEM = pl.BlockSpec(memory_space=pltpu.VMEM)
 ANY = pl.BlockSpec(memory_space=pl.ANY)
@@ -312,6 +312,10 @@
                 put(i, i, jnp.where(eye_of(lax.eq), ones[i:i + 1], whole))
 
 
+def relay_kernel(in_ref, out_ref):
+    out_ref[...] = in_ref[...]
+
+
 def sweeps_kernel(slot, diagonal_ref, weight_ref, mask_ref, high_ref, low_ref, *refs):
     out_ref, token_ref, result, changes, done = refs[-5:]
     features, hidden = result.shape
@@ -416,7 +420,7 @@
             [shape(left + (notes if kept else TILE), dtype=I16), shape(many)] + ([shape(left)] if kept else []),
             [SMEM] + [VMEM] * (2 + len(got)),
             scratch=[pltpu.VMEM((length, BLOCK), F32), pltpu.VMEM((rows, BLOCK), F32)],
-            moved=rows * BLOCK * 12, name=name, after=after,
+            name=name, after=after,
         )(where, keep, diagonal, *got)
 
     def reduce(a, before, after, behind):
@@ -433,18 +437,22 @@
             got = [over_rows(part, bit - 1) for part in sent]
             coded, diagonal, keep = stage(f"stage_{a}_{bit}", bit, keep, diagonal, got, cut, True, behind if bit == 1 else ())
             sent = [coded]
-            if bit == 1:
-                halved = coded
-        return halved, (coded, diagonal, keep)
+        return coded, diagonal, keep
 
     def end(a, sums, after):
         coded, diagonal, keep = sums
         return stage(f"total_{a}", halvings, keep, diagonal, [over_rows(coded, halvings)], False, False, after)
 
-    def pieces_of(coded):
+    def pieces_of(coded, after):
         held = [(0, coded)]
         for bit in range(halvings - 1, -1, -1):
-            held += [(flip ^ (1 << bit), over_rows(piece, bit)) for flip, piece in held]
+            came = [(flip ^ (1 << bit), over_rows(piece, bit)) for flip, piece in held]
+            if after and bit == halvings - 1 and bit > 0:
+                came = [
+                    (flip, call(relay_kernel, shape(piece.shape[0], dtype=I16), [VMEM], name="relay", after=after)(piece))
+                    for flip, piece in came
+                ]
+            held += came
         return held
 
     def gather(a, held, diagonal, after):
@@ -455,7 +463,7 @@
         )(where, diagonal, *[piece for _, piece in held])
         return diagonal, high, low
 
-    def sweeps(a, diagonal, high, low, result):
+    def sweeps(a, diagonal, high, low, result, after):
         args = [diagonal, down_weight, keep_mask, high, low] + ([] if result is None else [result])
         return call(
             functools.partial(sweeps_kernel, a),
@@ -468,18 +476,19 @@
             ],
             aliases={} if result is None else {5: 0},
             flops=2 * 3 * STEPS * features * hidden * hidden, moved=hidden * hidden * 4, name=f"sweeps_{a}",
+            after=after,
         )(*args)
 
-    result, held, halved = None, [], ()
+    early = [begin(a, ()) for a in range(slots)]
+    result, whole, total, sums, token = None, None, (), (), []
     for a in range(slots):
-        before = begin(a, halved)
-        halved, sums = reduce(a, before, [piece for _, piece in held[:1]], [piece for _, piece in held[1:2]])
-        halved, token = [halved], ()
+        sums = reduce(a, early[a], sums[:1], [*early[a + 1:a + 2], *total[:1]])
         if a > 0:
-            result, *token = sweeps(a - 1, *gather(a - 1, held, diagonal, [sums[0]]), result)
-        coded, diagonal = end(a, sums, token)
-        held = pieces_of(coded)
-    return sweeps(slots - 1, *gather(slots - 1, held, diagonal, ()), result)[0]
+            whole = gather(a - 1, pieces_of(total[0], token), total[1], ())
+        total = end(a, sums, whole[1:2] if whole else ())
+        if a > 0:
+            result, *token = sweeps(a - 1, *whole, result, total[:1])
+    return sweeps(slots - 1, *gather(slots - 1, pieces_of(total[0], token), total[1], ()), result, ())[0]
 
 
 def solution(mesh):

time: 82.5 us -> 81.3 us (0.985)
  waiting for transfers between devices: 33.2 us -> 24.9 us
  starting transfers between devices: 19.5 us -> 24 us
  local copies, waits for them, and re-layouts: 0.7 us -> 5.11 us
  Pallas kernels: 28.7 us -> 26.6 us
    ppermute x16, waiting for transfers between devices: 21.6 us -> 13.3 us  [over_rows(): lax.ppermute(array, 'rows', [(i, i ^ 1 << bit) for i in range(copies)])]
    unnamed x6 -> x18, local copies, waits for them, and re-layouts: 0.7 us -> 5.11 us
    ppermute x16, starting transfers between devices: 11.4 us -> 14.6 us  [over_rows(): lax.ppermute(array, 'rows', [(i, i ^ 1 << bit) for i in range(copies)])]
    pallas_call x16 -> x17, Pallas kernels: 28.7 us -> 26.6 us  [call(): return lambda *args: inner(*args, *after)]
    ppermute x6, starting transfers between devices: 8.09 us -> 9.44 us  [over_experts(): return lax.ppermute(array, 'expert', [(i, i ^ flip) for i in range(peers)])]
  transfers between devices with their start and end apart: 22 -> 22, of which waited for: 15 -> 12; matrix products, arithmetic and copies ran while one was open for 0% -> 0% of each run, Pallas kernels for 20% -> 20%
where the time goes in v8:
time: 81.3 us; the launch traced here: 81 us
  Pallas kernels  26.6 us (33%)
  waiting for transfers between devices  24.9 us (31%)
  starting transfers between devices  24 us (30%)
  local copies, waits for them, and re-layouts  5.11 us (6%)
    pallas_call x17, Pallas kernels, call(): return lambda *args: inner(*args, *after)  26.6 us
    ppermute x16, starting transfers between devices, over_rows(): lax.ppermute(array, 'rows', [(i, i ^ 1 << bit) for i in range(copies)])  14.6 us
    ppermute x16, waiting for transfers between devices, over_rows(): lax.ppermute(array, 'rows', [(i, i ^ 1 << bit) for i in range(copies)])  13.3 us
    ppermute x6, waiting for transfers between devices, over_experts(): return lax.ppermute(array, 'expert', [(i, i ^ flip) for i in range(peers)])  11.6 us
    ppermute x6, starting transfers between devices, over_experts(): return lax.ppermute(array, 'expert', [(i, i ^ flip) for i in range(peers)])  9.44 us
    unnamed x18, local copies, waits for them, and re-layouts  5.11 us
  transfers between devices with their start and end apart: 22, of which 12 were waited for; matrix products, arithmetic and copies ran while one was open for 0% of the time, Pallas kernels for 20%

profile of v8, /device:TPU:0, one launch (start us, length us, event | category | flops | bytes accessed | tf_op | source)
XLA Modules:
  0.0 81.0 jit_solution(758187663368474294)
XLA Ops:
  0.0 1.9 %copy-done = bf16[2048,768]{1,0:T(8,128)(2,1)S(1)} copy-done((bf16[2048,768]{1,0:T(8,128)(2,1)S(1)}, bf16[2048,768]{1,0:T(8,128)(2,1)}, u32[]{:S(2)}) %copy-start) | copy-done | bytes 3145752
  1.9 0.7 copy-done.4
  2.6 3.1 %place_first.1 = (s32[1,2048]{1,0:T(1,128)S(1)}, bf16[256,768]{1,0:T(8,128)(2,1)S(1)}, bf16[256,768]{1,0:T(8,128)(2,1)S(1)}, bf16[256,768]{1,0:T(8,128)(2,1)S(1)}) custom-call(s32[1]{0:T(128)} %bitcast.1.refs_0_, s32[1,2048]{1,0:T(1,128)S(1)} %bitcast.3, bf16[2048,768]{1,0:T(8,128)(2,1)S(1)} %copy-done), custom_call_target="tpu_custom_call" | custom-call | flops 2415919104 | bytes 6291456 | tf_op jit(solution)/shard_map/place_first/pallas_call | solution.py:47
  5.7 4.0 %collective-permute-start.3 = (bf16[256,768]{1,0:T(8,128)(2,1)S(1)}, bf16[256,768]{1,0:T(8,128)(2,1)}, u32[]{:S(2)}, u32[]{:S(2)}) collective-permute-start(bf16[256,768]{1,0:T(8,128)(2,1)S(1)} %get-tuple-element.53), channel_id=1, source_target_pairs={{0,24},{8,16},{16,8},{24,0},{1,25},{9,17},{17,9},{25,1},{2,26},{10... | collective-permute-start | bytes 1179656 | tf_op jit(solution)/shard_map/ppermute | solution.py:378
  9.6 0.5 collective-permute-start.4
  10.2 0.1 collective-permute-start.5
  10.3 4.3 %place_rest.1 = (bf16[256,768]{1,0:T(8,128)(2,1)S(1)}, bf16[256,768]{1,0:T(8,128)(2,1)S(1)}, bf16[256,768]{1,0:T(8,128)(2,1)S(1)}, bf16[256,768]{1,0:T(8,128)(2,1)S(1)}, bf16[256,768]{1,0:T(8,128)(2,1)S(1)}) custom-call(s32[1]{0:T(128)} %bitcast.1.refs_0_, s32[1,2048]{1,0:T(1,128)S(1)} %get-tuple-element.47.refs_1_, bf16[2048,768]{1,0:T(8,128)(2,1)S(1)} %copy-done.1), custom_call_target="tpu_custom_call" | custom-call | flops 4026531840 | bytes 6291456 | tf_op jit(solution)/shard_map/place_rest/pallas_call | solution.py:47
  14.6 0.0 copy-start.5
  14.6 0.7 copy-done.5
  15.4 0.8 copy-done.7
  16.1 2.8 %collective-permute-start = (bf16[256,768]{1,0:T(8,128)(2,1)S(1)}, bf16[256,768]{1,0:T(8,128)(2,1)S(1)}, u32[]{:S(2)}, u32[]{:S(2)}) collective-permute-start(bf16[256,768]{1,0:T(8,128)(2,1)S(1)} %get-tuple-element.49), channel_id=1, source_target_pairs={{0,24},{8,16},{16,8},{24,0},{1,25},{9,17},{17,9},{25,1},{2,26},{10... | collective-permute-start | bytes 1179656 | tf_op jit(solution)/shard_map/ppermute | solution.py:378
  19.0 0.8 collective-permute-done.3.refs_1_
  19.7 1.0 %copy-done.8 = bf16[256,768]{1,0:T(8,128)(2,1)S(1)} copy-done((bf16[256,768]{1,0:T(8,128)(2,1)S(1)}, bf16[256,768]{1,0:T(8,128)(2,1)}, u32[]{:S(2)}) %copy-start.8) | copy-done | bytes 393240
  20.7 1.6 %begin_0.1.refs_1_ = f32[2312,128]{1,0:T(8,128)S(1)} custom-call(bf16[256,768]{1,0:T(8,128)(2,1)S(1)} %copy-done.8, bf16[256,768]{1,0:T(8,128)(2,1)} %collective-permute-done.3.refs_1_), custom_call_target="tpu_custom_call" | custom-call | flops 603979776 | bytes 1179648 | tf_op jit(solution)/shard_map/begin_0/pallas_call | solution.py:47
  22.4 0.0 copy-start.6
  22.4 5.6 %collective-permute-done.4.refs_2_ = bf16[256,768]{1,0:T(8,128)(2,1)S(1)} collective-permute-done((bf16[256,768]{1,0:T(8,128)(2,1)S(1)}, bf16[256,768]{1,0:T(8,128)(2,1)S(1)}, u32[]{:S(2)}, u32[]{:S(2)}) %collective-permute-start.4) | collective-permute-done | bytes 393248 | tf_op jit(solution)/shard_map/ppermute | solution.py:378
  28.0 0.7 collective-permute-done.5.refs_3_
  28.6 0.8 gram_0.1
  29.4 0.1 collective-permute-start.6
  29.5 0.5 collective-permute-start.7
  30.0 1.4 %collective-permute-start.1 = (bf16[256,768]{1,0:T(8,128)(2,1)S(1)}, bf16[256,768]{1,0:T(8,128)(2,1)S(1)}, u32[]{:S(2)}, u32[]{:S(2)}) collective-permute-start(bf16[256,768]{1,0:T(8,128)(2,1)S(1)} %get-tuple-element.50), channel_id=1, source_target_pairs={{0,16},{8,24},{16,0},{24,8},{1,17},{9,25},{17,1},{25,9},{2,18},{10... | collective-permute-start | bytes 1179656 | tf_op jit(solution)/shard_map/ppermute | solution.py:378
  31.4 0.6 collective-permute-start.2
  32.0 4.5 %collective-permute-done.refs_1_ = bf16[256,768]{1,0:T(8,128)(2,1)S(1)} collective-permute-done((bf16[256,768]{1,0:T(8,128)(2,1)S(1)}, bf16[256,768]{1,0:T(8,128)(2,1)S(1)}, u32[]{:S(2)}, u32[]{:S(2)}) %collective-permute-start) | collective-permute-done | bytes 393248 | tf_op jit(solution)/shard_map/ppermute | solution.py:378
  36.5 0.6 begin_1.1.refs_5_.refs_1_
  37.2 0.4 stage_0_1.1
  37.6 2.2 %collective-permute-start.8 = (s16[608,128]{1,0:T(8,128)(2,1)S(1)}, s16[608,128]{1,0:T(8,128)(2,1)S(1)}, u32[]{:S(2)}, u32[]{:S(2)}) collective-permute-start(s16[608,128]{1,0:T(8,128)(2,1)S(1)} %get-tuple-element.62), channel_id=1, source_target_pairs={{0,2},{1,3},{2,0},{3,1},{4,6},{5,7},{6,4},{7,5},{8,10},{9,11},{10,... | collective-permute-start | bytes 466952 | tf_op jit(solution)/shard_map/ppermute | solution.py:381
  39.7 3.2 %collective-permute-done.8.refs_3_ = s16[608,128]{1,0:T(8,128)(2,1)S(1)} collective-permute-done((s16[608,128]{1,0:T(8,128)(2,1)S(1)}, s16[608,128]{1,0:T(8,128)(2,1)S(1)}, u32[]{:S(2)}, u32[]{:S(2)}) %collective-permute-start.8) | collective-permute-done | bytes 155680 | tf_op jit(solution)/shard_map/ppermute | solution.py:381
  42.9 0.6 stage_0_2.1
  43.5 3.1 %collective-permute-start.13 = (s16[608,128]{1,0:T(8,128)(2,1)S(1)}, s16[608,128]{1,0:T(8,128)(2,1)S(1)}, u32[]{:S(2)}, u32[]{:S(2)}) collective-permute-start(s16[608,128]{1,0:T(8,128)(2,1)S(1)} %get-tuple-element.63.refs_4_), channel_id=1, source_target_pairs={{0,4},{1,5},{2,6},{3,7},{4,0},{5,1},{6,2},{7,3},{8,12},{9,13},{10,... | collective-permute-start | bytes 466952 | tf_op jit(solution)/shard_map/ppermute | solution.py:381
  46.6 0.0 collective-permute-done.1.refs_2_
  46.6 0.0 collective-permute-done.2.refs_3_
  46.7 0.8 gram_1.1
  47.5 0.1 collective-permute-start.9
  47.5 0.5 collective-permute-start.10
  48.0 0.1 collective-permute-start.11
  48.1 0.4 collective-permute-start.12
  48.5 3.0 %collective-permute-done.13.refs_3_ = s16[608,128]{1,0:T(8,128)(2,1)S(1)} collective-permute-done((s16[608,128]{1,0:T(8,128)(2,1)S(1)}, s16[608,128]{1,0:T(8,128)(2,1)S(1)}, u32[]{:S(2)}, u32[]{:S(2)}) %collective-permute-start.13) | collective-permute-done | bytes 155680 | tf_op jit(solution)/shard_map/ppermute | solution.py:381
  51.5 0.5 total_0.1
  52.1 0.0 collective-permute-done.12.refs_6_
  52.1 0.0 collective-permute-done.9.refs_3_
  52.1 0.4 stage_1_1.1
  52.5 1.1 %collective-permute-start.14 = (s16[608,128]{1,0:T(8,128)(2,1)S(1)}, s16[608,128]{1,0:T(8,128)(2,1)S(1)}, u32[]{:S(2)}, u32[]{:S(2)}) collective-permute-start(s16[608,128]{1,0:T(8,128)(2,1)S(1)} %get-tuple-element.75), channel_id=1, source_target_pairs={{0,2},{1,3},{2,0},{3,1},{4,6},{5,7},{6,4},{7,5},{8,10},{9,11},{10,... | collective-permute-start | bytes 466952 | tf_op jit(solution)/shard_map/ppermute | solution.py:381
  53.6 1.0 %collective-permute-start.16 = (s16[592,128]{1,0:T(8,128)(2,1)S(1)}, s16[592,128]{1,0:T(8,128)(2,1)S(1)}, u32[]{:S(2)}, u32[]{:S(2)}) collective-permute-start(s16[592,128]{1,0:T(8,128)(2,1)S(1)} %get-tuple-element.72.refs_7_.refs_2_), channel_id=1, source_target_pairs={{0,2},{1,3},{2,0},{3,1},{4,6},{5,7},{6,4},{7,5},{8,10},{9,11},{10,... | collective-permute-start | bytes 454664 | tf_op jit(solution)/shard_map/ppermute | solution.py:381
  54.6 3.4 %collective-permute-done.14.refs_3_ = s16[608,128]{1,0:T(8,128)(2,1)S(1)} collective-permute-done((s16[608,128]{1,0:T(8,128)(2,1)S(1)}, s16[608,128]{1,0:T(8,128)(2,1)S(1)}, u32[]{:S(2)}, u32[]{:S(2)}) %collective-permute-start.14) | collective-permute-done | bytes 155680 | tf_op jit(solution)/shard_map/ppermute | solution.py:381
  58.0 0.6 stage_1_2.1
  58.6 0.0 copy-start.2
  58.6 0.0 copy-start.3
  58.6 2.4 %collective-permute-start.15 = (s16[608,128]{1,0:T(8,128)(2,1)S(1)}, s16[608,128]{1,0:T(8,128)(2,1)S(1)}, u32[]{:S(2)}, u32[]{:S(2)}) collective-permute-start(s16[608,128]{1,0:T(8,128)(2,1)S(1)} %get-tuple-element.78), channel_id=1, source_target_pairs={{0,4},{1,5},{2,6},{3,7},{4,0},{5,1},{6,2},{7,3},{8,12},{9,13},{10,... | collective-permute-start | bytes 466952 | tf_op jit(solution)/shard_map/ppermute | solution.py:381
  61.0 0.0 collective-permute-start.17
  61.0 0.1 collective-permute-done.16.refs_3_
  61.0 0.4 collective-permute-start.18
  61.5 0.9 %collective-permute-done.17.refs_4_ = s16[592,128]{1,0:T(8,128)(2,1)S(1)} collective-permute-done((s16[592,128]{1,0:T(8,128)(2,1)S(1)}, s16[592,128]{1,0:T(8,128)(2,1)S(1)}, u32[]{:S(2)}, u32[]{:S(2)}) %collective-permute-start.17) | collective-permute-done | bytes 151584 | tf_op jit(solution)/shard_map/ppermute | solution.py:381
  62.3 0.2 collective-permute-done.18.refs_5_
  62.6 0.9 %unpack_0.1 = (bf16[768,768]{1,0:T(8,128)(2,1)S(1)}, bf16[768,768]{1,0:T(8,128)(2,1)S(1)}) custom-call(s32[1]{0:T(128)} %bitcast.refs_0_, f32[8,128]{1,0:T(8,128)S(1)} %get-tuple-element.79.refs_1_.refs_0_, s16[592,128]{1,0:T(8,128)(2,1)S(1)} %get-tuple-element.72.refs_7_.refs_2_, s16[592,128]{1,0:T(8,128)(2,1)S(1)} %collective-permute-done.16.refs_3_, ...), custom_call_target="tpu_custom_call" | custom-call | bytes 1179648 | tf_op jit(solution)/shard_map/unpack_0/pallas_call | solution.py:47
  63.5 1.3 %collective-permute-done.15.refs_3_ = s16[608,128]{1,0:T(8,128)(2,1)S(1)} collective-permute-done((s16[608,128]{1,0:T(8,128)(2,1)S(1)}, s16[608,128]{1,0:T(8,128)(2,1)S(1)}, u32[]{:S(2)}, u32[]{:S(2)}) %collective-permute-start.15) | collective-permute-done | bytes 155680 | tf_op jit(solution)/shard_map/ppermute | solution.py:381
  64.8 0.6 total_1.1
  65.4 0.1 collective-permute-start.20
  65.4 2.5 %collective-permute-start.19 = (s16[592,128]{1,0:T(8,128)(2,1)S(1)}, s16[592,128]{1,0:T(8,128)(2,1)S(1)}, u32[]{:S(2)}, u32[]{:S(2)}) collective-permute-start(s16[592,128]{1,0:T(8,128)(2,1)S(1)} %get-tuple-element.82.refs_5_.refs_2_), channel_id=1, source_target_pairs={{0,2},{1,3},{2,0},{3,1},{4,6},{5,7},{6,4},{7,5},{8,10},{9,11},{10,... | collective-permute-start | bytes 454664 | tf_op jit(solution)/shard_map/ppermute | solution.py:381
  68.0 5.0 %sweeps_0.1 = (f32[2,256,768]{2,1,0:T(8,128)}, f32[8,128]{1,0:T(8,128)S(1)}) custom-call(f32[8,128]{1,0:T(8,128)S(1)} %get-tuple-element.79.refs_1_.refs_0_, bf16[2,256,768]{2,1,0:T(8,128)(2,1)S(1)} %copy-done.2, bf16[2,256,768]{2,1,0:T(8,128)(2,1)S(1)} %copy-done.3, bf16[768,768]{1,0:T(8,128)(2,1)S(1)} %get-tuple-element.80.refs_4_.refs_3_, ...), custom_call_target="tpu_custom_call" | custom-call | flops 3623878656 | bytes 2359296 | tf_op jit(solution)/shard_map/sweeps_0/pallas_call | solution.py:47
  73.0 0.0 collective-permute-done.19.refs_0_
  73.1 0.2 collective-permute-start.21
  73.3 1.2 %collective-permute-done.21.refs_5_ = s16[592,128]{1,0:T(8,128)(2,1)S(1)} collective-permute-done((s16[592,128]{1,0:T(8,128)(2,1)S(1)}, s16[592,128]{1,0:T(8,128)(2,1)S(1)}, u32[]{:S(2)}, u32[]{:S(2)}) %collective-permute-start.21) | collective-permute-done | bytes 151584 | tf_op jit(solution)/shard_map/ppermute | solution.py:381
  74.5 0.7 unpack_1.1
  75.2 5.6 %sweeps_1.1 = (f32[2,256,768]{2,1,0:T(8,128)}, f32[8,128]{1,0:T(8,128)}) custom-call(f32[8,128]{1,0:T(8,128)S(1)} %get-tuple-element.81.refs_1_.refs_0_, bf16[2,256,768]{2,1,0:T(8,128)(2,1)S(1)} %copy-done.2, bf16[2,256,768]{2,1,0:T(8,128)(2,1)S(1)} %copy-done.3, bf16[768,768]{1,0:T(8,128)(2,1)S(1)} %get-tuple-element.85.refs_3_, ...), custom_call_target="tpu_custom_call", output_to_operand_aliasing={{0}: (5, {})} | custom-call | flops 3623878656 | bytes 2359296 | tf_op jit(solution)/shard_map/sweeps_1/pallas_call | solution.py:47
  (15 shorter events, 0.0 us)
Async XLA Ops:
  0.0 1.9 %copy-start = (bf16[2048,768]{1,0:T(8,128)(2,1)S(1)}, bf16[2048,768]{1,0:T(8,128)(2,1)}, u32[]{:S(2)}) copy-start(bf16[2048,768]{1,0:T(8,128)(2,1)} %refs_2_.5) | copy-start | bytes 9437188
  1.9 0.7 copy-start.4
  2.6 7.7 %copy-start.1 = (bf16[2048,768]{1,0:T(8,128)(2,1)S(1)}, bf16[2048,768]{1,0:T(8,128)(2,1)}, u32[]{:S(2)}) copy-start(bf16[2048,768]{1,0:T(8,128)(2,1)} %refs_2_.5) | copy-start | bytes 9437188
  5.7 14.1 %collective-permute-start.3 = (bf16[256,768]{1,0:T(8,128)(2,1)S(1)}, bf16[256,768]{1,0:T(8,128)(2,1)}, u32[]{:S(2)}, u32[]{:S(2)}) collective-permute-start(bf16[256,768]{1,0:T(8,128)(2,1)S(1)} %get-tuple-element.53), channel_id=1, source_target_pairs={{0,24},{8,16},{16,8},{24,0},{1,25},{9,17},{17,9},{25,1},{2,26},{10... | collective-permute-start | bytes 1179656 | tf_op jit(solution)/shard_map/ppermute | solution.py:378
  9.6 18.3 %collective-permute-start.4 = (bf16[256,768]{1,0:T(8,128)(2,1)S(1)}, bf16[256,768]{1,0:T(8,128)(2,1)S(1)}, u32[]{:S(2)}, u32[]{:S(2)}) collective-permute-start(bf16[256,768]{1,0:T(8,128)(2,1)S(1)} %get-tuple-element.54), channel_id=1, source_target_pairs={{0,16},{8,24},{16,0},{24,8},{1,17},{9,25},{17,1},{25,9},{2,18},{10... | collective-permute-start | bytes 1179656 | tf_op jit(solution)/shard_map/ppermute | solution.py:378
  10.2 18.5 %collective-permute-start.5 = (bf16[256,768]{1,0:T(8,128)(2,1)S(1)}, bf16[256,768]{1,0:T(8,128)(2,1)S(1)}, u32[]{:S(2)}, u32[]{:S(2)}) collective-permute-start(bf16[256,768]{1,0:T(8,128)(2,1)S(1)} %get-tuple-element.55), channel_id=1, source_target_pairs={{0,8},{8,0},{16,24},{24,16},{1,9},{9,1},{17,25},{25,17},{2,10},{10... | collective-permute-start | bytes 1179656 | tf_op jit(solution)/shard_map/ppermute | solution.py:378
  14.6 0.7 copy-start.5
  15.4 0.8 copy-start.7
  16.1 20.4 %collective-permute-start = (bf16[256,768]{1,0:T(8,128)(2,1)S(1)}, bf16[256,768]{1,0:T(8,128)(2,1)S(1)}, u32[]{:S(2)}, u32[]{:S(2)}) collective-permute-start(bf16[256,768]{1,0:T(8,128)(2,1)S(1)} %get-tuple-element.49), channel_id=1, source_target_pairs={{0,24},{8,16},{16,8},{24,0},{1,25},{9,17},{17,9},{25,1},{2,26},{10... | collective-permute-start | bytes 1179656 | tf_op jit(solution)/shard_map/ppermute | solution.py:378
  19.7 1.0 %copy-start.8 = (bf16[256,768]{1,0:T(8,128)(2,1)S(1)}, bf16[256,768]{1,0:T(8,128)(2,1)}, u32[]{:S(2)}) copy-start(bf16[256,768]{1,0:T(8,128)(2,1)} %copy-done.7) | copy-start | bytes 1179652
  22.4 14.2 %copy-start.6 = (bf16[256,768]{1,0:T(8,128)(2,1)S(1)}, bf16[256,768]{1,0:T(8,128)(2,1)}, u32[]{:S(2)}) copy-start(bf16[256,768]{1,0:T(8,128)(2,1)} %copy-done.5) | copy-start | bytes 1179652
  29.4 7.7 %collective-permute-start.6 = (f32[584,128]{1,0:T(8,128)S(1)}, f32[584,128]{1,0:T(8,128)S(1)}, u32[]{:S(2)}, u32[]{:S(2)}) collective-permute-start(f32[584,128]{1,0:T(8,128)S(1)} %get-tuple-element.58), channel_id=1, source_target_pairs={{0,1},{1,0},{2,3},{3,2},{4,5},{5,4},{6,7},{7,6},{8,9},{9,8},{10,11... | collective-permute-start | bytes 897032 | tf_op jit(solution)/shard_map/ppermute | solution.py:381
  29.5 7.7 %collective-permute-start.7 = (f32[576,128]{1,0:T(8,128)S(1)}, f32[576,128]{1,0:T(8,128)S(1)}, u32[]{:S(2)}, u32[]{:S(2)}) collective-permute-start(f32[576,128]{1,0:T(8,128)S(1)} %get-tuple-element.59), channel_id=1, source_target_pairs={{0,1},{1,0},{2,3},{3,2},{4,5},{5,4},{6,7},{7,6},{8,9},{9,8},{10,11... | collective-permute-start | bytes 884744 | tf_op jit(solution)/shard_map/ppermute | solution.py:381
  30.0 16.6 %collective-permute-start.1 = (bf16[256,768]{1,0:T(8,128)(2,1)S(1)}, bf16[256,768]{1,0:T(8,128)(2,1)S(1)}, u32[]{:S(2)}, u32[]{:S(2)}) collective-permute-start(bf16[256,768]{1,0:T(8,128)(2,1)S(1)} %get-tuple-element.50), channel_id=1, source_target_pairs={{0,16},{8,24},{16,0},{24,8},{1,17},{9,25},{17,1},{25,9},{2,18},{10... | collective-permute-start | bytes 1179656 | tf_op jit(solution)/shard_map/ppermute | solution.py:378
  31.4 15.3 %collective-permute-start.2 = (bf16[256,768]{1,0:T(8,128)(2,1)S(1)}, bf16[256,768]{1,0:T(8,128)(2,1)S(1)}, u32[]{:S(2)}, u32[]{:S(2)}) collective-permute-start(bf16[256,768]{1,0:T(8,128)(2,1)S(1)} %get-tuple-element.51), channel_id=1, source_target_pairs={{0,8},{8,0},{16,24},{24,16},{1,9},{9,1},{17,25},{25,17},{2,10},{10... | collective-permute-start | bytes 1179656 | tf_op jit(solution)/shard_map/ppermute | solution.py:378
  37.6 5.4 %collective-permute-start.8 = (s16[608,128]{1,0:T(8,128)(2,1)S(1)}, s16[608,128]{1,0:T(8,128)(2,1)S(1)}, u32[]{:S(2)}, u32[]{:S(2)}) collective-permute-start(s16[608,128]{1,0:T(8,128)(2,1)S(1)} %get-tuple-element.62), channel_id=1, source_target_pairs={{0,2},{1,3},{2,0},{3,1},{4,6},{5,7},{6,4},{7,5},{8,10},{9,11},{10,... | collective-permute-start | bytes 466952 | tf_op jit(solution)/shard_map/ppermute | solution.py:381
  43.5 8.0 %collective-permute-start.13 = (s16[608,128]{1,0:T(8,128)(2,1)S(1)}, s16[608,128]{1,0:T(8,128)(2,1)S(1)}, u32[]{:S(2)}, u32[]{:S(2)}) collective-permute-start(s16[608,128]{1,0:T(8,128)(2,1)S(1)} %get-tuple-element.63.refs_4_), channel_id=1, source_target_pairs={{0,4},{1,5},{2,6},{3,7},{4,0},{5,1},{6,2},{7,3},{8,12},{9,13},{10,... | collective-permute-start | bytes 466952 | tf_op jit(solution)/shard_map/ppermute | solution.py:381
  47.5 4.7 %collective-permute-start.9 = (f32[296,128]{1,0:T(8,128)S(1)}, f32[296,128]{1,0:T(8,128)S(1)}, u32[]{:S(2)}, u32[]{:S(2)}) collective-permute-start(f32[296,128]{1,0:T(8,128)S(1)} %get-tuple-element.66), channel_id=1, source_target_pairs={{0,1},{1,0},{2,3},{3,2},{4,5},{5,4},{6,7},{7,6},{8,9},{9,8},{10,11... | collective-permute-start | bytes 454664 | tf_op jit(solution)/shard_map/ppermute | solution.py:381
  47.5 4.5 %collective-permute-start.10 = (f32[288,128]{1,0:T(8,128)S(1)}, f32[288,128]{1,0:T(8,128)S(1)}, u32[]{:S(2)}, u32[]{:S(2)}) collective-permute-start(f32[288,128]{1,0:T(8,128)S(1)} %get-tuple-element.67), channel_id=1, source_target_pairs={{0,1},{1,0},{2,3},{3,2},{4,5},{5,4},{6,7},{7,6},{8,9},{9,8},{10,11... | collective-permute-start | bytes 442376 | tf_op jit(solution)/shard_map/ppermute | solution.py:381
  48.0 4.1 %collective-permute-start.11 = (f32[288,128]{1,0:T(8,128)S(1)}, f32[288,128]{1,0:T(8,128)S(1)}, u32[]{:S(2)}, u32[]{:S(2)}) collective-permute-start(f32[288,128]{1,0:T(8,128)S(1)} %get-tuple-element.68), channel_id=1, source_target_pairs={{0,1},{1,0},{2,3},{3,2},{4,5},{5,4},{6,7},{7,6},{8,9},{9,8},{10,11... | collective-permute-start | bytes 442376 | tf_op jit(solution)/shard_map/ppermute | solution.py:381
  48.1 4.0 %collective-permute-start.12 = (f32[288,128]{1,0:T(8,128)S(1)}, f32[288,128]{1,0:T(8,128)S(1)}, u32[]{:S(2)}, u32[]{:S(2)}) collective-permute-start(f32[288,128]{1,0:T(8,128)S(1)} %get-tuple-element.69), channel_id=1, source_target_pairs={{0,1},{1,0},{2,3},{3,2},{4,5},{5,4},{6,7},{7,6},{8,9},{9,8},{10,11... | collective-permute-start | bytes 442376 | tf_op jit(solution)/shard_map/ppermute | solution.py:381
  52.5 5.4 %collective-permute-start.14 = (s16[608,128]{1,0:T(8,128)(2,1)S(1)}, s16[608,128]{1,0:T(8,128)(2,1)S(1)}, u32[]{:S(2)}, u32[]{:S(2)}) collective-permute-start(s16[608,128]{1,0:T(8,128)(2,1)S(1)} %get-tuple-element.75), channel_id=1, source_target_pairs={{0,2},{1,3},{2,0},{3,1},{4,6},{5,7},{6,4},{7,5},{8,10},{9,11},{10,... | collective-permute-start | bytes 466952 | tf_op jit(solution)/shard_map/ppermute | solution.py:381
  53.6 7.5 %collective-permute-start.16 = (s16[592,128]{1,0:T(8,128)(2,1)S(1)}, s16[592,128]{1,0:T(8,128)(2,1)S(1)}, u32[]{:S(2)}, u32[]{:S(2)}) collective-permute-start(s16[592,128]{1,0:T(8,128)(2,1)S(1)} %get-tuple-element.72.refs_7_.refs_2_), channel_id=1, source_target_pairs={{0,2},{1,3},{2,0},{3,1},{4,6},{5,7},{6,4},{7,5},{8,10},{9,11},{10,... | collective-permute-start | bytes 454664 | tf_op jit(solution)/shard_map/ppermute | solution.py:381
  58.6 9.4 %copy-start.2 = (bf16[2,256,768]{2,1,0:T(8,128)(2,1)S(1)}, bf16[2,256,768]{2,1,0:T(8,128)(2,1)}, u32[]{:S(2)}) copy-start(bf16[2,256,768]{2,1,0:T(8,128)(2,1)} %refs_1_.3) | copy-start | bytes 2359300
  58.6 9.4 %copy-start.3 = (bf16[2,256,768]{2,1,0:T(8,128)(2,1)S(1)}, bf16[2,256,768]{2,1,0:T(8,128)(2,1)}, u32[]{:S(2)}) copy-start(bf16[2,256,768]{2,1,0:T(8,128)(2,1)} %refs_2_.7) | copy-start | bytes 2359300
  58.6 6.2 %collective-permute-start.15 = (s16[608,128]{1,0:T(8,128)(2,1)S(1)}, s16[608,128]{1,0:T(8,128)(2,1)S(1)}, u32[]{:S(2)}, u32[]{:S(2)}) collective-permute-start(s16[608,128]{1,0:T(8,128)(2,1)S(1)} %get-tuple-element.78), channel_id=1, source_target_pairs={{0,4},{1,5},{2,6},{3,7},{4,0},{5,1},{6,2},{7,3},{8,12},{9,13},{10,... | collective-permute-start | bytes 466952 | tf_op jit(solution)/shard_map/ppermute | solution.py:381
  61.0 1.4 %collective-permute-start.17 = (s16[592,128]{1,0:T(8,128)(2,1)S(1)}, s16[592,128]{1,0:T(8,128)(2,1)S(1)}, u32[]{:S(2)}, u32[]{:S(2)}) collective-permute-start(s16[592,128]{1,0:T(8,128)(2,1)S(1)} %get-tuple-element.72.refs_7_.refs_2_), channel_id=1, source_target_pairs={{0,1},{1,0},{2,3},{3,2},{4,5},{5,4},{6,7},{7,6},{8,9},{9,8},{10,11... | collective-permute-start | bytes 454664 | tf_op jit(solution)/shard_map/ppermute | solution.py:381
  61.0 1.5 %collective-permute-start.18 = (s16[592,128]{1,0:T(8,128)(2,1)S(1)}, s16[592,128]{1,0:T(8,128)(2,1)S(1)}, u32[]{:S(2)}, u32[]{:S(2)}) collective-permute-start(s16[592,128]{1,0:T(8,128)(2,1)S(1)} %collective-permute-done.16.refs_3_), channel_id=1, source_target_pairs={{0,1},{1,0},{2,3},{3,2},{4,5},{5,4},{6,7},{7,6},{8,9},{9,8},{10,11... | collective-permute-start | bytes 454664 | tf_op jit(solution)/shard_map/ppermute | solution.py:381
  65.4 7.9 %collective-permute-start.20 = (s16[592,128]{1,0:T(8,128)(2,1)S(1)}, s16[592,128]{1,0:T(8,128)(2,1)S(1)}, u32[]{:S(2)}, u32[]{:S(2)}) collective-permute-start(s16[592,128]{1,0:T(8,128)(2,1)S(1)} %get-tuple-element.82.refs_5_.refs_2_), channel_id=1, source_target_pairs={{0,1},{1,0},{2,3},{3,2},{4,5},{5,4},{6,7},{7,6},{8,9},{9,8},{10,11... | collective-permute-start | bytes 454664 | tf_op jit(solution)/shard_map/ppermute | solution.py:381
  65.4 7.6 %collective-permute-start.19 = (s16[592,128]{1,0:T(8,128)(2,1)S(1)}, s16[592,128]{1,0:T(8,128)(2,1)S(1)}, u32[]{:S(2)}, u32[]{:S(2)}) collective-permute-start(s16[592,128]{1,0:T(8,128)(2,1)S(1)} %get-tuple-element.82.refs_5_.refs_2_), channel_id=1, source_target_pairs={{0,2},{1,3},{2,0},{3,1},{4,6},{5,7},{6,4},{7,5},{8,10},{9,11},{10,... | collective-permute-start | bytes 454664 | tf_op jit(solution)/shard_map/ppermute | solution.py:381
  73.1 1.4 %collective-permute-start.21 = (s16[592,128]{1,0:T(8,128)(2,1)S(1)}, s16[592,128]{1,0:T(8,128)(2,1)S(1)}, u32[]{:S(2)}, u32[]{:S(2)}) collective-permute-start(s16[592,128]{1,0:T(8,128)(2,1)S(1)} %relay.1.refs_3_), channel_id=1, source_target_pairs={{0,1},{1,0},{2,3},{3,2},{4,5},{5,4},{6,7},{7,6},{8,9},{9,8},{10,11... | collective-permute-start | bytes 454664 | tf_op jit(solution)/shard_map/ppermute | solution.py:381

commit v9 on v8

--- a/solution.py
+++ b/solution.py
@@ -11,13 +11,15 @@
 BLOCK = 128
 TILE = 16
 PARTS = 4
+COPIES = 8
 WIDTH = 2 * BLOCK
 LEVELS = 32760.0
 OCTAVE = 8.0
 relax_factor = 0.5
 diagonal_eps = 1e-06
 tiny = 1e-30
-VMEM_LIMIT = 32 * 2**20
+VMEM_LIMIT = 24
+PLACE_LIMITS = (50, 50)
 
 VMEM = pl.BlockSpec(memory_space=pltpu.VMEM)
 ANY = pl.BlockSpec(memory_space=pl.ANY)
@@ -26,7 +28,7 @@
 F32, BF16, I32, I16 = jnp.float32, jnp.bfloat16, jnp.int32, jnp.int16
 
 
-def call(kernel, out_shape, in_specs, scratch=(), flops=0, moved=0, out_specs=None, aliases=None, name=None, after=()):
+def call(kernel, out_shape, in_specs, scratch=(), flops=0, moved=0, out_specs=None, aliases=None, name=None, after=(), limit=VMEM_LIMIT):
     many = isinstance(out_shape, (list, tuple))
     used, idle = len(in_specs), len(after)
 
@@ -41,7 +43,7 @@
         scratch_shapes=list(scratch),
         input_output_aliases=aliases or {},
         cost_estimate=pl.CostEstimate(flops=flops, bytes_accessed=moved, transcendentals=0),
-        compiler_params=pltpu.CompilerParams(vmem_limit_bytes=VMEM_LIMIT),
+        compiler_params=pltpu.CompilerParams(vmem_limit_bytes=limit * 2**20),
         name=name,
     )
     return lambda *args: inner(*args, *after)
@@ -80,30 +82,47 @@
     )
     for c in range(0, hidden, WIDTH):
         got = jnp.dot(chosen, rows_ref[:, c:c + WIDTH], preferred_element_type=F32).astype(BF16)
-        for k, out_ref in enumerate(out_refs):
-            out_ref[:, c:c + WIDTH] = got[k * capacity:(k + 1) * capacity]
+        start = 0
+        for out_ref in out_refs:
+            out_ref[:, c:c + WIDTH] = got[start:start + out_ref.shape[0]]
+            start += out_ref.shape[0]
 
 
 def others(peers):
     return range(peers - 1, 0, -1)
+
+
+def bring(rows_any, rows_ref, done):
+    count = done.shape[0]
+    part = rows_ref.shape[0] // count
+    copies = []
+    for n in range(count):
+        rows = pl.ds(n * part, part)
+        copies.append(pltpu.make_async_copy(rows_any.at[rows], rows_ref.at[rows], done.at[n]))
+        copies[-1].start()
+    return copies
 
 
 def first_kernel(peers, slots, all_experts, capacity, me_ref, owner_any, rows_any, key_ref, *refs):
     out_refs, (owner_ref, rows_ref, owner_done, rows_done) = refs[:-4], refs[-4:]
     owner_copy = pltpu.make_async_copy(owner_any, owner_ref, owner_done)
     owner_copy.start()
-    rows_copy = pltpu.make_async_copy(rows_any, rows_ref, rows_done)
-    rows_copy.start()
+    rows_copies = bring(rows_any, rows_ref, rows_done)
     me = me_ref[0]
     owner_copy.wait()
     key = slots_of(owner_ref[...], all_experts, capacity)
     key_ref[...] = key
-    rows_copy.wait()
+    for copy in rows_copies:
+        copy.wait()
     place(key, rows_ref, [lax.bitwise_xor(me, k) * slots for k in others(peers)], capacity, out_refs)
 
 
-def second_kernel(peers, slots, capacity, me_ref, key_ref, rows_ref, *out_refs):
+def second_kernel(peers, slots, capacity, me_ref, key_ref, rows_any, *refs):
+    out_refs, (rows_ref, rows_done) = refs[:-2], refs[-2:]
+    rows_copies = bring(rows_any, rows_ref, rows_done)
     me = me_ref[0]
+    for copy in rows_copies:
+        copy.wait()
     where = [(0, a) for a in range(slots)] + [(k, a) for a in range(1, slots) for k in others(peers)]
     place(key_ref[...], rows_ref, [lax.bitwise_xor(me, k) * slots + a for k, a in where], capacity, out_refs)
 
@@ -387,20 +406,24 @@
         [shape(1, tokens, I32)] + [chunk] * (peers - 1), [SMEM, HBM, HBM],
         scratch=[
             pltpu.VMEM((1, tokens), I32), pltpu.VMEM((tokens, hidden), BF16),
-            pltpu.SemaphoreType.DMA, pltpu.SemaphoreType.DMA,
+            pltpu.SemaphoreType.DMA, pltpu.SemaphoreType.DMA((COPIES,)),
         ],
-        flops=place_flops * (peers - 1), moved=expert_inputs.size * 4, name="place_first",
+        flops=place_flops * (peers - 1), moved=expert_inputs.size * 4, name="place_first", limit=PLACE_LIMITS[0],
     )(me, owners, expert_inputs)
     arrived = [[over_experts(rows, k) for rows, k in zip(outgoing, others(peers))]]
     count = slots + (slots - 1) * (peers - 1)
+    parts = [shape(n, hidden, BF16) for n in cuts(capacity, 2)]
+    flips = [peers - 1, *others(peers)]
     rest = call(
-        functools.partial(second_kernel, peers, slots, capacity), [chunk] * count, [SMEM, VMEM, VMEM],
-        flops=place_flops * count, moved=expert_inputs.size * 4, name="place_rest",
+        functools.partial(second_kernel, peers, slots, capacity),
+        [chunk] * slots + (parts + [chunk] * (peers - 2)) * (slots - 1), [SMEM, VMEM, HBM],
+        scratch=[pltpu.VMEM((tokens, hidden), BF16), pltpu.SemaphoreType.DMA((COPIES,))],
+        flops=place_flops * count, moved=expert_inputs.size * 4, name="place_rest", limit=PLACE_LIMITS[1],
     )(me, key, expert_inputs)
     own = rest[:slots]
     for a in range(1, slots):
-        outgoing = rest[slots + (a - 1) * (peers - 1):slots + a * (peers - 1)]
-        arrived.append([over_experts(rows, k) for rows, k in zip(outgoing, others(peers))])
+        outgoing = rest[slots + (a - 1) * peers:slots + a * peers]
+        arrived.append([over_experts(rows, k) for rows, k in zip(outgoing, flips)])
 
     many = diagonal_rows(hidden)
     notes = -(-(8 + 3 * many) // TILE) * TILE
@@ -425,11 +448,11 @@
 
     def reduce(a, before, after, behind):
         size = length // 2
-        sizes = cuts(size, PARTS if a == slots - 1 else 2)
+        sizes = cuts(size, PARTS if a == slots - 1 else 3)
         keep, diagonal, *sent = call(
-            functools.partial(late_gram_kernel, halvings, peers - 2),
+            functools.partial(late_gram_kernel, halvings, len(arrived[a]) - 1),
             [shape(size), shape(many)] + [shape(n + (many if i == 0 else 0)) for i, n in enumerate(sizes)],
-            [SMEM] + [VMEM] * (peers - 1), scratch=[pltpu.VMEM((length + many, BLOCK), F32)],
+            [SMEM] + [VMEM] * len(arrived[a]), scratch=[pltpu.VMEM((length + many, BLOCK), F32)],
             name=f"gram_{a}", after=after,
         )(where, before, *arrived[a][1:])
         for bit in range(1, halvings + 1):

time: 81.3 us -> 83.4 us (1.026)
  Pallas kernels: 26.6 us -> 29.4 us
  local copies, waits for them, and re-layouts: 5.11 us -> 3.19 us
  waiting for transfers between devices: 24.9 us -> 26.7 us
    ppermute x16 -> x17, waiting for transfers between devices: 13.3 us -> 19.2 us  [over_rows(): lax.ppermute(array, 'rows', [(i, i ^ 1 << bit) for i in range(copies)])]
    ppermute x6 -> x7, waiting for transfers between devices: 11.6 us -> 7.5 us  [over_experts(): return lax.ppermute(array, 'expert', [(i, i ^ flip) for i in range(peers)])]
    pallas_call x17, Pallas kernels: 26.6 us -> 29.4 us  [call(): return lambda *args: inner(*args, *after)]
    ppermute x16 -> x17, starting transfers between devices: 14.6 us -> 11.9 us  [over_rows(): lax.ppermute(array, 'rows', [(i, i ^ 1 << bit) for i in range(copies)])]
    ppermute x6 -> x7, starting transfers between devices: 9.44 us -> 11.5 us  [over_experts(): return lax.ppermute(array, 'expert', [(i, i ^ flip) for i in range(peers)])]
    unnamed x18 -> x14, local copies, waits for them, and re-layouts: 5.11 us -> 3.19 us
  transfers between devices with their start and end apart: 22 -> 24, of which waited for: 12 -> 11; matrix products, arithmetic and copies ran while one was open for 0% -> 0% of each run, Pallas kernels for 20% -> 21%
where the time goes in v9:
time: 83.4 us; the launch traced here: 83.2 us
  Pallas kernels  29.4 us (35%)
  waiting for transfers between devices  26.7 us (32%)
  starting transfers between devices  23.4 us (28%)
  local copies, waits for them, and re-layouts  3.19 us (4%)
    pallas_call x17, Pallas kernels, call(): return lambda *args: inner(*args, *after)  29.4 us
    ppermute x17, waiting for transfers between devices, over_rows(): lax.ppermute(array, 'rows', [(i, i ^ 1 << bit) for i in range(copies)])  19.2 us
    ppermute x17, starting transfers between devices, over_rows(): lax.ppermute(array, 'rows', [(i, i ^ 1 << bit) for i in range(copies)])  11.9 us
    ppermute x7, starting transfers between devices, over_experts(): return lax.ppermute(array, 'expert', [(i, i ^ flip) for i in range(peers)])  11.5 us
    ppermute x7, waiting for transfers between devices, over_experts(): return lax.ppermute(array, 'expert', [(i, i ^ flip) for i in range(peers)])  7.5 us
    unnamed x14, local copies, waits for them, and re-layouts  3.19 us
  transfers between devices with their start and end apart: 24, of which 11 were waited for; matrix products, arithmetic and copies ran while one was open for 0% of the time, Pallas kernels for 21%

profile of v9, /device:TPU:0, one launch (start us, length us, event | category | flops | bytes accessed | tf_op | source)
XLA Modules:
  0.0 83.2 jit_solution(583178857935583452)
XLA Ops:
  0.0 0.7 copy-done.2
  0.7 4.5 %place_first.1 = (s32[1,2048]{1,0:T(1,128)S(1)}, bf16[256,768]{1,0:T(8,128)(2,1)S(1)}, bf16[256,768]{1,0:T(8,128)(2,1)S(1)}, bf16[256,768]{1,0:T(8,128)(2,1)S(1)}) custom-call(s32[1]{0:T(128)} %bitcast.1.refs_0_, s32[1,2048]{1,0:T(1,128)S(1)} %bitcast.3, bf16[2048,768]{1,0:T(8,128)(2,1)} %refs_2_.5), custom_call_target="tpu_custom_call" | custom-call | flops 2415919104 | bytes 6291456 | tf_op jit(solution)/shard_map/place_first/pallas_call | solution.py:49
  5.2 4.0 %collective-permute-start.4 = (bf16[256,768]{1,0:T(8,128)(2,1)S(1)}, bf16[256,768]{1,0:T(8,128)(2,1)S(1)}, u32[]{:S(2)}, u32[]{:S(2)}) collective-permute-start(bf16[256,768]{1,0:T(8,128)(2,1)S(1)} %get-tuple-element.56), channel_id=1, source_target_pairs={{0,24},{8,16},{16,8},{24,0},{1,25},{9,17},{17,9},{25,1},{2,26},{10... | collective-permute-start | bytes 1179656 | tf_op jit(solution)/shard_map/ppermute | solution.py:397
  9.2 0.5 collective-permute-start.5
  9.7 0.1 collective-permute-start.6
  9.8 6.7 %place_rest.1 = (bf16[256,768]{1,0:T(8,128)(2,1)S(1)}, bf16[256,768]{1,0:T(8,128)(2,1)S(1)}, bf16[128,768]{1,0:T(8,128)(2,1)}, bf16[128,768]{1,0:T(8,128)(2,1)S(...) custom-call(s32[1]{0:T(128)} %bitcast.1.refs_0_, s32[1,2048]{1,0:T(1,128)S(1)} %get-tuple-element.49.refs_1_, ...), custom_call_target="tpu_custom_call" | custom-call | flops 4026531840 | bytes 6291456 | tf_op jit(solution)/shard_map/place_rest/pallas_call | solution.py:49
  16.5 0.7 copy-done.3
  17.3 0.7 copy-done.5
  18.0 2.8 %collective-permute-start = (bf16[128,768]{1,0:T(8,128)(2,1)}, bf16[128,768]{1,0:T(8,128)(2,1)S(1)}, u32[]{:S(2)}, u32[]{:S(2)}) collective-permute-start(bf16[128,768]{1,0:T(8,128)(2,1)} %get-tuple-element.51), channel_id=1, source_target_pairs={{0,24},{8,16},{16,8},{24,0},{1,25},{9,17},{17,9},{25,1},{2,26},{10... | collective-permute-start | bytes 589832 | tf_op jit(solution)/shard_map/ppermute | solution.py:397
  20.9 1.0 %copy-done.4 = bf16[256,768]{1,0:T(8,128)(2,1)S(1)} copy-done((bf16[256,768]{1,0:T(8,128)(2,1)S(1)}, bf16[256,768]{1,0:T(8,128)(2,1)}, u32[]{:S(2)}) %copy-start.4) | copy-done | bytes 393240
  21.9 0.6 begin_0.1.refs_1_
  22.5 0.0 copy-start.6
  22.5 5.0 %collective-permute-done.5.refs_2_ = bf16[256,768]{1,0:T(8,128)(2,1)S(1)} collective-permute-done((bf16[256,768]{1,0:T(8,128)(2,1)S(1)}, bf16[256,768]{1,0:T(8,128)(2,1)S(1)}, u32[]{:S(2)}, u32[]{:S(2)}) %collective-permute-start.5) | collective-permute-done | bytes 393248 | tf_op jit(solution)/shard_map/ppermute | solution.py:397
  27.5 0.7 collective-permute-done.6.refs_3_
  28.2 0.8 gram_0.1
  29.0 0.1 collective-permute-start.8
  29.0 1.4 %collective-permute-start.2 = (bf16[256,768]{1,0:T(8,128)(2,1)S(1)}, bf16[256,768]{1,0:T(8,128)(2,1)S(1)}, u32[]{:S(2)}, u32[]{:S(2)}) collective-permute-start(bf16[256,768]{1,0:T(8,128)(2,1)S(1)} %get-tuple-element.53), channel_id=1, source_target_pairs={{0,16},{8,24},{16,0},{24,8},{1,17},{9,25},{17,1},{25,9},{2,18},{10... | collective-permute-start | bytes 1179656 | tf_op jit(solution)/shard_map/ppermute | solution.py:397
  30.5 0.6 collective-permute-start.3
  31.1 0.0 collective-permute-start.7
  31.1 0.0 collective-permute-done.refs_1_
  31.1 0.5 collective-permute-start.9
  31.6 0.0 collective-permute-done.8.refs_4_
  31.6 2.0 %collective-permute-start.1 = (bf16[128,768]{1,0:T(8,128)(2,1)S(1)}, bf16[128,768]{1,0:T(8,128)(2,1)S(1)}, u32[]{:S(2)}, u32[]{:S(2)}) collective-permute-start(bf16[128,768]{1,0:T(8,128)(2,1)S(1)} %get-tuple-element.52), channel_id=1, source_target_pairs={{0,24},{8,16},{16,8},{24,0},{1,25},{9,17},{17,9},{25,1},{2,26},{10... | collective-permute-start | bytes 589832 | tf_op jit(solution)/shard_map/ppermute | solution.py:397
  33.6 0.6 begin_1.1.refs_6_.refs_1_
  34.3 0.0 collective-permute-done.7.refs_3_
  34.3 0.4 stage_0_1.1
  34.7 1.6 %collective-permute-start.10 = (s16[608,128]{1,0:T(8,128)(2,1)S(1)}, s16[608,128]{1,0:T(8,128)(2,1)S(1)}, u32[]{:S(2)}, u32[]{:S(2)}) collective-permute-start(s16[608,128]{1,0:T(8,128)(2,1)S(1)} %get-tuple-element.66), channel_id=1, source_target_pairs={{0,2},{1,3},{2,0},{3,1},{4,6},{5,7},{6,4},{7,5},{8,10},{9,11},{10,... | collective-permute-start | bytes 466952 | tf_op jit(solution)/shard_map/ppermute | solution.py:400
  36.3 4.6 %collective-permute-done.10.refs_3_ = s16[608,128]{1,0:T(8,128)(2,1)S(1)} collective-permute-done((s16[608,128]{1,0:T(8,128)(2,1)S(1)}, s16[608,128]{1,0:T(8,128)(2,1)S(1)}, u32[]{:S(2)}, u32[]{:S(2)}) %collective-permute-start.10) | collective-permute-done | bytes 155680 | tf_op jit(solution)/shard_map/ppermute | solution.py:400
  40.9 0.6 stage_0_2.1
  41.5 2.7 %collective-permute-start.15 = (s16[608,128]{1,0:T(8,128)(2,1)S(1)}, s16[608,128]{1,0:T(8,128)(2,1)S(1)}, u32[]{:S(2)}, u32[]{:S(2)}) collective-permute-start(s16[608,128]{1,0:T(8,128)(2,1)S(1)} %get-tuple-element.67.refs_5_), channel_id=1, source_target_pairs={{0,4},{1,5},{2,6},{3,7},{4,0},{5,1},{6,2},{7,3},{8,12},{9,13},{10,... | collective-permute-start | bytes 466952 | tf_op jit(solution)/shard_map/ppermute | solution.py:400
  44.2 1.8 %collective-permute-done.1.refs_2_ = bf16[128,768]{1,0:T(8,128)(2,1)S(1)} collective-permute-done((bf16[128,768]{1,0:T(8,128)(2,1)S(1)}, bf16[128,768]{1,0:T(8,128)(2,1)S(1)}, u32[]{:S(2)}, u32[]{:S(2)}) %collective-permute-start.1) | collective-permute-done | bytes 196640 | tf_op jit(solution)/shard_map/ppermute | solution.py:397
  46.0 0.0 collective-permute-done.2.refs_3_
  46.0 1.1 %gram_1.1 = (f32[1152,128]{1,0:T(8,128)S(1)}, f32[8,128]{1,0:T(8,128)S(1)}, f32[296,128]{1,0:T(8,128)S(1)}, f32[288,128]{1,0:T(8,128)S(1)}, f32[288,128]{1,0:T(8,128)S(1)}, /*index=5*/f32[288,128]{1,0:T(8,128)S(1)}) custom-call(s32[1]{0:T(128)} %bitcast.refs_0_, f32[2312,128]{1,0:T(8,128)S(1)} %begin_1.1.refs_6_.refs_1_, ...), custom_call_target="tpu_custom_call" | custom-call | tf_op jit(solution)/shard_map/gram_1/pallas_call | solution.py:49
  47.0 0.1 collective-permute-start.11
  47.1 0.5 collective-permute-start.12
  47.6 0.1 collective-permute-start.13
  47.7 0.4 collective-permute-start.14
  48.1 3.0 %collective-permute-done.15.refs_3_ = s16[608,128]{1,0:T(8,128)(2,1)S(1)} collective-permute-done((s16[608,128]{1,0:T(8,128)(2,1)S(1)}, s16[608,128]{1,0:T(8,128)(2,1)S(1)}, u32[]{:S(2)}, u32[]{:S(2)}) %collective-permute-start.15) | collective-permute-done | bytes 155680 | tf_op jit(solution)/shard_map/ppermute | solution.py:400
  51.2 0.6 total_0.1
  51.7 0.0 collective-permute-done.12.refs_4_
  51.7 0.0 collective-permute-done.13.refs_5_
  51.8 0.4 stage_1_1.1
  52.2 0.7 collective-permute-start.16
  52.9 1.4 %collective-permute-start.18 = (s16[592,128]{1,0:T(8,128)(2,1)S(1)}, s16[592,128]{1,0:T(8,128)(2,1)S(1)}, u32[]{:S(2)}, u32[]{:S(2)}) collective-permute-start(s16[592,128]{1,0:T(8,128)(2,1)S(1)} %get-tuple-element.76.refs_7_.refs_2_), channel_id=1, source_target_pairs={{0,2},{1,3},{2,0},{3,1},{4,6},{5,7},{6,4},{7,5},{8,10},{9,11},{10,... | collective-permute-start | bytes 454664 | tf_op jit(solution)/shard_map/ppermute | solution.py:400
  54.2 4.5 %collective-permute-done.16.refs_3_ = s16[608,128]{1,0:T(8,128)(2,1)S(1)} collective-permute-done((s16[608,128]{1,0:T(8,128)(2,1)S(1)}, s16[608,128]{1,0:T(8,128)(2,1)S(1)}, u32[]{:S(2)}, u32[]{:S(2)}) %collective-permute-start.16) | collective-permute-done | bytes 155680 | tf_op jit(solution)/shard_map/ppermute | solution.py:400
  58.7 0.6 stage_1_2.1
  59.3 0.0 copy-start
  59.4 0.0 copy-start.1
  59.4 2.4 %collective-permute-start.17 = (s16[608,128]{1,0:T(8,128)(2,1)S(1)}, s16[608,128]{1,0:T(8,128)(2,1)S(1)}, u32[]{:S(2)}, u32[]{:S(2)}) collective-permute-start(s16[608,128]{1,0:T(8,128)(2,1)S(1)} %get-tuple-element.82), channel_id=1, source_target_pairs={{0,4},{1,5},{2,6},{3,7},{4,0},{5,1},{6,2},{7,3},{8,12},{9,13},{10,... | collective-permute-start | bytes 466952 | tf_op jit(solution)/shard_map/ppermute | solution.py:400
  61.8 0.0 collective-permute-start.19
  61.8 0.5 collective-permute-start.20
  62.3 0.9 %collective-permute-done.19.refs_4_ = s16[592,128]{1,0:T(8,128)(2,1)S(1)} collective-permute-done((s16[592,128]{1,0:T(8,128)(2,1)S(1)}, s16[592,128]{1,0:T(8,128)(2,1)S(1)}, u32[]{:S(2)}, u32[]{:S(2)}) %collective-permute-start.19) | collective-permute-done | bytes 151584 | tf_op jit(solution)/shard_map/ppermute | solution.py:400
  63.2 0.2 collective-permute-done.20.refs_5_
  63.4 0.7 unpack_0.1
  64.1 4.1 %collective-permute-done.17.refs_3_ = s16[608,128]{1,0:T(8,128)(2,1)S(1)} collective-permute-done((s16[608,128]{1,0:T(8,128)(2,1)S(1)}, s16[608,128]{1,0:T(8,128)(2,1)S(1)}, u32[]{:S(2)}, u32[]{:S(2)}) %collective-permute-start.17) | collective-permute-done | bytes 155680 | tf_op jit(solution)/shard_map/ppermute | solution.py:400
  68.2 0.6 total_1.1
  68.8 0.1 collective-permute-start.22
  68.8 0.8 collective-permute-start.21
  69.6 5.0 %sweeps_0.1 = (f32[2,256,768]{2,1,0:T(8,128)}, f32[8,128]{1,0:T(8,128)S(1)}) custom-call(f32[8,128]{1,0:T(8,128)S(1)} %get-tuple-element.83.refs_1_.refs_0_, bf16[2,256,768]{2,1,0:T(8,128)(2,1)S(1)} %copy-done, bf16[2,256,768]{2,1,0:T(8,128)(2,1)S(1)} %copy-done.1, bf16[768,768]{1,0:T(8,128)(2,1)S(1)} %get-tuple-element.84.refs_4_.refs_3_, ...), custom_call_target="tpu_custom_call" | custom-call | flops 3623878656 | bytes 2359296 | tf_op jit(solution)/shard_map/sweeps_0/pallas_call | solution.py:49
  74.6 0.6 collective-permute-done.21.refs_0_
  75.2 0.1 collective-permute-start.23
  75.3 1.4 %collective-permute-done.23.refs_5_ = s16[592,128]{1,0:T(8,128)(2,1)S(1)} collective-permute-done((s16[592,128]{1,0:T(8,128)(2,1)S(1)}, s16[592,128]{1,0:T(8,128)(2,1)S(1)}, u32[]{:S(2)}, u32[]{:S(2)}) %collective-permute-start.23) | collective-permute-done | bytes 151584 | tf_op jit(solution)/shard_map/ppermute | solution.py:400
  76.7 0.7 unpack_1.1
  77.4 5.6 %sweeps_1.1 = (f32[2,256,768]{2,1,0:T(8,128)}, f32[8,128]{1,0:T(8,128)}) custom-call(f32[8,128]{1,0:T(8,128)S(1)} %get-tuple-element.85.refs_1_.refs_0_, bf16[2,256,768]{2,1,0:T(8,128)(2,1)S(1)} %copy-done, bf16[2,256,768]{2,1,0:T(8,128)(2,1)S(1)} %copy-done.1, bf16[768,768]{1,0:T(8,128)(2,1)S(1)} %get-tuple-element.89.refs_3_, ...), custom_call_target="tpu_custom_call", output_to_operand_aliasing={{0}: (5, {})} | custom-call | flops 3623878656 | bytes 2359296 | tf_op jit(solution)/shard_map/sweeps_1/pallas_call | solution.py:49
  (15 shorter events, 0.0 us)
Async XLA Ops:
  0.0 0.7 copy-start.2
  5.2 15.6 %collective-permute-start.4 = (bf16[256,768]{1,0:T(8,128)(2,1)S(1)}, bf16[256,768]{1,0:T(8,128)(2,1)S(1)}, u32[]{:S(2)}, u32[]{:S(2)}) collective-permute-start(bf16[256,768]{1,0:T(8,128)(2,1)S(1)} %get-tuple-element.56), channel_id=1, source_target_pairs={{0,24},{8,16},{16,8},{24,0},{1,25},{9,17},{17,9},{25,1},{2,26},{10... | collective-permute-start | bytes 1179656 | tf_op jit(solution)/shard_map/ppermute | solution.py:397
  9.2 18.3 %collective-permute-start.5 = (bf16[256,768]{1,0:T(8,128)(2,1)S(1)}, bf16[256,768]{1,0:T(8,128)(2,1)S(1)}, u32[]{:S(2)}, u32[]{:S(2)}) collective-permute-start(bf16[256,768]{1,0:T(8,128)(2,1)S(1)} %get-tuple-element.57), channel_id=1, source_target_pairs={{0,16},{8,24},{16,0},{24,8},{1,17},{9,25},{17,1},{25,9},{2,18},{10... | collective-permute-start | bytes 1179656 | tf_op jit(solution)/shard_map/ppermute | solution.py:397
  9.7 18.5 %collective-permute-start.6 = (bf16[256,768]{1,0:T(8,128)(2,1)S(1)}, bf16[256,768]{1,0:T(8,128)(2,1)S(1)}, u32[]{:S(2)}, u32[]{:S(2)}) collective-permute-start(bf16[256,768]{1,0:T(8,128)(2,1)S(1)} %get-tuple-element.58), channel_id=1, source_target_pairs={{0,8},{8,0},{16,24},{24,16},{1,9},{9,1},{17,25},{25,17},{2,10},{10... | collective-permute-start | bytes 1179656 | tf_op jit(solution)/shard_map/ppermute | solution.py:397
  16.5 0.7 copy-start.3
  17.3 0.7 copy-start.5
  18.0 13.1 %collective-permute-start = (bf16[128,768]{1,0:T(8,128)(2,1)}, bf16[128,768]{1,0:T(8,128)(2,1)S(1)}, u32[]{:S(2)}, u32[]{:S(2)}) collective-permute-start(bf16[128,768]{1,0:T(8,128)(2,1)} %get-tuple-element.51), channel_id=1, source_target_pairs={{0,24},{8,16},{16,8},{24,0},{1,25},{9,17},{17,9},{25,1},{2,26},{10... | collective-permute-start | bytes 589832 | tf_op jit(solution)/shard_map/ppermute | solution.py:397
  20.9 1.0 %copy-start.4 = (bf16[256,768]{1,0:T(8,128)(2,1)S(1)}, bf16[256,768]{1,0:T(8,128)(2,1)}, u32[]{:S(2)}) copy-start(bf16[256,768]{1,0:T(8,128)(2,1)} %copy-done.3) | copy-start | bytes 1179652
  22.5 11.2 %copy-start.6 = (bf16[256,768]{1,0:T(8,128)(2,1)S(1)}, bf16[256,768]{1,0:T(8,128)(2,1)}, u32[]{:S(2)}) copy-start(bf16[256,768]{1,0:T(8,128)(2,1)} %copy-done.5) | copy-start | bytes 1179652
  29.0 2.7 %collective-permute-start.8 = (f32[384,128]{1,0:T(8,128)S(1)}, f32[384,128]{1,0:T(8,128)S(1)}, u32[]{:S(2)}, u32[]{:S(2)}) collective-permute-start(f32[384,128]{1,0:T(8,128)S(1)} %get-tuple-element.62), channel_id=1, source_target_pairs={{0,1},{1,0},{2,3},{3,2},{4,5},{5,4},{6,7},{7,6},{8,9},{9,8},{10,11... | collective-permute-start | bytes 589832 | tf_op jit(solution)/shard_map/ppermute | solution.py:400
  29.0 16.9 %collective-permute-start.2 = (bf16[256,768]{1,0:T(8,128)(2,1)S(1)}, bf16[256,768]{1,0:T(8,128)(2,1)S(1)}, u32[]{:S(2)}, u32[]{:S(2)}) collective-permute-start(bf16[256,768]{1,0:T(8,128)(2,1)S(1)} %get-tuple-element.53), channel_id=1, source_target_pairs={{0,16},{8,24},{16,0},{24,8},{1,17},{9,25},{17,1},{25,9},{2,18},{10... | collective-permute-start | bytes 1179656 | tf_op jit(solution)/shard_map/ppermute | solution.py:397
  30.5 15.5 %collective-permute-start.3 = (bf16[256,768]{1,0:T(8,128)(2,1)S(1)}, bf16[256,768]{1,0:T(8,128)(2,1)S(1)}, u32[]{:S(2)}, u32[]{:S(2)}) collective-permute-start(bf16[256,768]{1,0:T(8,128)(2,1)S(1)} %get-tuple-element.54), channel_id=1, source_target_pairs={{0,8},{8,0},{16,24},{24,16},{1,9},{9,1},{17,25},{25,17},{2,10},{10... | collective-permute-start | bytes 1179656 | tf_op jit(solution)/shard_map/ppermute | solution.py:397
  31.1 3.2 %collective-permute-start.7 = (f32[392,128]{1,0:T(8,128)S(1)}, f32[392,128]{1,0:T(8,128)S(1)}, u32[]{:S(2)}, u32[]{:S(2)}) collective-permute-start(f32[392,128]{1,0:T(8,128)S(1)} %get-tuple-element.61), channel_id=1, source_target_pairs={{0,1},{1,0},{2,3},{3,2},{4,5},{5,4},{6,7},{7,6},{8,9},{9,8},{10,11... | collective-permute-start | bytes 602120 | tf_op jit(solution)/shard_map/ppermute | solution.py:400
  31.1 3.1 %collective-permute-start.9 = (f32[384,128]{1,0:T(8,128)S(1)}, f32[384,128]{1,0:T(8,128)S(1)}, u32[]{:S(2)}, u32[]{:S(2)}) collective-permute-start(f32[384,128]{1,0:T(8,128)S(1)} %get-tuple-element.63), channel_id=1, source_target_pairs={{0,1},{1,0},{2,3},{3,2},{4,5},{5,4},{6,7},{7,6},{8,9},{9,8},{10,11... | collective-permute-start | bytes 589832 | tf_op jit(solution)/shard_map/ppermute | solution.py:400
  31.6 14.3 %collective-permute-start.1 = (bf16[128,768]{1,0:T(8,128)(2,1)S(1)}, bf16[128,768]{1,0:T(8,128)(2,1)S(1)}, u32[]{:S(2)}, u32[]{:S(2)}) collective-permute-start(bf16[128,768]{1,0:T(8,128)(2,1)S(1)} %get-tuple-element.52), channel_id=1, source_target_pairs={{0,24},{8,16},{16,8},{24,0},{1,25},{9,17},{17,9},{25,1},{2,26},{10... | collective-permute-start | bytes 589832 | tf_op jit(solution)/shard_map/ppermute | solution.py:397
  34.7 6.2 %collective-permute-start.10 = (s16[608,128]{1,0:T(8,128)(2,1)S(1)}, s16[608,128]{1,0:T(8,128)(2,1)S(1)}, u32[]{:S(2)}, u32[]{:S(2)}) collective-permute-start(s16[608,128]{1,0:T(8,128)(2,1)S(1)} %get-tuple-element.66), channel_id=1, source_target_pairs={{0,2},{1,3},{2,0},{3,1},{4,6},{5,7},{6,4},{7,5},{8,10},{9,11},{10,... | collective-permute-start | bytes 466952 | tf_op jit(solution)/shard_map/ppermute | solution.py:400
  41.5 9.6 %collective-permute-start.15 = (s16[608,128]{1,0:T(8,128)(2,1)S(1)}, s16[608,128]{1,0:T(8,128)(2,1)S(1)}, u32[]{:S(2)}, u32[]{:S(2)}) collective-permute-start(s16[608,128]{1,0:T(8,128)(2,1)S(1)} %get-tuple-element.67.refs_5_), channel_id=1, source_target_pairs={{0,4},{1,5},{2,6},{3,7},{4,0},{5,1},{6,2},{7,3},{8,12},{9,13},{10,... | collective-permute-start | bytes 466952 | tf_op jit(solution)/shard_map/ppermute | solution.py:400
  47.0 4.7 %collective-permute-start.11 = (f32[296,128]{1,0:T(8,128)S(1)}, f32[296,128]{1,0:T(8,128)S(1)}, u32[]{:S(2)}, u32[]{:S(2)}) collective-permute-start(f32[296,128]{1,0:T(8,128)S(1)} %get-tuple-element.70), channel_id=1, source_target_pairs={{0,1},{1,0},{2,3},{3,2},{4,5},{5,4},{6,7},{7,6},{8,9},{9,8},{10,11... | collective-permute-start | bytes 454664 | tf_op jit(solution)/shard_map/ppermute | solution.py:400
  47.1 4.6 %collective-permute-start.12 = (f32[288,128]{1,0:T(8,128)S(1)}, f32[288,128]{1,0:T(8,128)S(1)}, u32[]{:S(2)}, u32[]{:S(2)}) collective-permute-start(f32[288,128]{1,0:T(8,128)S(1)} %get-tuple-element.71), channel_id=1, source_target_pairs={{0,1},{1,0},{2,3},{3,2},{4,5},{5,4},{6,7},{7,6},{8,9},{9,8},{10,11... | collective-permute-start | bytes 442376 | tf_op jit(solution)/shard_map/ppermute | solution.py:400
  47.6 4.1 %collective-permute-start.13 = (f32[288,128]{1,0:T(8,128)S(1)}, f32[288,128]{1,0:T(8,128)S(1)}, u32[]{:S(2)}, u32[]{:S(2)}) collective-permute-start(f32[288,128]{1,0:T(8,128)S(1)} %get-tuple-element.72), channel_id=1, source_target_pairs={{0,1},{1,0},{2,3},{3,2},{4,5},{5,4},{6,7},{7,6},{8,9},{9,8},{10,11... | collective-permute-start | bytes 442376 | tf_op jit(solution)/shard_map/ppermute | solution.py:400
  47.7 4.1 %collective-permute-start.14 = (f32[288,128]{1,0:T(8,128)S(1)}, f32[288,128]{1,0:T(8,128)S(1)}, u32[]{:S(2)}, u32[]{:S(2)}) collective-permute-start(f32[288,128]{1,0:T(8,128)S(1)} %get-tuple-element.73), channel_id=1, source_target_pairs={{0,1},{1,0},{2,3},{3,2},{4,5},{5,4},{6,7},{7,6},{8,9},{9,8},{10,11... | collective-permute-start | bytes 442376 | tf_op jit(solution)/shard_map/ppermute | solution.py:400
  52.2 6.6 %collective-permute-start.16 = (s16[608,128]{1,0:T(8,128)(2,1)S(1)}, s16[608,128]{1,0:T(8,128)(2,1)S(1)}, u32[]{:S(2)}, u32[]{:S(2)}) collective-permute-start(s16[608,128]{1,0:T(8,128)(2,1)S(1)} %get-tuple-element.79), channel_id=1, source_target_pairs={{0,2},{1,3},{2,0},{3,1},{4,6},{5,7},{6,4},{7,5},{8,10},{9,11},{10,... | collective-permute-start | bytes 466952 | tf_op jit(solution)/shard_map/ppermute | solution.py:400
  52.9 8.9 %collective-permute-start.18 = (s16[592,128]{1,0:T(8,128)(2,1)S(1)}, s16[592,128]{1,0:T(8,128)(2,1)S(1)}, u32[]{:S(2)}, u32[]{:S(2)}) collective-permute-start(s16[592,128]{1,0:T(8,128)(2,1)S(1)} %get-tuple-element.76.refs_7_.refs_2_), channel_id=1, source_target_pairs={{0,2},{1,3},{2,0},{3,1},{4,6},{5,7},{6,4},{7,5},{8,10},{9,11},{10,... | collective-permute-start | bytes 454664 | tf_op jit(solution)/shard_map/ppermute | solution.py:400
  59.3 10.3 %copy-start = (bf16[2,256,768]{2,1,0:T(8,128)(2,1)S(1)}, bf16[2,256,768]{2,1,0:T(8,128)(2,1)}, u32[]{:S(2)}) copy-start(bf16[2,256,768]{2,1,0:T(8,128)(2,1)} %refs_1_.3) | copy-start | bytes 2359300
  59.4 10.3 %copy-start.1 = (bf16[2,256,768]{2,1,0:T(8,128)(2,1)S(1)}, bf16[2,256,768]{2,1,0:T(8,128)(2,1)}, u32[]{:S(2)}) copy-start(bf16[2,256,768]{2,1,0:T(8,128)(2,1)} %refs_2_.7) | copy-start | bytes 2359300
  59.4 8.8 %collective-permute-start.17 = (s16[608,128]{1,0:T(8,128)(2,1)S(1)}, s16[608,128]{1,0:T(8,128)(2,1)S(1)}, u32[]{:S(2)}, u32[]{:S(2)}) collective-permute-start(s16[608,128]{1,0:T(8,128)(2,1)S(1)} %get-tuple-element.82), channel_id=1, source_target_pairs={{0,4},{1,5},{2,6},{3,7},{4,0},{5,1},{6,2},{7,3},{8,12},{9,13},{10,... | collective-permute-start | bytes 466952 | tf_op jit(solution)/shard_map/ppermute | solution.py:400
  61.8 1.4 %collective-permute-start.19 = (s16[592,128]{1,0:T(8,128)(2,1)S(1)}, s16[592,128]{1,0:T(8,128)(2,1)S(1)}, u32[]{:S(2)}, u32[]{:S(2)}) collective-permute-start(s16[592,128]{1,0:T(8,128)(2,1)S(1)} %get-tuple-element.76.refs_7_.refs_2_), channel_id=1, source_target_pairs={{0,1},{1,0},{2,3},{3,2},{4,5},{5,4},{6,7},{7,6},{8,9},{9,8},{10,11... | collective-permute-start | bytes 454664 | tf_op jit(solution)/shard_map/ppermute | solution.py:400
  61.8 1.6 %collective-permute-start.20 = (s16[592,128]{1,0:T(8,128)(2,1)S(1)}, s16[592,128]{1,0:T(8,128)(2,1)S(1)}, u32[]{:S(2)}, u32[]{:S(2)}) collective-permute-start(s16[592,128]{1,0:T(8,128)(2,1)S(1)} %collective-permute-done.18.refs_3_), channel_id=1, source_target_pairs={{0,1},{1,0},{2,3},{3,2},{4,5},{5,4},{6,7},{7,6},{8,9},{9,8},{10,11... | collective-permute-start | bytes 454664 | tf_op jit(solution)/shard_map/ppermute | solution.py:400
  68.8 6.5 %collective-permute-start.22 = (s16[592,128]{1,0:T(8,128)(2,1)S(1)}, s16[592,128]{1,0:T(8,128)(2,1)S(1)}, u32[]{:S(2)}, u32[]{:S(2)}) collective-permute-start(s16[592,128]{1,0:T(8,128)(2,1)S(1)} %get-tuple-element.86.refs_5_.refs_2_), channel_id=1, source_target_pairs={{0,1},{1,0},{2,3},{3,2},{4,5},{5,4},{6,7},{7,6},{8,9},{9,8},{10,11... | collective-permute-start | bytes 454664 | tf_op jit(solution)/shard_map/ppermute | solution.py:400
  68.8 6.4 %collective-permute-start.21 = (s16[592,128]{1,0:T(8,128)(2,1)S(1)}, s16[592,128]{1,0:T(8,128)(2,1)S(1)}, u32[]{:S(2)}, u32[]{:S(2)}) collective-permute-start(s16[592,128]{1,0:T(8,128)(2,1)S(1)} %get-tuple-element.86.refs_5_.refs_2_), channel_id=1, source_target_pairs={{0,2},{1,3},{2,0},{3,1},{4,6},{5,7},{6,4},{7,5},{8,10},{9,11},{10,... | collective-permute-start | bytes 454664 | tf_op jit(solution)/shard_map/ppermute | solution.py:400
  75.2 1.4 %collective-permute-start.23 = (s16[592,128]{1,0:T(8,128)(2,1)S(1)}, s16[592,128]{1,0:T(8,128)(2,1)S(1)}, u32[]{:S(2)}, u32[]{:S(2)}) collective-permute-start(s16[592,128]{1,0:T(8,128)(2,1)S(1)} %relay.1.refs_3_), channel_id=1, source_target_pairs={{0,1},{1,0},{2,3},{3,2},{4,5},{5,4},{6,7},{7,6},{8,9},{9,8},{10,11... | collective-permute-start | bytes 454664 | tf_op jit(solution)/shard_map/ppermute | solution.py:400

commit v10 on v9

--- a/solution.py
+++ b/solution.py
@@ -18,8 +18,7 @@
 relax_factor = 0.5
 diagonal_eps = 1e-06
 tiny = 1e-30
-VMEM_LIMIT = 24
-PLACE_LIMITS = (50, 50)
+VMEM_LIMIT = 32
 
 VMEM = pl.BlockSpec(memory_space=pltpu.VMEM)
 ANY = pl.BlockSpec(memory_space=pl.ANY)
@@ -117,12 +116,8 @@
     place(key, rows_ref, [lax.bitwise_xor(me, k) * slots for k in others(peers)], capacity, out_refs)
 
 
-def second_kernel(peers, slots, capacity, me_ref, key_ref, rows_any, *refs):
-    out_refs, (rows_ref, rows_done) = refs[:-2], refs[-2:]
-    rows_copies = bring(rows_any, rows_ref, rows_done)
+def second_kernel(peers, slots, capacity, me_ref, key_ref, rows_ref, *out_refs):
     me = me_ref[0]
-    for copy in rows_copies:
-        copy.wait()
     where = [(0, a) for a in range(slots)] + [(k, a) for a in range(1, slots) for k in others(peers)]
     place(key_ref[...], rows_ref, [lax.bitwise_xor(me, k) * slots + a for k, a in where], capacity, out_refs)
 
@@ -408,7 +403,7 @@
             pltpu.VMEM((1, tokens), I32), pltpu.VMEM((tokens, hidden), BF16),
             pltpu.SemaphoreType.DMA, pltpu.SemaphoreType.DMA((COPIES,)),
         ],
-        flops=place_flops * (peers - 1), moved=expert_inputs.size * 4, name="place_first", limit=PLACE_LIMITS[0],
+        flops=place_flops * (peers - 1), moved=expert_inputs.size * 4, name="place_first",
     )(me, owners, expert_inputs)
     arrived = [[over_experts(rows, k) for rows, k in zip(outgoing, others(peers))]]
     count = slots + (slots - 1) * (peers - 1)
@@ -416,9 +411,8 @@
     flips = [peers - 1, *others(peers)]
     rest = call(
         functools.partial(second_kernel, peers, slots, capacity),
-        [chunk] * slots + (parts + [chunk] * (peers - 2)) * (slots - 1), [SMEM, VMEM, HBM],
-        scratch=[pltpu.VMEM((tokens, hidden), BF16), pltpu.SemaphoreType.DMA((COPIES,))],
-        flops=place_flops * count, moved=expert_inputs.size * 4, name="place_rest", limit=PLACE_LIMITS[1],
+        [chunk] * slots + (parts + [chunk] * (peers - 2)) * (slots - 1), [SMEM, VMEM, VMEM],
+        flops=place_flops * count, moved=expert_inputs.size * 4, name="place_rest",
     )(me, key, expert_inputs)
     own = rest[:slots]
     for a in range(1, slots):

time: 83.4 us -> 85.2 us (1.022)
  local copies, waits for them, and re-layouts: 3.19 us -> 5.1 us
  Pallas kernels: 29.4 us -> 27.5 us
  waiting for transfers between devices: 26.7 us -> 28.5 us
    pallas_call x17, Pallas kernels: 29.4 us -> 27.5 us  [call(): return lambda *args: inner(*args, *after)]
    unnamed x14 -> x18, local copies, waits for them, and re-layouts: 3.19 us -> 5.1 us
    ppermute x7, waiting for transfers between devices: 7.5 us -> 9.36 us  [over_experts(): return lax.ppermute(array, 'expert', [(i, i ^ flip) for i in range(peers)])]
  transfers between devices with their start and end apart: 24 -> 24, of which waited for: 11 -> 12; matrix products, arithmetic and copies ran while one was open for 0% -> 0% of each run, Pallas kernels for 21% -> 19%
where the time goes in v10:
time: 85.2 us; the launch traced here: 85 us
  waiting for transfers between devices  28.5 us (33%)
  Pallas kernels  27.5 us (32%)
  starting transfers between devices  23.4 us (27%)
  local copies, waits for them, and re-layouts  5.1 us (6%)
    pallas_call x17, Pallas kernels, call(): return lambda *args: inner(*args, *after)  27.5 us
    ppermute x17, waiting for transfers between devices, over_rows(): lax.ppermute(array, 'rows', [(i, i ^ 1 << bit) for i in range(copies)])  19.2 us
    ppermute x17, starting transfers between devices, over_rows(): lax.ppermute(array, 'rows', [(i, i ^ 1 << bit) for i in range(copies)])  11.9 us
    ppermute x7, starting transfers between devices, over_experts(): return lax.ppermute(array, 'expert', [(i, i ^ flip) for i in range(peers)])  11.5 us
    ppermute x7, waiting for transfers between devices, over_experts(): return lax.ppermute(array, 'expert', [(i, i ^ flip) for i in range(peers)])  9.36 us
    unnamed x18, local copies, waits for them, and re-layouts  5.1 us
  transfers between devices with their start and end apart: 24, of which 12 were waited for; matrix products, arithmetic and copies ran while one was open for 0% of the time, Pallas kernels for 19%

profile of v10, /device:TPU:0, one launch (start us, length us, event | category | flops | bytes accessed | tf_op | source)
XLA Modules:
  0.0 85.0 jit_solution(271188780496805395)
XLA Ops:
  0.0 1.9 %copy-done = bf16[2048,768]{1,0:T(8,128)(2,1)S(1)} copy-done((bf16[2048,768]{1,0:T(8,128)(2,1)S(1)}, bf16[2048,768]{1,0:T(8,128)(2,1)}, u32[]{:S(2)}) %copy-start) | copy-done | bytes 3145752
  1.9 0.7 copy-done.4
  2.6 4.4 %place_first.1 = (s32[1,2048]{1,0:T(1,128)S(1)}, bf16[256,768]{1,0:T(8,128)(2,1)S(1)}, bf16[256,768]{1,0:T(8,128)(2,1)S(1)}, bf16[256,768]{1,0:T(8,128)(2,1)S(1)}) custom-call(s32[1]{0:T(128)} %bitcast.1.refs_0_, s32[1,2048]{1,0:T(1,128)S(1)} %bitcast.3, bf16[2048,768]{1,0:T(8,128)(2,1)S(1)} %copy-done), custom_call_target="tpu_custom_call" | custom-call | flops 2415919104 | bytes 6291456 | tf_op jit(solution)/shard_map/place_first/pallas_call | solution.py:48
  7.0 4.0 %collective-permute-start.4 = (bf16[256,768]{1,0:T(8,128)(2,1)S(1)}, bf16[256,768]{1,0:T(8,128)(2,1)S(1)}, u32[]{:S(2)}, u32[]{:S(2)}) collective-permute-start(bf16[256,768]{1,0:T(8,128)(2,1)S(1)} %get-tuple-element.56), channel_id=1, source_target_pairs={{0,24},{8,16},{16,8},{24,0},{1,25},{9,17},{17,9},{25,1},{2,26},{10... | collective-permute-start | bytes 1179656 | tf_op jit(solution)/shard_map/ppermute | solution.py:392
  11.0 0.5 collective-permute-start.5
  11.5 0.1 collective-permute-start.6
  11.6 4.8 %place_rest.1 = (bf16[256,768]{1,0:T(8,128)(2,1)S(1)}, bf16[256,768]{1,0:T(8,128)(2,1)S(1)}, bf16[128,768]{1,0:T(8,128)(2,1)}, bf16[128,768]{1,0:T(8,128)(2,1)S(...) custom-call(s32[1]{0:T(128)} %bitcast.1.refs_0_, s32[1,2048]{1,0:T(1,128)S(1)} %get-tuple-element.49.refs_1_, ...), custom_call_target="tpu_custom_call" | custom-call | flops 4026531840 | bytes 6291456 | tf_op jit(solution)/shard_map/place_rest/pallas_call | solution.py:48
  16.5 0.7 copy-done.5
  17.2 0.7 copy-done.7
  18.0 2.8 %collective-permute-start = (bf16[128,768]{1,0:T(8,128)(2,1)}, bf16[128,768]{1,0:T(8,128)(2,1)S(1)}, u32[]{:S(2)}, u32[]{:S(2)}) collective-permute-start(bf16[128,768]{1,0:T(8,128)(2,1)} %get-tuple-element.51), channel_id=1, source_target_pairs={{0,24},{8,16},{16,8},{24,0},{1,25},{9,17},{17,9},{25,1},{2,26},{10... | collective-permute-start | bytes 589832 | tf_op jit(solution)/shard_map/ppermute | solution.py:392
  20.8 0.2 collective-permute-done.4.refs_1_
  21.0 1.0 %copy-done.6 = bf16[256,768]{1,0:T(8,128)(2,1)S(1)} copy-done((bf16[256,768]{1,0:T(8,128)(2,1)S(1)}, bf16[256,768]{1,0:T(8,128)(2,1)}, u32[]{:S(2)}) %copy-start.6) | copy-done | bytes 393240
  22.0 0.6 begin_0.1.refs_1_
  22.6 0.0 copy-start.8
  22.6 6.7 %collective-permute-done.5.refs_2_ = bf16[256,768]{1,0:T(8,128)(2,1)S(1)} collective-permute-done((bf16[256,768]{1,0:T(8,128)(2,1)S(1)}, bf16[256,768]{1,0:T(8,128)(2,1)S(1)}, u32[]{:S(2)}, u32[]{:S(2)}) %collective-permute-start.5) | collective-permute-done | bytes 393248 | tf_op jit(solution)/shard_map/ppermute | solution.py:392
  29.3 0.7 collective-permute-done.6.refs_3_
  30.0 0.8 gram_0.1
  30.8 0.1 collective-permute-start.8
  30.9 1.4 %collective-permute-start.2 = (bf16[256,768]{1,0:T(8,128)(2,1)S(1)}, bf16[256,768]{1,0:T(8,128)(2,1)S(1)}, u32[]{:S(2)}, u32[]{:S(2)}) collective-permute-start(bf16[256,768]{1,0:T(8,128)(2,1)S(1)} %get-tuple-element.53), channel_id=1, source_target_pairs={{0,16},{8,24},{16,0},{24,8},{1,17},{9,25},{17,1},{25,9},{2,18},{10... | collective-permute-start | bytes 1179656 | tf_op jit(solution)/shard_map/ppermute | solution.py:392
  32.3 0.6 collective-permute-start.3
  32.9 0.0 collective-permute-start.7
  32.9 0.0 collective-permute-done.refs_1_
  32.9 0.5 collective-permute-start.9
  33.4 0.0 collective-permute-done.8.refs_4_
  33.4 2.0 %collective-permute-start.1 = (bf16[128,768]{1,0:T(8,128)(2,1)S(1)}, bf16[128,768]{1,0:T(8,128)(2,1)S(1)}, u32[]{:S(2)}, u32[]{:S(2)}) collective-permute-start(bf16[128,768]{1,0:T(8,128)(2,1)S(1)} %get-tuple-element.52), channel_id=1, source_target_pairs={{0,24},{8,16},{16,8},{24,0},{1,25},{9,17},{17,9},{25,1},{2,26},{10... | collective-permute-start | bytes 589832 | tf_op jit(solution)/shard_map/ppermute | solution.py:392
  35.4 0.6 begin_1.1.refs_6_.refs_1_
  36.1 0.0 collective-permute-done.9.refs_5_
  36.1 0.4 stage_0_1.1
  36.5 1.6 %collective-permute-start.10 = (s16[608,128]{1,0:T(8,128)(2,1)S(1)}, s16[608,128]{1,0:T(8,128)(2,1)S(1)}, u32[]{:S(2)}, u32[]{:S(2)}) collective-permute-start(s16[608,128]{1,0:T(8,128)(2,1)S(1)} %get-tuple-element.66), channel_id=1, source_target_pairs={{0,2},{1,3},{2,0},{3,1},{4,6},{5,7},{6,4},{7,5},{8,10},{9,11},{10,... | collective-permute-start | bytes 466952 | tf_op jit(solution)/shard_map/ppermute | solution.py:395
  38.1 4.6 %collective-permute-done.10.refs_3_ = s16[608,128]{1,0:T(8,128)(2,1)S(1)} collective-permute-done((s16[608,128]{1,0:T(8,128)(2,1)S(1)}, s16[608,128]{1,0:T(8,128)(2,1)S(1)}, u32[]{:S(2)}, u32[]{:S(2)}) %collective-permute-start.10) | collective-permute-done | bytes 155680 | tf_op jit(solution)/shard_map/ppermute | solution.py:395
  42.7 0.6 stage_0_2.1
  43.3 2.7 %collective-permute-start.15 = (s16[608,128]{1,0:T(8,128)(2,1)S(1)}, s16[608,128]{1,0:T(8,128)(2,1)S(1)}, u32[]{:S(2)}, u32[]{:S(2)}) collective-permute-start(s16[608,128]{1,0:T(8,128)(2,1)S(1)} %get-tuple-element.67.refs_5_), channel_id=1, source_target_pairs={{0,4},{1,5},{2,6},{3,7},{4,0},{5,1},{6,2},{7,3},{8,12},{9,13},{10,... | collective-permute-start | bytes 466952 | tf_op jit(solution)/shard_map/ppermute | solution.py:395
  46.0 1.8 %collective-permute-done.1.refs_2_ = bf16[128,768]{1,0:T(8,128)(2,1)S(1)} collective-permute-done((bf16[128,768]{1,0:T(8,128)(2,1)S(1)}, bf16[128,768]{1,0:T(8,128)(2,1)S(1)}, u32[]{:S(2)}, u32[]{:S(2)}) %collective-permute-start.1) | collective-permute-done | bytes 196640 | tf_op jit(solution)/shard_map/ppermute | solution.py:392
  47.8 1.1 %gram_1.1 = (f32[1152,128]{1,0:T(8,128)S(1)}, f32[8,128]{1,0:T(8,128)S(1)}, f32[296,128]{1,0:T(8,128)S(1)}, f32[288,128]{1,0:T(8,128)S(1)}, f32[288,128]{1,0:T(8,128)S(1)}, /*index=5*/f32[288,128]{1,0:T(8,128)S(1)}) custom-call(s32[1]{0:T(128)} %bitcast.refs_0_, f32[2312,128]{1,0:T(8,128)S(1)} %begin_1.1.refs_6_.refs_1_, ...), custom_call_target="tpu_custom_call" | custom-call | tf_op jit(solution)/shard_map/gram_1/pallas_call | solution.py:48
  48.8 0.1 collective-permute-start.11
  48.9 0.5 collective-permute-start.12
  49.4 0.1 collective-permute-start.13
  49.5 0.4 collective-permute-start.14
  49.9 3.0 %collective-permute-done.15.refs_3_ = s16[608,128]{1,0:T(8,128)(2,1)S(1)} collective-permute-done((s16[608,128]{1,0:T(8,128)(2,1)S(1)}, s16[608,128]{1,0:T(8,128)(2,1)S(1)}, u32[]{:S(2)}, u32[]{:S(2)}) %collective-permute-start.15) | collective-permute-done | bytes 155680 | tf_op jit(solution)/shard_map/ppermute | solution.py:395
  53.0 0.6 total_0.1
  53.5 0.0 collective-permute-done.12.refs_4_
  53.6 0.4 stage_1_1.1
  54.0 0.7 collective-permute-start.16
  54.7 1.3 %collective-permute-start.18 = (s16[592,128]{1,0:T(8,128)(2,1)S(1)}, s16[592,128]{1,0:T(8,128)(2,1)S(1)}, u32[]{:S(2)}, u32[]{:S(2)}) collective-permute-start(s16[592,128]{1,0:T(8,128)(2,1)S(1)} %get-tuple-element.76.refs_7_.refs_2_), channel_id=1, source_target_pairs={{0,2},{1,3},{2,0},{3,1},{4,6},{5,7},{6,4},{7,5},{8,10},{9,11},{10,... | collective-permute-start | bytes 454664 | tf_op jit(solution)/shard_map/ppermute | solution.py:395
  56.1 4.5 %collective-permute-done.16.refs_3_ = s16[608,128]{1,0:T(8,128)(2,1)S(1)} collective-permute-done((s16[608,128]{1,0:T(8,128)(2,1)S(1)}, s16[608,128]{1,0:T(8,128)(2,1)S(1)}, u32[]{:S(2)}, u32[]{:S(2)}) %collective-permute-start.16) | collective-permute-done | bytes 155680 | tf_op jit(solution)/shard_map/ppermute | solution.py:395
  60.5 0.6 stage_1_2.1
  61.2 0.0 copy-start.2
  61.2 0.0 copy-start.3
  61.2 2.4 %collective-permute-start.17 = (s16[608,128]{1,0:T(8,128)(2,1)S(1)}, s16[608,128]{1,0:T(8,128)(2,1)S(1)}, u32[]{:S(2)}, u32[]{:S(2)}) collective-permute-start(s16[608,128]{1,0:T(8,128)(2,1)S(1)} %get-tuple-element.82), channel_id=1, source_target_pairs={{0,4},{1,5},{2,6},{3,7},{4,0},{5,1},{6,2},{7,3},{8,12},{9,13},{10,... | collective-permute-start | bytes 466952 | tf_op jit(solution)/shard_map/ppermute | solution.py:395
  63.6 0.0 collective-permute-start.19
  63.6 0.5 collective-permute-start.20
  64.1 0.9 %collective-permute-done.19.refs_4_ = s16[592,128]{1,0:T(8,128)(2,1)S(1)} collective-permute-done((s16[592,128]{1,0:T(8,128)(2,1)S(1)}, s16[592,128]{1,0:T(8,128)(2,1)S(1)}, u32[]{:S(2)}, u32[]{:S(2)}) %collective-permute-start.19) | collective-permute-done | bytes 151584 | tf_op jit(solution)/shard_map/ppermute | solution.py:395
  65.0 0.2 collective-permute-done.20.refs_5_
  65.2 0.7 unpack_0.1
  65.9 4.1 %collective-permute-done.17.refs_3_ = s16[608,128]{1,0:T(8,128)(2,1)S(1)} collective-permute-done((s16[608,128]{1,0:T(8,128)(2,1)S(1)}, s16[608,128]{1,0:T(8,128)(2,1)S(1)}, u32[]{:S(2)}, u32[]{:S(2)}) %collective-permute-start.17) | collective-permute-done | bytes 155680 | tf_op jit(solution)/shard_map/ppermute | solution.py:395
  70.0 0.6 total_1.1
  70.6 0.1 collective-permute-start.22
  70.7 0.8 collective-permute-start.21
  71.4 5.0 %sweeps_0.1 = (f32[2,256,768]{2,1,0:T(8,128)}, f32[8,128]{1,0:T(8,128)S(1)}) custom-call(f32[8,128]{1,0:T(8,128)S(1)} %get-tuple-element.83.refs_1_.refs_0_, bf16[2,256,768]{2,1,0:T(8,128)(2,1)S(1)} %copy-done.2, bf16[2,256,768]{2,1,0:T(8,128)(2,1)S(1)} %copy-done.3, bf16[768,768]{1,0:T(8,128)(2,1)S(1)} %get-tuple-element.84.refs_4_.refs_3_, ...), custom_call_target="tpu_custom_call" | custom-call | flops 3623878656 | bytes 2359296 | tf_op jit(solution)/shard_map/sweeps_0/pallas_call | solution.py:48
  76.5 0.5 collective-permute-done.21.refs_0_
  77.0 0.1 collective-permute-start.23
  77.1 1.4 %collective-permute-done.23.refs_5_ = s16[592,128]{1,0:T(8,128)(2,1)S(1)} collective-permute-done((s16[592,128]{1,0:T(8,128)(2,1)S(1)}, s16[592,128]{1,0:T(8,128)(2,1)S(1)}, u32[]{:S(2)}, u32[]{:S(2)}) %collective-permute-start.23) | collective-permute-done | bytes 151584 | tf_op jit(solution)/shard_map/ppermute | solution.py:395
  78.5 0.7 unpack_1.1
  79.2 5.6 %sweeps_1.1 = (f32[2,256,768]{2,1,0:T(8,128)}, f32[8,128]{1,0:T(8,128)}) custom-call(f32[8,128]{1,0:T(8,128)S(1)} %get-tuple-element.85.refs_1_.refs_0_, bf16[2,256,768]{2,1,0:T(8,128)(2,1)S(1)} %copy-done.2, bf16[2,256,768]{2,1,0:T(8,128)(2,1)S(1)} %copy-done.3, bf16[768,768]{1,0:T(8,128)(2,1)S(1)} %get-tuple-element.89.refs_3_, ...), custom_call_target="tpu_custom_call", output_to_operand_aliasing={{0}: (5, {})} | custom-call | flops 3623878656 | bytes 2359296 | tf_op jit(solution)/shard_map/sweeps_1/pallas_call | solution.py:48
  (19 shorter events, 0.0 us)
Async XLA Ops:
  0.0 1.9 %copy-start = (bf16[2048,768]{1,0:T(8,128)(2,1)S(1)}, bf16[2048,768]{1,0:T(8,128)(2,1)}, u32[]{:S(2)}) copy-start(bf16[2048,768]{1,0:T(8,128)(2,1)} %refs_2_.5) | copy-start | bytes 9437188
  1.9 0.7 copy-start.4
  2.6 9.1 %copy-start.1 = (bf16[2048,768]{1,0:T(8,128)(2,1)S(1)}, bf16[2048,768]{1,0:T(8,128)(2,1)}, u32[]{:S(2)}) copy-start(bf16[2048,768]{1,0:T(8,128)(2,1)} %refs_2_.5) | copy-start | bytes 9437188
  7.0 14.0 %collective-permute-start.4 = (bf16[256,768]{1,0:T(8,128)(2,1)S(1)}, bf16[256,768]{1,0:T(8,128)(2,1)S(1)}, u32[]{:S(2)}, u32[]{:S(2)}) collective-permute-start(bf16[256,768]{1,0:T(8,128)(2,1)S(1)} %get-tuple-element.56), channel_id=1, source_target_pairs={{0,24},{8,16},{16,8},{24,0},{1,25},{9,17},{17,9},{25,1},{2,26},{10... | collective-permute-start | bytes 1179656 | tf_op jit(solution)/shard_map/ppermute | solution.py:392
  11.0 18.3 %collective-permute-start.5 = (bf16[256,768]{1,0:T(8,128)(2,1)S(1)}, bf16[256,768]{1,0:T(8,128)(2,1)S(1)}, u32[]{:S(2)}, u32[]{:S(2)}) collective-permute-start(bf16[256,768]{1,0:T(8,128)(2,1)S(1)} %get-tuple-element.57), channel_id=1, source_target_pairs={{0,16},{8,24},{16,0},{24,8},{1,17},{9,25},{17,1},{25,9},{2,18},{10... | collective-permute-start | bytes 1179656 | tf_op jit(solution)/shard_map/ppermute | solution.py:392
  11.5 18.5 %collective-permute-start.6 = (bf16[256,768]{1,0:T(8,128)(2,1)S(1)}, bf16[256,768]{1,0:T(8,128)(2,1)S(1)}, u32[]{:S(2)}, u32[]{:S(2)}) collective-permute-start(bf16[256,768]{1,0:T(8,128)(2,1)S(1)} %get-tuple-element.58), channel_id=1, source_target_pairs={{0,8},{8,0},{16,24},{24,16},{1,9},{9,1},{17,25},{25,17},{2,10},{10... | collective-permute-start | bytes 1179656 | tf_op jit(solution)/shard_map/ppermute | solution.py:392
  16.5 0.7 copy-start.5
  17.2 0.7 copy-start.7
  18.0 15.0 %collective-permute-start = (bf16[128,768]{1,0:T(8,128)(2,1)}, bf16[128,768]{1,0:T(8,128)(2,1)S(1)}, u32[]{:S(2)}, u32[]{:S(2)}) collective-permute-start(bf16[128,768]{1,0:T(8,128)(2,1)} %get-tuple-element.51), channel_id=1, source_target_pairs={{0,24},{8,16},{16,8},{24,0},{1,25},{9,17},{17,9},{25,1},{2,26},{10... | collective-permute-start | bytes 589832 | tf_op jit(solution)/shard_map/ppermute | solution.py:392
  21.0 1.0 %copy-start.6 = (bf16[256,768]{1,0:T(8,128)(2,1)S(1)}, bf16[256,768]{1,0:T(8,128)(2,1)}, u32[]{:S(2)}) copy-start(bf16[256,768]{1,0:T(8,128)(2,1)} %copy-done.5) | copy-start | bytes 1179652
  22.6 12.8 %copy-start.8 = (bf16[256,768]{1,0:T(8,128)(2,1)S(1)}, bf16[256,768]{1,0:T(8,128)(2,1)}, u32[]{:S(2)}) copy-start(bf16[256,768]{1,0:T(8,128)(2,1)} %copy-done.7) | copy-start | bytes 1179652
  30.8 2.7 %collective-permute-start.8 = (f32[384,128]{1,0:T(8,128)S(1)}, f32[384,128]{1,0:T(8,128)S(1)}, u32[]{:S(2)}, u32[]{:S(2)}) collective-permute-start(f32[384,128]{1,0:T(8,128)S(1)} %get-tuple-element.62), channel_id=1, source_target_pairs={{0,1},{1,0},{2,3},{3,2},{4,5},{5,4},{6,7},{7,6},{8,9},{9,8},{10,11... | collective-permute-start | bytes 589832 | tf_op jit(solution)/shard_map/ppermute | solution.py:395
  30.9 16.9 %collective-permute-start.2 = (bf16[256,768]{1,0:T(8,128)(2,1)S(1)}, bf16[256,768]{1,0:T(8,128)(2,1)S(1)}, u32[]{:S(2)}, u32[]{:S(2)}) collective-permute-start(bf16[256,768]{1,0:T(8,128)(2,1)S(1)} %get-tuple-element.53), channel_id=1, source_target_pairs={{0,16},{8,24},{16,0},{24,8},{1,17},{9,25},{17,1},{25,9},{2,18},{10... | collective-permute-start | bytes 1179656 | tf_op jit(solution)/shard_map/ppermute | solution.py:392
  32.3 15.5 %collective-permute-start.3 = (bf16[256,768]{1,0:T(8,128)(2,1)S(1)}, bf16[256,768]{1,0:T(8,128)(2,1)S(1)}, u32[]{:S(2)}, u32[]{:S(2)}) collective-permute-start(bf16[256,768]{1,0:T(8,128)(2,1)S(1)} %get-tuple-element.54), channel_id=1, source_target_pairs={{0,8},{8,0},{16,24},{24,16},{1,9},{9,1},{17,25},{25,17},{2,10},{10... | collective-permute-start | bytes 1179656 | tf_op jit(solution)/shard_map/ppermute | solution.py:392
  32.9 3.1 %collective-permute-start.7 = (f32[392,128]{1,0:T(8,128)S(1)}, f32[392,128]{1,0:T(8,128)S(1)}, u32[]{:S(2)}, u32[]{:S(2)}) collective-permute-start(f32[392,128]{1,0:T(8,128)S(1)} %get-tuple-element.61), channel_id=1, source_target_pairs={{0,1},{1,0},{2,3},{3,2},{4,5},{5,4},{6,7},{7,6},{8,9},{9,8},{10,11... | collective-permute-start | bytes 602120 | tf_op jit(solution)/shard_map/ppermute | solution.py:395
  32.9 3.1 %collective-permute-start.9 = (f32[384,128]{1,0:T(8,128)S(1)}, f32[384,128]{1,0:T(8,128)S(1)}, u32[]{:S(2)}, u32[]{:S(2)}) collective-permute-start(f32[384,128]{1,0:T(8,128)S(1)} %get-tuple-element.63), channel_id=1, source_target_pairs={{0,1},{1,0},{2,3},{3,2},{4,5},{5,4},{6,7},{7,6},{8,9},{9,8},{10,11... | collective-permute-start | bytes 589832 | tf_op jit(solution)/shard_map/ppermute | solution.py:395
  33.4 14.3 %collective-permute-start.1 = (bf16[128,768]{1,0:T(8,128)(2,1)S(1)}, bf16[128,768]{1,0:T(8,128)(2,1)S(1)}, u32[]{:S(2)}, u32[]{:S(2)}) collective-permute-start(bf16[128,768]{1,0:T(8,128)(2,1)S(1)} %get-tuple-element.52), channel_id=1, source_target_pairs={{0,24},{8,16},{16,8},{24,0},{1,25},{9,17},{17,9},{25,1},{2,26},{10... | collective-permute-start | bytes 589832 | tf_op jit(solution)/shard_map/ppermute | solution.py:392
  36.5 6.2 %collective-permute-start.10 = (s16[608,128]{1,0:T(8,128)(2,1)S(1)}, s16[608,128]{1,0:T(8,128)(2,1)S(1)}, u32[]{:S(2)}, u32[]{:S(2)}) collective-permute-start(s16[608,128]{1,0:T(8,128)(2,1)S(1)} %get-tuple-element.66), channel_id=1, source_target_pairs={{0,2},{1,3},{2,0},{3,1},{4,6},{5,7},{6,4},{7,5},{8,10},{9,11},{10,... | collective-permute-start | bytes 466952 | tf_op jit(solution)/shard_map/ppermute | solution.py:395
  43.3 9.6 %collective-permute-start.15 = (s16[608,128]{1,0:T(8,128)(2,1)S(1)}, s16[608,128]{1,0:T(8,128)(2,1)S(1)}, u32[]{:S(2)}, u32[]{:S(2)}) collective-permute-start(s16[608,128]{1,0:T(8,128)(2,1)S(1)} %get-tuple-element.67.refs_5_), channel_id=1, source_target_pairs={{0,4},{1,5},{2,6},{3,7},{4,0},{5,1},{6,2},{7,3},{8,12},{9,13},{10,... | collective-permute-start | bytes 466952 | tf_op jit(solution)/shard_map/ppermute | solution.py:395
  48.8 4.7 %collective-permute-start.11 = (f32[296,128]{1,0:T(8,128)S(1)}, f32[296,128]{1,0:T(8,128)S(1)}, u32[]{:S(2)}, u32[]{:S(2)}) collective-permute-start(f32[296,128]{1,0:T(8,128)S(1)} %get-tuple-element.70), channel_id=1, source_target_pairs={{0,1},{1,0},{2,3},{3,2},{4,5},{5,4},{6,7},{7,6},{8,9},{9,8},{10,11... | collective-permute-start | bytes 454664 | tf_op jit(solution)/shard_map/ppermute | solution.py:395
  48.9 4.6 %collective-permute-start.12 = (f32[288,128]{1,0:T(8,128)S(1)}, f32[288,128]{1,0:T(8,128)S(1)}, u32[]{:S(2)}, u32[]{:S(2)}) collective-permute-start(f32[288,128]{1,0:T(8,128)S(1)} %get-tuple-element.71), channel_id=1, source_target_pairs={{0,1},{1,0},{2,3},{3,2},{4,5},{5,4},{6,7},{7,6},{8,9},{9,8},{10,11... | collective-permute-start | bytes 442376 | tf_op jit(solution)/shard_map/ppermute | solution.py:395
  49.4 4.1 %collective-permute-start.13 = (f32[288,128]{1,0:T(8,128)S(1)}, f32[288,128]{1,0:T(8,128)S(1)}, u32[]{:S(2)}, u32[]{:S(2)}) collective-permute-start(f32[288,128]{1,0:T(8,128)S(1)} %get-tuple-element.72), channel_id=1, source_target_pairs={{0,1},{1,0},{2,3},{3,2},{4,5},{5,4},{6,7},{7,6},{8,9},{9,8},{10,11... | collective-permute-start | bytes 442376 | tf_op jit(solution)/shard_map/ppermute | solution.py:395
  49.5 4.1 %collective-permute-start.14 = (f32[288,128]{1,0:T(8,128)S(1)}, f32[288,128]{1,0:T(8,128)S(1)}, u32[]{:S(2)}, u32[]{:S(2)}) collective-permute-start(f32[288,128]{1,0:T(8,128)S(1)} %get-tuple-element.73), channel_id=1, source_target_pairs={{0,1},{1,0},{2,3},{3,2},{4,5},{5,4},{6,7},{7,6},{8,9},{9,8},{10,11... | collective-permute-start | bytes 442376 | tf_op jit(solution)/shard_map/ppermute | solution.py:395
  54.0 6.6 %collective-permute-start.16 = (s16[608,128]{1,0:T(8,128)(2,1)S(1)}, s16[608,128]{1,0:T(8,128)(2,1)S(1)}, u32[]{:S(2)}, u32[]{:S(2)}) collective-permute-start(s16[608,128]{1,0:T(8,128)(2,1)S(1)} %get-tuple-element.79), channel_id=1, source_target_pairs={{0,2},{1,3},{2,0},{3,1},{4,6},{5,7},{6,4},{7,5},{8,10},{9,11},{10,... | collective-permute-start | bytes 466952 | tf_op jit(solution)/shard_map/ppermute | solution.py:395
  54.7 8.9 %collective-permute-start.18 = (s16[592,128]{1,0:T(8,128)(2,1)S(1)}, s16[592,128]{1,0:T(8,128)(2,1)S(1)}, u32[]{:S(2)}, u32[]{:S(2)}) collective-permute-start(s16[592,128]{1,0:T(8,128)(2,1)S(1)} %get-tuple-element.76.refs_7_.refs_2_), channel_id=1, source_target_pairs={{0,2},{1,3},{2,0},{3,1},{4,6},{5,7},{6,4},{7,5},{8,10},{9,11},{10,... | collective-permute-start | bytes 454664 | tf_op jit(solution)/shard_map/ppermute | solution.py:395
  61.2 10.3 %copy-start.2 = (bf16[2,256,768]{2,1,0:T(8,128)(2,1)S(1)}, bf16[2,256,768]{2,1,0:T(8,128)(2,1)}, u32[]{:S(2)}) copy-start(bf16[2,256,768]{2,1,0:T(8,128)(2,1)} %refs_1_.3) | copy-start | bytes 2359300
  61.2 10.3 %copy-start.3 = (bf16[2,256,768]{2,1,0:T(8,128)(2,1)S(1)}, bf16[2,256,768]{2,1,0:T(8,128)(2,1)}, u32[]{:S(2)}) copy-start(bf16[2,256,768]{2,1,0:T(8,128)(2,1)} %refs_2_.7) | copy-start | bytes 2359300
  61.2 8.8 %collective-permute-start.17 = (s16[608,128]{1,0:T(8,128)(2,1)S(1)}, s16[608,128]{1,0:T(8,128)(2,1)S(1)}, u32[]{:S(2)}, u32[]{:S(2)}) collective-permute-start(s16[608,128]{1,0:T(8,128)(2,1)S(1)} %get-tuple-element.82), channel_id=1, source_target_pairs={{0,4},{1,5},{2,6},{3,7},{4,0},{5,1},{6,2},{7,3},{8,12},{9,13},{10,... | collective-permute-start | bytes 466952 | tf_op jit(solution)/shard_map/ppermute | solution.py:395
  63.6 1.4 %collective-permute-start.19 = (s16[592,128]{1,0:T(8,128)(2,1)S(1)}, s16[592,128]{1,0:T(8,128)(2,1)S(1)}, u32[]{:S(2)}, u32[]{:S(2)}) collective-permute-start(s16[592,128]{1,0:T(8,128)(2,1)S(1)} %get-tuple-element.76.refs_7_.refs_2_), channel_id=1, source_target_pairs={{0,1},{1,0},{2,3},{3,2},{4,5},{5,4},{6,7},{7,6},{8,9},{9,8},{10,11... | collective-permute-start | bytes 454664 | tf_op jit(solution)/shard_map/ppermute | solution.py:395
  63.6 1.6 %collective-permute-start.20 = (s16[592,128]{1,0:T(8,128)(2,1)S(1)}, s16[592,128]{1,0:T(8,128)(2,1)S(1)}, u32[]{:S(2)}, u32[]{:S(2)}) collective-permute-start(s16[592,128]{1,0:T(8,128)(2,1)S(1)} %collective-permute-done.18.refs_3_), channel_id=1, source_target_pairs={{0,1},{1,0},{2,3},{3,2},{4,5},{5,4},{6,7},{7,6},{8,9},{9,8},{10,11... | collective-permute-start | bytes 454664 | tf_op jit(solution)/shard_map/ppermute | solution.py:395
  70.6 6.5 %collective-permute-start.22 = (s16[592,128]{1,0:T(8,128)(2,1)S(1)}, s16[592,128]{1,0:T(8,128)(2,1)S(1)}, u32[]{:S(2)}, u32[]{:S(2)}) collective-permute-start(s16[592,128]{1,0:T(8,128)(2,1)S(1)} %get-tuple-element.86.refs_5_.refs_2_), channel_id=1, source_target_pairs={{0,1},{1,0},{2,3},{3,2},{4,5},{5,4},{6,7},{7,6},{8,9},{9,8},{10,11... | collective-permute-start | bytes 454664 | tf_op jit(solution)/shard_map/ppermute | solution.py:395
  70.7 6.4 %collective-permute-start.21 = (s16[592,128]{1,0:T(8,128)(2,1)S(1)}, s16[592,128]{1,0:T(8,128)(2,1)S(1)}, u32[]{:S(2)}, u32[]{:S(2)}) collective-permute-start(s16[592,128]{1,0:T(8,128)(2,1)S(1)} %get-tuple-element.86.refs_5_.refs_2_), channel_id=1, source_target_pairs={{0,2},{1,3},{2,0},{3,1},{4,6},{5,7},{6,4},{7,5},{8,10},{9,11},{10,... | collective-permute-start | bytes 454664 | tf_op jit(solution)/shard_map/ppermute | solution.py:395
  77.0 1.4 %collective-permute-start.23 = (s16[592,128]{1,0:T(8,128)(2,1)S(1)}, s16[592,128]{1,0:T(8,128)(2,1)S(1)}, u32[]{:S(2)}, u32[]{:S(2)}) collective-permute-start(s16[592,128]{1,0:T(8,128)(2,1)S(1)} %relay.1.refs_3_), channel_id=1, source_target_pairs={{0,1},{1,0},{2,3},{3,2},{4,5},{5,4},{6,7},{7,6},{8,9},{9,8},{10,11... | collective-permute-start | bytes 454664 | tf_op jit(solution)/shard_map/ppermute | solution.py:395

commit v11 on v8

--- a/solution.py
+++ b/solution.py
@@ -17,7 +17,8 @@
 relax_factor = 0.5
 diagonal_eps = 1e-06
 tiny = 1e-30
-VMEM_LIMIT = 32 * 2**20
+VMEM_LIMIT = 24 * 2**20
+PLACE_LIMIT = 50 * 2**20
 
 VMEM = pl.BlockSpec(memory_space=pltpu.VMEM)
 ANY = pl.BlockSpec(memory_space=pl.ANY)
@@ -26,7 +27,7 @@
 F32, BF16, I32, I16 = jnp.float32, jnp.bfloat16, jnp.int32, jnp.int16
 
 
-def call(kernel, out_shape, in_specs, scratch=(), flops=0, moved=0, out_specs=None, aliases=None, name=None, after=()):
+def call(kernel, out_shape, in_specs, scratch=(), flops=0, moved=0, out_specs=None, aliases=None, name=None, after=(), limit=VMEM_LIMIT):
     many = isinstance(out_shape, (list, tuple))
     used, idle = len(in_specs), len(after)
 
@@ -41,7 +42,7 @@
         scratch_shapes=list(scratch),
         input_output_aliases=aliases or {},
         cost_estimate=pl.CostEstimate(flops=flops, bytes_accessed=moved, transcendentals=0),
-        compiler_params=pltpu.CompilerParams(vmem_limit_bytes=VMEM_LIMIT),
+        compiler_params=pltpu.CompilerParams(vmem_limit_bytes=limit),
         name=name,
     )
     return lambda *args: inner(*args, *after)
@@ -72,12 +73,16 @@
     return owners * capacity + rank.astype(I32)
 
 
-def place(key, rows_ref, experts, capacity, out_refs):
+def place(key, rows_ref, experts, capacity, out_refs, chosen_ref=None, ready=None):
     tokens, hidden = rows_ref.shape
     places = lax.broadcasted_iota(I32, (capacity, tokens), 0)
     chosen = jnp.concatenate(
         [(places == key - e * capacity).astype(F32).astype(BF16) for e in experts], axis=0
     )
+    if ready is not None:
+        chosen_ref[...] = chosen
+        ready()
+        chosen = chosen_ref[...]
     for c in range(0, hidden, WIDTH):
         got = jnp.dot(chosen, rows_ref[:, c:c + WIDTH], preferred_element_type=F32).astype(BF16)
         for k, out_ref in enumerate(out_refs):
@@ -89,7 +94,7 @@
 
 
 def first_kernel(peers, slots, all_experts, capacity, me_ref, owner_any, rows_any, key_ref, *refs):
-    out_refs, (owner_ref, rows_ref, owner_done, rows_done) = refs[:-4], refs[-4:]
+    out_refs, (owner_ref, rows_ref, chosen_ref, owner_done, rows_done) = refs[:-5], refs[-5:]
     owner_copy = pltpu.make_async_copy(owner_any, owner_ref, owner_done)
     owner_copy.start()
     rows_copy = pltpu.make_async_copy(rows_any, rows_ref, rows_done)
@@ -98,8 +103,8 @@
     owner_copy.wait()
     key = slots_of(owner_ref[...], all_experts, capacity)
     key_ref[...] = key
-    rows_copy.wait()
-    place(key, rows_ref, [lax.bitwise_xor(me, k) * slots for k in others(peers)], capacity, out_refs)
+    experts = [lax.bitwise_xor(me, k) * slots for k in others(peers)]
+    place(key, rows_ref, experts, capacity, out_refs, chosen_ref, rows_copy.wait)
 
 
 def second_kernel(peers, slots, capacity, me_ref, key_ref, rows_ref, *out_refs):
@@ -387,15 +392,16 @@
         [shape(1, tokens, I32)] + [chunk] * (peers - 1), [SMEM, HBM, HBM],
         scratch=[
             pltpu.VMEM((1, tokens), I32), pltpu.VMEM((tokens, hidden), BF16),
+            pltpu.VMEM(((peers - 1) * capacity, tokens), BF16),
             pltpu.SemaphoreType.DMA, pltpu.SemaphoreType.DMA,
         ],
-        flops=place_flops * (peers - 1), moved=expert_inputs.size * 4, name="place_first",
+        flops=place_flops * (peers - 1), moved=expert_inputs.size * 4, name="place_first", limit=PLACE_LIMIT,
     )(me, owners, expert_inputs)
     arrived = [[over_experts(rows, k) for rows, k in zip(outgoing, others(peers))]]
     count = slots + (slots - 1) * (peers - 1)
     rest = call(
         functools.partial(second_kernel, peers, slots, capacity), [chunk] * count, [SMEM, VMEM, VMEM],
-        flops=place_flops * count, moved=expert_inputs.size * 4, name="place_rest",
+        flops=place_flops * count, moved=expert_inputs.size * 4, name="place_rest", limit=PLACE_LIMIT,
     )(me, key, expert_inputs)
     own = rest[:slots]
     for a in range(1, slots):

time: 81.3 us -> 80.8 us (level)
  Pallas kernels: 26.6 us -> 29.9 us
  local copies, waits for them, and re-layouts: 5.11 us -> 3.21 us
  waiting for transfers between devices: 24.9 us -> 23.1 us
    pallas_call x17, Pallas kernels: 26.6 us -> 29.9 us  [call(): return lambda *args: inner(*args, *after)]
    unnamed x18 -> x14, local copies, waits for them, and re-layouts: 5.11 us -> 3.21 us
    ppermute x6, waiting for transfers between devices: 11.6 us -> 9.72 us  [over_experts(): return lax.ppermute(array, 'expert', [(i, i ^ flip) for i in range(peers)])]
  transfers between devices with their start and end apart: 22 -> 22, of which waited for: 12 -> 10; matrix products, arithmetic and copies ran while one was open for 0% -> 0% of each run, Pallas kernels for 20% -> 22%
where the time goes in v11:
time: 80.8 us; the launch traced here: 80.5 us
  Pallas kernels  29.9 us (37%)
  starting transfers between devices  24 us (30%)
  waiting for transfers between devices  23.1 us (29%)
  local copies, waits for them, and re-layouts  3.21 us (4%)
    pallas_call x17, Pallas kernels, call(): return lambda *args: inner(*args, *after)  29.9 us
    ppermute x16, starting transfers between devices, over_rows(): lax.ppermute(array, 'rows', [(i, i ^ 1 << bit) for i in range(copies)])  14.6 us
    ppermute x16, waiting for transfers between devices, over_rows(): lax.ppermute(array, 'rows', [(i, i ^ 1 << bit) for i in range(copies)])  13.3 us
    ppermute x6, waiting for transfers between devices, over_experts(): return lax.ppermute(array, 'expert', [(i, i ^ flip) for i in range(peers)])  9.72 us
    ppermute x6, starting transfers between devices, over_experts(): return lax.ppermute(array, 'expert', [(i, i ^ flip) for i in range(peers)])  9.45 us
    unnamed x14, local copies, waits for them, and re-layouts  3.21 us
  transfers between devices with their start and end apart: 22, of which 10 were waited for; matrix products, arithmetic and copies ran while one was open for 0% of the time, Pallas kernels for 22%

profile of v11, /device:TPU:0, one launch (start us, length us, event | category | flops | bytes accessed | tf_op | source)
XLA Modules:
  0.0 80.5 jit_solution(2149276750903409133)
XLA Ops:
  0.0 0.7 copy-done.2
  0.7 4.5 %place_first.1 = (s32[1,2048]{1,0:T(1,128)S(1)}, bf16[256,768]{1,0:T(8,128)(2,1)S(1)}, bf16[256,768]{1,0:T(8,128)(2,1)S(1)}, bf16[256,768]{1,0:T(8,128)(2,1)S(1)}) custom-call(s32[1]{0:T(128)} %bitcast.1.refs_0_, s32[1,2048]{1,0:T(1,128)S(1)} %bitcast.3, bf16[2048,768]{1,0:T(8,128)(2,1)} %refs_2_.5), custom_call_target="tpu_custom_call" | custom-call | flops 2415919104 | bytes 6291456 | tf_op jit(solution)/shard_map/place_first/pallas_call | solution.py:48
  5.2 4.0 %collective-permute-start.3 = (bf16[256,768]{1,0:T(8,128)(2,1)S(1)}, bf16[256,768]{1,0:T(8,128)(2,1)}, u32[]{:S(2)}, u32[]{:S(2)}) collective-permute-start(bf16[256,768]{1,0:T(8,128)(2,1)S(1)} %get-tuple-element.53), channel_id=1, source_target_pairs={{0,24},{8,16},{16,8},{24,0},{1,25},{9,17},{17,9},{25,1},{2,26},{10... | collective-permute-start | bytes 1179656 | tf_op jit(solution)/shard_map/ppermute | solution.py:383
  9.2 0.5 collective-permute-start.4
  9.7 0.1 collective-permute-start.5
  9.8 6.2 %place_rest.1 = (bf16[256,768]{1,0:T(8,128)(2,1)S(1)}, bf16[256,768]{1,0:T(8,128)(2,1)S(1)}, bf16[256,768]{1,0:T(8,128)(2,1)S(1)}, bf16[256,768]{1,0:T(8,128)(2,1)S(1)}, bf16[256,768]{1,0:T(8,128)(2,1)S(1)}) custom-call(s32[1]{0:T(128)} %bitcast.1.refs_0_, s32[1,2048]{1,0:T(1,128)S(1)} %get-tuple-element.47.refs_1_, bf16[2048,768]{1,0:T(8,128)(2,1)} %refs_2_.5), custom_call_target="tpu_custom_call" | custom-call | flops 4026531840 | bytes 6291456 | tf_op jit(solution)/shard_map/place_rest/pallas_call | solution.py:48
  16.0 0.0 copy-start.3
  16.0 0.7 copy-done.3
  16.8 0.8 copy-done.5
  17.5 2.8 %collective-permute-start = (bf16[256,768]{1,0:T(8,128)(2,1)S(1)}, bf16[256,768]{1,0:T(8,128)(2,1)S(1)}, u32[]{:S(2)}, u32[]{:S(2)}) collective-permute-start(bf16[256,768]{1,0:T(8,128)(2,1)S(1)} %get-tuple-element.49), channel_id=1, source_target_pairs={{0,24},{8,16},{16,8},{24,0},{1,25},{9,17},{17,9},{25,1},{2,26},{10... | collective-permute-start | bytes 1179656 | tf_op jit(solution)/shard_map/ppermute | solution.py:383
  20.4 0.0 collective-permute-done.3.refs_1_
  20.4 1.0 %copy-done.6 = bf16[256,768]{1,0:T(8,128)(2,1)S(1)} copy-done((bf16[256,768]{1,0:T(8,128)(2,1)S(1)}, bf16[256,768]{1,0:T(8,128)(2,1)}, u32[]{:S(2)}) %copy-start.6) | copy-done | bytes 393240
  21.4 1.6 %begin_0.1.refs_1_ = f32[2312,128]{1,0:T(8,128)S(1)} custom-call(bf16[256,768]{1,0:T(8,128)(2,1)S(1)} %copy-done.6, bf16[256,768]{1,0:T(8,128)(2,1)} %collective-permute-done.3.refs_1_), custom_call_target="tpu_custom_call" | custom-call | flops 603979776 | bytes 1179648 | tf_op jit(solution)/shard_map/begin_0/pallas_call | solution.py:48
  23.0 0.0 copy-start.4
  23.0 4.5 %collective-permute-done.4.refs_2_ = bf16[256,768]{1,0:T(8,128)(2,1)S(1)} collective-permute-done((bf16[256,768]{1,0:T(8,128)(2,1)S(1)}, bf16[256,768]{1,0:T(8,128)(2,1)S(1)}, u32[]{:S(2)}, u32[]{:S(2)}) %collective-permute-start.4) | collective-permute-done | bytes 393248 | tf_op jit(solution)/shard_map/ppermute | solution.py:383
  27.5 0.6 collective-permute-done.5.refs_3_
  28.2 0.8 gram_0.1
  29.0 0.1 collective-permute-start.6
  29.0 0.5 collective-permute-start.7
  29.5 1.4 %collective-permute-start.1 = (bf16[256,768]{1,0:T(8,128)(2,1)S(1)}, bf16[256,768]{1,0:T(8,128)(2,1)S(1)}, u32[]{:S(2)}, u32[]{:S(2)}) collective-permute-start(bf16[256,768]{1,0:T(8,128)(2,1)S(1)} %get-tuple-element.50), channel_id=1, source_target_pairs={{0,16},{8,24},{16,0},{24,8},{1,17},{9,25},{17,1},{25,9},{2,18},{10... | collective-permute-start | bytes 1179656 | tf_op jit(solution)/shard_map/ppermute | solution.py:383
  30.9 0.6 collective-permute-start.2
  31.5 4.5 %collective-permute-done.refs_1_ = bf16[256,768]{1,0:T(8,128)(2,1)S(1)} collective-permute-done((bf16[256,768]{1,0:T(8,128)(2,1)S(1)}, bf16[256,768]{1,0:T(8,128)(2,1)S(1)}, u32[]{:S(2)}, u32[]{:S(2)}) %collective-permute-start) | collective-permute-done | bytes 393248 | tf_op jit(solution)/shard_map/ppermute | solution.py:383
  36.1 0.6 begin_1.1.refs_5_.refs_1_
  36.7 0.0 collective-permute-done.7.refs_4_
  36.7 0.4 stage_0_1.1
  37.1 2.1 %collective-permute-start.8 = (s16[608,128]{1,0:T(8,128)(2,1)S(1)}, s16[608,128]{1,0:T(8,128)(2,1)S(1)}, u32[]{:S(2)}, u32[]{:S(2)}) collective-permute-start(s16[608,128]{1,0:T(8,128)(2,1)S(1)} %get-tuple-element.62), channel_id=1, source_target_pairs={{0,2},{1,3},{2,0},{3,1},{4,6},{5,7},{6,4},{7,5},{8,10},{9,11},{10,... | collective-permute-start | bytes 466952 | tf_op jit(solution)/shard_map/ppermute | solution.py:386
  39.3 3.2 %collective-permute-done.8.refs_3_ = s16[608,128]{1,0:T(8,128)(2,1)S(1)} collective-permute-done((s16[608,128]{1,0:T(8,128)(2,1)S(1)}, s16[608,128]{1,0:T(8,128)(2,1)S(1)}, u32[]{:S(2)}, u32[]{:S(2)}) %collective-permute-start.8) | collective-permute-done | bytes 155680 | tf_op jit(solution)/shard_map/ppermute | solution.py:386
  42.5 0.6 stage_0_2.1
  43.1 3.1 %collective-permute-start.13 = (s16[608,128]{1,0:T(8,128)(2,1)S(1)}, s16[608,128]{1,0:T(8,128)(2,1)S(1)}, u32[]{:S(2)}, u32[]{:S(2)}) collective-permute-start(s16[608,128]{1,0:T(8,128)(2,1)S(1)} %get-tuple-element.63.refs_4_), channel_id=1, source_target_pairs={{0,4},{1,5},{2,6},{3,7},{4,0},{5,1},{6,2},{7,3},{8,12},{9,13},{10,... | collective-permute-start | bytes 466952 | tf_op jit(solution)/shard_map/ppermute | solution.py:386
  46.2 0.0 collective-permute-done.1.refs_2_
  46.2 0.0 collective-permute-done.2.refs_3_
  46.2 0.8 gram_1.1
  47.0 0.1 collective-permute-start.9
  47.1 0.5 collective-permute-start.10
  47.6 0.1 collective-permute-start.11
  47.7 0.4 collective-permute-start.12
  48.1 3.0 %collective-permute-done.13.refs_3_ = s16[608,128]{1,0:T(8,128)(2,1)S(1)} collective-permute-done((s16[608,128]{1,0:T(8,128)(2,1)S(1)}, s16[608,128]{1,0:T(8,128)(2,1)S(1)}, u32[]{:S(2)}, u32[]{:S(2)}) %collective-permute-start.13) | collective-permute-done | bytes 155680 | tf_op jit(solution)/shard_map/ppermute | solution.py:386
  51.1 0.5 total_0.1
  51.6 0.0 collective-permute-done.10.refs_4_
  51.6 0.0 collective-permute-done.12.refs_6_
  51.7 0.0 collective-permute-done.9.refs_3_
  51.7 0.4 stage_1_1.1
  52.1 1.1 %collective-permute-start.14 = (s16[608,128]{1,0:T(8,128)(2,1)S(1)}, s16[608,128]{1,0:T(8,128)(2,1)S(1)}, u32[]{:S(2)}, u32[]{:S(2)}) collective-permute-start(s16[608,128]{1,0:T(8,128)(2,1)S(1)} %get-tuple-element.75), channel_id=1, source_target_pairs={{0,2},{1,3},{2,0},{3,1},{4,6},{5,7},{6,4},{7,5},{8,10},{9,11},{10,... | collective-permute-start | bytes 466952 | tf_op jit(solution)/shard_map/ppermute | solution.py:386
  53.1 1.0 %collective-permute-start.16 = (s16[592,128]{1,0:T(8,128)(2,1)S(1)}, s16[592,128]{1,0:T(8,128)(2,1)S(1)}, u32[]{:S(2)}, u32[]{:S(2)}) collective-permute-start(s16[592,128]{1,0:T(8,128)(2,1)S(1)} %get-tuple-element.72.refs_7_.refs_2_), channel_id=1, source_target_pairs={{0,2},{1,3},{2,0},{3,1},{4,6},{5,7},{6,4},{7,5},{8,10},{9,11},{10,... | collective-permute-start | bytes 454664 | tf_op jit(solution)/shard_map/ppermute | solution.py:386
  54.2 3.3 %collective-permute-done.14.refs_3_ = s16[608,128]{1,0:T(8,128)(2,1)S(1)} collective-permute-done((s16[608,128]{1,0:T(8,128)(2,1)S(1)}, s16[608,128]{1,0:T(8,128)(2,1)S(1)}, u32[]{:S(2)}, u32[]{:S(2)}) %collective-permute-start.14) | collective-permute-done | bytes 155680 | tf_op jit(solution)/shard_map/ppermute | solution.py:386
  57.5 0.8 stage_1_2.1
  58.3 0.0 copy-start
  58.3 0.0 copy-start.1
  58.3 2.4 %collective-permute-start.15 = (s16[608,128]{1,0:T(8,128)(2,1)S(1)}, s16[608,128]{1,0:T(8,128)(2,1)S(1)}, u32[]{:S(2)}, u32[]{:S(2)}) collective-permute-start(s16[608,128]{1,0:T(8,128)(2,1)S(1)} %get-tuple-element.78), channel_id=1, source_target_pairs={{0,4},{1,5},{2,6},{3,7},{4,0},{5,1},{6,2},{7,3},{8,12},{9,13},{10,... | collective-permute-start | bytes 466952 | tf_op jit(solution)/shard_map/ppermute | solution.py:386
  60.7 0.0 collective-permute-start.17
  60.7 0.0 collective-permute-done.16.refs_3_
  60.7 0.5 collective-permute-start.18
  61.2 0.9 %collective-permute-done.17.refs_4_ = s16[592,128]{1,0:T(8,128)(2,1)S(1)} collective-permute-done((s16[592,128]{1,0:T(8,128)(2,1)S(1)}, s16[592,128]{1,0:T(8,128)(2,1)S(1)}, u32[]{:S(2)}, u32[]{:S(2)}) %collective-permute-start.17) | collective-permute-done | bytes 151584 | tf_op jit(solution)/shard_map/ppermute | solution.py:386
  62.0 0.2 collective-permute-done.18.refs_5_
  62.3 0.7 unpack_0.1
  63.0 1.5 %collective-permute-done.15.refs_3_ = s16[608,128]{1,0:T(8,128)(2,1)S(1)} collective-permute-done((s16[608,128]{1,0:T(8,128)(2,1)S(1)}, s16[608,128]{1,0:T(8,128)(2,1)S(1)}, u32[]{:S(2)}, u32[]{:S(2)}) %collective-permute-start.15) | collective-permute-done | bytes 155680 | tf_op jit(solution)/shard_map/ppermute | solution.py:386
  64.5 0.6 total_1.1
  65.1 0.1 collective-permute-start.20
  65.1 2.4 %collective-permute-start.19 = (s16[592,128]{1,0:T(8,128)(2,1)S(1)}, s16[592,128]{1,0:T(8,128)(2,1)S(1)}, u32[]{:S(2)}, u32[]{:S(2)}) collective-permute-start(s16[592,128]{1,0:T(8,128)(2,1)S(1)} %get-tuple-element.82.refs_5_.refs_2_), channel_id=1, source_target_pairs={{0,2},{1,3},{2,0},{3,1},{4,6},{5,7},{6,4},{7,5},{8,10},{9,11},{10,... | collective-permute-start | bytes 454664 | tf_op jit(solution)/shard_map/ppermute | solution.py:386
  67.5 5.0 %sweeps_0.1 = (f32[2,256,768]{2,1,0:T(8,128)}, f32[8,128]{1,0:T(8,128)S(1)}) custom-call(f32[8,128]{1,0:T(8,128)S(1)} %get-tuple-element.79.refs_1_.refs_0_, bf16[2,256,768]{2,1,0:T(8,128)(2,1)S(1)} %copy-done, bf16[2,256,768]{2,1,0:T(8,128)(2,1)S(1)} %copy-done.1, bf16[768,768]{1,0:T(8,128)(2,1)S(1)} %get-tuple-element.80.refs_4_.refs_3_, ...), custom_call_target="tpu_custom_call" | custom-call | flops 3623878656 | bytes 2359296 | tf_op jit(solution)/shard_map/sweeps_0/pallas_call | solution.py:48
  72.6 0.2 collective-permute-start.21
  72.8 1.2 %collective-permute-done.21.refs_5_ = s16[592,128]{1,0:T(8,128)(2,1)S(1)} collective-permute-done((s16[592,128]{1,0:T(8,128)(2,1)S(1)}, s16[592,128]{1,0:T(8,128)(2,1)S(1)}, u32[]{:S(2)}, u32[]{:S(2)}) %collective-permute-start.21) | collective-permute-done | bytes 151584 | tf_op jit(solution)/shard_map/ppermute | solution.py:386
  74.0 0.7 unpack_1.1
  74.8 5.6 %sweeps_1.1 = (f32[2,256,768]{2,1,0:T(8,128)}, f32[8,128]{1,0:T(8,128)}) custom-call(f32[8,128]{1,0:T(8,128)S(1)} %get-tuple-element.81.refs_1_.refs_0_, bf16[2,256,768]{2,1,0:T(8,128)(2,1)S(1)} %copy-done, bf16[2,256,768]{2,1,0:T(8,128)(2,1)S(1)} %copy-done.1, bf16[768,768]{1,0:T(8,128)(2,1)S(1)} %get-tuple-element.85.refs_3_, ...), custom_call_target="tpu_custom_call", output_to_operand_aliasing={{0}: (5, {})} | custom-call | flops 3623878656 | bytes 2359296 | tf_op jit(solution)/shard_map/sweeps_1/pallas_call | solution.py:48
  (11 shorter events, 0.0 us)
Async XLA Ops:
  0.0 0.7 copy-start.2
  5.2 15.1 %collective-permute-start.3 = (bf16[256,768]{1,0:T(8,128)(2,1)S(1)}, bf16[256,768]{1,0:T(8,128)(2,1)}, u32[]{:S(2)}, u32[]{:S(2)}) collective-permute-start(bf16[256,768]{1,0:T(8,128)(2,1)S(1)} %get-tuple-element.53), channel_id=1, source_target_pairs={{0,24},{8,16},{16,8},{24,0},{1,25},{9,17},{17,9},{25,1},{2,26},{10... | collective-permute-start | bytes 1179656 | tf_op jit(solution)/shard_map/ppermute | solution.py:383
  9.2 18.3 %collective-permute-start.4 = (bf16[256,768]{1,0:T(8,128)(2,1)S(1)}, bf16[256,768]{1,0:T(8,128)(2,1)S(1)}, u32[]{:S(2)}, u32[]{:S(2)}) collective-permute-start(bf16[256,768]{1,0:T(8,128)(2,1)S(1)} %get-tuple-element.54), channel_id=1, source_target_pairs={{0,16},{8,24},{16,0},{24,8},{1,17},{9,25},{17,1},{25,9},{2,18},{10... | collective-permute-start | bytes 1179656 | tf_op jit(solution)/shard_map/ppermute | solution.py:383
  9.7 18.5 %collective-permute-start.5 = (bf16[256,768]{1,0:T(8,128)(2,1)S(1)}, bf16[256,768]{1,0:T(8,128)(2,1)S(1)}, u32[]{:S(2)}, u32[]{:S(2)}) collective-permute-start(bf16[256,768]{1,0:T(8,128)(2,1)S(1)} %get-tuple-element.55), channel_id=1, source_target_pairs={{0,8},{8,0},{16,24},{24,16},{1,9},{9,1},{17,25},{25,17},{2,10},{10... | collective-permute-start | bytes 1179656 | tf_op jit(solution)/shard_map/ppermute | solution.py:383
  16.0 0.7 copy-start.3
  16.8 0.8 copy-start.5
  17.5 18.6 %collective-permute-start = (bf16[256,768]{1,0:T(8,128)(2,1)S(1)}, bf16[256,768]{1,0:T(8,128)(2,1)S(1)}, u32[]{:S(2)}, u32[]{:S(2)}) collective-permute-start(bf16[256,768]{1,0:T(8,128)(2,1)S(1)} %get-tuple-element.49), channel_id=1, source_target_pairs={{0,24},{8,16},{16,8},{24,0},{1,25},{9,17},{17,9},{25,1},{2,26},{10... | collective-permute-start | bytes 1179656 | tf_op jit(solution)/shard_map/ppermute | solution.py:383
  20.4 1.0 %copy-start.6 = (bf16[256,768]{1,0:T(8,128)(2,1)S(1)}, bf16[256,768]{1,0:T(8,128)(2,1)}, u32[]{:S(2)}) copy-start(bf16[256,768]{1,0:T(8,128)(2,1)} %copy-done.5) | copy-start | bytes 1179652
  23.0 13.1 %copy-start.4 = (bf16[256,768]{1,0:T(8,128)(2,1)S(1)}, bf16[256,768]{1,0:T(8,128)(2,1)}, u32[]{:S(2)}) copy-start(bf16[256,768]{1,0:T(8,128)(2,1)} %copy-done.3) | copy-start | bytes 1179652
  29.0 7.7 %collective-permute-start.6 = (f32[584,128]{1,0:T(8,128)S(1)}, f32[584,128]{1,0:T(8,128)S(1)}, u32[]{:S(2)}, u32[]{:S(2)}) collective-permute-start(f32[584,128]{1,0:T(8,128)S(1)} %get-tuple-element.58), channel_id=1, source_target_pairs={{0,1},{1,0},{2,3},{3,2},{4,5},{5,4},{6,7},{7,6},{8,9},{9,8},{10,11... | collective-permute-start | bytes 897032 | tf_op jit(solution)/shard_map/ppermute | solution.py:386
  29.0 7.7 %collective-permute-start.7 = (f32[576,128]{1,0:T(8,128)S(1)}, f32[576,128]{1,0:T(8,128)S(1)}, u32[]{:S(2)}, u32[]{:S(2)}) collective-permute-start(f32[576,128]{1,0:T(8,128)S(1)} %get-tuple-element.59), channel_id=1, source_target_pairs={{0,1},{1,0},{2,3},{3,2},{4,5},{5,4},{6,7},{7,6},{8,9},{9,8},{10,11... | collective-permute-start | bytes 884744 | tf_op jit(solution)/shard_map/ppermute | solution.py:386
  29.5 16.7 %collective-permute-start.1 = (bf16[256,768]{1,0:T(8,128)(2,1)S(1)}, bf16[256,768]{1,0:T(8,128)(2,1)S(1)}, u32[]{:S(2)}, u32[]{:S(2)}) collective-permute-start(bf16[256,768]{1,0:T(8,128)(2,1)S(1)} %get-tuple-element.50), channel_id=1, source_target_pairs={{0,16},{8,24},{16,0},{24,8},{1,17},{9,25},{17,1},{25,9},{2,18},{10... | collective-permute-start | bytes 1179656 | tf_op jit(solution)/shard_map/ppermute | solution.py:383
  30.9 15.3 %collective-permute-start.2 = (bf16[256,768]{1,0:T(8,128)(2,1)S(1)}, bf16[256,768]{1,0:T(8,128)(2,1)S(1)}, u32[]{:S(2)}, u32[]{:S(2)}) collective-permute-start(bf16[256,768]{1,0:T(8,128)(2,1)S(1)} %get-tuple-element.51), channel_id=1, source_target_pairs={{0,8},{8,0},{16,24},{24,16},{1,9},{9,1},{17,25},{25,17},{2,10},{10... | collective-permute-start | bytes 1179656 | tf_op jit(solution)/shard_map/ppermute | solution.py:383
  37.1 5.4 %collective-permute-start.8 = (s16[608,128]{1,0:T(8,128)(2,1)S(1)}, s16[608,128]{1,0:T(8,128)(2,1)S(1)}, u32[]{:S(2)}, u32[]{:S(2)}) collective-permute-start(s16[608,128]{1,0:T(8,128)(2,1)S(1)} %get-tuple-element.62), channel_id=1, source_target_pairs={{0,2},{1,3},{2,0},{3,1},{4,6},{5,7},{6,4},{7,5},{8,10},{9,11},{10,... | collective-permute-start | bytes 466952 | tf_op jit(solution)/shard_map/ppermute | solution.py:386
  43.1 8.0 %collective-permute-start.13 = (s16[608,128]{1,0:T(8,128)(2,1)S(1)}, s16[608,128]{1,0:T(8,128)(2,1)S(1)}, u32[]{:S(2)}, u32[]{:S(2)}) collective-permute-start(s16[608,128]{1,0:T(8,128)(2,1)S(1)} %get-tuple-element.63.refs_4_), channel_id=1, source_target_pairs={{0,4},{1,5},{2,6},{3,7},{4,0},{5,1},{6,2},{7,3},{8,12},{9,13},{10,... | collective-permute-start | bytes 466952 | tf_op jit(solution)/shard_map/ppermute | solution.py:386
  47.0 4.7 %collective-permute-start.9 = (f32[296,128]{1,0:T(8,128)S(1)}, f32[296,128]{1,0:T(8,128)S(1)}, u32[]{:S(2)}, u32[]{:S(2)}) collective-permute-start(f32[296,128]{1,0:T(8,128)S(1)} %get-tuple-element.66), channel_id=1, source_target_pairs={{0,1},{1,0},{2,3},{3,2},{4,5},{5,4},{6,7},{7,6},{8,9},{9,8},{10,11... | collective-permute-start | bytes 454664 | tf_op jit(solution)/shard_map/ppermute | solution.py:386
  47.1 4.6 %collective-permute-start.10 = (f32[288,128]{1,0:T(8,128)S(1)}, f32[288,128]{1,0:T(8,128)S(1)}, u32[]{:S(2)}, u32[]{:S(2)}) collective-permute-start(f32[288,128]{1,0:T(8,128)S(1)} %get-tuple-element.67), channel_id=1, source_target_pairs={{0,1},{1,0},{2,3},{3,2},{4,5},{5,4},{6,7},{7,6},{8,9},{9,8},{10,11... | collective-permute-start | bytes 442376 | tf_op jit(solution)/shard_map/ppermute | solution.py:386
  47.6 4.1 %collective-permute-start.11 = (f32[288,128]{1,0:T(8,128)S(1)}, f32[288,128]{1,0:T(8,128)S(1)}, u32[]{:S(2)}, u32[]{:S(2)}) collective-permute-start(f32[288,128]{1,0:T(8,128)S(1)} %get-tuple-element.68), channel_id=1, source_target_pairs={{0,1},{1,0},{2,3},{3,2},{4,5},{5,4},{6,7},{7,6},{8,9},{9,8},{10,11... | collective-permute-start | bytes 442376 | tf_op jit(solution)/shard_map/ppermute | solution.py:386
  47.7 4.0 %collective-permute-start.12 = (f32[288,128]{1,0:T(8,128)S(1)}, f32[288,128]{1,0:T(8,128)S(1)}, u32[]{:S(2)}, u32[]{:S(2)}) collective-permute-start(f32[288,128]{1,0:T(8,128)S(1)} %get-tuple-element.69), channel_id=1, source_target_pairs={{0,1},{1,0},{2,3},{3,2},{4,5},{5,4},{6,7},{7,6},{8,9},{9,8},{10,11... | collective-permute-start | bytes 442376 | tf_op jit(solution)/shard_map/ppermute | solution.py:386
  52.1 5.4 %collective-permute-start.14 = (s16[608,128]{1,0:T(8,128)(2,1)S(1)}, s16[608,128]{1,0:T(8,128)(2,1)S(1)}, u32[]{:S(2)}, u32[]{:S(2)}) collective-permute-start(s16[608,128]{1,0:T(8,128)(2,1)S(1)} %get-tuple-element.75), channel_id=1, source_target_pairs={{0,2},{1,3},{2,0},{3,1},{4,6},{5,7},{6,4},{7,5},{8,10},{9,11},{10,... | collective-permute-start | bytes 466952 | tf_op jit(solution)/shard_map/ppermute | solution.py:386
  53.1 7.5 %collective-permute-start.16 = (s16[592,128]{1,0:T(8,128)(2,1)S(1)}, s16[592,128]{1,0:T(8,128)(2,1)S(1)}, u32[]{:S(2)}, u32[]{:S(2)}) collective-permute-start(s16[592,128]{1,0:T(8,128)(2,1)S(1)} %get-tuple-element.72.refs_7_.refs_2_), channel_id=1, source_target_pairs={{0,2},{1,3},{2,0},{3,1},{4,6},{5,7},{6,4},{7,5},{8,10},{9,11},{10,... | collective-permute-start | bytes 454664 | tf_op jit(solution)/shard_map/ppermute | solution.py:386
  58.3 9.2 %copy-start = (bf16[2,256,768]{2,1,0:T(8,128)(2,1)S(1)}, bf16[2,256,768]{2,1,0:T(8,128)(2,1)}, u32[]{:S(2)}) copy-start(bf16[2,256,768]{2,1,0:T(8,128)(2,1)} %refs_1_.3) | copy-start | bytes 2359300
  58.3 9.2 %copy-start.1 = (bf16[2,256,768]{2,1,0:T(8,128)(2,1)S(1)}, bf16[2,256,768]{2,1,0:T(8,128)(2,1)}, u32[]{:S(2)}) copy-start(bf16[2,256,768]{2,1,0:T(8,128)(2,1)} %refs_2_.7) | copy-start | bytes 2359300
  58.3 6.2 %collective-permute-start.15 = (s16[608,128]{1,0:T(8,128)(2,1)S(1)}, s16[608,128]{1,0:T(8,128)(2,1)S(1)}, u32[]{:S(2)}, u32[]{:S(2)}) collective-permute-start(s16[608,128]{1,0:T(8,128)(2,1)S(1)} %get-tuple-element.78), channel_id=1, source_target_pairs={{0,4},{1,5},{2,6},{3,7},{4,0},{5,1},{6,2},{7,3},{8,12},{9,13},{10,... | collective-permute-start | bytes 466952 | tf_op jit(solution)/shard_map/ppermute | solution.py:386
  60.7 1.4 %collective-permute-start.17 = (s16[592,128]{1,0:T(8,128)(2,1)S(1)}, s16[592,128]{1,0:T(8,128)(2,1)S(1)}, u32[]{:S(2)}, u32[]{:S(2)}) collective-permute-start(s16[592,128]{1,0:T(8,128)(2,1)S(1)} %get-tuple-element.72.refs_7_.refs_2_), channel_id=1, source_target_pairs={{0,1},{1,0},{2,3},{3,2},{4,5},{5,4},{6,7},{7,6},{8,9},{9,8},{10,11... | collective-permute-start | bytes 454664 | tf_op jit(solution)/shard_map/ppermute | solution.py:386
  60.7 1.6 %collective-permute-start.18 = (s16[592,128]{1,0:T(8,128)(2,1)S(1)}, s16[592,128]{1,0:T(8,128)(2,1)S(1)}, u32[]{:S(2)}, u32[]{:S(2)}) collective-permute-start(s16[592,128]{1,0:T(8,128)(2,1)S(1)} %collective-permute-done.16.refs_3_), channel_id=1, source_target_pairs={{0,1},{1,0},{2,3},{3,2},{4,5},{5,4},{6,7},{7,6},{8,9},{9,8},{10,11... | collective-permute-start | bytes 454664 | tf_op jit(solution)/shard_map/ppermute | solution.py:386
  65.1 7.8 %collective-permute-start.20 = (s16[592,128]{1,0:T(8,128)(2,1)S(1)}, s16[592,128]{1,0:T(8,128)(2,1)S(1)}, u32[]{:S(2)}, u32[]{:S(2)}) collective-permute-start(s16[592,128]{1,0:T(8,128)(2,1)S(1)} %get-tuple-element.82.refs_5_.refs_2_), channel_id=1, source_target_pairs={{0,1},{1,0},{2,3},{3,2},{4,5},{5,4},{6,7},{7,6},{8,9},{9,8},{10,11... | collective-permute-start | bytes 454664 | tf_op jit(solution)/shard_map/ppermute | solution.py:386
  65.1 7.4 %collective-permute-start.19 = (s16[592,128]{1,0:T(8,128)(2,1)S(1)}, s16[592,128]{1,0:T(8,128)(2,1)S(1)}, u32[]{:S(2)}, u32[]{:S(2)}) collective-permute-start(s16[592,128]{1,0:T(8,128)(2,1)S(1)} %get-tuple-element.82.refs_5_.refs_2_), channel_id=1, source_target_pairs={{0,2},{1,3},{2,0},{3,1},{4,6},{5,7},{6,4},{7,5},{8,10},{9,11},{10,... | collective-permute-start | bytes 454664 | tf_op jit(solution)/shard_map/ppermute | solution.py:386
  72.6 1.4 %collective-permute-start.21 = (s16[592,128]{1,0:T(8,128)(2,1)S(1)}, s16[592,128]{1,0:T(8,128)(2,1)S(1)}, u32[]{:S(2)}, u32[]{:S(2)}) collective-permute-start(s16[592,128]{1,0:T(8,128)(2,1)S(1)} %relay.1.refs_3_), channel_id=1, source_target_pairs={{0,1},{1,0},{2,3},{3,2},{4,5},{5,4},{6,7},{7,6},{8,9},{9,8},{10,11... | collective-permute-start | bytes 454664 | tf_op jit(solution)/shard_map/ppermute | solution.py:386

commit v12 on v11

--- a/solution.py
+++ b/solution.py
@@ -488,7 +488,7 @@
     early = [begin(a, ()) for a in range(slots)]
     result, whole, total, sums, token = None, None, (), (), []
     for a in range(slots):
-        sums = reduce(a, early[a], sums[:1], [*early[a + 1:a + 2], *total[:1]])
+        sums = reduce(a, early[a], sums[:1], [*(rows[0] for rows in arrived[a + 1:a + 2]), *total[:1]])
         if a > 0:
             whole = gather(a - 1, pieces_of(total[0], token), total[1], ())
         total = end(a, sums, whole[1:2] if whole else ())

time: 80.8 us -> 81.4 us (level)
  waiting for transfers between devices: 23.1 us -> 26.7 us
  starting transfers between devices: 24 us -> 20.9 us
    ppermute x16, waiting for transfers between devices: 13.3 us -> 17 us  [over_rows(): lax.ppermute(array, 'rows', [(i, i ^ 1 << bit) for i in range(copies)])]
    ppermute x16, starting transfers between devices: 14.6 us -> 11.5 us  [over_rows(): lax.ppermute(array, 'rows', [(i, i ^ 1 << bit) for i in range(copies)])]
  transfers between devices with their start and end apart: 22 -> 22, of which waited for: 10 -> 12; matrix products, arithmetic and copies ran while one was open for 0% -> 0% of each run, Pallas kernels for 22% -> 22%
where the time goes in v12:
time: 81.4 us; the launch traced here: 81.1 us
  Pallas kernels  29.9 us (37%)
  waiting for transfers between devices  26.7 us (33%)
  starting transfers between devices  20.9 us (26%)
  local copies, waits for them, and re-layouts  3.21 us (4%)
    pallas_call x17, Pallas kernels, call(): return lambda *args: inner(*args, *after)  29.9 us
    ppermute x16, waiting for transfers between devices, over_rows(): lax.ppermute(array, 'rows', [(i, i ^ 1 << bit) for i in range(copies)])  17 us
    ppermute x16, starting transfers between devices, over_rows(): lax.ppermute(array, 'rows', [(i, i ^ 1 << bit) for i in range(copies)])  11.5 us
    ppermute x6, waiting for transfers between devices, over_experts(): return lax.ppermute(array, 'expert', [(i, i ^ flip) for i in range(peers)])  9.72 us
    ppermute x6, starting transfers between devices, over_experts(): return lax.ppermute(array, 'expert', [(i, i ^ flip) for i in range(peers)])  9.45 us
    unnamed x14, local copies, waits for them, and re-layouts  3.21 us
  transfers between devices with their start and end apart: 22, of which 12 were waited for; matrix products, arithmetic and copies ran while one was open for 0% of the time, Pallas kernels for 22%

profile of v12, /device:TPU:0, one launch (start us, length us, event | category | flops | bytes accessed | tf_op | source)
XLA Modules:
  0.0 81.1 jit_solution(6203415298700928876)
XLA Ops:
  0.0 0.7 copy-done.2
  0.7 4.5 %place_first.1 = (s32[1,2048]{1,0:T(1,128)S(1)}, bf16[256,768]{1,0:T(8,128)(2,1)S(1)}, bf16[256,768]{1,0:T(8,128)(2,1)S(1)}, bf16[256,768]{1,0:T(8,128)(2,1)S(1)}) custom-call(s32[1]{0:T(128)} %bitcast.1.refs_0_, s32[1,2048]{1,0:T(1,128)S(1)} %bitcast.3, bf16[2048,768]{1,0:T(8,128)(2,1)} %refs_2_.5), custom_call_target="tpu_custom_call" | custom-call | flops 2415919104 | bytes 6291456 | tf_op jit(solution)/shard_map/place_first/pallas_call | solution.py:48
  5.2 4.0 %collective-permute-start.3 = (bf16[256,768]{1,0:T(8,128)(2,1)S(1)}, bf16[256,768]{1,0:T(8,128)(2,1)}, u32[]{:S(2)}, u32[]{:S(2)}) collective-permute-start(bf16[256,768]{1,0:T(8,128)(2,1)S(1)} %get-tuple-element.53), channel_id=1, source_target_pairs={{0,24},{8,16},{16,8},{24,0},{1,25},{9,17},{17,9},{25,1},{2,26},{10... | collective-permute-start | bytes 1179656 | tf_op jit(solution)/shard_map/ppermute | solution.py:383
  9.2 0.5 collective-permute-start.4
  9.7 0.1 collective-permute-start.5
  9.8 6.2 %place_rest.1 = (bf16[256,768]{1,0:T(8,128)(2,1)S(1)}, bf16[256,768]{1,0:T(8,128)(2,1)S(1)}, bf16[256,768]{1,0:T(8,128)(2,1)S(1)}, bf16[256,768]{1,0:T(8,128)(2,1)S(1)}, bf16[256,768]{1,0:T(8,128)(2,1)S(1)}) custom-call(s32[1]{0:T(128)} %bitcast.1.refs_0_, s32[1,2048]{1,0:T(1,128)S(1)} %get-tuple-element.47.refs_1_, bf16[2048,768]{1,0:T(8,128)(2,1)} %refs_2_.5), custom_call_target="tpu_custom_call" | custom-call | flops 4026531840 | bytes 6291456 | tf_op jit(solution)/shard_map/place_rest/pallas_call | solution.py:48
  16.0 0.0 copy-start.3
  16.0 0.7 copy-done.3
  16.8 0.8 copy-done.5
  17.5 2.8 %collective-permute-start = (bf16[256,768]{1,0:T(8,128)(2,1)S(1)}, bf16[256,768]{1,0:T(8,128)(2,1)S(1)}, u32[]{:S(2)}, u32[]{:S(2)}) collective-permute-start(bf16[256,768]{1,0:T(8,128)(2,1)S(1)} %get-tuple-element.49), channel_id=1, source_target_pairs={{0,24},{8,16},{16,8},{24,0},{1,25},{9,17},{17,9},{25,1},{2,26},{10... | collective-permute-start | bytes 1179656 | tf_op jit(solution)/shard_map/ppermute | solution.py:383
  20.4 0.0 collective-permute-done.3.refs_1_
  20.4 1.0 %copy-done.6 = bf16[256,768]{1,0:T(8,128)(2,1)S(1)} copy-done((bf16[256,768]{1,0:T(8,128)(2,1)S(1)}, bf16[256,768]{1,0:T(8,128)(2,1)}, u32[]{:S(2)}) %copy-start.6) | copy-done | bytes 393240
  21.4 1.6 %begin_0.1.refs_1_ = f32[2312,128]{1,0:T(8,128)S(1)} custom-call(bf16[256,768]{1,0:T(8,128)(2,1)S(1)} %copy-done.6, bf16[256,768]{1,0:T(8,128)(2,1)} %collective-permute-done.3.refs_1_), custom_call_target="tpu_custom_call" | custom-call | flops 603979776 | bytes 1179648 | tf_op jit(solution)/shard_map/begin_0/pallas_call | solution.py:48
  23.0 4.5 %collective-permute-done.4.refs_2_ = bf16[256,768]{1,0:T(8,128)(2,1)S(1)} collective-permute-done((bf16[256,768]{1,0:T(8,128)(2,1)S(1)}, bf16[256,768]{1,0:T(8,128)(2,1)S(1)}, u32[]{:S(2)}, u32[]{:S(2)}) %collective-permute-start.4) | collective-permute-done | bytes 393248 | tf_op jit(solution)/shard_map/ppermute | solution.py:383
  27.5 0.6 collective-permute-done.5.refs_3_
  28.2 0.8 gram_0.1
  29.0 0.0 copy-start.4
  29.0 0.1 collective-permute-start.6
  29.1 0.5 collective-permute-start.7
  29.6 1.4 %collective-permute-start.1 = (bf16[256,768]{1,0:T(8,128)(2,1)S(1)}, bf16[256,768]{1,0:T(8,128)(2,1)S(1)}, u32[]{:S(2)}, u32[]{:S(2)}) collective-permute-start(bf16[256,768]{1,0:T(8,128)(2,1)S(1)} %get-tuple-element.50), channel_id=1, source_target_pairs={{0,16},{8,24},{16,0},{24,8},{1,17},{9,25},{17,1},{25,9},{2,18},{10... | collective-permute-start | bytes 1179656 | tf_op jit(solution)/shard_map/ppermute | solution.py:383
  30.9 0.6 collective-permute-start.2
  31.6 4.5 %collective-permute-done.refs_1_.refs_5_ = bf16[256,768]{1,0:T(8,128)(2,1)S(1)} collective-permute-done((bf16[256,768]{1,0:T(8,128)(2,1)S(1)}, bf16[256,768]{1,0:T(8,128)(2,1)S(1)}, u32[]{:S(2)}, u32[]{:S(2)}) %collective-permute-start) | collective-permute-done | bytes 393248 | tf_op jit(solution)/shard_map/ppermute | solution.py:383
  36.1 0.0 collective-permute-done.7.refs_4_
  36.1 0.0 collective-permute-done.6.refs_3_
  36.1 0.4 stage_0_1.1
  36.5 2.1 %collective-permute-start.8 = (s16[608,128]{1,0:T(8,128)(2,1)S(1)}, s16[608,128]{1,0:T(8,128)(2,1)S(1)}, u32[]{:S(2)}, u32[]{:S(2)}) collective-permute-start(s16[608,128]{1,0:T(8,128)(2,1)S(1)} %get-tuple-element.62), channel_id=1, source_target_pairs={{0,2},{1,3},{2,0},{3,1},{4,6},{5,7},{6,4},{7,5},{8,10},{9,11},{10,... | collective-permute-start | bytes 466952 | tf_op jit(solution)/shard_map/ppermute | solution.py:386
  38.6 3.2 %collective-permute-done.8.refs_3_ = s16[608,128]{1,0:T(8,128)(2,1)S(1)} collective-permute-done((s16[608,128]{1,0:T(8,128)(2,1)S(1)}, s16[608,128]{1,0:T(8,128)(2,1)S(1)}, u32[]{:S(2)}, u32[]{:S(2)}) %collective-permute-start.8) | collective-permute-done | bytes 155680 | tf_op jit(solution)/shard_map/ppermute | solution.py:386
  41.8 0.6 stage_0_2.1
  42.5 3.1 %collective-permute-start.13 = (s16[608,128]{1,0:T(8,128)(2,1)S(1)}, s16[608,128]{1,0:T(8,128)(2,1)S(1)}, u32[]{:S(2)}, u32[]{:S(2)}) collective-permute-start(s16[608,128]{1,0:T(8,128)(2,1)S(1)} %get-tuple-element.63.refs_4_), channel_id=1, source_target_pairs={{0,4},{1,5},{2,6},{3,7},{4,0},{5,1},{6,2},{7,3},{8,12},{9,13},{10,... | collective-permute-start | bytes 466952 | tf_op jit(solution)/shard_map/ppermute | solution.py:386
  45.6 0.6 begin_1.1.refs_1_
  46.2 0.0 collective-permute-done.1.refs_2_
  46.2 0.0 collective-permute-done.2.refs_3_
  46.2 0.8 gram_1.1
  47.0 0.1 collective-permute-start.9
  47.1 0.5 collective-permute-start.10
  47.6 0.1 collective-permute-start.11
  47.7 0.4 collective-permute-start.12
  48.1 2.3 %collective-permute-done.13.refs_3_ = s16[608,128]{1,0:T(8,128)(2,1)S(1)} collective-permute-done((s16[608,128]{1,0:T(8,128)(2,1)S(1)}, s16[608,128]{1,0:T(8,128)(2,1)S(1)}, u32[]{:S(2)}, u32[]{:S(2)}) %collective-permute-start.13) | collective-permute-done | bytes 155680 | tf_op jit(solution)/shard_map/ppermute | solution.py:386
  50.4 0.6 total_0.1
  51.0 0.0 collective-permute-done.10.refs_4_
  51.0 0.0 collective-permute-done.11.refs_5_
  51.0 0.4 stage_1_1.1
  51.4 1.1 %collective-permute-start.14 = (s16[608,128]{1,0:T(8,128)(2,1)S(1)}, s16[608,128]{1,0:T(8,128)(2,1)S(1)}, u32[]{:S(2)}, u32[]{:S(2)}) collective-permute-start(s16[608,128]{1,0:T(8,128)(2,1)S(1)} %get-tuple-element.75), channel_id=1, source_target_pairs={{0,2},{1,3},{2,0},{3,1},{4,6},{5,7},{6,4},{7,5},{8,10},{9,11},{10,... | collective-permute-start | bytes 466952 | tf_op jit(solution)/shard_map/ppermute | solution.py:386
  52.5 1.0 %collective-permute-start.16 = (s16[592,128]{1,0:T(8,128)(2,1)S(1)}, s16[592,128]{1,0:T(8,128)(2,1)S(1)}, u32[]{:S(2)}, u32[]{:S(2)}) collective-permute-start(s16[592,128]{1,0:T(8,128)(2,1)S(1)} %get-tuple-element.72.refs_7_.refs_2_), channel_id=1, source_target_pairs={{0,2},{1,3},{2,0},{3,1},{4,6},{5,7},{6,4},{7,5},{8,10},{9,11},{10,... | collective-permute-start | bytes 454664 | tf_op jit(solution)/shard_map/ppermute | solution.py:386
  53.5 4.0 %collective-permute-done.14.refs_3_ = s16[608,128]{1,0:T(8,128)(2,1)S(1)} collective-permute-done((s16[608,128]{1,0:T(8,128)(2,1)S(1)}, s16[608,128]{1,0:T(8,128)(2,1)S(1)}, u32[]{:S(2)}, u32[]{:S(2)}) %collective-permute-start.14) | collective-permute-done | bytes 155680 | tf_op jit(solution)/shard_map/ppermute | solution.py:386
  57.5 0.8 stage_1_2.1
  58.3 0.0 copy-start
  58.3 0.0 copy-start.1
  58.3 1.9 %collective-permute-start.15 = (s16[608,128]{1,0:T(8,128)(2,1)S(1)}, s16[608,128]{1,0:T(8,128)(2,1)S(1)}, u32[]{:S(2)}, u32[]{:S(2)}) collective-permute-start(s16[608,128]{1,0:T(8,128)(2,1)S(1)} %get-tuple-element.78), channel_id=1, source_target_pairs={{0,4},{1,5},{2,6},{3,7},{4,0},{5,1},{6,2},{7,3},{8,12},{9,13},{10,... | collective-permute-start | bytes 466952 | tf_op jit(solution)/shard_map/ppermute | solution.py:386
  60.2 0.5 collective-permute-done.16.refs_3_
  60.7 0.0 collective-permute-start.18
  60.7 0.9 %collective-permute-done.17.refs_4_ = s16[592,128]{1,0:T(8,128)(2,1)S(1)} collective-permute-done((s16[592,128]{1,0:T(8,128)(2,1)S(1)}, s16[592,128]{1,0:T(8,128)(2,1)S(1)}, u32[]{:S(2)}, u32[]{:S(2)}) %collective-permute-start.17) | collective-permute-done | bytes 151584 | tf_op jit(solution)/shard_map/ppermute | solution.py:386
  61.6 0.5 collective-permute-done.18.refs_5_
  62.1 0.7 unpack_0.1
  62.8 3.4 %collective-permute-done.15.refs_3_ = s16[608,128]{1,0:T(8,128)(2,1)S(1)} collective-permute-done((s16[608,128]{1,0:T(8,128)(2,1)S(1)}, s16[608,128]{1,0:T(8,128)(2,1)S(1)}, u32[]{:S(2)}, u32[]{:S(2)}) %collective-permute-start.15) | collective-permute-done | bytes 155680 | tf_op jit(solution)/shard_map/ppermute | solution.py:386
  66.2 0.6 total_1.1
  66.7 0.1 collective-permute-start.20
  66.8 0.5 collective-permute-start.19
  67.3 5.0 %sweeps_0.1 = (f32[2,256,768]{2,1,0:T(8,128)}, f32[8,128]{1,0:T(8,128)S(1)}) custom-call(f32[8,128]{1,0:T(8,128)S(1)} %get-tuple-element.79.refs_1_.refs_0_, bf16[2,256,768]{2,1,0:T(8,128)(2,1)S(1)} %copy-done, bf16[2,256,768]{2,1,0:T(8,128)(2,1)S(1)} %copy-done.1, bf16[768,768]{1,0:T(8,128)(2,1)S(1)} %get-tuple-element.80.refs_4_.refs_3_, ...), custom_call_target="tpu_custom_call" | custom-call | flops 3623878656 | bytes 2359296 | tf_op jit(solution)/shard_map/sweeps_0/pallas_call | solution.py:48
  72.3 0.8 %collective-permute-done.19.refs_0_ = s16[592,128]{1,0:T(8,128)(2,1)S(1)} collective-permute-done((s16[592,128]{1,0:T(8,128)(2,1)S(1)}, s16[592,128]{1,0:T(8,128)(2,1)S(1)}, u32[]{:S(2)}, u32[]{:S(2)}) %collective-permute-start.19) | collective-permute-done | bytes 151584 | tf_op jit(solution)/shard_map/ppermute | solution.py:386
  73.2 0.1 collective-permute-start.21
  73.3 1.4 %collective-permute-done.21.refs_5_ = s16[592,128]{1,0:T(8,128)(2,1)S(1)} collective-permute-done((s16[592,128]{1,0:T(8,128)(2,1)S(1)}, s16[592,128]{1,0:T(8,128)(2,1)S(1)}, u32[]{:S(2)}, u32[]{:S(2)}) %collective-permute-start.21) | collective-permute-done | bytes 151584 | tf_op jit(solution)/shard_map/ppermute | solution.py:386
  74.6 0.7 unpack_1.1
  75.3 5.6 %sweeps_1.1 = (f32[2,256,768]{2,1,0:T(8,128)}, f32[8,128]{1,0:T(8,128)}) custom-call(f32[8,128]{1,0:T(8,128)S(1)} %get-tuple-element.81.refs_1_.refs_0_, bf16[2,256,768]{2,1,0:T(8,128)(2,1)S(1)} %copy-done, bf16[2,256,768]{2,1,0:T(8,128)(2,1)S(1)} %copy-done.1, bf16[768,768]{1,0:T(8,128)(2,1)S(1)} %get-tuple-element.85.refs_3_, ...), custom_call_target="tpu_custom_call", output_to_operand_aliasing={{0}: (5, {})} | custom-call | flops 3623878656 | bytes 2359296 | tf_op jit(solution)/shard_map/sweeps_1/pallas_call | solution.py:48
  (11 shorter events, 0.0 us)
Async XLA Ops:
  0.0 0.7 copy-start.2
  5.2 15.1 %collective-permute-start.3 = (bf16[256,768]{1,0:T(8,128)(2,1)S(1)}, bf16[256,768]{1,0:T(8,128)(2,1)}, u32[]{:S(2)}, u32[]{:S(2)}) collective-permute-start(bf16[256,768]{1,0:T(8,128)(2,1)S(1)} %get-tuple-element.53), channel_id=1, source_target_pairs={{0,24},{8,16},{16,8},{24,0},{1,25},{9,17},{17,9},{25,1},{2,26},{10... | collective-permute-start | bytes 1179656 | tf_op jit(solution)/shard_map/ppermute | solution.py:383
  9.2 18.3 %collective-permute-start.4 = (bf16[256,768]{1,0:T(8,128)(2,1)S(1)}, bf16[256,768]{1,0:T(8,128)(2,1)S(1)}, u32[]{:S(2)}, u32[]{:S(2)}) collective-permute-start(bf16[256,768]{1,0:T(8,128)(2,1)S(1)} %get-tuple-element.54), channel_id=1, source_target_pairs={{0,16},{8,24},{16,0},{24,8},{1,17},{9,25},{17,1},{25,9},{2,18},{10... | collective-permute-start | bytes 1179656 | tf_op jit(solution)/shard_map/ppermute | solution.py:383
  9.7 18.5 %collective-permute-start.5 = (bf16[256,768]{1,0:T(8,128)(2,1)S(1)}, bf16[256,768]{1,0:T(8,128)(2,1)S(1)}, u32[]{:S(2)}, u32[]{:S(2)}) collective-permute-start(bf16[256,768]{1,0:T(8,128)(2,1)S(1)} %get-tuple-element.55), channel_id=1, source_target_pairs={{0,8},{8,0},{16,24},{24,16},{1,9},{9,1},{17,25},{25,17},{2,10},{10... | collective-permute-start | bytes 1179656 | tf_op jit(solution)/shard_map/ppermute | solution.py:383
  16.0 0.7 copy-start.3
  16.8 0.8 copy-start.5
  17.5 18.6 %collective-permute-start = (bf16[256,768]{1,0:T(8,128)(2,1)S(1)}, bf16[256,768]{1,0:T(8,128)(2,1)S(1)}, u32[]{:S(2)}, u32[]{:S(2)}) collective-permute-start(bf16[256,768]{1,0:T(8,128)(2,1)S(1)} %get-tuple-element.49), channel_id=1, source_target_pairs={{0,24},{8,16},{16,8},{24,0},{1,25},{9,17},{17,9},{25,1},{2,26},{10... | collective-permute-start | bytes 1179656 | tf_op jit(solution)/shard_map/ppermute | solution.py:383
  20.4 1.0 %copy-start.6 = (bf16[256,768]{1,0:T(8,128)(2,1)S(1)}, bf16[256,768]{1,0:T(8,128)(2,1)}, u32[]{:S(2)}) copy-start(bf16[256,768]{1,0:T(8,128)(2,1)} %copy-done.5) | copy-start | bytes 1179652
  29.0 16.6 %copy-start.4 = (bf16[256,768]{1,0:T(8,128)(2,1)S(1)}, bf16[256,768]{1,0:T(8,128)(2,1)}, u32[]{:S(2)}) copy-start(bf16[256,768]{1,0:T(8,128)(2,1)} %copy-done.3) | copy-start | bytes 1179652
  29.0 7.1 %collective-permute-start.6 = (f32[584,128]{1,0:T(8,128)S(1)}, f32[584,128]{1,0:T(8,128)S(1)}, u32[]{:S(2)}, u32[]{:S(2)}) collective-permute-start(f32[584,128]{1,0:T(8,128)S(1)} %get-tuple-element.58), channel_id=1, source_target_pairs={{0,1},{1,0},{2,3},{3,2},{4,5},{5,4},{6,7},{7,6},{8,9},{9,8},{10,11... | collective-permute-start | bytes 897032 | tf_op jit(solution)/shard_map/ppermute | solution.py:386
  29.1 7.0 %collective-permute-start.7 = (f32[576,128]{1,0:T(8,128)S(1)}, f32[576,128]{1,0:T(8,128)S(1)}, u32[]{:S(2)}, u32[]{:S(2)}) collective-permute-start(f32[576,128]{1,0:T(8,128)S(1)} %get-tuple-element.59), channel_id=1, source_target_pairs={{0,1},{1,0},{2,3},{3,2},{4,5},{5,4},{6,7},{7,6},{8,9},{9,8},{10,11... | collective-permute-start | bytes 884744 | tf_op jit(solution)/shard_map/ppermute | solution.py:386
  29.6 16.6 %collective-permute-start.1 = (bf16[256,768]{1,0:T(8,128)(2,1)S(1)}, bf16[256,768]{1,0:T(8,128)(2,1)S(1)}, u32[]{:S(2)}, u32[]{:S(2)}) collective-permute-start(bf16[256,768]{1,0:T(8,128)(2,1)S(1)} %get-tuple-element.50), channel_id=1, source_target_pairs={{0,16},{8,24},{16,0},{24,8},{1,17},{9,25},{17,1},{25,9},{2,18},{10... | collective-permute-start | bytes 1179656 | tf_op jit(solution)/shard_map/ppermute | solution.py:383
  30.9 15.3 %collective-permute-start.2 = (bf16[256,768]{1,0:T(8,128)(2,1)S(1)}, bf16[256,768]{1,0:T(8,128)(2,1)S(1)}, u32[]{:S(2)}, u32[]{:S(2)}) collective-permute-start(bf16[256,768]{1,0:T(8,128)(2,1)S(1)} %get-tuple-element.51), channel_id=1, source_target_pairs={{0,8},{8,0},{16,24},{24,16},{1,9},{9,1},{17,25},{25,17},{2,10},{10... | collective-permute-start | bytes 1179656 | tf_op jit(solution)/shard_map/ppermute | solution.py:383
  36.5 5.4 %collective-permute-start.8 = (s16[608,128]{1,0:T(8,128)(2,1)S(1)}, s16[608,128]{1,0:T(8,128)(2,1)S(1)}, u32[]{:S(2)}, u32[]{:S(2)}) collective-permute-start(s16[608,128]{1,0:T(8,128)(2,1)S(1)} %get-tuple-element.62), channel_id=1, source_target_pairs={{0,2},{1,3},{2,0},{3,1},{4,6},{5,7},{6,4},{7,5},{8,10},{9,11},{10,... | collective-permute-start | bytes 466952 | tf_op jit(solution)/shard_map/ppermute | solution.py:386
  42.5 8.0 %collective-permute-start.13 = (s16[608,128]{1,0:T(8,128)(2,1)S(1)}, s16[608,128]{1,0:T(8,128)(2,1)S(1)}, u32[]{:S(2)}, u32[]{:S(2)}) collective-permute-start(s16[608,128]{1,0:T(8,128)(2,1)S(1)} %get-tuple-element.63.refs_4_), channel_id=1, source_target_pairs={{0,4},{1,5},{2,6},{3,7},{4,0},{5,1},{6,2},{7,3},{8,12},{9,13},{10,... | collective-permute-start | bytes 466952 | tf_op jit(solution)/shard_map/ppermute | solution.py:386
  47.0 4.0 %collective-permute-start.9 = (f32[296,128]{1,0:T(8,128)S(1)}, f32[296,128]{1,0:T(8,128)S(1)}, u32[]{:S(2)}, u32[]{:S(2)}) collective-permute-start(f32[296,128]{1,0:T(8,128)S(1)} %get-tuple-element.66), channel_id=1, source_target_pairs={{0,1},{1,0},{2,3},{3,2},{4,5},{5,4},{6,7},{7,6},{8,9},{9,8},{10,11... | collective-permute-start | bytes 454664 | tf_op jit(solution)/shard_map/ppermute | solution.py:386
  47.1 3.9 %collective-permute-start.10 = (f32[288,128]{1,0:T(8,128)S(1)}, f32[288,128]{1,0:T(8,128)S(1)}, u32[]{:S(2)}, u32[]{:S(2)}) collective-permute-start(f32[288,128]{1,0:T(8,128)S(1)} %get-tuple-element.67), channel_id=1, source_target_pairs={{0,1},{1,0},{2,3},{3,2},{4,5},{5,4},{6,7},{7,6},{8,9},{9,8},{10,11... | collective-permute-start | bytes 442376 | tf_op jit(solution)/shard_map/ppermute | solution.py:386
  47.6 3.4 %collective-permute-start.11 = (f32[288,128]{1,0:T(8,128)S(1)}, f32[288,128]{1,0:T(8,128)S(1)}, u32[]{:S(2)}, u32[]{:S(2)}) collective-permute-start(f32[288,128]{1,0:T(8,128)S(1)} %get-tuple-element.68), channel_id=1, source_target_pairs={{0,1},{1,0},{2,3},{3,2},{4,5},{5,4},{6,7},{7,6},{8,9},{9,8},{10,11... | collective-permute-start | bytes 442376 | tf_op jit(solution)/shard_map/ppermute | solution.py:386
  47.7 3.4 %collective-permute-start.12 = (f32[288,128]{1,0:T(8,128)S(1)}, f32[288,128]{1,0:T(8,128)S(1)}, u32[]{:S(2)}, u32[]{:S(2)}) collective-permute-start(f32[288,128]{1,0:T(8,128)S(1)} %get-tuple-element.69), channel_id=1, source_target_pairs={{0,1},{1,0},{2,3},{3,2},{4,5},{5,4},{6,7},{7,6},{8,9},{9,8},{10,11... | collective-permute-start | bytes 442376 | tf_op jit(solution)/shard_map/ppermute | solution.py:386
  51.4 6.0 %collective-permute-start.14 = (s16[608,128]{1,0:T(8,128)(2,1)S(1)}, s16[608,128]{1,0:T(8,128)(2,1)S(1)}, u32[]{:S(2)}, u32[]{:S(2)}) collective-permute-start(s16[608,128]{1,0:T(8,128)(2,1)S(1)} %get-tuple-element.75), channel_id=1, source_target_pairs={{0,2},{1,3},{2,0},{3,1},{4,6},{5,7},{6,4},{7,5},{8,10},{9,11},{10,... | collective-permute-start | bytes 466952 | tf_op jit(solution)/shard_map/ppermute | solution.py:386
  52.5 8.2 %collective-permute-start.16 = (s16[592,128]{1,0:T(8,128)(2,1)S(1)}, s16[592,128]{1,0:T(8,128)(2,1)S(1)}, u32[]{:S(2)}, u32[]{:S(2)}) collective-permute-start(s16[592,128]{1,0:T(8,128)(2,1)S(1)} %get-tuple-element.72.refs_7_.refs_2_), channel_id=1, source_target_pairs={{0,2},{1,3},{2,0},{3,1},{4,6},{5,7},{6,4},{7,5},{8,10},{9,11},{10,... | collective-permute-start | bytes 454664 | tf_op jit(solution)/shard_map/ppermute | solution.py:386
  58.3 9.0 %copy-start = (bf16[2,256,768]{2,1,0:T(8,128)(2,1)S(1)}, bf16[2,256,768]{2,1,0:T(8,128)(2,1)}, u32[]{:S(2)}) copy-start(bf16[2,256,768]{2,1,0:T(8,128)(2,1)} %refs_1_.3) | copy-start | bytes 2359300
  58.3 9.0 %copy-start.1 = (bf16[2,256,768]{2,1,0:T(8,128)(2,1)S(1)}, bf16[2,256,768]{2,1,0:T(8,128)(2,1)}, u32[]{:S(2)}) copy-start(bf16[2,256,768]{2,1,0:T(8,128)(2,1)} %refs_2_.7) | copy-start | bytes 2359300
  58.3 7.9 %collective-permute-start.15 = (s16[608,128]{1,0:T(8,128)(2,1)S(1)}, s16[608,128]{1,0:T(8,128)(2,1)S(1)}, u32[]{:S(2)}, u32[]{:S(2)}) collective-permute-start(s16[608,128]{1,0:T(8,128)(2,1)S(1)} %get-tuple-element.78), channel_id=1, source_target_pairs={{0,4},{1,5},{2,6},{3,7},{4,0},{5,1},{6,2},{7,3},{8,12},{9,13},{10,... | collective-permute-start | bytes 466952 | tf_op jit(solution)/shard_map/ppermute | solution.py:386
  60.2 1.4 %collective-permute-start.17 = (s16[592,128]{1,0:T(8,128)(2,1)S(1)}, s16[592,128]{1,0:T(8,128)(2,1)S(1)}, u32[]{:S(2)}, u32[]{:S(2)}) collective-permute-start(s16[592,128]{1,0:T(8,128)(2,1)S(1)} %get-tuple-element.72.refs_7_.refs_2_), channel_id=1, source_target_pairs={{0,1},{1,0},{2,3},{3,2},{4,5},{5,4},{6,7},{7,6},{8,9},{9,8},{10,11... | collective-permute-start | bytes 454664 | tf_op jit(solution)/shard_map/ppermute | solution.py:386
  60.7 1.4 %collective-permute-start.18 = (s16[592,128]{1,0:T(8,128)(2,1)S(1)}, s16[592,128]{1,0:T(8,128)(2,1)S(1)}, u32[]{:S(2)}, u32[]{:S(2)}) collective-permute-start(s16[592,128]{1,0:T(8,128)(2,1)S(1)} %collective-permute-done.16.refs_3_), channel_id=1, source_target_pairs={{0,1},{1,0},{2,3},{3,2},{4,5},{5,4},{6,7},{7,6},{8,9},{9,8},{10,11... | collective-permute-start | bytes 454664 | tf_op jit(solution)/shard_map/ppermute | solution.py:386
  66.7 6.5 %collective-permute-start.20 = (s16[592,128]{1,0:T(8,128)(2,1)S(1)}, s16[592,128]{1,0:T(8,128)(2,1)S(1)}, u32[]{:S(2)}, u32[]{:S(2)}) collective-permute-start(s16[592,128]{1,0:T(8,128)(2,1)S(1)} %get-tuple-element.82.refs_5_.refs_2_), channel_id=1, source_target_pairs={{0,1},{1,0},{2,3},{3,2},{4,5},{5,4},{6,7},{7,6},{8,9},{9,8},{10,11... | collective-permute-start | bytes 454664 | tf_op jit(solution)/shard_map/ppermute | solution.py:386
  66.8 6.4 %collective-permute-start.19 = (s16[592,128]{1,0:T(8,128)(2,1)S(1)}, s16[592,128]{1,0:T(8,128)(2,1)S(1)}, u32[]{:S(2)}, u32[]{:S(2)}) collective-permute-start(s16[592,128]{1,0:T(8,128)(2,1)S(1)} %get-tuple-element.82.refs_5_.refs_2_), channel_id=1, source_target_pairs={{0,2},{1,3},{2,0},{3,1},{4,6},{5,7},{6,4},{7,5},{8,10},{9,11},{10,... | collective-permute-start | bytes 454664 | tf_op jit(solution)/shard_map/ppermute | solution.py:386
  73.2 1.4 %collective-permute-start.21 = (s16[592,128]{1,0:T(8,128)(2,1)S(1)}, s16[592,128]{1,0:T(8,128)(2,1)S(1)}, u32[]{:S(2)}, u32[]{:S(2)}) collective-permute-start(s16[592,128]{1,0:T(8,128)(2,1)S(1)} %relay.1.refs_3_), channel_id=1, source_target_pairs={{0,1},{1,0},{2,3},{3,2},{4,5},{5,4},{6,7},{7,6},{8,9},{9,8},{10,11... | collective-permute-start | bytes 454664 | tf_op jit(solution)/shard_map/ppermute | solution.py:386
